TPU v7x, 32 devices: a whole 2x2x4 slice. The times are simulated.
32 devices in a mesh: dp: 8 (over y, x, core), tensor: 4 (over z).
Axes of the slice: x: 2, y: 2, z: 4, core: 2. Of those that a mesh axis runs over, the one named last changes fastest.
Arguments:
- x_in: bfloat16 [8192, 1536], P(('dp', 'tensor')), may hold values from -6 to 6
- segments: int32 [8192], P('dp'), may hold values from 0 to 2, as said below
- norm_gain: float32 [2, 1536], replicated, may hold values from 0.5 to 1.5
- w_z: bfloat16 [2, 1536, 3072], P(None, 'dp', 'tensor'), may hold values from -0.15625 to 0.15625
- w_x: bfloat16 [2, 1536, 3072], P(None, 'dp', 'tensor'), may hold values from -0.15625 to 0.15625
- w_bc: bfloat16 [2, 1536, 256], P(None, 'dp'), may hold values from -0.15625 to 0.15625
- w_dt: bfloat16 [2, 1536, 48], P(None, 'dp', 'tensor'), may hold values from -0.15625 to 0.15625
- conv_x: float32 [2, 4, 3072], P(None, None, 'tensor'), may hold values from -3 to 3
- conv_x_bias: float32 [2, 3072], P(None, 'tensor'), may hold values from -0.5 to 0.5
- conv_bc: float32 [2, 4, 256], replicated, may hold values from -3 to 3
- conv_bc_bias: float32 [2, 256], replicated, may hold values from -0.5 to 0.5
- dt_bias: float32 [2, 48], P(None, 'tensor'), may hold values from -6 to -2
- a_log: float32 [2, 48], P(None, 'tensor'), may hold values from 0 to 2.7
- d_skip: float32 [2, 48], P(None, 'tensor'), may hold values from 0.5 to 1.5
- gate_gain: float32 [2, 3072], P(None, 'tensor'), may hold values from 0.5 to 1.5
- w_out: bfloat16 [2, 3072, 1536], P(None, 'tensor', 'dp'), may hold values from -0.109375 to 0.109375
- cotangent: float32 [8192, 1536], P(('dp', 'tensor')), may hold values from -6 to 6
Outputs:
- y_out: float32 [8192, 1536], P(('dp', 'tensor'))
- grad_in: float32 [8192, 1536], P(('dp', 'tensor'))
- g_norm_gain: float32 [2, 1536], replicated
- g_w_z: float32 [2, 1536, 3072], P(None, 'dp', 'tensor')
- g_w_x: float32 [2, 1536, 3072], P(None, 'dp', 'tensor')
- g_w_bc: float32 [2, 1536, 256], P(None, 'dp')
- g_w_dt: float32 [2, 1536, 48], P(None, 'dp', 'tensor')
- g_conv_x: float32 [2, 4, 3072], P(None, None, 'tensor')
- g_conv_x_bias: float32 [2, 3072], P(None, 'tensor')
- g_conv_bc: float32 [2, 4, 256], replicated
- g_conv_bc_bias: float32 [2, 256], replicated
- g_dt_bias: float32 [2, 48], P(None, 'tensor')
- g_a_log: float32 [2, 48], P(None, 'tensor')
- g_d_skip: float32 [2, 48], P(None, 'tensor')
- g_gate_gain: float32 [2, 3072], P(None, 'tensor')
- g_w_out: float32 [2, 3072, 1536], P(None, 'tensor', 'dp')
Inputs may be any that keep to these rules, and one draw needn't show every extreme that they name: `segments`: each sequence of 1024 tokens holds three documents numbered 0, 1, 2 in order (the first and last cut by the packing, each non-empty); document 1 starts within the first 256 tokens, ends within the last 256 tokens and is at most 1000 / 1024 of 1024 tokens long.
All inputs are finite; a program needn't handle non-finite values.
Results may differ from a plain program's by a relative error of at most 0.034.
Values may be sent and summed in bfloat16 or wider, within the bound.
No kernel may reach another device: no remote copies, remote signals or barrier semaphores. Data moves between devices by JAX's collectives and lax.ppermute only.
A program may use at most 256 MiB of HBM per device.

v0:
```python
import jax
import jax.numpy as jnp
from jax import lax
from jax.sharding import PartitionSpec as P

INNER = 3072
HEADDIM = 64
STATE = 128
STRETCH = 256
LAYERS = 2


EPSILON = 1e-05
HIGH = lax.Precision.HIGHEST


def shifted_conv(values, kernel, offset, seg_rows):
    length = values.shape[0]
    width_taps = kernel.shape[0]
    summed = offset[None, :] + kernel[width_taps - 1][None, :] * values
    for lag_steps in range(1, width_taps):
        earlier = jnp.pad(values, ((lag_steps, 0), (0, 0)))[:length]
        earlier_seg = jnp.pad(seg_rows, (lag_steps, 0), constant_values=-1)[:length]
        allowed = (earlier_seg == seg_rows).astype(jnp.float32)[:, None]
        summed = summed + kernel[width_taps - 1 - lag_steps][None, :] * earlier * allowed
    return summed


def scan_state(x_heads, b_rows, c_rows, step_size, decay_rates, seg_rows):
    length, head_count, head_size = x_heads.shape
    block_count = length // STRETCH
    log_decay = -step_size * decay_rates[None, :]
    x_blocks = x_heads.reshape(block_count, STRETCH, head_count, head_size)
    b_blocks = b_rows.reshape(block_count, STRETCH, b_rows.shape[1])
    c_blocks = c_rows.reshape(block_count, STRETCH, c_rows.shape[1])
    step_blocks = step_size.reshape(block_count, STRETCH, head_count)
    seg_blocks = seg_rows.reshape(block_count, STRETCH)
    cumulative = jnp.cumsum(log_decay.reshape(block_count, STRETCH, head_count), axis=1)
    position = jnp.arange(STRETCH)
    allowed = (seg_blocks[:, :, None] == seg_blocks[:, None, :]) & (
        position[:, None] >= position[None, :]
    )[None]
    spread = cumulative[:, :, None, :] - cumulative[:, None, :, :]
    decays = jnp.exp(jnp.where(allowed[..., None], spread, -1e30))
    scores = jnp.einsum("ktn,ksn->kts", c_blocks, b_blocks, precision=HIGH)
    weights = scores[..., None] * decays * step_blocks[:, None, :, :]
    within = jnp.einsum("ktsh,kshp->kthp", weights, x_blocks, precision=HIGH)
    block_end = cumulative[:, -1, :]
    end_seg = seg_blocks[:, -1]
    tail_keep = (seg_blocks == end_seg[:, None]).astype(jnp.float32)
    state_gain = jnp.exp(block_end[:, None, :] - cumulative) * step_blocks * tail_keep[:, :, None]
    states = jnp.einsum("ksh,ksn,kshp->khnp", state_gain, b_blocks, x_blocks, precision=HIGH)
    before_seg = jnp.concatenate([jnp.full((1,), -1, jnp.int32), end_seg[:-1]])
    carry_link = jnp.exp(block_end) * (end_seg == before_seg).astype(jnp.float32)[:, None]

    def advance(running, element):
        link_now, state_now = element
        return (link_now[:, None, None] * running + state_now, running)

    start_state = jnp.zeros(states.shape[1:], jnp.float32)
    incoming = lax.scan(advance, start_state, (carry_link, states))[1]
    entry_gain = (
        jnp.exp(cumulative) * (seg_blocks == before_seg[:, None]).astype(jnp.float32)[:, :, None]
    )
    carried = jnp.einsum("kth,ktn,khnp->kthp", entry_gain, c_blocks, incoming, precision=HIGH)
    return (within + carried).reshape(length, head_count, head_size)


def mixer_core(x_rows, bc_rows, step_size, a_log_row, skip_row, seg_rows):
    length, inner_dev = x_rows.shape
    x_heads = x_rows.reshape(length, inner_dev // HEADDIM, HEADDIM)
    mixed_heads = scan_state(
        x_heads, bc_rows[:, :STATE], bc_rows[:, STATE:], step_size, jnp.exp(a_log_row), seg_rows
    )
    return (mixed_heads + skip_row[None, :, None] * x_heads).reshape(length, inner_dev)


def front_part(raw_rows, layer_consts, seg_rows):
    conv_xw, conv_xb, conv_bcw, conv_bcb, bias_dt = layer_consts
    inner_dev = conv_xw.shape[1]
    x_rows = jax.nn.silu(shifted_conv(raw_rows[:, :inner_dev], conv_xw, conv_xb, seg_rows))
    bc_rows = jax.nn.silu(
        shifted_conv(raw_rows[:, inner_dev : inner_dev + 2 * STATE], conv_bcw, conv_bcb, seg_rows)
    )
    step_size = jax.nn.softplus(raw_rows[:, inner_dev + 2 * STATE :] + bias_dt[None, :])
    return (x_rows, bc_rows, step_size)


def contract_rows(left, right):
    return lax.dot_general(
        left, right, (((0,), (0,)), ((), ())), preferred_element_type=jnp.float32
    )


def contract_cols(left, right):
    return lax.dot_general(
        left, right, (((1,), (1,)), ((), ())), preferred_element_type=jnp.float32
    )


def local(
    x_in,
    segments,
    norm_gain,
    w_z,
    w_x,
    w_bc,
    w_dt,
    conv_x,
    conv_x_bias,
    conv_bc,
    conv_bc_bias,
    dt_bias,
    a_log,
    d_skip,
    gate_gain,
    w_out,
    cotangent,
):
    inner_dev = w_z.shape[2]
    residual = x_in.astype(jnp.float32)
    stored = []
    for layer_index in range(LAYERS):
        gathered_w = (
            lax.all_gather(w_z[layer_index], "dp", axis=0, tiled=True),
            lax.all_gather(w_x[layer_index], "dp", axis=0, tiled=True),
            lax.all_gather(w_bc[layer_index], "dp", axis=0, tiled=True),
            lax.all_gather(w_dt[layer_index], "dp", axis=0, tiled=True),
            lax.all_gather(w_out[layer_index], "dp", axis=1, tiled=True),
        )
        in_weight = jnp.concatenate(
            [gathered_w[0], gathered_w[1], gathered_w[2], gathered_w[3]], axis=1
        )
        out_weight = gathered_w[4]
        inv_rms = lax.rsqrt(jnp.mean(residual * residual, axis=-1, keepdims=True) + EPSILON)
        normed = (residual * inv_rms * norm_gain[layer_index][None, :]).astype(jnp.bfloat16)
        all_tokens = lax.all_gather(normed, "tensor", axis=0, tiled=True)
        projected = jnp.dot(all_tokens, in_weight, preferred_element_type=jnp.float32)
        layer_consts = (
            conv_x[layer_index],
            conv_x_bias[layer_index],
            conv_bc[layer_index],
            conv_bc_bias[layer_index],
            dt_bias[layer_index],
        )
        (x_rows, bc_rows, step_size), front_pull = jax.vjp(
            lambda raw_rows, consts: front_part(raw_rows, consts, segments),
            projected[:, inner_dev:],
            layer_consts,
        )
        x_low = x_rows.astype(jnp.bfloat16)
        bc_low = bc_rows.astype(jnp.bfloat16)
        core_out, core_pull = jax.vjp(
            lambda x_vals, bc_vals, steps, rates, skips: mixer_core(
                x_vals, bc_vals, steps, rates, skips, segments
            ),
            x_low.astype(jnp.float32),
            bc_low.astype(jnp.float32),
            step_size,
            a_log[layer_index],
            d_skip[layer_index],
        )
        gate_act = jax.nn.silu(projected[:, :inner_dev])
        gated = core_out * gate_act
        squares = lax.psum(jnp.sum(gated * gated, axis=-1), "tensor")
        inv_gate = lax.rsqrt(squares / INNER + EPSILON)
        gnormed = (gated * inv_gate[:, None] * gate_gain[layer_index][None, :]).astype(jnp.bfloat16)
        mixed_sum = lax.psum_scatter(
            jnp.dot(gnormed, out_weight, preferred_element_type=jnp.float32).astype(jnp.bfloat16),
            "tensor",
            scatter_dimension=0,
            tiled=True,
        ).astype(jnp.float32)
        stored.append(
            (
                residual,
                inv_rms,
                normed,
                all_tokens,
                in_weight,
                out_weight,
                projected,
                core_out,
                gate_act,
                gated,
                inv_gate,
                gnormed,
                core_pull,
                front_pull,
            )
        )
        residual = residual + mixed_sum
    output = residual
    gradient = cotangent
    grads_store = []
    for layer_index in reversed(range(LAYERS)):
        (
            residual,
            inv_rms,
            normed,
            all_tokens,
            in_weight,
            out_weight,
            projected,
            core_out,
            gate_act,
            gated,
            inv_gate,
            gnormed,
            core_pull,
            front_pull,
        ) = stored[layer_index]
        grad_mixed = gradient.astype(jnp.bfloat16)
        shard_rows = lax.all_gather(grad_mixed, "tensor", axis=0, tiled=True)
        grad_out_w = contract_rows(gnormed, shard_rows)
        grad_rows = contract_cols(shard_rows, out_weight)
        grad_gnorm, grad_out_w = (grad_rows, grad_out_w)
        gain_row = gate_gain[layer_index][None, :]
        grad_gate_gain = jnp.sum(grad_gnorm * gated * inv_gate[:, None], axis=0)
        weighted = lax.psum(jnp.sum(grad_gnorm * gain_row * gated, axis=-1), "tensor")
        cube_gate = inv_gate * inv_gate * inv_gate
        grad_gated = (
            inv_gate[:, None] * gain_row * grad_gnorm
            - gated * (cube_gate * weighted / INNER)[:, None]
        )
        grad_core = (grad_gated * gate_act).astype(jnp.bfloat16).astype(jnp.float32)
        z_rows = projected[:, :inner_dev]
        sigmoid_z = jax.nn.sigmoid(z_rows)
        grad_z = grad_gated * core_out * sigmoid_z * (1.0 + z_rows * (1.0 - sigmoid_z))
        grad_x, grad_bc, grad_step, grad_alog, grad_skip = core_pull(grad_core)
        grad_raw, grad_consts = front_pull((grad_x, grad_bc, grad_step))
        grad_proj = jnp.concatenate([grad_z, grad_raw], axis=1).astype(jnp.bfloat16)
        grad_in_w = contract_rows(all_tokens, grad_proj)
        grad_normed = lax.psum_scatter(
            contract_cols(grad_proj, in_weight).astype(jnp.bfloat16),
            "tensor",
            scatter_dimension=0,
            tiled=True,
        ).astype(jnp.float32)
        gain_vec = norm_gain[layer_index][None, :]
        grad_norm_gain = jnp.sum(grad_normed * residual * inv_rms, axis=0)
        inner_term = jnp.mean(grad_normed * gain_vec * residual, axis=-1, keepdims=True)
        cube_rms = inv_rms * inv_rms * inv_rms
        gradient = gradient + inv_rms * gain_vec * grad_normed - residual * cube_rms * inner_term
        layer_grads = (
            grad_in_w[:, :inner_dev],
            grad_in_w[:, inner_dev : 2 * inner_dev],
            grad_in_w[:, 2 * inner_dev : 2 * inner_dev + 2 * STATE],
            grad_in_w[:, 2 * inner_dev + 2 * STATE :],
            grad_out_w,
        )
        layer_grads = (
            lax.psum_scatter(
                layer_grads[0].astype(jnp.bfloat16), "dp", scatter_dimension=0, tiled=True
            ).astype(jnp.float32),
            lax.psum_scatter(
                layer_grads[1].astype(jnp.bfloat16), "dp", scatter_dimension=0, tiled=True
            ).astype(jnp.float32),
            lax.psum_scatter(
                layer_grads[2].astype(jnp.bfloat16), "dp", scatter_dimension=0, tiled=True
            ).astype(jnp.float32),
            lax.psum_scatter(
                layer_grads[3].astype(jnp.bfloat16), "dp", scatter_dimension=0, tiled=True
            ).astype(jnp.float32),
            lax.psum_scatter(
                layer_grads[4].astype(jnp.bfloat16), "dp", scatter_dimension=1, tiled=True
            ).astype(jnp.float32),
        )
        grads_store.append(
            (layer_grads, grad_consts, grad_alog, grad_skip, grad_gate_gain, grad_norm_gain)
        )
    grads_store = grads_store[::-1]
    large_grads = tuple(
        (jnp.stack([record[0][member] for record in grads_store]) for member in range(5))
    )
    conv_x_grad = jnp.stack([record[1][0] for record in grads_store])
    conv_xb_grad = jnp.stack([record[1][1] for record in grads_store])
    conv_bc_grad = jnp.stack([record[1][2] for record in grads_store])
    conv_bcb_grad = jnp.stack([record[1][3] for record in grads_store])
    dt_bias_grad = jnp.stack([record[1][4] for record in grads_store])
    a_log_grad = jnp.stack([record[2] for record in grads_store])
    skip_grad = jnp.stack([record[3] for record in grads_store])
    gate_gain_grad = jnp.stack([record[4] for record in grads_store])
    norm_gain_grad = jnp.stack([record[5] for record in grads_store])
    shared = (
        lax.psum(large_grads[2].astype(jnp.bfloat16), "tensor").astype(jnp.float32),
        lax.psum(conv_bc_grad.astype(jnp.bfloat16), "tensor").astype(jnp.float32),
        lax.psum(conv_bcb_grad.astype(jnp.bfloat16), "tensor").astype(jnp.float32),
        lax.psum(norm_gain_grad.astype(jnp.bfloat16), "tensor").astype(jnp.float32),
    )
    small_grads = (
        lax.psum(conv_x_grad.astype(jnp.bfloat16), "dp").astype(jnp.float32),
        lax.psum(conv_xb_grad.astype(jnp.bfloat16), "dp").astype(jnp.float32),
        lax.psum(dt_bias_grad.astype(jnp.bfloat16), "dp").astype(jnp.float32),
        lax.psum(a_log_grad.astype(jnp.bfloat16), "dp").astype(jnp.float32),
        lax.psum(skip_grad.astype(jnp.bfloat16), "dp").astype(jnp.float32),
        lax.psum(gate_gain_grad.astype(jnp.bfloat16), "dp").astype(jnp.float32),
        lax.psum(shared[1].astype(jnp.bfloat16), "dp").astype(jnp.float32),
        lax.psum(shared[2].astype(jnp.bfloat16), "dp").astype(jnp.float32),
        lax.psum(shared[3].astype(jnp.bfloat16), "dp").astype(jnp.float32),
    )
    return (
        output,
        gradient,
        small_grads[8],
        large_grads[0],
        large_grads[1],
        shared[0],
        large_grads[3],
        small_grads[0],
        small_grads[1],
        small_grads[6],
        small_grads[7],
        small_grads[2],
        small_grads[3],
        small_grads[4],
        small_grads[5],
        large_grads[4],
    )


def solution(mesh):
    placed = (
        P(("dp", "tensor"), None),
        P("dp"),
        P(),
        P(None, "dp", "tensor"),
        P(None, "dp", "tensor"),
        P(None, "dp", None),
        P(None, "dp", "tensor"),
        P(None, None, "tensor"),
        P(None, "tensor"),
        P(),
        P(),
        P(None, "tensor"),
        P(None, "tensor"),
        P(None, "tensor"),
        P(None, "tensor"),
        P(None, "tensor", "dp"),
        P(("dp", "tensor"), None),
    )
    return jax.shard_map(
        local,
        mesh=mesh,
        in_specs=placed,
        out_specs=(
            P(("dp", "tensor"), None),
            P(("dp", "tensor"), None),
            P(),
            P(None, "dp", "tensor"),
            P(None, "dp", "tensor"),
            P(None, "dp", None),
            P(None, "dp", "tensor"),
            P(None, None, "tensor"),
            P(None, "tensor"),
            P(),
            P(),
            P(None, "tensor"),
            P(None, "tensor"),
            P(None, "tensor"),
            P(None, "tensor"),
            P(None, "tensor", "dp"),
        ),
        check_vma=False,
    )
```

profile of v0, /device:TPU:1, one launch (start us, length us, event | category | flops | bytes accessed | tf_op | source)
XLA Modules:
  0.0 1555.4 jit_solution(14508106041628076623)
XLA Ops:
  16.5 13.6 all-gather.3
  30.9 13.4 all-gather.2
  51.2 26.5 %all-gather.31.cloned.1.call-done = bf16[1,1536,768]{2,1,0:T(8,128)(2,1)} async-done(((bf16[1,192,768]{2,1,0:T(8,128)(2,1)}), bf16[1,1536,768]{2,1,0:T(8,128)(2,1)}) %all-gather.31.cloned.1.call-update) | async-done | bytes 2359312 | tf_op jit(solution)/shard_map/all_gather | solution.py:126
  77.7 65.2 %all-gather.21.cloned.1.call-done = bf16[1024,1536]{1,0:T(8,128)(2,1)} async-done(((bf16[256,1536]{1,0:T(8,128)(2,1)}), bf16[1024,1536]{1,0:T(8,128)(2,1)}) %all-gather.21.cloned.1.call-update) | async-done | bytes 3145744 | tf_op jit(solution)/shard_map/all_gather | solution.py:137
  237.6 59.6 %reduce-scatter.31.cloned.1.call-done = bf16[256,1536]{1,0:T(8,128)(2,1)} async-done(((bf16[1024,1536]{1,0:T(8,128)(2,1)}), bf16[256,1536]{1,0:T(8,128)(2,1)}) %reduce-scatter.31.cloned.1.call-update) | async-done | bytes 786448 | tf_op jit(solution)/shard_map/reduce_scatter | solution.py:168
  303.6 13.0 all-gather.8
  317.3 13.6 all-gather.7
  332.9 31.3 %all-gather.37.cloned.1.call-done = bf16[1,1536,768]{2,1,0:T(8,128)(2,1)} async-done(((bf16[1,192,768]{2,1,0:T(8,128)(2,1)}), bf16[1,1536,768]{2,1,0:T(8,128)(2,1)}) %all-gather.37.cloned.1.call-update) | async-done | bytes 2359312 | tf_op jit(solution)/shard_map/all_gather | solution.py:126
  364.2 65.2 %all-gather.23.cloned.1.call-done = bf16[1024,1536]{1,0:T(8,128)(2,1)} async-done(((bf16[256,1536]{1,0:T(8,128)(2,1)}), bf16[1024,1536]{1,0:T(8,128)(2,1)}) %all-gather.23.cloned.1.call-update) | async-done | bytes 3145744 | tf_op jit(solution)/shard_map/all_gather | solution.py:137
  480.7 22.1 %while.69 = (s32[]{:T(128)}, f32[12,128,64]{2,1,0:T(8,128)S(1)}, f32[4,12,128,64]{3,2,1,0:T(8,128)}, f32[4,12,1,1]{1,3,2,0:T(1,128)}, f32[4,12]{1,0:T(4,128)}, /...) while((s32[]{:T(128)}, f32[12,128,64]{2,1,0:T(8,128)S(1)}, f32[4,12,128,64]{3,2,1,0:T(8,128)}, ...), condition=%wide.region_12.14_spmd.clone, body=%wide.region_11.13_spmd.clone.sunk | while | flops 393219 | bytes 3934456 | solution.py:61
  568.8 11.2 fusion.21
  580.0 10.8 fusion.141
  592.9 17.7 %while.70 = (s32[]{:T(128)}, f32[12,128,64]{2,1,0:T(8,128)S(1)}, f32[4,12]{1,0:T(4,128)S(1)}, f32[4,12,128,64]{3,2,1,0:T(8,128)}, f32[4,12,128,64]{2,3,1,0:T(8,1...) while((s32[]{:T(128)}, f32[12,128,64]{2,1,0:T(8,128)S(1)}, ...), condition=%wide.region_20.22_spmd.clone, body=%wide.region_18.21_spmd.clone.sunk | while | flops 589816 | bytes 4325808 | solution.py:61
  615.4 11.2 fusion.144
  687.2 62.9 %reduce-scatter.35.cloned.1.call-done = bf16[256,1536]{1,0:T(8,128)(2,1)} async-done(((bf16[1024,1536]{1,0:T(8,128)(2,1)}), bf16[256,1536]{1,0:T(8,128)(2,1)}) %reduce-scatter.35.cloned.1.call-update) | async-done | bytes 786448 | tf_op jit(solution)/shard_map/reduce_scatter | solution.py:234
  767.8 50.9 %all-gather.27.cloned.1.call-done = bf16[1024,1536]{1,0:T(8,128)(2,1)} async-done(((bf16[256,1536]{1,0:T(8,128)(2,1)}), bf16[1024,1536]{1,0:T(8,128)(2,1)}) %all-gather.27.cloned.1.call-update) | async-done | bytes 3145744 | tf_op jit(solution)/shard_map/all_gather | solution.py:214
  877.7 22.6 %while.71 = (s32[]{:T(128)}, f32[12,128,64]{2,1,0:T(8,128)S(1)}, f32[4,12]{1,0:T(4,128)}, f32[4,12,128,64]{3,2,1,0:T(8,128)}, f32[4,12,128,64]{2,3,1,0:T(8,128)}...) while((s32[]{:T(128)}, f32[12,128,64]{2,1,0:T(8,128)S(1)}, ...), condition=%wide.region_34.36_spmd.clone, body=%wide.region_32.35_spmd.clone.sunk | while | flops 589816 | bytes 4325808 | solution.py:61
  905.1 11.3 fusion.150
  1008.6 21.4 %reduce-scatter.51.cloned.1.call-done = bf16[192,256]{1,0:T(8,128)(2,1)} async-done(((bf16[1536,256]{1,0:T(8,128)(2,1)}), bf16[192,256]{1,0:T(8,128)(2,1)}) %reduce-scatter.51.cloned.1.call-update) | async-done | bytes 98320
  1056.8 11.2 convolution_convert_fusion.2
  1077.8 35.5 %reduce-scatter.49.cloned.1.call-done = bf16[192,768]{1,0:T(8,128)(2,1)} async-done(((bf16[1536,768]{1,0:T(8,128)(2,1)}), bf16[192,768]{1,0:T(8,128)(2,1)}) %reduce-scatter.49.cloned.1.call-update) | async-done | bytes 294928
  1114.5 45.0 %reduce-scatter.45.cloned.1.call-done = bf16[192,768]{1,0:T(8,128)(2,1)} async-done(((bf16[1536,768]{1,0:T(8,128)(2,1)}), bf16[192,768]{1,0:T(8,128)(2,1)}) %reduce-scatter.45.cloned.1.call-update) | async-done | bytes 294928
  1161.4 34.9 %reduce-scatter.55.cloned.1.call-done = bf16[192,12]{1,0:T(8,128)(2,1)} async-done(((bf16[1536,12]{1,0:T(8,128)(2,1)}), bf16[192,12]{1,0:T(8,128)(2,1)}) %reduce-scatter.55.cloned.1.call-update) | async-done | bytes 4624
  1197.8 35.8 %all-reduce.59.cloned.1.call-done = bf16[2,192,256]{1,2,0:T(8,128)(2,1)} async-done(((bf16[2,192,256]{1,2,0:T(8,128)(2,1)}), bf16[2,192,256]{1,2,0:T(8,128)(2,1)}) %all-reduce.59.cloned.1.call-update) | async-done | bytes 196624 | tf_op jit(solution)/shard_map/psum | solution.py:286
  1235.5 45.4 %reduce-scatter.47.cloned.1.call-done = bf16[192,768]{1,0:T(8,128)(2,1)} async-done(((bf16[1536,768]{1,0:T(8,128)(2,1)}), bf16[192,768]{1,0:T(8,128)(2,1)}) %reduce-scatter.47.cloned.1.call-update) | async-done | bytes 294928
  1283.7 43.1 %reduce-scatter.43.cloned.1.call-done = bf16[192,768]{1,0:T(8,128)(2,1)} async-done(((bf16[1536,768]{1,0:T(8,128)(2,1)}), bf16[192,768]{1,0:T(8,128)(2,1)}) %reduce-scatter.43.cloned.1.call-update) | async-done | bytes 294928
  1332.3 40.7 %reduce-scatter.41.cloned.1.call-done = bf16[768,192]{0,1:T(8,128)(2,1)} async-done(((bf16[768,1536]{0,1:T(8,128)(2,1)}), bf16[768,192]{0,1:T(8,128)(2,1)}) %reduce-scatter.41.cloned.1.call-update) | async-done | bytes 294928 | tf_op jit(solution)/shard_map/reduce_scatter | solution.py:265
  1373.0 45.9 %reduce-scatter.39.cloned.1.call-done = bf16[768,192]{0,1:T(8,128)(2,1)} async-done(((bf16[768,1536]{0,1:T(8,128)(2,1)}), bf16[768,192]{0,1:T(8,128)(2,1)}) %reduce-scatter.39.cloned.1.call-update) | async-done | bytes 294928 | tf_op jit(solution)/shard_map/reduce_scatter | solution.py:265
  1421.0 60.3 %reduce-scatter.37.cloned.1.call-done = bf16[256,1536]{1,0:T(8,128)(2,1)} async-done(((bf16[1024,1536]{1,0:T(8,128)(2,1)}), bf16[256,1536]{1,0:T(8,128)(2,1)}) %reduce-scatter.37.cloned.1.call-update) | async-done | bytes 786448 | tf_op jit(solution)/shard_map/reduce_scatter | solution.py:234
  1482.9 14.7 all-reduce.56
  1497.6 23.9 %all-reduce.55 = (bf16[2,1536]{1,0:T(2,128)(2,1)S(1)}, bf16[2,4,768]{2,1,0:T(4,128)(2,1)S(1)}, bf16[2,768]{1,0:T(2,128)(2,1)S(1)}, bf16[2,4,256]{2,1,0:T(4,128)(...) all-reduce(bf16[2,1536]{1,0:T(2,128)(2,1)S(1)} %get-tuple-element.8, ...), channel_id=1, replica_groups=mesh['dp'=8,'tensor'=4] {'dp'}, use_global_device_ids=true, to_apply=%region_47.49 | all-reduce | flops 14920 | bytes 59680 | tf_op jit(solution)/shard_map/psum | solution.py:300
  1526.9 17.2 %reduce-scatter.33.cloned.1.call-done = bf16[256,1536]{1,0:T(8,128)(2,1)} async-done(((bf16[1024,1536]{1,0:T(8,128)(2,1)}), bf16[256,1536]{1,0:T(8,128)(2,1)}) %reduce-scatter.33.cloned.1.call-update) | async-done | bytes 786448 | tf_op jit(solution)/shard_map/reduce_scatter | solution.py:168
  (980 shorter events, 611.9 us)
Async XLA Ops:
  7.2 44.0 %all-gather.29.cloned.1.call-start = ((), (), s32[]{:S(2)}) async-start(), calls=%async_computation.25 | async-start | bytes 2654208 | tf_op jit(solution)/shard_map/all_gather | solution.py:125
  9.3 68.4 %all-gather.31.cloned.1.call-start = ((), (), s32[]{:S(2)}) async-start(), calls=%async_computation.26 | async-start | bytes 2654208 | tf_op jit(solution)/shard_map/all_gather | solution.py:126
  11.3 131.7 %all-gather.21.cloned.1.call-start = ((), (), s32[]{:S(2)}) async-start(), calls=%async_computation.14 | async-start | bytes 3932160 | tf_op jit(solution)/shard_map/all_gather | solution.py:137
  12.2 287.0 %copy-start.116 = (f32[1536]{0:T(1024)}, f32[1536]{0:T(1024)S(1)}, u32[]{:S(2)}) copy-start(f32[1536]{0:T(1024)S(1)} %get-tuple-element.778) | copy-start | bytes 18436
  14.2 215.7 %all-gather.33.cloned.1.call-start = ((), (), s32[]{:S(2)}) async-start(), calls=%async_computation.27 | async-start | bytes 2654208 | tf_op jit(solution)/shard_map/all_gather | solution.py:129
  15.2 281.9 %reduce-scatter.31.cloned.1.call-start = ((), (), s32[]{:S(2)}) async-start(), calls=%async_computation.15 | async-start | bytes 3932160 | tf_op jit(solution)/shard_map/reduce_scatter | solution.py:168
  236.2 96.7 %all-gather.35.cloned.1.call-start = ((), (), s32[]{:S(2)}) async-start(), calls=%async_computation.28 | async-start | bytes 2654208 | tf_op jit(solution)/shard_map/all_gather | solution.py:125
  236.8 127.4 %all-gather.37.cloned.1.call-start = ((), (), s32[]{:S(2)}) async-start(), calls=%async_computation.29 | async-start | bytes 2654208 | tf_op jit(solution)/shard_map/all_gather | solution.py:126
  237.5 191.9 %all-gather.23.cloned.1.call-start = ((), (), s32[]{:S(2)}) async-start(), calls=%async_computation.16 | async-start | bytes 3932160 | tf_op jit(solution)/shard_map/all_gather | solution.py:137
  301.5 232.3 %all-gather.39.cloned.1.call-start = ((), (), s32[]{:S(2)}) async-start(), calls=%async_computation.30 | async-start | bytes 2654208 | tf_op jit(solution)/shard_map/all_gather | solution.py:129
  302.2 231.6 %all-gather.25.cloned.1.call-start = ((), (), s32[]{:S(2)}) async-start(), calls=%async_computation.18 | async-start | bytes 3932160 | tf_op jit(solution)/shard_map/all_gather | solution.py:214
  303.3 446.7 %reduce-scatter.35.cloned.1.call-start = ((), (), s32[]{:S(2)}) async-start(), calls=%async_computation.19 | async-start | bytes 3932160 | tf_op jit(solution)/shard_map/reduce_scatter | solution.py:234
  687.1 131.6 %all-gather.27.cloned.1.call-start = ((), (), s32[]{:S(2)}) async-start(), calls=%async_computation.20 | async-start | bytes 3932160 | tf_op jit(solution)/shard_map/all_gather | solution.py:214
  755.0 251.6 %reduce-scatter.53.cloned.1.call-start = ((), (), s32[]{:S(2)}) async-start(), calls=%async_computation.36 | async-start | bytes 884736
  767.4 262.6 %reduce-scatter.51.cloned.1.call-start = ((), (), s32[]{:S(2)}) async-start(), calls=%async_computation.35 | async-start | bytes 884736
  994.4 82.6 %reduce-scatter.57.cloned.1.call-start = ((), (), s32[]{:S(2)}) async-start(), calls=%async_computation.38 | async-start | bytes 442368
  995.4 117.9 %reduce-scatter.49.cloned.1.call-start = ((), (), s32[]{:S(2)}) async-start(), calls=%async_computation.34 | async-start | bytes 2654208
  1003.9 155.6 %reduce-scatter.45.cloned.1.call-start = ((), (), s32[]{:S(2)}) async-start(), calls=%async_computation.32 | async-start | bytes 2654208
  1006.4 189.9 %reduce-scatter.55.cloned.1.call-start = ((), (), s32[]{:S(2)}) async-start(), calls=%async_computation.37 | async-start | bytes 442368
  1008.5 225.1 %all-reduce.59.cloned.1.call-start = ((), (), s32[]{:S(2)}) async-start(), calls=%async_computation.22 | async-start | bytes 524288 | tf_op jit(solution)/shard_map/psum | solution.py:286
  1031.7 249.1 %reduce-scatter.47.cloned.1.call-start = ((), (), s32[]{:S(2)}) async-start(), calls=%async_computation.33 | async-start | bytes 2654208
  1040.2 286.5 %reduce-scatter.43.cloned.1.call-start = ((), (), s32[]{:S(2)}) async-start(), calls=%async_computation.31 | async-start | bytes 2654208
  1042.8 330.2 %reduce-scatter.41.cloned.1.call-start = ((), (), s32[]{:S(2)}) async-start(), calls=%async_computation.24 | async-start | bytes 2654208 | tf_op jit(solution)/shard_map/reduce_scatter | solution.py:265
  1050.3 368.6 %reduce-scatter.39.cloned.1.call-start = ((), (), s32[]{:S(2)}) async-start(), calls=%async_computation.23 | async-start | bytes 2654208 | tf_op jit(solution)/shard_map/reduce_scatter | solution.py:265
  1056.8 424.5 %reduce-scatter.37.cloned.1.call-start = ((), (), s32[]{:S(2)}) async-start(), calls=%async_computation.21 | async-start | bytes 3932160 | tf_op jit(solution)/shard_map/reduce_scatter | solution.py:234
  1068.1 476.0 %reduce-scatter.33.cloned.1.call-start = ((), (), s32[]{:S(2)}) async-start(), calls=%async_computation.17 | async-start | bytes 3932160 | tf_op jit(solution)/shard_map/reduce_scatter | solution.py:168
  1329.2 214.8 %copy-start.35 = (f32[256,1536]{1,0:T(8,128)S(1)}, f32[256,1536]{1,0:T(8,128)}, u32[]{:S(2)}) copy-start(f32[256,1536]{1,0:T(8,128)} %param.42) | copy-start | bytes 4718596
  1329.3 214.8 %copy-start.118 = (f32[1536]{0:T(1024)S(1)}, f32[1536]{0:T(1024)}, u32[]{:S(2)}) copy-start(f32[1536]{0:T(1024)} %copy-done.116) | copy-start | bytes 18436
  1329.3 214.8 %copy-start.167 = (f32[256]{0:T(256)S(1)}, f32[256]{0:T(256)}, u32[]{:S(2)}) copy-start(f32[256]{0:T(256)} %copy-done.165) | copy-start | bytes 3076
  1329.3 214.8 %copy-start.197 = (f32[256]{0:T(256)S(1)}, f32[256]{0:T(256)}, u32[]{:S(2)}) copy-start(f32[256]{0:T(256)} %get-tuple-element.947) | copy-start | bytes 3076
  1329.3 214.8 %copy-start.206 = (f32[256]{0:T(256)S(1)}, f32[256]{0:T(256)}, u32[]{:S(2)}) copy-start(f32[256]{0:T(256)} %copy-done.205) | copy-start | bytes 3076
  1329.3 214.8 %copy-start.228 = (f32[256]{0:T(256)S(1)}, f32[256]{0:T(256)}, u32[]{:S(2)}) copy-start(f32[256]{0:T(256)} %get-tuple-element.945) | copy-start | bytes 3076
  (251 other events, 6296.6 us)
Sparse Core Ops, SparseCore 0:
  10.5 35.6 all-gather.28
  48.7 29.0 all-gather.30
  79.9 63.0 all-gather.20
  145.2 28.1 all-gather.32
  236.3 60.7 reduce-scatter.30
  298.8 33.9 all-gather.34
  335.3 28.7 all-gather.36
  366.3 63.0 all-gather.22
  431.3 28.1 all-gather.38
  460.9 62.9 all-gather.24
  687.3 62.7 reduce-scatter.34
  755.1 63.6 all-gather.26
  821.9 33.3 reduce-scatter.52
  994.5 35.3 reduce-scatter.50
  1033.4 33.6 reduce-scatter.56
  1070.3 42.9 reduce-scatter.48
  1116.9 42.4 reduce-scatter.44
  1162.9 33.3 reduce-scatter.54
  1199.2 34.3 all-reduce.58
  1237.2 43.6 reduce-scatter.46
  1284.2 42.4 reduce-scatter.42
  1330.4 42.4 reduce-scatter.40
  1376.3 42.4 reduce-scatter.38
  1421.1 60.0 reduce-scatter.36
  1483.7 60.3 reduce-scatter.32
where the time goes:
time: 1570 us; the launch traced here: 1560 us
  waiting for transfers between devices  790 us (50%)
  matrix products  248 us (16%)
  other arithmetic  192 us (12%)
  local copies, waits for them, and re-layouts  184 us (12%)
  blocking collectives  121 us (8%)
  between operations  18.2 us (1%)
    unnamed x33, waiting for transfers between devices  227 us
    all_gather x2, waiting for transfers between devices, local(): all_tokens = lax.all_gather(normed, 'tensor', axis=0, tiled=True)  130 us
    reduce_scatter x2, waiting for transfers between devices, local(): lax.psum_scatter(contract_cols(grad_proj, in_weight).astype(jnp.bfloat16)...  123 us
    reduce_scatter x2, waiting for transfers between devices, local(): lax.psum_scatter(layer_grads[4].astype(jnp.bfloat16), 'dp', scatter_dimen...  86.5 us
    reduce_scatter x2, waiting for transfers between devices, local(): lax.psum_scatter(jnp.dot(gnormed, out_weight, preferred_element_type=jnp....  76.8 us
    unnamed x550, local copies, waits for them, and re-layouts  61.1 us
    dot_general x6, matrix products, scan_state(): within = jnp.einsum('ktsh,kshp->kthp', weights, x_blocks, precision=HIGH)  60.4 us
    all_gather x2, waiting for transfers between devices, local(): lax.all_gather(w_x[layer_index], 'dp', axis=0, tiled=True)  57.8 us
  transfers between devices with their start and end apart: 25, of which 19 were waited for; matrix products, arithmetic and copies ran while one was open for 28% of the time, Pallas kernels for 0%

commit v1 on v0

v1 whole, which is shorter than its diff:
```python
import functools

import jax
import jax.numpy as jnp
import numpy as np
from jax import lax
from jax.experimental import pallas as pl
from jax.experimental.pallas import tpu as pltpu
from jax.sharding import PartitionSpec as P

INNER = 3072
HEADDIM = 64
STATE = 128
LAYERS = 2
EPSILON = 1e-05
HALO = 16
CHUNK = 128
LANES = 128

BF = jnp.bfloat16
F32 = jnp.float32
EXACT = lax.Precision.HIGHEST
VMEM_BYTES = 50 * 1024 * 1024


def dot(left, right, dims=((1,), (0,)), precision=None):
    return lax.dot_general(
        left, right, (dims, ((), ())), preferred_element_type=F32, precision=precision
    )


def split(values):
    high = values.astype(BF)
    return high, (values - high.astype(F32)).astype(BF)


def spread(values, e2_ref):
    return dot(jnp.concatenate(split(values), axis=1), e2_ref[...])


def head_sum(values, hm_ref):
    high, low = split(values)
    return dot(high, hm_ref[...]) + dot(low, hm_ref[...])


def softplus(values):
    return jnp.maximum(values, 0.0) + jnp.log1p(jnp.exp(-jnp.abs(values)))


def triangle(size, lower):
    rows = lax.broadcasted_iota(jnp.int32, (size, size), 0)
    cols = lax.broadcasted_iota(jnp.int32, (size, size), 1)
    return rows >= cols if lower else rows <= cols


def convolve(window, marks, cw, lanes):
    size = window.shape[0] - 8
    total = cw[4:5, lanes] + cw[3:4, lanes] * window[8:]
    for lag in (1, 2, 3):
        earlier = window[8 - lag : 8 - lag + size]
        total = total + cw[3 - lag : 4 - lag, lanes] * (earlier * marks[:, lag - 1 : lag])
    return total


def front_kernel(
    raw_ref, cm_ref, lnk_ref, cw_ref, hp_ref, e2_ref,
    xb_ref, aux_ref, sloc_ref, send_ref, state_ref,
    *, inner,
):
    count = xb_ref.shape[0]
    lower = triangle(CHUNK, True).astype(F32)
    state_ref[...] = jnp.zeros_like(state_ref)

    def step_chunk(k, carry):
        base = pl.multiple_of(k * CHUNK, CHUNK)
        here = pl.ds(base, CHUNK)
        marks = cm_ref[pl.ds(base + HALO, CHUNK), :]
        for low in range(0, inner + 2 * STATE, STATE):
            lanes = slice(low, low + STATE)
            window = raw_ref[pl.ds(base + HALO - 8, CHUNK + 8), lanes]
            pre = convolve(window, marks, cw_ref, lanes)
            xb_ref[here, lanes] = (pre * jax.nn.sigmoid(pre)).astype(BF)
        raw_dt = raw_ref[pl.ds(base + HALO, CHUNK), inner + 2 * STATE :]
        step = softplus(raw_dt + hp_ref[0:1, :])
        cum = dot(lower, -hp_ref[1:2, :] * step, precision=EXACT)
        aux_ref[here, :LANES] = step
        aux_ref[here, LANES:] = cum
        end = cum[CHUNK - 1 :, :]
        gain = jnp.exp(end - cum) * marks[:, 3:4] * step
        scaled = (spread(gain, e2_ref) * xb_ref[here, :inner].astype(F32)).astype(BF)
        b_rows = xb_ref[here, inner : inner + STATE]
        local = dot(b_rows, scaled, ((0,), (0,)))
        keep = spread(jnp.exp(end) * lnk_ref[pl.ds(k * 8, 8), :], e2_ref)[0:1]
        sloc_ref[k] = state_ref[...]
        state_ref[...] = keep * state_ref[...] + local
        return carry

    lax.fori_loop(0, count // CHUNK, step_chunk, 0)
    send_ref[...] = state_ref[...].astype(BF)


def scan_kernel(
    xb_ref, aux_ref, sloc_ref, send_ref, sin_ref, z_ref, cm_ref, segr_ref, lnk_ref, gp_ref, e2_ref,
    core_ref, act_ref, ssq_ref, sst_ref, decay_ref,
    *, inner,
):
    count = xb_ref.shape[0]
    lower = triangle(CHUNK, True)
    first = lax.broadcasted_iota(jnp.int32, (CHUNK, STATE), 1) < HEADDIM
    decay_ref[...] = jnp.ones_like(decay_ref)

    def step_chunk(k, carry):
        base = pl.multiple_of(k * CHUNK, CHUNK)
        here = pl.ds(base, CHUNK)
        there = pl.ds(base + HALO, CHUNK)
        marks = cm_ref[there, :]
        incoming = (sloc_ref[k] + decay_ref[0:1, :] * sin_ref[...].astype(F32)).astype(BF)
        sst_ref[k] = incoming
        b_rows = xb_ref[here, inner : inner + STATE]
        c_rows = xb_ref[here, inner + STATE : inner + 2 * STATE]
        scores = dot(c_rows, b_rows, ((1,), (1,)))
        allowed = (marks[:, 5:6] == segr_ref[0:1, here]) & lower
        scores = jnp.where(allowed, scores, 0.0)
        step = aux_ref[here, :LANES]
        cum = aux_ref[here, LANES:]
        cum_t = jnp.transpose(cum)
        step_wide = spread(step, e2_ref)
        carried = spread(jnp.exp(cum) * marks[:, 4:5], e2_ref) * dot(c_rows, incoming)
        squares = jnp.zeros((CHUNK, STATE), F32)
        for pair in range(inner // STATE):
            lanes = slice(pair * STATE, (pair + 1) * STATE)
            x_rows = xb_ref[here, lanes].astype(F32)
            scaled = step_wide[:, lanes] * x_rows
            within = carried[:, lanes] + gp_ref[1:2, lanes] * x_rows
            for half in range(2):
                head = 2 * pair + half
                decay = jnp.exp(
                    jnp.minimum(cum[:, head : head + 1] - cum_t[head : head + 1, :], 0.0)
                )
                mine = first if half == 0 else ~first
                part = jnp.where(mine, scaled, 0.0).astype(BF)
                within = within + dot((scores * decay).astype(BF), part)
            core_ref[here, lanes] = within
            z_rows = z_ref[there, lanes]
            gated = within * (z_rows * jax.nn.sigmoid(z_rows))
            act_ref[here, lanes] = (gated * gp_ref[0:1, lanes]).astype(BF)
            squares = squares + gated * gated
        total = jnp.sum(jnp.transpose(squares), axis=0, keepdims=True)
        ssq_ref[:, here] = jnp.broadcast_to(total, (8, CHUNK))
        end = cum[CHUNK - 1 :, :]
        keep = spread(jnp.exp(end) * lnk_ref[pl.ds(k * 8, 8), :], e2_ref)
        decay_ref[...] = decay_ref[...] * keep
        return carry

    chunks = count // CHUNK
    lax.fori_loop(0, chunks, step_chunk, 0)
    last = send_ref[...].astype(F32) + decay_ref[0:1, :] * sin_ref[...].astype(F32)
    sst_ref[chunks] = last.astype(BF)


def gate_back_kernel(
    gg_ref, core_ref, z_ref, coef_ref, xb_ref, aux_ref, cm_ref, lnk_ref, gp_ref, e2_ref,
    gcore_ref, gz_ref, ggain_ref, dsin_ref, state_ref,
    *, inner,
):
    count = xb_ref.shape[0]
    chunks = count // CHUNK
    state_ref[...] = jnp.zeros_like(state_ref)
    ggain_ref[...] = jnp.zeros_like(ggain_ref)
    gz_ref[:HALO, :] = jnp.zeros((HALO, inner), BF)

    def step_chunk(turn, carry):
        k = chunks - 1 - turn
        base = pl.multiple_of(k * CHUNK, CHUNK)
        here = pl.ds(base, CHUNK)
        there = pl.ds(base + HALO, CHUNK)
        marks = cm_ref[there, :]
        coef = coef_ref[here, 0:1]
        cum = aux_ref[here, LANES:]
        entry = spread(jnp.exp(cum) * marks[:, 4:5], e2_ref)
        c_rows = xb_ref[here, inner + STATE : inner + 2 * STATE]
        end = cum[CHUNK - 1 :, :]
        keep = spread(jnp.exp(end) * lnk_ref[pl.ds(k * 8, 8), :], e2_ref)[0:1]
        for pair in range(inner // STATE):
            lanes = slice(pair * STATE, (pair + 1) * STATE)
            z_rows = z_ref[there, lanes]
            core = core_ref[here, lanes]
            grad = gg_ref[here, lanes]
            sig = jax.nn.sigmoid(z_rows)
            act = z_rows * sig
            gated = core * act
            ggain_ref[0:1, lanes] += jnp.sum(grad * gated, axis=0, keepdims=True)
            grad_gated = gp_ref[0:1, lanes] * grad - coef * gated
            gcore = (grad_gated * act).astype(BF)
            gcore_ref[here, lanes] = gcore
            gz_ref[there, lanes] = (
                grad_gated * core * (sig * (1.0 + z_rows * (1.0 - sig)))
            ).astype(BF)
            scaled = (entry[:, lanes] * gcore.astype(F32)).astype(BF)
            state_ref[:, lanes] = keep[:, lanes] * state_ref[:, lanes] + dot(
                c_rows, scaled, ((0,), (0,))
            )
        return carry

    lax.fori_loop(0, chunks, step_chunk, 0)
    dsin_ref[...] = state_ref[...].astype(BF)


def scan_back_kernel(
    gcore_ref, xb_ref, aux_ref, core_ref, sst_ref, dso_ref, raw_ref, cm_ref, segr_ref, lnk_ref,
    gp_ref, cw_ref, hp_ref, e2_ref, hm_ref,
    graw_ref, sgrad_ref, hgrad_ref, state_ref, dpre_ref, qv_ref, xd_ref,
    *, inner,
):
    count = xb_ref.shape[0]
    chunks = count // CHUNK
    wide = inner + 2 * STATE
    upper = triangle(CHUNK, False)
    first = lax.broadcasted_iota(jnp.int32, (CHUNK, STATE), 1) < HEADDIM
    state_ref[...] = dso_ref[...].astype(F32)
    sgrad_ref[...] = jnp.zeros_like(sgrad_ref)
    hgrad_ref[...] = jnp.zeros_like(hgrad_ref)
    dpre_ref[:HALO, :] = jnp.zeros((HALO, wide), F32)
    dpre_ref[HALO + count :, :] = jnp.zeros((HALO, wide), F32)
    graw_ref[:HALO, wide:] = jnp.zeros((HALO, LANES), BF)

    def step_chunk(turn, carry):
        k = chunks - 1 - turn
        base = pl.multiple_of(k * CHUNK, CHUNK)
        here = pl.ds(base, CHUNK)
        there = pl.ds(base + HALO, CHUNK)
        marks = cm_ref[there, :]
        step = aux_ref[here, :LANES]
        cum = aux_ref[here, LANES:]
        cum_t = jnp.transpose(cum)
        end = cum[CHUNK - 1 :, :]
        b_rows = xb_ref[here, inner : inner + STATE]
        c_rows = xb_ref[here, inner + STATE : wide]
        after = state_ref[...]
        after_low = after.astype(BF)
        product = jnp.sum(
            sst_ref[k + 1].astype(F32) * after_low.astype(F32), axis=0, keepdims=True
        )
        at_end = head_sum(jnp.broadcast_to(product, (8, inner)), hm_ref)[0:1]
        scores_t = dot(b_rows, c_rows, ((1,), (1,)))
        allowed = (marks[:, 5:6] == segr_ref[0:1, here]) & upper
        scores_t = jnp.where(allowed, scores_t, 0.0)
        gain = spread(jnp.exp(end - cum) * marks[:, 3:4], e2_ref)
        step_wide = spread(step, e2_ref)
        entry = spread(jnp.exp(cum) * marks[:, 4:5], e2_ref)
        keep = spread(jnp.exp(end) * lnk_ref[pl.ds(k * 8, 8), :], e2_ref)[0:1]
        outer = gain * dot(b_rows, after_low)
        scaled_grad = (entry * gcore_ref[here, :].astype(F32)).astype(BF)
        grad_c = dot(scaled_grad, sst_ref[k], ((1,), (1,)))
        scaled_x = (gain * (step_wide * xb_ref[here, :inner].astype(F32))).astype(BF)
        grad_b = dot(scaled_x, after_low, ((1,), (1,)))
        state_ref[...] = keep * after + dot(c_rows, scaled_grad, ((0,), (0,)))
        grad_scores = jnp.zeros((CHUNK, CHUNK), F32)
        for pair in range(inner // STATE):
            lanes = slice(pair * STATE, (pair + 1) * STATE)
            grad_low = gcore_ref[here, lanes]
            grad = grad_low.astype(F32)
            x_rows = xb_ref[here, lanes].astype(F32)
            wide_step = step_wide[:, lanes]
            scaled = wide_step * x_rows
            grad_u = outer[:, lanes]
            for half in range(2):
                head = 2 * pair + half
                decay = jnp.exp(
                    jnp.minimum(cum_t[head : head + 1, :] - cum[:, head : head + 1], 0.0)
                )
                mine = first if half == 0 else ~first
                part = jnp.where(mine, scaled, 0.0).astype(BF)
                grad_part = jnp.where(mine, grad, 0.0).astype(BF)
                grad_u = grad_u + dot((scores_t * decay).astype(BF), grad_part)
                grad_scores = grad_scores + dot(part, grad_low, ((1,), (1,))) * decay
            skip = gp_ref[1:2, lanes]
            qv_ref[:, lanes] = grad * (core_ref[here, lanes] - skip * x_rows) - (
                scaled.astype(BF).astype(F32) * grad_u
            )
            xd_ref[:, lanes] = x_rows * grad_u
            dpre_ref[there, lanes] = wide_step * grad_u + skip * grad
            sgrad_ref[5:6, lanes] += jnp.sum(grad * x_rows, axis=0, keepdims=True)
        grad_scores = jnp.where(allowed, grad_scores, 0.0).astype(BF)
        dpre_ref[there, inner : inner + STATE] = grad_b + dot(grad_scores, c_rows)
        dpre_ref[there, inner + STATE :] = grad_c + dot(grad_scores, b_rows, ((0,), (0,)))
        rate = hp_ref[1:2, :]
        grad_log = dot(upper.astype(F32), head_sum(qv_ref[...], hm_ref), precision=EXACT) + at_end
        grad_step = head_sum(xd_ref[...], hm_ref) - rate * grad_log
        raw_dt = raw_ref[there, wide:]
        grad_dt = grad_step * jax.nn.sigmoid(raw_dt + hp_ref[0:1, :])
        graw_ref[there, wide:] = grad_dt.astype(BF)
        hgrad_ref[0:1, :] += jnp.sum(grad_dt, axis=0, keepdims=True)
        hgrad_ref[1:2, :] -= rate * jnp.sum(step * grad_log, axis=0, keepdims=True)
        return carry

    lax.fori_loop(0, chunks, step_chunk, 0)

    def conv_chunk(k, carry):
        base = pl.multiple_of(k * CHUNK, CHUNK)
        there = pl.ds(base + HALO, CHUNK)
        marks = cm_ref[there, :]
        for low in range(0, wide, STATE):
            lanes = slice(low, low + STATE)
            window = raw_ref[pl.ds(base + HALO - 8, CHUNK + 8), lanes]
            pre = convolve(window, marks, cw_ref, lanes)
            sig = jax.nn.sigmoid(pre)
            grad = dpre_ref[there, lanes] * (sig * (1.0 + pre * (1.0 - sig)))
            dpre_ref[there, lanes] = grad
            sgrad_ref[4:5, lanes] += jnp.sum(grad, axis=0, keepdims=True)
            sgrad_ref[3:4, lanes] += jnp.sum(grad * window[8:], axis=0, keepdims=True)
            for lag in (1, 2, 3):
                earlier = window[8 - lag : 8 - lag + CHUNK]
                sgrad_ref[3 - lag : 4 - lag, lanes] += jnp.sum(
                    grad * (earlier * marks[:, lag - 1 : lag]), axis=0, keepdims=True
                )
        return carry

    lax.fori_loop(0, chunks, conv_chunk, 0)

    def transpose_rows(start, size):
        marks = cm_ref[pl.ds(start, size + 8), :]
        for low in range(0, wide, STATE):
            lanes = slice(low, low + STATE)
            window = dpre_ref[pl.ds(start, size + 8), lanes]
            total = cw_ref[3:4, lanes] * window[:size]
            for lag in (1, 2, 3):
                masked = window[lag : lag + size] * marks[lag : lag + size, lag - 1 : lag]
                total = total + cw_ref[3 - lag : 4 - lag, lanes] * masked
            graw_ref[pl.ds(start, size), lanes] = total.astype(BF)

    transpose_rows(0, HALO)

    def back_chunk(k, carry):
        transpose_rows(pl.multiple_of(k * CHUNK, CHUNK) + HALO, CHUNK)
        return carry

    lax.fori_loop(0, chunks, back_chunk, 0)


def run(kernel, operands, per_stream, outs, scratch, inner, flops):
    streams = 2

    def spec(shape, split_here):
        if split_here:
            return pl.BlockSpec((None,) + shape[1:], lambda s: (s,) + (0,) * (len(shape) - 1))
        return pl.BlockSpec(shape, lambda s: (0,) * len(shape))

    moved = sum(int(np.prod(v.shape)) * v.dtype.itemsize for v in operands)
    moved += sum(streams * int(np.prod(s)) * jnp.dtype(t).itemsize for s, t in outs)
    return pl.pallas_call(
        functools.partial(kernel, inner=inner),
        grid=(streams,),
        in_specs=[spec(v.shape, flag) for v, flag in zip(operands, per_stream)],
        out_specs=[spec((streams,) + s, True) for s, _ in outs],
        out_shape=[jax.ShapeDtypeStruct((streams,) + s, t) for s, t in outs],
        scratch_shapes=[pltpu.VMEM(s, t) for s, t in scratch],
        compiler_params=pltpu.CompilerParams(vmem_limit_bytes=VMEM_BYTES),
        cost_estimate=pl.CostEstimate(flops=flops, bytes_accessed=moved, transcendentals=0),
    )(*operands)


def build(n_dp, n_tensor):
    axes = ("dp", "tensor")
    half_size = n_tensor // 2
    planes = [[d for d in range(n_dp) if d % 2 == c] for c in range(2)]

    def pairs(route):
        found = []
        for d in range(n_dp):
            for t in range(n_tensor):
                goal = route(d, t)
                if goal is not None:
                    found.append((d * n_tensor + t, goal[0] * n_tensor + goal[1]))
        return found

    def send(value, route):
        return lax.ppermute(value, axes, pairs(route))

    def back(value, route):
        return lax.ppermute(value, axes, [(b, a) for a, b in pairs(route)])

    def to_core(d, t):
        return d ^ 1, t

    def to_piece(j):
        return lambda d, t: (d, (t // half_size) * half_size + ((t % half_size) ^ j))

    def to_later(d, t):
        return (d, t + half_size) if t < half_size else None

    def to_halo(j):
        return lambda d, t: (d, half_size + j) if t == half_size - 1 else None

    def to_group(turn):
        def route(d, t):
            return (d & ~1) | (t % 2), t // 2 + half_size * ((d & 1) ^ turn)

        return route

    def local(
        x_in, segments, norm_gain, w_z, w_x, w_bc, w_dt, conv_x, conv_x_bias, conv_bc, conv_bc_bias,
        dt_bias, a_log, d_skip, gate_gain, w_out, cotangent,
    ):
        inner = w_z.shape[2]
        heads = dt_bias.shape[1]
        piece, width = x_in.shape
        count = half_size * piece
        rows = count + HALO
        chunks = count // CHUNK
        shard = w_z.shape[1]
        wide = inner + 2 * STATE
        place = lax.axis_index("tensor")
        core = lax.axis_index("dp") % 2
        half = place // half_size
        mine = place % half_size

        def pad_lanes(value):
            return jnp.pad(value, ((0, 0), (0, LANES - value.shape[1])))

        def regroup(value):
            one, two = send(value, to_group(0)), send(value, to_group(1))
            return jnp.concatenate(
                [jnp.where(half == 0, one, two), jnp.where(half == 0, two, one)], axis=0
            )

        def over_plane(value):
            return lax.all_gather(value, "dp", axis=0, tiled=True, axis_index_groups=planes)

        def bc_rows(l):
            other = send(w_bc[l], to_core)
            return jnp.concatenate(
                [jnp.where(core == 0, w_bc[l], other), jnp.where(core == 0, other, w_bc[l])], axis=0
            )

        front_w, z_w, out_w = [], [], []
        for l in range(LAYERS):
            part = regroup(jnp.concatenate([w_x[l], pad_lanes(w_dt[l])], axis=1))
            front_w.append(
                over_plane(jnp.concatenate([part[:, :inner], bc_rows(l), part[:, inner:]], axis=1))
            )
            part = regroup(jnp.concatenate([w_z[l], w_out[l].T], axis=1))
            z_w.append(over_plane(part[:, :inner]))
            out_w.append(over_plane(part[:, inner:]))

        def row(value, size):
            return jnp.pad(value, ((0, 0), (0, size - value.shape[1])))[:, None]

        packed = jnp.concatenate(
            [conv_x, conv_x_bias[:, None], gate_gain[:, None]]
            + [jnp.concatenate([row(v, LANES) for v in (dt_bias, a_log, d_skip)], axis=2)
               if inner == 3 * LANES
               else jnp.pad(
                   jnp.concatenate([row(v, LANES) for v in (dt_bias, a_log, d_skip)], axis=2),
                   ((0, 0), (0, 0), (0, inner - 3 * LANES)))],
            axis=1,
        )
        packed = send(packed, to_group(0))
        taps, bias, gain_own = packed[:, :4], packed[:, 4:5], packed[:, 5:6]
        dt_own, a_own, skip_own = (packed[:, 6, i * LANES : (i + 1) * LANES] for i in range(3))
        head_ok = jnp.arange(LANES) < heads
        rate_own = jnp.where(head_ok, jnp.exp(a_own), 0.0)
        skip_wide = jnp.repeat(skip_own[:, :heads], HEADDIM, axis=1)
        conv_w = jnp.concatenate(
            [
                jnp.concatenate([taps, conv_bc], axis=2),
                jnp.concatenate([bias, conv_bc_bias[:, None]], axis=2),
                jnp.zeros((LAYERS, 3, wide), F32),
            ],
            axis=1,
        )
        gate_p = jnp.concatenate(
            [gain_own, skip_wide[:, None], jnp.zeros((LAYERS, 6, inner), F32)], axis=1
        )
        head_p = jnp.concatenate(
            [dt_own[:, None], rate_own[:, None], jnp.zeros((LAYERS, 6, LANES), F32)], axis=1
        )
        member = np.arange(inner)[None, :] // HEADDIM == np.arange(LANES)[:, None]
        e2 = jnp.asarray(np.concatenate([member, member], axis=0), BF)
        hm = jnp.asarray(member.T, BF)

        seg_own = jnp.concatenate([jnp.full((HALO,), -1.0, F32), segments.astype(F32)])
        seg_own = lax.dynamic_slice(seg_own, (half * count,), (rows,))
        seg = jnp.stack([seg_own, send(seg_own, to_core)])
        seg = jnp.where(
            (half == 0) & (jnp.arange(rows) < HALO)[None, :], -1.0, seg
        )
        tokens = seg[:, HALO:]
        lagged = [
            (tokens == seg[:, HALO - k : HALO - k + count]).astype(F32) for k in (1, 2, 3)
        ]
        by_chunk = tokens.reshape(2, chunks, CHUNK)
        last = by_chunk[:, :, -1]
        before = jnp.concatenate([seg[:, HALO - 1 : HALO], last[:, :-1]], axis=1)
        stays = (by_chunk == last[:, :, None]).astype(F32).reshape(2, count)
        enters = (by_chunk == before[:, :, None]).astype(F32).reshape(2, count)
        marks = jnp.stack(lagged + [stays, enters, tokens, tokens, tokens], axis=-1)
        marks = jnp.pad(marks, ((0, 0), (HALO, HALO), (0, 0)))
        seg_row = jnp.broadcast_to(tokens[:, None, :], (2, 8, count))
        links = (last == before).astype(F32)
        links = jnp.broadcast_to(links[:, :, None, None], (2, chunks, 8, LANES))
        links = links.reshape(2, chunks * 8, LANES)

        def gather(value, halo):
            offset = HALO if halo else 0
            block = jnp.zeros((offset + count,) + value.shape[1:], value.dtype)
            if halo:
                edge = value[piece - HALO :]
                came = send(edge, to_halo(0))
                for j in range(1, half_size):
                    came = came + send(edge, to_halo(j))
                block = lax.dynamic_update_slice(block, came, (0,) * value.ndim)
            rest = (0,) * (value.ndim - 1)
            parts = [value] + [send(value, to_piece(j)) for j in range(1, half_size)]
            for j, part in enumerate(parts):
                block = lax.dynamic_update_slice(
                    block, part, (offset + (mine ^ j) * piece,) + rest
                )
            return jnp.stack([block, send(block, to_core)])

        def scatter(own, other, halo):
            offset = HALO if halo else 0
            kind = own.dtype
            total = own.astype(F32) + send(other, to_core).astype(F32)
            rest = (0,) * (own.ndim - 1)
            size = (piece,) + own.shape[1:]

            def part_of(j):
                return lax.dynamic_slice(total, (offset + (mine ^ j) * piece,) + rest, size)

            result = part_of(0)
            for j in range(1, half_size):
                result = result + send(part_of(j).astype(kind), to_piece(j)).astype(F32)
            if halo:
                edge = total[:HALO].astype(kind)
                came = back(edge, to_halo(0)).astype(F32)
                for j in range(1, half_size):
                    came = came + back(edge, to_halo(j)).astype(F32)
                result = result.at[piece - HALO :].add(came)
            return result

        def matmul(left, right, dims):
            return lax.dot_general(left, right, (dims, ((), ())), preferred_element_type=F32)

        tok_flops = 2 * count

        residual = x_in.astype(F32)
        stored = []
        for l in range(LAYERS):
            inv_rms = lax.rsqrt(jnp.mean(residual * residual, axis=-1, keepdims=True) + EPSILON)
            normed = (residual * inv_rms * norm_gain[l][None, :]).astype(BF)
            toks = gather(normed, True)
            raw = matmul(toks, front_w[l], ((2,), (0,)))
            xb, aux, sloc, ends = run(
                front_kernel,
                [raw, marks, links, conv_w[l], head_p[l], e2],
                [True, True, True, False, False, False],
                [((count, wide), BF), ((count, 2 * LANES), F32),
                 ((chunks, STATE, inner), F32), ((STATE, inner), BF)],
                [((STATE, inner), F32)],
                inner,
                tok_flops * inner * STATE * 4,
            )
            begins = send(ends, to_later)
            z = matmul(toks, z_w[l], ((2,), (0,)))
            core_out, act, ssq, sst = run(
                scan_kernel,
                [xb, aux, sloc, ends, begins, z, marks, seg_row, links, gate_p[l], e2],
                [True, True, True, True, True, True, True, True, True, False, False],
                [((count, inner), F32), ((count, inner), BF), ((8, count), F32),
                 ((chunks + 1, STATE, inner), BF)],
                [((8, inner), F32)],
                inner,
                tok_flops * inner * STATE * 8,
            )
            part_other = matmul(act[1], out_w[l], ((1,), (1,))).astype(BF)
            part_own = matmul(act[0], out_w[l], ((1,), (1,))).astype(BF)
            squares = scatter(ssq[0, 0], ssq[1, 0], False)
            mixed = scatter(part_own, part_other, False)
            inv_gate = lax.rsqrt(squares / INNER + EPSILON)[:, None]
            stored.append(
                (residual, inv_rms, toks, raw, xb, aux, z, core_out, act, sst, mixed, inv_gate)
            )
            residual = residual + inv_gate * mixed
        output = residual

        def plane_sum(value):
            return lax.psum_scatter(
                value, "dp", scatter_dimension=0, tiled=True, axis_index_groups=planes
            )

        def ungroup(value):
            first_rows = lax.dynamic_slice(value, (half * shard, 0), (shard, value.shape[1]))
            other_rows = lax.dynamic_slice(value, ((1 - half) * shard, 0), (shard, value.shape[1]))
            one, two = back(first_rows, to_group(0)), back(other_rows, to_group(1))
            return one.astype(F32) + two.astype(F32)

        def over_tensor(value, kind):
            bit = 1
            while bit < n_tensor:
                value = value + send(value.astype(kind), lambda d, t: (d, t ^ bit)).astype(F32)
                bit *= 2
            return value

        gradient = cotangent
        found = [None] * LAYERS
        for l in reversed(range(LAYERS)):
            (residual, inv_rms, toks, raw, xb, aux, z, core_out, act, sst, mixed, inv_gate) = stored[l]
            scaled = (inv_gate * gradient).astype(BF)
            coef = inv_gate[:, 0] ** 2 * jnp.sum(scaled.astype(F32) * mixed, axis=-1) / INNER
            grows = gather(scaled, False)
            coefs = gather(coef, False)
            coefs = jnp.broadcast_to(coefs[:, :, None], (2, count, 8))
            gg = matmul(grows, out_w[l], ((2,), (0,)))
            gcore, gz, ggain, dsin = run(
                gate_back_kernel,
                [gg, core_out, z, coefs, xb, aux, marks, links, gate_p[l], e2],
                [True, True, True, True, True, True, True, True, False, False],
                [((count, inner), BF), ((rows, inner), BF), ((8, inner), F32),
                 ((STATE, inner), BF)],
                [((STATE, inner), F32)],
                inner,
                tok_flops * inner * STATE * 4,
            )
            dsout = back(dsin, to_later)
            g_out_w = matmul(grows, act, ((0, 1), (0, 1))).astype(BF)
            g_z_w = matmul(toks, gz, ((0, 1), (0, 1))).astype(BF)
            graw, sgrad, hgrad = run(
                scan_back_kernel,
                [gcore, xb, aux, core_out, sst, dsout, raw, marks, seg_row, links,
                 gate_p[l], conv_w[l], head_p[l], e2, hm],
                [True] * 10 + [False] * 5,
                [((rows, wide + LANES), BF), ((8, wide), F32), ((8, LANES), F32)],
                [((STATE, inner), F32), ((count + 2 * HALO, wide), F32),
                 ((CHUNK, inner), F32), ((CHUNK, inner), F32)],
                inner,
                tok_flops * inner * STATE * 16,
            )

            def normed_part(s):
                return (
                    matmul(gz[s], z_w[l], ((1,), (1,))) + matmul(graw[s], front_w[l], ((1,), (1,)))
                ).astype(BF)

            part_other = normed_part(1)
            part_own = normed_part(0)
            g_front_w = matmul(toks, graw, ((0, 1), (0, 1))).astype(BF)
            grad_normed = scatter(part_own, part_other, True)
            gain_vec = norm_gain[l][None, :]
            g_norm_gain = jnp.sum(grad_normed * residual * inv_rms, axis=0)
            inner_term = jnp.mean(grad_normed * gain_vec * residual, axis=-1, keepdims=True)
            gradient = (
                gradient + inv_rms * gain_vec * grad_normed
                - residual * (inv_rms * inv_rms * inv_rms) * inner_term
            )
            g_zo = ungroup(plane_sum(jnp.concatenate([g_z_w, g_out_w], axis=1)))
            g_front = plane_sum(g_front_w)
            g_xd = ungroup(jnp.concatenate([g_front[:, :inner], g_front[:, wide:]], axis=1))
            bc_part = g_front[:, inner:wide]
            keep_rows = lax.dynamic_slice(bc_part, (core * shard, 0), (shard, 2 * STATE))
            send_rows = lax.dynamic_slice(bc_part, ((1 - core) * shard, 0), (shard, 2 * STATE))
            g_bc = keep_rows.astype(F32) + send(send_rows, to_core).astype(F32)
            g_bc = over_tensor(g_bc, BF)
            found[l] = (g_zo, g_xd, g_bc, ggain, sgrad, hgrad, g_norm_gain)

        def small(l):
            _, _, _, ggain, sgrad, hgrad, g_norm_gain = found[l]
            sums = sgrad[0] + sgrad[1]
            head_rows = hgrad[0, :2] + hgrad[1, :2]
            skips = jnp.sum(sums[5, :inner].reshape(heads, HEADDIM), axis=1)
            last_row = jnp.concatenate(
                [head_rows[0], head_rows[1], jnp.pad(skips, (0, LANES - heads)),
                 jnp.zeros((inner - 3 * LANES,), F32)]
            )
            group = jnp.concatenate(
                [sums[:5, :inner], (ggain[0, :1] + ggain[1, :1]), last_row[None]], axis=0
            )
            shared = jnp.concatenate([sums[:5, inner:].reshape(-1), g_norm_gain])
            return group, shared

        group, shared = (jnp.stack(v) for v in zip(*[small(l) for l in range(LAYERS)]))
        group = back(group, to_group(0)) + back(group, to_group(1))
        shared = shared + send(shared, to_core)
        shared = over_tensor(shared, F32)
        everything = jnp.concatenate([group.reshape(-1), shared.reshape(-1)])
        bit = 2
        while bit < n_dp:
            everything = everything + send(everything, lambda d, t: (d ^ bit, t))
            bit *= 2
        group, shared = everything[: group.size].reshape(group.shape), everything[
            group.size :
        ].reshape(shared.shape)
        five = shared[:, : 5 * 2 * STATE].reshape(LAYERS, 5, 2 * STATE)
        head_grads = [group[:, 6, i * LANES : i * LANES + heads] for i in range(3)]

        def both(pick):
            return jnp.stack([pick(found[l]) for l in range(LAYERS)])

        return (
            output,
            gradient,
            shared[:, 5 * 2 * STATE :],
            both(lambda f: f[0][:, :inner]),
            both(lambda f: f[1][:, :inner]),
            both(lambda f: f[2]),
            both(lambda f: f[1][:, inner : inner + heads]),
            group[:, :4],
            group[:, 4],
            five[:, :4],
            five[:, 4],
            head_grads[0],
            head_grads[1],
            head_grads[2],
            group[:, 5],
            both(lambda f: f[0][:, inner:].T),
        )

    return local


def solution(mesh):
    n_dp, n_tensor = mesh.shape["dp"], mesh.shape["tensor"]
    tokens = P(("dp", "tensor"), None)
    columns = P(None, "dp", "tensor")
    placed = (
        tokens,
        P("dp"),
        P(),
        columns,
        columns,
        P(None, "dp", None),
        columns,
        P(None, None, "tensor"),
        P(None, "tensor"),
        P(),
        P(),
        P(None, "tensor"),
        P(None, "tensor"),
        P(None, "tensor"),
        P(None, "tensor"),
        P(None, "tensor", "dp"),
        tokens,
    )
    return jax.shard_map(
        build(n_dp, n_tensor),
        mesh=mesh,
        in_specs=placed,
        out_specs=(
            tokens,
            tokens,
            P(),
            columns,
            columns,
            P(None, "dp", None),
            columns,
            P(None, None, "tensor"),
            P(None, "tensor"),
            P(),
            P(),
            P(None, "tensor"),
            P(None, "tensor"),
            P(None, "tensor"),
            P(None, "tensor"),
            P(None, "tensor", "dp"),
        ),
        check_vma=False,
    )
```

time: 1570 us -> 799 us (0.51)
  waiting for transfers between devices: 790 us -> 291 us
  other arithmetic: 192 us -> 42.5 us
  starting transfers between devices: 1.69 us -> 130 us
  local copies, waits for them, and re-layouts: 184 us -> 60.1 us
  blocking collectives: 121 us -> 0 us
  Pallas kernels: 0 us -> 117 us
  matrix products: 248 us -> 132 us
    ppermute x0 -> x69, waiting for transfers between devices: none -> 290 us  [the longest x53 184 us: send(): return lax.ppermute(value, axes, pairs(route))]
    reduce_scatter x6 -> x2, waiting for transfers between devices: 286 us -> 0.02 us  [plane_sum(): lax.psum_scatter(value, 'dp', scatter_dimension=0, tiled=True, axis_index...]
    all_gather x10 -> x6, waiting for transfers between devices: 240 us -> 0.79 us  [over_plane(): lax.all_gather(value, 'dp', axis=0, tiled=True, axis_index_groups=planes)]
    unnamed x33 -> x12, waiting for transfers between devices: 227 us -> 0.21 us
    ppermute x0 -> x69, starting transfers between devices: none -> 129 us  [the longest x53 103 us: send(): return lax.ppermute(value, axes, pairs(route))]
    pallas_call x0 -> x8, Pallas kernels: none -> 117 us  [run(): pl.pallas_call(functools.partial(kernel, inner=inner), grid=(streams,), i...]
    dot_general x36 -> x24, matrix products: 248 us -> 132 us  [matmul(): lax.dot_general(left, right, (dims, ((), ())), preferred_element_type=F32)]
    psum x6 -> x0, blocking collectives: 67.9 us -> none  [the longest x1 23.9 us: local(): lax.psum(shared[3].astype(jnp.bfloat16), 'dp').astype(jnp.float32)]
  transfers between devices with their start and end apart: 25 -> 79, of which waited for: 19 -> 40; matrix products, arithmetic and copies ran while one was open for 28% -> 25% of each run, Pallas kernels for 0% -> 10%
where the time goes in v1:
time: 799 us; the launch traced here: 789 us
  waiting for transfers between devices  291 us (36%)
  matrix products  132 us (17%)
  starting transfers between devices  130 us (16%)
  Pallas kernels  117 us (15%)
  local copies, waits for them, and re-layouts  60.1 us (8%)
  other arithmetic  42.5 us (5%)
  between operations  16.4 us (2%)
    ppermute x53, waiting for transfers between devices, send(): return lax.ppermute(value, axes, pairs(route))  184 us
    dot_general x24, matrix products, matmul(): lax.dot_general(left, right, (dims, ((), ())), preferred_element_type=F32)  132 us
    pallas_call x8, Pallas kernels, run(): pl.pallas_call(functools.partial(kernel, inner=inner), grid=(streams,), i...  117 us
    ppermute x16, waiting for transfers between devices, back(): return lax.ppermute(value, axes, [(b, a) for a, b in pairs(route)])  106 us
    ppermute x53, starting transfers between devices, send(): return lax.ppermute(value, axes, pairs(route))  103 us
    ppermute x16, starting transfers between devices, back(): return lax.ppermute(value, axes, [(b, a) for a, b in pairs(route)])  26 us
    unnamed x156, local copies, waits for them, and re-layouts  21 us
  transfers between devices with their start and end apart: 79, of which 40 were waited for; matrix products, arithmetic and copies ran while one was open for 25% of the time, Pallas kernels for 10%

profile of v1, /device:TPU:1, one launch (start us, length us, event | category | flops | bytes accessed | tf_op | source)
XLA Modules:
  0.0 789.4 jit_solution(14127148898650946243)
XLA Ops:
  24.8 10.0 %collective-permute-start.10 = (bf16[192,1536]{1,0:T(8,128)(2,1)S(1)}, bf16[192,1536]{1,0:T(8,128)(2,1)S(1)}, u32[]{:S(2)}, u32[]{:S(2)}) collective-permute-start(bf16[192,1536]{1,0:T(8,128)(2,1)S(1)} %pad_maximum_fusion.15), channel_id=1, source_target_pairs={{0,0},{1,4},{2,1},{3,5},{4,2},{5,6},{6,3},{7,7},{8,8},{9,12},{10,9... | collective-permute-start | bytes 1769480 | tf_op jit(solution)/shard_map/ppermute | solution.py:378
  34.9 15.4 %collective-permute-done.10 = bf16[192,1536]{1,0:T(8,128)(2,1)S(1)} collective-permute-done((bf16[192,1536]{1,0:T(8,128)(2,1)S(1)}, bf16[192,1536]{1,0:T(8,128)(2,1)S(1)}, u32[]{:S(2)}, u32[]{:S(2)}) %collective-permute-start.10) | collective-permute-done | bytes 589856 | tf_op jit(solution)/shard_map/ppermute | solution.py:378
  52.6 12.9 %collective-permute-start.20 = (bf16[192,896]{1,0:T(8,128)(2,1)}, bf16[192,896]{1,0:T(8,128)(2,1)}, u32[]{:S(2)}, u32[]{:S(2)}) collective-permute-start(bf16[192,896]{1,0:T(8,128)(2,1)} %fusion.69), channel_id=1, source_target_pairs={{0,0},{1,4},{2,1},{3,5},{4,2},{5,6},{6,3},{7,7},{8,8},{9,12},{10,9... | collective-permute-start | bytes 1032200 | tf_op jit(solution)/shard_map/ppermute | solution.py:378
  102.2 16.0 %collective-permute-done.2 = bf16[256,1536]{1,0:T(8,128)(2,1)} collective-permute-done((bf16[256,1536]{1,0:T(8,128)(2,1)}, bf16[256,1536]{1,0:T(8,128)(2,1)}, u32[]{:S(2)}, u32[]{:S(2)}) %collective-permute-start.2) | collective-permute-done | bytes 786464 | tf_op jit(solution)/shard_map/ppermute | solution.py:378
  123.1 9.1 %fusion.4.raw_ref = f32[2,528,1152]{2,1,0:T(8,128)} fusion(bf16[1536,1152]{1,0:T(8,128)(2,1)} %all-gather.7.cloned.1.call-done, bf16[1,528,1536]{2,1,0:T(8,128)(2,1)} %bitcast.1, bf16[1,528,1536]{2,1,0:T(8,128)(2,1)S(1)} %bitcast.232), kind=kOutput, calls=%fused_computation.12 | convolution fusion | flops 3738746880 | bytes 11649024 | tf_op jit(solution)/shard_map/dot_general | solution.py:543
  132.3 11.4 %shard_map.306 = (bf16[2,512,1024]{2,1,0:T(8,128)(2,1)}, f32[2,512,256]{2,1,0:T(8,128)S(1)}, f32[2,4,128,768]{3,2,1,0:T(8,128)}, bf16[2,128,768]{2,1,0:T(8,128)(2,1)S(1)}) custom-call(f32[2,528,1152]{2,1,0:T(8,128)} %fusion.4.raw_ref, f32[2,544,8]{2,1,0:T(8,128)S(1)} %pad.40.cm_ref, f32[2,32,128]{2,1,0:T(8,128)S(1)} %broadcast_in_dim.97.lnk_ref, ...), custom_call_target="tpu_custom_call" | custom-call | flops 402653184 | bytes 12048384 | tf_op jit(solution)/shard_map/pallas_call | solution.py:351
  156.9 9.7 %shard_map.307 = (f32[2,512,768]{2,1,0:T(8,128)}, bf16[2,512,768]{2,1,0:T(8,128)(2,1)}, f32[2,8,512]{2,1,0:T(8,128)S(1)}, bf16[2,5,128,768]{3,2,1,0:T(8,128)(2,1)}) custom-call(bf16[2,512,1024]{2,1,0:T(8,128)(2,1)} %get-tuple-element.70.xb_ref, f32[2,512,256]{2,1,0:T(8,128)S(1)} %get-tuple-element.71.aux_ref, f32[2,4,128,768]{3,2,1,0:T(8,128)} %get-tuple-element.72.sloc_ref, ...), custom_call_target="tpu_custom_call" | custom-call | flops 805306368 | bytes 17557504 | tf_op jit(solution)/shard_map/pallas_call | solution.py:351
  183.6 9.5 %collective-permute-start.15 = (bf16[256,1536]{1,0:T(8,128)(2,1)}, bf16[256,1536]{1,0:T(8,128)(2,1)}, u32[]{:S(2)}, u32[]{:S(2)}) collective-permute-start(bf16[256,1536]{1,0:T(8,128)(2,1)} %dynamic-slice_convert_fusion.3), channel_id=1, source_target_pairs={{0,1},{1,0},{2,3},{3,2},{4,5},{5,4},{6,7},{7,6},{8,9},{9,8},{10,11... | collective-permute-start | bytes 2359304 | tf_op jit(solution)/shard_map/ppermute | solution.py:378
  194.7 16.4 %collective-permute-done.13 = f32[256]{0:T(256)S(1)} collective-permute-done((f32[256]{0:T(256)S(1)}, f32[256]{0:T(256)S(1)}, u32[]{:S(2)}, u32[]{:S(2)}) %collective-permute-start.13) | collective-permute-done | bytes 1056 | tf_op jit(solution)/shard_map/ppermute | solution.py:378
  220.5 12.5 %collective-permute-done.18 = bf16[256,1536]{1,0:T(8,128)(2,1)} collective-permute-done((bf16[256,1536]{1,0:T(8,128)(2,1)S(1)}, bf16[256,1536]{1,0:T(8,128)(2,1)}, u32[]{:S(2)}, u32[]{:S(2)}) %collective-permute-start.18) | collective-permute-done | bytes 786464 | tf_op jit(solution)/shard_map/ppermute | solution.py:378
  240.3 9.5 %fusion.2.raw_ref = f32[2,528,1152]{2,1,0:T(8,128)} fusion(bf16[1536,1152]{1,0:T(8,128)(2,1)} %all-gather.13.cloned.1.call-done, bf16[1,528,1536]{2,1,0:T(8,128)(2,1)} %bitcast.29, bf16[1,528,1536]{2,1,0:T(8,128)(2,1)} %bitcast.28), kind=kOutput, calls=%fused_computation.10 | convolution fusion | flops 3738746880 | bytes 11649024 | tf_op jit(solution)/shard_map/dot_general | solution.py:543
  249.9 11.4 %shard_map.308 = (bf16[2,512,1024]{2,1,0:T(8,128)(2,1)}, f32[2,512,256]{2,1,0:T(8,128)S(1)}, f32[2,4,128,768]{3,2,1,0:T(8,128)}, bf16[2,128,768]{2,1,0:T(8,128)(2,1)S(1)}) custom-call(f32[2,528,1152]{2,1,0:T(8,128)} %fusion.2.raw_ref, f32[2,544,8]{2,1,0:T(8,128)S(1)} %pad.40.cm_ref, f32[2,32,128]{2,1,0:T(8,128)S(1)} %broadcast_in_dim.97.lnk_ref, ...), custom_call_target="tpu_custom_call" | custom-call | flops 402653184 | bytes 12048384 | tf_op jit(solution)/shard_map/pallas_call | solution.py:351
  268.2 7.2 fusion.10.z_ref
  275.4 9.8 %shard_map.309 = (f32[2,512,768]{2,1,0:T(8,128)}, bf16[2,512,768]{2,1,0:T(8,128)(2,1)}, f32[2,8,512]{2,1,0:T(8,128)S(1)}, bf16[2,5,128,768]{3,2,1,0:T(8,128)(2,1)}) custom-call(bf16[2,512,1024]{2,1,0:T(8,128)(2,1)} %get-tuple-element.76.xb_ref, f32[2,512,256]{2,1,0:T(8,128)S(1)} %get-tuple-element.77.aux_ref, f32[2,4,128,768]{3,2,1,0:T(8,128)} %get-tuple-element.78.sloc_ref, ...), custom_call_target="tpu_custom_call" | custom-call | flops 805306368 | bytes 17557504 | tf_op jit(solution)/shard_map/pallas_call | solution.py:351
  295.3 9.1 %collective-permute-start.29 = (bf16[256,1536]{1,0:T(8,128)(2,1)S(1)}, bf16[256,1536]{1,0:T(8,128)(2,1)S(1)}, u32[]{:S(2)}, u32[]{:S(2)}) collective-permute-start(bf16[256,1536]{1,0:T(8,128)(2,1)S(1)} %dynamic-slice_convert_fusion.2), channel_id=1, source_target_pairs={{0,1},{1,0},{2,3},{3,2},{4,5},{5,4},{6,7},{7,6},{8,9},{9,8},{10,11... | collective-permute-start | bytes 2359304 | tf_op jit(solution)/shard_map/ppermute | solution.py:378
  306.7 15.3 %collective-permute-done.27 = f32[256]{0:T(256)S(1)} collective-permute-done((f32[256]{0:T(256)S(1)}, f32[256]{0:T(256)S(1)}, u32[]{:S(2)}, u32[]{:S(2)}) %collective-permute-start.27) | collective-permute-done | bytes 1056 | tf_op jit(solution)/shard_map/ppermute | solution.py:378
  327.1 14.8 %collective-permute-done.30 = bf16[256,1536]{1,0:T(8,128)(2,1)S(1)} collective-permute-done((bf16[256,1536]{1,0:T(8,128)(2,1)S(1)}, bf16[256,1536]{1,0:T(8,128)(2,1)S(1)}, u32[]{:S(2)}, u32[]{:S(2)}) %collective-permute-start.30) | collective-permute-done | bytes 786464 | tf_op jit(solution)/shard_map/ppermute | solution.py:378
  356.4 8.7 %shard_map.310 = (bf16[2,512,768]{2,1,0:T(8,128)(2,1)}, bf16[2,528,768]{2,1,0:T(8,128)(2,1)}, f32[2,8,768]{2,1,0:T(8,128)S(1)}, bf16[2,128,768]{2,1,0:T(8,128)(2,1)S(1)}) custom-call(f32[2,512,768]{2,1,0:T(8,128)} %fusion.8.gg_ref, f32[2,512,768]{2,1,0:T(8,128)} %get-tuple-element.82.core_ref, f32[2,528,768]{2,1,0:T(8,128)} %fusion.10.z_ref, ...), custom_call_target="tpu_custom_call" | custom-call | flops 402653184 | bytes 16836608 | tf_op jit(solution)/shard_map/pallas_call | solution.py:351
  366.6 20.6 %collective-permute-done.34.dso_ref = bf16[2,128,768]{2,1,0:T(8,128)(2,1)S(1)} collective-permute-done((bf16[2,128,768]{2,1,0:T(8,128)(2,1)S(1)}, bf16[2,128,768]{2,1,0:T(8,128)(2,1)S(1)}, u32[]{:S(2)}, u32[]{:S(2)}) %collective-permute-start.34) | collective-permute-done | bytes 393248 | tf_op jit(solution)/shard_map/ppermute | solution.py:381
  387.2 28.8 %shard_map.311 = (bf16[2,528,1152]{2,1,0:T(8,128)(2,1)}, f32[2,8,1024]{2,1,0:T(8,128)S(1)}, f32[2,8,128]{2,1,0:T(8,128)S(1)}) custom-call(bf16[2,512,768]{2,1,0:T(8,128)(2,1)} %get-tuple-element.84.gcore_ref, bf16[2,512,1024]{2,1,0:T(8,128)(2,1)} %get-tuple-element.76.xb_ref, f32[2,512,256]{2,1,0:T(8,128)S(1)} %get-tuple-element.77.aux_ref, ...), custom_call_target="tpu_custom_call" | custom-call | flops 1610612736 | bytes 18348032 | tf_op jit(solution)/shard_map/pallas_call | solution.py:351
  416.0 8.9 %fusion.1 = bf16[1536,1152]{1,0:T(8,128)(2,1)} fusion(bf16[2,528,1152]{2,1,0:T(8,128)(2,1)} %get-tuple-element.87, bf16[1,528,1536]{2,1,0:T(8,128)(2,1)} %bitcast.29, bf16[1,528,1536]{2,1,0:T(8,128)(2,1)} %bitcast.28), kind=kOutput, calls=%fused_computation.3 | convolution fusion | flops 3740516352 | bytes 9216000 | tf_op jit(solution)/shard_map/dot_general | solution.py:543
  462.7 17.8 %collective-permute-done.36 = bf16[256,1536]{1,0:T(8,128)(2,1)S(1)} collective-permute-done((bf16[256,1536]{1,0:T(8,128)(2,1)S(1)}, bf16[256,1536]{1,0:T(8,128)(2,1)S(1)}, u32[]{:S(2)}, u32[]{:S(2)}) %collective-permute-start.36) | collective-permute-done | bytes 786464 | tf_op jit(solution)/shard_map/ppermute | solution.py:378
  488.2 16.2 %collective-permute-done.39 = bf16[256,1536]{1,0:T(8,128)(2,1)S(1)} collective-permute-done((bf16[256,1536]{1,0:T(8,128)(2,1)S(1)}, bf16[256,1536]{1,0:T(8,128)(2,1)S(1)}, u32[]{:S(2)}, u32[]{:S(2)}) %collective-permute-start.39) | collective-permute-done | bytes 786464 | tf_op jit(solution)/shard_map/ppermute | solution.py:378
  518.5 8.6 %shard_map.312 = (bf16[2,512,768]{2,1,0:T(8,128)(2,1)}, bf16[2,528,768]{2,1,0:T(8,128)(2,1)}, f32[2,8,768]{2,1,0:T(8,128)S(1)}, bf16[2,128,768]{2,1,0:T(8,128)(2,1)S(1)}) custom-call(f32[2,512,768]{2,1,0:T(8,128)} %fusion.6.gg_ref, f32[2,512,768]{2,1,0:T(8,128)} %get-tuple-element.88.core_ref, f32[2,528,768]{2,1,0:T(8,128)} %fusion.12.z_ref, ...), custom_call_target="tpu_custom_call" | custom-call | flops 402653184 | bytes 16836608 | tf_op jit(solution)/shard_map/pallas_call | solution.py:351
  528.4 21.0 %collective-permute-done.43.dso_ref = bf16[2,128,768]{2,1,0:T(8,128)(2,1)S(1)} collective-permute-done((bf16[2,128,768]{2,1,0:T(8,128)(2,1)S(1)}, bf16[2,128,768]{2,1,0:T(8,128)(2,1)S(1)}, u32[]{:S(2)}, u32[]{:S(2)}) %collective-permute-start.43) | collective-permute-done | bytes 393248 | tf_op jit(solution)/shard_map/ppermute | solution.py:381
  549.4 28.9 %shard_map.313 = (bf16[2,528,1152]{2,1,0:T(8,128)(2,1)}, f32[2,8,1024]{2,1,0:T(8,128)S(1)}, f32[2,8,128]{2,1,0:T(8,128)S(1)}) custom-call(bf16[2,512,768]{2,1,0:T(8,128)(2,1)} %get-tuple-element.90.gcore_ref, bf16[2,512,1024]{2,1,0:T(8,128)(2,1)} %get-tuple-element.70.xb_ref, f32[2,512,256]{2,1,0:T(8,128)S(1)} %get-tuple-element.71.aux_ref, ...), custom_call_target="tpu_custom_call" | custom-call | flops 1610612736 | bytes 18348032 | tf_op jit(solution)/shard_map/pallas_call | solution.py:351
  578.3 8.6 %fusion = bf16[1536,1152]{1,0:T(8,128)(2,1)} fusion(bf16[2,528,1152]{2,1,0:T(8,128)(2,1)} %get-tuple-element.93, bf16[1,528,1536]{2,1,0:T(8,128)(2,1)} %bitcast.1, bf16[1,528,1536]{2,1,0:T(8,128)(2,1)S(1)} %bitcast.234), kind=kOutput, calls=%fused_computation.2 | convolution fusion | flops 3740516352 | bytes 9216000 | tf_op jit(solution)/shard_map/dot_general | solution.py:543
  633.9 18.4 %collective-permute-done.67 = bf16[192,256]{1,0:T(8,128)(2,1)S(1)} collective-permute-done((bf16[192,256]{1,0:T(8,128)(2,1)S(1)}, bf16[192,256]{1,0:T(8,128)(2,1)S(1)}, u32[]{:S(2)}, u32[]{:S(2)}) %collective-permute-start.67) | collective-permute-done | bytes 98336 | tf_op jit(solution)/shard_map/ppermute | solution.py:378
  666.7 8.3 %collective-permute-done.61 = bf16[192,896]{1,0:T(8,128)(2,1)S(1)} collective-permute-done((bf16[192,896]{1,0:T(8,128)(2,1)S(1)}, bf16[192,896]{1,0:T(8,128)(2,1)S(1)}, u32[]{:S(2)}, u32[]{:S(2)}) %collective-permute-start.61) | collective-permute-done | bytes 344096 | tf_op jit(solution)/shard_map/ppermute | solution.py:381
  704.5 20.2 %collective-permute-done.57 = bf16[192,1536]{1,0:T(8,128)(2,1)S(1)} collective-permute-done((bf16[192,1536]{1,0:T(8,128)(2,1)S(1)}, bf16[192,1536]{1,0:T(8,128)(2,1)S(1)}, u32[]{:S(2)}, u32[]{:S(2)}) %collective-permute-start.57) | collective-permute-done | bytes 589856 | tf_op jit(solution)/shard_map/ppermute | solution.py:381
  736.2 12.8 %collective-permute-done.59 = bf16[192,896]{1,0:T(8,128)(2,1)S(1)} collective-permute-done((bf16[192,896]{1,0:T(8,128)(2,1)S(1)}, bf16[192,896]{1,0:T(8,128)(2,1)S(1)}, u32[]{:S(2)}, u32[]{:S(2)}) %collective-permute-start.59) | collective-permute-done | bytes 344096 | tf_op jit(solution)/shard_map/ppermute | solution.py:381
  759.2 19.5 %collective-permute-done.55 = bf16[192,1536]{1,0:T(8,128)(2,1)} collective-permute-done((bf16[192,1536]{1,0:T(8,128)(2,1)}, bf16[192,1536]{1,0:T(8,128)(2,1)}, u32[]{:S(2)}, u32[]{:S(2)}) %collective-permute-start.55) | collective-permute-done | bytes 589856 | tf_op jit(solution)/shard_map/ppermute | solution.py:381
  (544 shorter events, 325.8 us)
Async XLA Ops:
  7.2 115.9 %all-gather.7.cloned.1.call-start = ((), (), s32[]{:S(2)}) async-start(), calls=%async_computation.4 | async-start | bytes 4423680 | tf_op jit(solution)/shard_map/all_gather | solution.py:428
  23.7 125.1 %all-gather.9.cloned.1.call-start = ((), (), s32[]{:S(2)}) async-start(), calls=%async_computation.5 | async-start | bytes 2949120 | tf_op jit(solution)/shard_map/all_gather | solution.py:428
  24.8 25.5 %collective-permute-start.10 = (bf16[192,1536]{1,0:T(8,128)(2,1)S(1)}, bf16[192,1536]{1,0:T(8,128)(2,1)S(1)}, u32[]{:S(2)}, u32[]{:S(2)}) collective-permute-start(bf16[192,1536]{1,0:T(8,128)(2,1)S(1)} %pad_maximum_fusion.15), channel_id=1, source_target_pairs={{0,0},{1,4},{2,1},{3,5},{4,2},{5,6},{6,3},{7,7},{8,8},{9,12},{10,9... | collective-permute-start | bytes 1769480 | tf_op jit(solution)/shard_map/ppermute | solution.py:378
  51.6 115.0 %all-gather.11.cloned.1.call-start = ((), (), s32[]{:S(2)}) async-start(), calls=%async_computation.6 | async-start | bytes 2949120 | tf_op jit(solution)/shard_map/all_gather | solution.py:428
  52.6 41.8 %collective-permute-start.20 = (bf16[192,896]{1,0:T(8,128)(2,1)}, bf16[192,896]{1,0:T(8,128)(2,1)}, u32[]{:S(2)}, u32[]{:S(2)}) collective-permute-start(bf16[192,896]{1,0:T(8,128)(2,1)} %fusion.69), channel_id=1, source_target_pairs={{0,0},{1,4},{2,1},{3,5},{4,2},{5,6},{6,3},{7,7},{8,8},{9,12},{10,9... | collective-permute-start | bytes 1032200 | tf_op jit(solution)/shard_map/ppermute | solution.py:378
  65.5 34.1 %collective-permute-start.21 = (bf16[192,896]{1,0:T(8,128)(2,1)}, bf16[192,896]{1,0:T(8,128)(2,1)}, u32[]{:S(2)}, u32[]{:S(2)}) collective-permute-start(bf16[192,896]{1,0:T(8,128)(2,1)} %fusion.69), channel_id=1, source_target_pairs={{0,2},{1,6},{2,3},{3,7},{4,0},{5,4},{6,1},{7,5},{8,10},{9,14},{10,... | collective-permute-start | bytes 1032200 | tf_op jit(solution)/shard_map/ppermute | solution.py:378
  65.6 171.3 %all-gather.13.cloned.1.call-start = ((), (), s32[]{:S(2)}) async-start(), calls=%async_computation.7 | async-start | bytes 4423680 | tf_op jit(solution)/shard_map/all_gather | solution.py:428
  68.8 21.1 %collective-permute-start = (bf16[16,1536]{1,0:T(8,128)(2,1)}, bf16[16,1536]{1,0:T(8,128)(2,1)}, u32[]{:S(2)}, u32[]{:S(2)}) collective-permute-start(bf16[16,1536]{1,0:T(8,128)(2,1)} %slice.492), channel_id=1, source_target_pairs={{1,2},{5,6},{9,10},{13,14},{17,18},{21,22},{25,26},{29,30}} | collective-permute-start | bytes 147464 | tf_op jit(solution)/shard_map/ppermute | solution.py:378
  70.1 23.3 %collective-permute-start.1 = (bf16[16,1536]{1,0:T(8,128)(2,1)}, bf16[16,1536]{1,0:T(8,128)(2,1)}, u32[]{:S(2)}, u32[]{:S(2)}) collective-permute-start(bf16[16,1536]{1,0:T(8,128)(2,1)} %slice.492), channel_id=1, source_target_pairs={{1,3},{5,7},{9,11},{13,15},{17,19},{21,23},{25,27},{29,31}} | collective-permute-start | bytes 147464 | tf_op jit(solution)/shard_map/ppermute | solution.py:378
  77.7 94.7 %collective-permute-start.24 = (bf16[192,1536]{1,0:T(8,128)(2,1)}, bf16[192,1536]{1,0:T(8,128)(2,1)}, u32[]{:S(2)}, u32[]{:S(2)}) collective-permute-start(bf16[192,1536]{1,0:T(8,128)(2,1)} %pad_maximum_fusion.16), channel_id=1, source_target_pairs={{0,0},{1,4},{2,1},{3,5},{4,2},{5,6},{6,3},{7,7},{8,8},{9,12},{10,9... | collective-permute-start | bytes 1769480 | tf_op jit(solution)/shard_map/ppermute | solution.py:378
  89.9 82.4 %collective-permute-start.25 = (bf16[192,1536]{1,0:T(8,128)(2,1)}, bf16[192,1536]{1,0:T(8,128)(2,1)}, u32[]{:S(2)}, u32[]{:S(2)}) collective-permute-start(bf16[192,1536]{1,0:T(8,128)(2,1)} %pad_maximum_fusion.16), channel_id=1, source_target_pairs={{0,2},{1,6},{2,3},{3,7},{4,0},{5,4},{6,1},{7,5},{8,10},{9,14},{10,... | collective-permute-start | bytes 1769480 | tf_op jit(solution)/shard_map/ppermute | solution.py:378
  93.5 24.7 %collective-permute-start.2 = (bf16[256,1536]{1,0:T(8,128)(2,1)}, bf16[256,1536]{1,0:T(8,128)(2,1)}, u32[]{:S(2)}, u32[]{:S(2)}) collective-permute-start(bf16[256,1536]{1,0:T(8,128)(2,1)} %copy-done.25), channel_id=1, source_target_pairs={{0,1},{1,0},{2,3},{3,2},{4,5},{5,4},{6,7},{7,6},{8,9},{9,8},{10,11... | collective-permute-start | bytes 2359304 | tf_op jit(solution)/shard_map/ppermute | solution.py:378
  94.4 25.2 %collective-permute-start.8 = (f32[2,7,768]{2,1,0:T(8,128)S(1)}, f32[2,7,768]{2,1,0:T(8,128)S(1)}, u32[]{:S(2)}, u32[]{:S(2)}) collective-permute-start(f32[2,7,768]{2,1,0:T(8,128)S(1)} %copy-done.36), channel_id=1, source_target_pairs={{0,0},{1,4},{2,1},{3,5},{4,2},{5,6},{6,3},{7,7},{8,8},{9,12},{10,9... | collective-permute-start | bytes 129032 | tf_op jit(solution)/shard_map/ppermute | solution.py:378
  101.9 166.3 %all-gather.15.cloned.1.call-start = ((), (), s32[]{:S(2)}) async-start(), calls=%async_computation.8 | async-start | bytes 2949120 | tf_op jit(solution)/shard_map/all_gather | solution.py:428
  174.8 111.7 %all-gather.17.cloned.1.call-start = ((), (), s32[]{:S(2)}) async-start(), calls=%async_computation.9 | async-start | bytes 2949120 | tf_op jit(solution)/shard_map/all_gather | solution.py:428
  183.6 27.5 %collective-permute-start.15 = (bf16[256,1536]{1,0:T(8,128)(2,1)}, bf16[256,1536]{1,0:T(8,128)(2,1)}, u32[]{:S(2)}, u32[]{:S(2)}) collective-permute-start(bf16[256,1536]{1,0:T(8,128)(2,1)} %dynamic-slice_convert_fusion.3), channel_id=1, source_target_pairs={{0,1},{1,0},{2,3},{3,2},{4,5},{5,4},{6,7},{7,6},{8,9},{9,8},{10,11... | collective-permute-start | bytes 2359304 | tf_op jit(solution)/shard_map/ppermute | solution.py:378
  217.2 411.6 %reduce-scatter.11.cloned.1.call-start = ((), (), s32[]{:S(2)}) async-start(), calls=%async_computation.11 | async-start | bytes 4423680 | tf_op jit(solution)/shard_map/reduce_scatter | solution.py:588
  295.3 26.8 %collective-permute-start.29 = (bf16[256,1536]{1,0:T(8,128)(2,1)S(1)}, bf16[256,1536]{1,0:T(8,128)(2,1)S(1)}, u32[]{:S(2)}, u32[]{:S(2)}) collective-permute-start(bf16[256,1536]{1,0:T(8,128)(2,1)S(1)} %dynamic-slice_convert_fusion.2), channel_id=1, source_target_pairs={{0,1},{1,0},{2,3},{3,2},{4,5},{5,4},{6,7},{7,6},{8,9},{9,8},{10,11... | collective-permute-start | bytes 2359304 | tf_op jit(solution)/shard_map/ppermute | solution.py:378
  365.1 22.1 %collective-permute-start.34 = (bf16[2,128,768]{2,1,0:T(8,128)(2,1)S(1)}, bf16[2,128,768]{2,1,0:T(8,128)(2,1)S(1)}, u32[]{:S(2)}, u32[]{:S(2)}) collective-permute-start(bf16[2,128,768]{2,1,0:T(8,128)(2,1)S(1)} %get-tuple-element.86), channel_id=1, source_target_pairs={{2,0},{3,1},{6,4},{7,5},{10,8},{11,9},{14,12},{15,13},{18,16},{19,... | collective-permute-start | bytes 1179656 | tf_op jit(solution)/shard_map/ppermute | solution.py:381
  424.9 267.1 %reduce-scatter.15.cloned.1.call-start = ((), (), s32[]{:S(2)}) async-start(), calls=%async_computation.13 | async-start | bytes 5898240
  453.1 250.4 %reduce-scatter.9.cloned.1.call-start = ((), (), s32[]{:S(2)}) async-start(), calls=%async_computation.10 | async-start | bytes 4423680 | tf_op jit(solution)/shard_map/reduce_scatter | solution.py:588
  461.3 19.4 %collective-permute-start.38 = (bf16[16,1536]{1,0:T(8,128)(2,1)S(1)}, bf16[16,1536]{1,0:T(8,128)(2,1)S(1)}, u32[]{:S(2)}, u32[]{:S(2)}) collective-permute-start(bf16[16,1536]{1,0:T(8,128)(2,1)S(1)} %slice.700), channel_id=1, source_target_pairs={{3,1},{7,5},{11,9},{15,13},{19,17},{23,21},{27,25},{31,29}} | collective-permute-start | bytes 147464 | tf_op jit(solution)/shard_map/ppermute | solution.py:381
  527.1 22.2 %collective-permute-start.43 = (bf16[2,128,768]{2,1,0:T(8,128)(2,1)S(1)}, bf16[2,128,768]{2,1,0:T(8,128)(2,1)S(1)}, u32[]{:S(2)}, u32[]{:S(2)}) collective-permute-start(bf16[2,128,768]{2,1,0:T(8,128)(2,1)S(1)} %get-tuple-element.92), channel_id=1, source_target_pairs={{2,0},{3,1},{6,4},{7,5},{10,8},{11,9},{14,12},{15,13},{18,16},{19,... | collective-permute-start | bytes 1179656 | tf_op jit(solution)/shard_map/ppermute | solution.py:381
  587.0 162.1 %reduce-scatter.13.cloned.1.call-start = ((), (), s32[]{:S(2)}) async-start(), calls=%async_computation.12 | async-start | bytes 5898240
  630.9 33.2 %collective-permute-start.45 = (bf16[256,1536]{1,0:T(8,128)(2,1)S(1)}, bf16[256,1536]{1,0:T(8,128)(2,1)S(1)}, u32[]{:S(2)}, u32[]{:S(2)}) collective-permute-start(bf16[256,1536]{1,0:T(8,128)(2,1)S(1)} %dynamic-slice_convert_fusion), channel_id=1, source_target_pairs={{0,1},{1,0},{2,3},{3,2},{4,5},{5,4},{6,7},{7,6},{8,9},{9,8},{10,11... | collective-permute-start | bytes 2359304 | tf_op jit(solution)/shard_map/ppermute | solution.py:378
  631.8 20.5 %collective-permute-start.67 = (bf16[192,256]{1,0:T(8,128)(2,1)S(1)}, bf16[192,256]{1,0:T(8,128)(2,1)S(1)}, u32[]{:S(2)}, u32[]{:S(2)}) collective-permute-start(bf16[192,256]{1,0:T(8,128)(2,1)S(1)} %fusion.71), channel_id=1, source_target_pairs={{0,1},{1,0},{2,3},{3,2},{4,5},{5,4},{6,7},{7,6},{8,9},{9,8},{10,11... | collective-permute-start | bytes 294920 | tf_op jit(solution)/shard_map/ppermute | solution.py:378
  632.6 33.3 %collective-permute-start.47 = (bf16[16,1536]{1,0:T(8,128)(2,1)S(1)}, bf16[16,1536]{1,0:T(8,128)(2,1)S(1)}, u32[]{:S(2)}, u32[]{:S(2)}) collective-permute-start(bf16[16,1536]{1,0:T(8,128)(2,1)S(1)} %slice.699), channel_id=1, source_target_pairs={{3,1},{7,5},{11,9},{15,13},{19,17},{23,21},{27,25},{31,29}} | collective-permute-start | bytes 147464 | tf_op jit(solution)/shard_map/ppermute | solution.py:381
  633.3 32.6 %collective-permute-start.46 = (bf16[16,1536]{1,0:T(8,128)(2,1)S(1)}, bf16[16,1536]{1,0:T(8,128)(2,1)S(1)}, u32[]{:S(2)}, u32[]{:S(2)}) collective-permute-start(bf16[16,1536]{1,0:T(8,128)(2,1)S(1)} %slice.699), channel_id=1, source_target_pairs={{2,1},{6,5},{10,9},{14,13},{18,17},{22,21},{26,25},{30,29}} | collective-permute-start | bytes 147464 | tf_op jit(solution)/shard_map/ppermute | solution.py:381
  694.1 30.6 %collective-permute-start.57 = (bf16[192,1536]{1,0:T(8,128)(2,1)S(1)}, bf16[192,1536]{1,0:T(8,128)(2,1)S(1)}, u32[]{:S(2)}, u32[]{:S(2)}) collective-permute-start(bf16[192,1536]{1,0:T(8,128)(2,1)S(1)} %get-tuple-element.270), channel_id=1, source_target_pairs={{0,0},{4,1},{1,2},{5,3},{2,4},{6,5},{3,6},{7,7},{8,8},{12,9},{9,10... | collective-permute-start | bytes 1769480 | tf_op jit(solution)/shard_map/ppermute | solution.py:381
  704.4 20.4 %collective-permute-start.63 = (bf16[192,256]{1,0:T(8,128)(2,1)S(1)}, bf16[192,256]{1,0:T(8,128)(2,1)S(1)}, u32[]{:S(2)}, u32[]{:S(2)}) collective-permute-start(bf16[192,256]{1,0:T(8,128)(2,1)S(1)} %constant_dynamic-slice_fusion.1), channel_id=1, source_target_pairs={{0,4},{1,5},{2,6},{3,7},{4,0},{5,1},{6,2},{7,3},{8,12},{9,13},{10,... | collective-permute-start | bytes 294920 | tf_op jit(solution)/shard_map/ppermute | solution.py:378
  729.0 20.0 %collective-permute-start.59 = (bf16[192,896]{1,0:T(8,128)(2,1)S(1)}, bf16[192,896]{1,0:T(8,128)(2,1)S(1)}, u32[]{:S(2)}, u32[]{:S(2)}) collective-permute-start(bf16[192,896]{1,0:T(8,128)(2,1)S(1)} %get-tuple-element.280), channel_id=1, source_target_pairs={{0,0},{4,1},{1,2},{5,3},{2,4},{6,5},{3,6},{7,7},{8,8},{12,9},{9,10... | collective-permute-start | bytes 1032200 | tf_op jit(solution)/shard_map/ppermute | solution.py:381
  752.1 26.7 %collective-permute-start.55 = (bf16[192,1536]{1,0:T(8,128)(2,1)}, bf16[192,1536]{1,0:T(8,128)(2,1)}, u32[]{:S(2)}, u32[]{:S(2)}) collective-permute-start(bf16[192,1536]{1,0:T(8,128)(2,1)} %get-tuple-element.268), channel_id=1, source_target_pairs={{0,0},{4,1},{1,2},{5,3},{2,4},{6,5},{3,6},{7,7},{8,8},{12,9},{9,10... | collective-permute-start | bytes 1769480 | tf_op jit(solution)/shard_map/ppermute | solution.py:381
  (124 other events, 1379.9 us)
Sparse Core Ops, SparseCore 0:
  23.8 54.2 all-gather.6
  80.5 37.4 all-gather.8
  120.5 37.4 all-gather.10
  160.3 47.2 all-gather.12
  209.8 37.4 all-gather.14
  249.0 37.4 all-gather.16
  425.0 45.7 reduce-scatter.10
  473.8 57.0 reduce-scatter.14
  587.1 45.4 reduce-scatter.8
  635.4 58.3 reduce-scatter.12

commit v2 on v1

v2 whole, which is shorter than its diff:
```python
import functools

import jax
import jax.numpy as jnp
import numpy as np
from jax import lax
from jax.experimental import pallas as pl
from jax.experimental.pallas import tpu as pltpu
from jax.sharding import PartitionSpec as P

INNER = 3072
HEADDIM = 64
STATE = 128
LAYERS = 2
EPSILON = 1e-05
HALO = 16
CHUNK = 128
LANES = 128

BF = jnp.bfloat16
F32 = jnp.float32
EXACT = lax.Precision.HIGHEST


def dot(left, right, dims=((1,), (0,)), precision=None):
    return lax.dot_general(
        left, right, (dims, ((), ())), preferred_element_type=F32, precision=precision
    )


def split(values):
    high = values.astype(BF)
    return high, (values - high.astype(F32)).astype(BF)


def spread(values, e2_ref):
    return dot(jnp.concatenate(split(values), axis=1), e2_ref[...])


def head_sum(values, hm_ref):
    high, low = split(values)
    return dot(high, hm_ref[...]) + dot(low, hm_ref[...])


def softplus(values):
    return jnp.maximum(values, 0.0) + jnp.log1p(jnp.exp(-jnp.abs(values)))


def triangle(size, lower):
    rows = lax.broadcasted_iota(jnp.int32, (size, size), 0)
    cols = lax.broadcasted_iota(jnp.int32, (size, size), 1)
    return rows >= cols if lower else rows <= cols


def convolve(window, marks, cw, lanes):
    size = window.shape[0] - 8
    total = cw[4:5, lanes] + cw[3:4, lanes] * window[8:]
    for lag in (1, 2, 3):
        earlier = window[8 - lag : 8 - lag + size]
        total = total + cw[3 - lag : 4 - lag, lanes] * (earlier * marks[:, lag - 1 : lag])
    return total


def place(at_ref, j, side, piece, block):
    return pl.multiple_of((at_ref[0] ^ j) * piece + side * block, block)


def fetch_front(at_ref, pieces, w_ref, sems):
    size = pieces[0].shape[0]
    copies = []
    for j, piece in enumerate(pieces):
        row = pl.multiple_of((at_ref[2] ^ j) * size, size) if len(pieces) > 1 else 0
        copies.append(pltpu.make_async_copy(piece, w_ref.at[pl.ds(row, size), :], sems.at[j]))
    for copy in copies:
        copy.start()
    return copies


def start_copy(source, target, sem):
    copy = pltpu.make_async_copy(source, target, sem)
    copy.start()
    return copy


def fetch_rest(rest_ref, low, w_ref, sem):
    copy = pltpu.make_async_copy(rest_ref.at[:, pl.ds(low, w_ref.shape[1])], w_ref, sem)
    copy.start()
    return copy


def front_kernel(*refs, inner, half_size, chips, ready):
    at_ref, refs = refs[0], refs[1:]
    ours, theirs, refs = refs[:half_size], refs[half_size : 2 * half_size], refs[2 * half_size :]
    pieces, refs = refs[:chips], refs[chips:]
    cm_ref, lnk_ref, cw_ref, hp_ref, e2_ref = refs[:5]
    (far_toks_ref, far_raw_ref, head_ref, xb_ref, aux_ref, sloc_ref, tail_ref, edge_ref, send_ref,
     state_ref, raw_ref, w_ref, toks_ref, rawl_ref, sems) = refs[-15:]
    copies = fetch_front(at_ref, pieces, w_ref, sems)
    count = xb_ref.shape[0]
    wide = inner + 2 * STATE
    block = ours[0].shape[0]
    core = at_ref[1]
    toks_ref[:HALO, :] = jnp.zeros((HALO, toks_ref.shape[1]), BF)
    for j in range(half_size):
        for part, side in ((ours[j], core), (theirs[j], 1 - core)):
            row = place(at_ref, j, side, 2 * block, block) + HALO
            toks_ref[pl.ds(pl.multiple_of(row, HALO), block), :] = part[...]
    leaving = [start_copy(toks_ref, far_toks_ref, sems.at[chips])]
    for copy in copies:
        copy.wait()
    for low in range(0, wide + LANES, 2 * LANES):
        lanes = slice(low, min(low + 2 * LANES, wide + LANES))
        raw_ref[:, lanes] = dot(toks_ref[...], w_ref[:, lanes])
        rawl_ref[:, lanes] = raw_ref[:, lanes].astype(BF)
    leaving.append(start_copy(rawl_ref, far_raw_ref, sems.at[chips + 1]))
    head_ref[...] = raw_ref[HALO : 2 * HALO, :wide]
    tail_ref[...] = raw_ref[count + HALO - 8 :, :wide]
    edge_ref[...] = toks_ref[count:, :]
    ready()
    lower = triangle(CHUNK, True).astype(F32)
    state_ref[...] = jnp.zeros_like(state_ref)

    def step_chunk(k, carry):
        base = pl.multiple_of(k * CHUNK, CHUNK)
        here = pl.ds(base, CHUNK)
        marks = cm_ref[pl.ds(base + HALO, CHUNK), :]
        for low in range(0, wide, STATE):
            lanes = slice(low, low + STATE)
            window = raw_ref[pl.ds(base + HALO - 8, CHUNK + 8), lanes]
            pre = convolve(window, marks, cw_ref, lanes)
            xb_ref[here, lanes] = (pre * jax.nn.sigmoid(pre)).astype(BF)
        raw_dt = raw_ref[pl.ds(base + HALO, CHUNK), wide:]
        step = softplus(raw_dt + hp_ref[0:1, :])
        cum = dot(lower, -hp_ref[1:2, :] * step, precision=EXACT)
        aux_ref[here, :LANES] = step
        aux_ref[here, LANES:] = cum
        end = cum[CHUNK - 1 :, :]
        gain = jnp.exp(end - cum) * marks[:, 3:4] * step
        scaled = (spread(gain, e2_ref) * xb_ref[here, :inner].astype(F32)).astype(BF)
        b_rows = xb_ref[here, inner : inner + STATE]
        local = dot(b_rows, scaled, ((0,), (0,)))
        keep = spread(jnp.exp(end) * lnk_ref[pl.ds(k * 8, 8), :], e2_ref)[0:1]
        sloc_ref[k] = state_ref[...].astype(BF)
        state_ref[...] = keep * state_ref[...] + local
        return carry

    lax.fori_loop(0, count // CHUNK, step_chunk, 0)
    send_ref[...] = state_ref[...].astype(BF)
    for copy in leaving:
        copy.wait()


def pair_lanes(values, lane):
    high = values.astype(BF).astype(F32)
    return jnp.where(lane == 0, high, jnp.where(lane == 1, values - high, 0.0)).astype(BF)


def read_pair(tile):
    return tile[:, 0:1].astype(F32) + tile[:, 1:2].astype(F32)


def scan_kernel(*refs, inner, half_size, ready):
    (at_ref, far_toks_ref, old_ref, rest_ref, aux_ref, sloc_ref, send_ref, sin_ref, tail_ref,
     head_ref, cm_ref, segr_ref, lnk_ref, gp_ref, cw_ref, e2_ref) = refs[:16]
    (*far_refs, part_ref, xb_ref, zl_ref, core_ref, act_ref, sst_ref, toks_ref,
     extra_ref, z_ref, wz_ref, wo_ref, sems) = refs[-17:]
    copy_toks = start_copy(far_toks_ref, toks_ref, sems.at[2])
    copy_z = fetch_rest(rest_ref, 0, wz_ref, sems.at[0])
    copy_out = fetch_rest(rest_ref, inner, wo_ref, sems.at[1])
    count = xb_ref.shape[0]
    wide = inner + 2 * STATE
    width = toks_ref.shape[1]
    lower = triangle(CHUNK, True)
    lane = lax.broadcasted_iota(jnp.int32, (CHUNK, STATE), 1)
    first = lane < HEADDIM
    copy_toks.wait()
    copy_z.wait()
    for low in range(0, inner, 2 * LANES):
        lanes = slice(low, min(low + 2 * LANES, inner))
        z_ref[:, lanes] = dot(toks_ref[HALO:, :], wz_ref[:, lanes])
    ready()
    xb_ref[...] = old_ref[...]
    marks = cm_ref[HALO : 2 * HALO, :]
    for low in range(0, wide, STATE):
        lanes = slice(low, low + STATE)
        window = jnp.concatenate([tail_ref[:, lanes], head_ref[:, lanes]], axis=0)
        pre = convolve(window, marks, cw_ref, lanes)
        xb_ref[:HALO, lanes] = (pre * jax.nn.sigmoid(pre)).astype(BF)
    end = aux_ref[CHUNK - 1 : CHUNK, LANES:]
    gain = jnp.exp(end - aux_ref[:HALO, LANES:]) * marks[:, 3:4] * aux_ref[:HALO, :LANES]
    gain = spread(gain, e2_ref)

    def local_state(rows):
        scaled = (gain * rows[:, :inner].astype(F32)).astype(BF)
        return dot(rows[:, inner : inner + STATE], scaled, ((0,), (0,)))

    change = local_state(xb_ref[:HALO, :]) - local_state(old_ref[:HALO, :])
    extra_ref[...] = sin_ref[...].astype(F32)

    def step_chunk(k, carry):
        base = pl.multiple_of(k * CHUNK, CHUNK)
        here = pl.ds(base, CHUNK)
        marks = cm_ref[pl.ds(base + HALO, CHUNK), :]
        incoming = (sloc_ref[k].astype(F32) + extra_ref[...]).astype(BF)
        sst_ref[k] = incoming
        b_rows = xb_ref[here, inner : inner + STATE]
        c_rows = xb_ref[here, inner + STATE : inner + 2 * STATE]
        scores = dot(c_rows, b_rows, ((1,), (1,)))
        allowed = (marks[:, 5:6] == segr_ref[0:1, here]) & lower
        scores = jnp.where(allowed, scores, 0.0)
        step = aux_ref[here, :LANES]
        cum = aux_ref[here, LANES:]
        cum_t = jnp.transpose(cum)
        step_wide = spread(step, e2_ref)
        carried = spread(jnp.exp(cum) * marks[:, 4:5], e2_ref) * dot(c_rows, incoming)
        squares = jnp.zeros((CHUNK, STATE), F32)
        for pair in range(inner // STATE):
            lanes = slice(pair * STATE, (pair + 1) * STATE)
            x_rows = xb_ref[here, lanes].astype(F32)
            scaled = step_wide[:, lanes] * x_rows
            within = carried[:, lanes] + gp_ref[1:2, lanes] * x_rows
            for half in range(2):
                head = 2 * pair + half
                decay = jnp.exp(
                    jnp.minimum(cum[:, head : head + 1] - cum_t[head : head + 1, :], 0.0)
                )
                mine = first if half == 0 else ~first
                part = jnp.where(mine, scaled, 0.0).astype(BF)
                within = within + dot((scores * decay).astype(BF), part)
            core_ref[here, lanes] = within
            z_rows = z_ref[here, lanes]
            zl_ref[here, lanes] = z_rows.astype(BF)
            gated = within * (z_rows * jax.nn.sigmoid(z_rows))
            act_ref[here, lanes] = (gated * gp_ref[0:1, lanes]).astype(BF)
            squares = squares + gated * gated
        part_ref[here, width:] = jnp.where(lane == 0, jnp.sum(squares, axis=1, keepdims=True), 0.0)
        end = cum[CHUNK - 1 :, :]
        keep = spread(jnp.exp(end) * lnk_ref[pl.ds(k * 8, 8), :], e2_ref)[0:1]
        extra_ref[...] = keep * extra_ref[...] + jnp.where(k == 0, change, 0.0)
        return carry

    chunks = count // CHUNK
    lax.fori_loop(0, chunks, step_chunk, 0)
    sst_ref[chunks] = (send_ref[...].astype(F32) + extra_ref[...]).astype(BF)
    here_refs = (xb_ref, zl_ref, core_ref, act_ref, sst_ref)
    leaving = [
        start_copy(near, far, sems.at[3 + i]) for i, (near, far) in enumerate(zip(here_refs, far_refs))
    ]
    copy_out.wait()
    for low in range(0, width, 2 * LANES):
        lanes = slice(low, low + 2 * LANES)
        part_ref[:, lanes] = dot(act_ref[...], wo_ref[lanes, :], ((1,), (1,)))
    for copy in leaving:
        copy.wait()


def sum_kernel(*refs, half_size, offset, noted, ready):
    at_ref, part_ref, came_ref = refs[:3]
    outs = refs[-half_size:] if noted else refs[-half_size - 1 : -1]
    block = outs[0].shape[0]
    width = part_ref.shape[1] - (LANES if noted else 0)
    lane = lax.broadcasted_iota(jnp.int32, (block, LANES), 1)
    for j in range(half_size):
        at = slice(j * block, (j + 1) * block)
        row = place(at_ref, j, at_ref[1], 2 * block, block) + offset
        stay = pl.ds(pl.multiple_of(row, HALO), block)
        total = part_ref[stay, :width] + came_ref[at, :width].astype(F32)
        outs[j][:, :width] = total.astype(outs[j].dtype)
        if noted:
            line = part_ref[stay, width : width + 1] + read_pair(came_ref[at, width:])
            if j == 0:
                outs[j][:, width:] = jnp.where(lane == 0, line, 0.0)
            else:
                outs[j][:, width:] = pair_lanes(line, lane)
    if offset:
        low = half_size * block
        refs[-1][...] = (part_ref[:offset, :] + came_ref[low:, :].astype(F32)).astype(BF)


def normalize(values, gain_ref):
    size = 1.0 / values.shape[1]
    inv_rms = lax.rsqrt(jnp.sum(values * values, axis=1, keepdims=True) * size + EPSILON)
    return values * inv_rms * gain_ref[0:1, :]


def grad_message(msg_ref, grad, mixed, inv_gate):
    width = grad.shape[1]
    scaled = (inv_gate * grad).astype(BF)
    msg_ref[:, :width] = scaled
    weight = jnp.sum(scaled.astype(F32) * mixed, axis=1, keepdims=True)
    lane = lax.broadcasted_iota(jnp.int32, (grad.shape[0], LANES), 1)
    msg_ref[:, width:] = pair_lanes(inv_gate * inv_gate * weight * (1.0 / INNER), lane)


def first_kernel(*refs, ready):
    x_ref, gain_ref = refs[:2]
    res_ref, normed_ref = refs[-2:]
    values = x_ref[...].astype(F32)
    res_ref[...] = values
    normed_ref[...] = normalize(values, gain_ref).astype(BF)


def own_kernel(*refs, half_size, top, ready):
    ready()
    sum_ref, others, refs = refs[0], refs[1:half_size], refs[half_size:]
    res_ref, more_ref = refs[:2]
    mixed_ref, gate_ref, new_ref, msg_ref = refs[-4:]
    width = res_ref.shape[1]
    mixed = sum_ref[:, :width]
    line = sum_ref[:, width : width + 1]
    for other in others:
        mixed = mixed + other[:, :width].astype(F32)
        line = line + read_pair(other[:, width:])
    inv_gate = lax.rsqrt(line * (1.0 / INNER) + EPSILON)
    mixed_ref[...] = mixed
    gate_ref[...] = jnp.broadcast_to(inv_gate, gate_ref.shape)
    values = res_ref[...] + inv_gate * mixed
    new_ref[...] = values
    if top:
        grad_message(msg_ref, more_ref[...], mixed, inv_gate)
    else:
        msg_ref[...] = normalize(values, more_ref).astype(BF)


def own_back_kernel(*refs, half_size, bottom, ready):
    ready()
    sum_ref, others, refs = refs[0], refs[1:half_size], refs[half_size:]
    halos, refs = refs[:half_size], refs[half_size:]
    grad_ref, res_ref, gain_ref = refs[:3]
    if bottom:
        new_ref, gnorm_ref, buf_ref = refs[-3:]
    else:
        mixed_ref, gate_ref = refs[3:5]
        new_ref, gnorm_ref, msg_ref, buf_ref = refs[-4:]
    block = sum_ref.shape[0]
    total = sum_ref[...]
    for other in others:
        total = total + other[...].astype(F32)
    buf_ref[...] = total
    for halo in halos:
        buf_ref[block - HALO :, :] += halo[...].astype(F32)
    total = buf_ref[...]
    values = res_ref[...]
    size = 1.0 / values.shape[1]
    inv_rms = lax.rsqrt(jnp.sum(values * values, axis=1, keepdims=True) * size + EPSILON)
    gnorm = jnp.sum(total * values * inv_rms, axis=0, keepdims=True)
    gnorm_ref[...] = jnp.broadcast_to(gnorm, gnorm_ref.shape)
    scaled = total * gain_ref[0:1, :]
    inner_term = jnp.sum(scaled * values, axis=1, keepdims=True) * size
    grad = grad_ref[...] + inv_rms * scaled - values * (inv_rms * inv_rms * inv_rms) * inner_term
    new_ref[...] = grad
    if not bottom:
        grad_message(msg_ref, grad, mixed_ref[...], gate_ref[:, 0:1])


def gate_back_kernel(*refs, inner, half_size, ready):
    at_ref, refs = refs[0], refs[1:]
    ours, theirs, refs = refs[:half_size], refs[half_size : 2 * half_size], refs[2 * half_size :]
    rest_ref, far_core_ref, far_z_ref, far_xb_ref, aux_ref, cm_ref, lnk_ref, gp_ref, e2_ref = refs[:9]
    (far_grows_ref, gcore_ref, gz_ref, ggain_ref, dsin_ref, state_ref, gg_ref, coef_ref,
     wo_ref, core_ref, z_ref, xb_ref, grows_ref, sems) = refs[-14:]
    copy_out = fetch_rest(rest_ref, inner, wo_ref, sems.at[0])
    copies = [
        start_copy(far_core_ref, core_ref, sems.at[1]),
        start_copy(far_z_ref, z_ref, sems.at[2]),
        start_copy(far_xb_ref, xb_ref, sems.at[3]),
    ]
    count = xb_ref.shape[0]
    chunks = count // CHUNK
    width = grows_ref.shape[1]
    block = ours[0].shape[0]
    core_at = at_ref[1]
    for j in range(half_size):
        for part, side in ((ours[j], core_at), (theirs[j], 1 - core_at)):
            at = pl.ds(place(at_ref, j, side, 2 * block, block), block)
            grows_ref[at, :] = part[:, :width]
            coef_ref[at, :] = jnp.broadcast_to(read_pair(part[:, width:]), (block, LANES))
    leaving = start_copy(grows_ref, far_grows_ref, sems.at[4])
    copy_out.wait()
    for low in range(0, inner, 2 * LANES):
        lanes = slice(low, min(low + 2 * LANES, inner))
        gg_ref[:, lanes] = dot(grows_ref[...], wo_ref[:, lanes])
    for copy in copies:
        copy.wait()
    ready()
    state_ref[...] = jnp.zeros_like(state_ref)
    ggain_ref[...] = jnp.zeros_like(ggain_ref)
    gz_ref[:HALO, :] = jnp.zeros((HALO, inner), BF)

    def step_chunk(turn, carry):
        k = chunks - 1 - turn
        base = pl.multiple_of(k * CHUNK, CHUNK)
        here = pl.ds(base, CHUNK)
        there = pl.ds(pl.multiple_of(base + HALO, HALO), CHUNK)
        marks = cm_ref[there, :]
        coef = coef_ref[here, 0:1]
        cum = aux_ref[here, LANES:]
        entry = spread(jnp.exp(cum) * marks[:, 4:5], e2_ref)
        c_rows = xb_ref[here, inner + STATE : inner + 2 * STATE]
        end = cum[CHUNK - 1 :, :]
        keep = spread(jnp.exp(end) * lnk_ref[pl.ds(k * 8, 8), :], e2_ref)[0:1]
        for pair in range(inner // STATE):
            lanes = slice(pair * STATE, (pair + 1) * STATE)
            z_rows = z_ref[here, lanes].astype(F32)
            core = core_ref[here, lanes]
            grad = gg_ref[here, lanes]
            sig = jax.nn.sigmoid(z_rows)
            act = z_rows * sig
            gated = core * act
            ggain_ref[0:1, lanes] += jnp.sum(grad * gated, axis=0, keepdims=True)
            grad_gated = gp_ref[0:1, lanes] * grad - coef * gated
            gcore = (grad_gated * act).astype(BF)
            gcore_ref[here, lanes] = gcore
            gz_ref[there, lanes] = (
                grad_gated * core * (sig * (1.0 + z_rows * (1.0 - sig)))
            ).astype(BF)
            scaled = (entry[:, lanes] * gcore.astype(F32)).astype(BF)
            state_ref[:, lanes] = keep[:, lanes] * state_ref[:, lanes] + dot(
                c_rows, scaled, ((0,), (0,))
            )
        return carry

    lax.fori_loop(0, chunks, step_chunk, 0)
    dsin_ref[...] = state_ref[...].astype(BF)
    leaving.wait()


def scan_back_kernel(*refs, inner, half_size, chips, ready):
    at_ref, refs = refs[0], refs[1:]
    pieces, refs = refs[:chips], refs[chips:]
    (rest_ref, far_raw_ref, far_xb_ref, far_core_ref, far_sst_ref, gcore_ref, gz_ref, aux_ref,
     dso_ref, tail_ref, cm_ref, segr_ref, lnk_ref, gp_ref, cw_ref, hp_ref, e2_ref, hm_ref) = refs[:18]
    (graw_ref, sgrad_ref, hgrad_ref, part_ref, state_ref, dpre_ref, qv_ref, xd_ref,
     raw_ref, wf_ref, wz_ref, xb_ref, core_ref, sst_ref, sems) = refs[-15:]
    first_copies = [
        start_copy(far_xb_ref, xb_ref, sems.at[chips + 2]),
        start_copy(far_sst_ref, sst_ref, sems.at[chips + 3]),
        start_copy(far_core_ref, core_ref, sems.at[chips + 4]),
    ]
    copy_raw = start_copy(far_raw_ref, raw_ref, sems.at[chips])
    copies = fetch_front(at_ref, pieces, wf_ref, sems)
    copies.append(fetch_rest(rest_ref, 0, wz_ref, sems.at[chips + 1]))
    count = xb_ref.shape[0]
    chunks = count // CHUNK
    wide = inner + 2 * STATE
    upper = triangle(CHUNK, False)
    first = lax.broadcasted_iota(jnp.int32, (CHUNK, STATE), 1) < HEADDIM
    state_ref[...] = dso_ref[...].astype(F32)
    sgrad_ref[...] = jnp.zeros_like(sgrad_ref)
    hgrad_ref[...] = jnp.zeros_like(hgrad_ref)
    dpre_ref[:HALO, :] = jnp.zeros((HALO, wide), F32)
    dpre_ref[HALO + count :, :] = jnp.zeros((HALO, wide), F32)
    graw_ref[:HALO, wide:] = jnp.zeros((HALO, LANES), BF)

    ready()
    for copy in first_copies:
        copy.wait()
    copy_raw.wait()
    raw_ref[:HALO, :wide] = jnp.concatenate(
        [jnp.zeros((HALO - 8, wide), F32), tail_ref[...]], axis=0
    ).astype(BF)

    def step_chunk(turn, carry):
        k = chunks - 1 - turn
        base = pl.multiple_of(k * CHUNK, CHUNK)
        here = pl.ds(base, CHUNK)
        there = pl.ds(pl.multiple_of(base + HALO, HALO), CHUNK)
        marks = cm_ref[there, :]
        step = aux_ref[here, :LANES]
        cum = aux_ref[here, LANES:]
        cum_t = jnp.transpose(cum)
        end = cum[CHUNK - 1 :, :]
        b_rows = xb_ref[here, inner : inner + STATE]
        c_rows = xb_ref[here, inner + STATE : wide]
        after = state_ref[...]
        after_low = after.astype(BF)
        product = jnp.sum(
            sst_ref[k + 1].astype(F32) * after_low.astype(F32), axis=0, keepdims=True
        )
        at_end = head_sum(jnp.broadcast_to(product, (8, inner)), hm_ref)[0:1]
        scores_t = dot(b_rows, c_rows, ((1,), (1,)))
        allowed = (marks[:, 5:6] == segr_ref[0:1, here]) & upper
        scores_t = jnp.where(allowed, scores_t, 0.0)
        gain = spread(jnp.exp(end - cum) * marks[:, 3:4], e2_ref)
        step_wide = spread(step, e2_ref)
        entry = spread(jnp.exp(cum) * marks[:, 4:5], e2_ref)
        keep = spread(jnp.exp(end) * lnk_ref[pl.ds(k * 8, 8), :], e2_ref)[0:1]
        outer = gain * dot(b_rows, after_low)
        scaled_grad = (entry * gcore_ref[here, :].astype(F32)).astype(BF)
        grad_c = dot(scaled_grad, sst_ref[k], ((1,), (1,)))
        scaled_x = (gain * (step_wide * xb_ref[here, :inner].astype(F32))).astype(BF)
        grad_b = dot(scaled_x, after_low, ((1,), (1,)))
        state_ref[...] = keep * after + dot(c_rows, scaled_grad, ((0,), (0,)))
        grad_scores = jnp.zeros((CHUNK, CHUNK), F32)
        for pair in range(inner // STATE):
            lanes = slice(pair * STATE, (pair + 1) * STATE)
            grad_low = gcore_ref[here, lanes]
            grad = grad_low.astype(F32)
            x_rows = xb_ref[here, lanes].astype(F32)
            wide_step = step_wide[:, lanes]
            scaled = wide_step * x_rows
            grad_u = outer[:, lanes]
            for half in range(2):
                head = 2 * pair + half
                decay = jnp.exp(
                    jnp.minimum(cum_t[head : head + 1, :] - cum[:, head : head + 1], 0.0)
                )
                mine = first if half == 0 else ~first
                part = jnp.where(mine, scaled, 0.0).astype(BF)
                grad_part = jnp.where(mine, grad, 0.0).astype(BF)
                grad_u = grad_u + dot((scores_t * decay).astype(BF), grad_part)
                grad_scores = grad_scores + dot(part, grad_low, ((1,), (1,))) * decay
            skip = gp_ref[1:2, lanes]
            qv_ref[:, lanes] = grad * (core_ref[here, lanes] - skip * x_rows) - (
                scaled.astype(BF).astype(F32) * grad_u
            )
            xd_ref[:, lanes] = x_rows * grad_u
            dpre_ref[there, lanes] = wide_step * grad_u + skip * grad
            sgrad_ref[5:6, lanes] += jnp.sum(grad * x_rows, axis=0, keepdims=True)
        grad_scores = jnp.where(allowed, grad_scores, 0.0).astype(BF)
        dpre_ref[there, inner : inner + STATE] = grad_b + dot(grad_scores, c_rows)
        dpre_ref[there, inner + STATE :] = grad_c + dot(grad_scores, b_rows, ((0,), (0,)))
        rate = hp_ref[1:2, :]
        grad_log = dot(upper.astype(F32), head_sum(qv_ref[...], hm_ref), precision=EXACT) + at_end
        grad_step = head_sum(xd_ref[...], hm_ref) - rate * grad_log
        raw_dt = raw_ref[there, wide:].astype(F32)
        grad_dt = grad_step * jax.nn.sigmoid(raw_dt + hp_ref[0:1, :])
        graw_ref[there, wide:] = grad_dt.astype(BF)
        hgrad_ref[0:1, :] += jnp.sum(grad_dt, axis=0, keepdims=True)
        hgrad_ref[1:2, :] -= rate * jnp.sum(step * grad_log, axis=0, keepdims=True)
        return carry

    lax.fori_loop(0, chunks, step_chunk, 0)

    def conv_chunk(k, carry):
        base = pl.multiple_of(k * CHUNK, CHUNK)
        there = pl.ds(pl.multiple_of(base + HALO, HALO), CHUNK)
        marks = cm_ref[there, :]
        for low in range(0, wide, STATE):
            lanes = slice(low, low + STATE)
            window = raw_ref[pl.ds(base, CHUNK + HALO), lanes].astype(F32)[HALO - 8 :]
            pre = convolve(window, marks, cw_ref, lanes)
            sig = jax.nn.sigmoid(pre)
            grad = dpre_ref[there, lanes] * (sig * (1.0 + pre * (1.0 - sig)))
            dpre_ref[there, lanes] = grad
            sgrad_ref[4:5, lanes] += jnp.sum(grad, axis=0, keepdims=True)
            sgrad_ref[3:4, lanes] += jnp.sum(grad * window[8:], axis=0, keepdims=True)
            for lag in (1, 2, 3):
                earlier = window[8 - lag : 8 - lag + CHUNK]
                sgrad_ref[3 - lag : 4 - lag, lanes] += jnp.sum(
                    grad * (earlier * marks[:, lag - 1 : lag]), axis=0, keepdims=True
                )
        return carry

    lax.fori_loop(0, chunks, conv_chunk, 0)

    def transpose_rows(start, size):
        marks = cm_ref[pl.ds(start, size + 8), :]
        for low in range(0, wide, STATE):
            lanes = slice(low, low + STATE)
            window = dpre_ref[pl.ds(start, size + 8), lanes]
            total = cw_ref[3:4, lanes] * window[:size]
            for lag in (1, 2, 3):
                masked = window[lag : lag + size] * marks[lag : lag + size, lag - 1 : lag]
                total = total + cw_ref[3 - lag : 4 - lag, lanes] * masked
            graw_ref[pl.ds(start, size), lanes] = total.astype(BF)

    transpose_rows(0, HALO)

    def back_chunk(k, carry):
        transpose_rows(pl.multiple_of(k * CHUNK + HALO, HALO), CHUNK)
        return carry

    lax.fori_loop(0, chunks, back_chunk, 0)
    width = part_ref.shape[1]
    for copy in copies:
        copy.wait()
    for low in range(0, width, 2 * LANES):
        lanes = slice(low, low + 2 * LANES)
        part_ref[:, lanes] = dot(gz_ref[...], wz_ref[lanes, :], ((1,), (1,))) + dot(
            graw_ref[...], wf_ref[lanes, :], ((1,), (1,))
        )


def weight_kernel(*refs, terms, halo, far, pieces, ready):
    refs = list(refs)
    sems = refs.pop()
    at_ref = refs.pop(0) if pieces else None
    out_ref = refs.pop()
    near = refs[-len(far) :]
    outs = refs[len(refs) - len(far) - max(pieces, 1) : len(refs) - len(far)]
    leaving = []
    copies = {}
    for i, (place_of, target) in enumerate(zip(far, near)):
        copies[place_of] = start_copy(refs[place_of], target, sems.at[i])
        refs[place_of] = target
    ready()
    tile = 2 * LANES
    low = 0
    for term in range(terms):
        left_a, right_a, left_b, right_b = refs[4 * term : 4 * term + 4]
        size = right_a.shape[1]
        for place_of in range(4 * term, 4 * term + 4):
            if place_of in copies:
                copies[place_of].wait()

        def step_tile(r, carry):
            at = pl.ds(pl.multiple_of(r * tile, tile), tile)
            total = dot(left_a[:, at], right_a[...], ((0,), (0,)))
            total = total + dot(left_b[:, at], right_b[...], ((0,), (0,)))
            if halo:
                edge_a, edge_b = refs[4 * terms : 4 * terms + 2]
                total = total + dot(edge_a[:, at], right_a[:HALO, :], ((0,), (0,)))
                total = total + dot(edge_b[:, at], right_b[:HALO, :], ((0,), (0,)))
            out_ref[at, low : low + size] = total.astype(BF)
            return carry

        lax.fori_loop(0, out_ref.shape[0] // tile, step_tile, 0)
        if not pieces:
            lanes = pl.ds(low, size)
            leaving.append(
                start_copy(out_ref.at[:, lanes], outs[0].at[:, lanes], sems.at[len(far) + term])
            )
        low += size
    for copy in leaving:
        copy.wait()
    if pieces:
        for j, piece_ref in enumerate(outs):
            size = piece_ref.shape[0]
            row = pl.multiple_of((at_ref[2] ^ j) * size, size)
            piece_ref[...] = out_ref[pl.ds(row, size), :]


def hold_kernel(*refs, ready):
    refs[-1][...] = refs[0][...]


def pick_kernel(*refs, inner, shard, layer, front, rest, ready):
    ready()
    at_ref, one_ref, two_ref = refs[:3]
    outs = refs[-(front + rest) :]
    for side in range(2):
        rows = slice(side * shard, (side + 1) * shard)
        value = jnp.where(at_ref[3] == side, one_ref[...], two_ref[...])
        low = 0
        if front:
            own_ref, other_ref = refs[3:5]
            outs[0][rows, :inner] = value[:, :inner]
            outs[0][rows, inner : inner + 2 * STATE] = jnp.where(
                at_ref[1] == side, own_ref[layer], other_ref[layer]
            )
            outs[0][rows, inner + 2 * STATE :] = value[:, inner : inner + LANES]
            low = inner + LANES
        if rest:
            outs[-1][rows, :] = value[:, low:]


def split_kernel(*refs, terms, shard, inner, front, ready):
    ready()
    at_ref, refs = refs[0], refs[1:]
    buf_ref = refs[-1]
    buf_ref[...] = tree_sum([ref[...] for ref in refs[:terms]])
    half, core = at_ref[3], at_ref[1]
    if front:
        one_ref, two_ref, keep_ref, away_ref = refs[-5:-1]
    else:
        one_ref, two_ref = refs[-3:-1]
    for out_ref, side in ((one_ref, half), (two_ref, 1 - half)):
        rows = pl.ds(pl.multiple_of(side * shard, HALO), shard)
        if front:
            out_ref[:, :inner] = buf_ref[rows, :inner].astype(BF)
            out_ref[:, inner:] = buf_ref[rows, inner + 2 * STATE :].astype(BF)
        else:
            out_ref[...] = buf_ref[rows, :].astype(BF)
    if front:
        lanes = slice(inner, inner + 2 * STATE)
        rows = pl.ds(pl.multiple_of(core * shard, HALO), shard)
        keep_ref[...] = buf_ref[rows, lanes]
        rows = pl.ds(pl.multiple_of((1 - core) * shard, HALO), shard)
        away_ref[...] = buf_ref[rows, lanes].astype(BF)


def final_kernel(*refs, layers, inner, heads, tensors, ready):
    gz_ref, gx_ref, gbc_ref, gdt_ref, gout_ref = refs[-5:]
    for l in range(layers):
        rest_one, rest_two, front_one, front_two = refs[4 * l : 4 * l + 4]
        total = rest_one[...].astype(F32) + rest_two[...].astype(F32)
        gz_ref[l] = total[:, :inner]
        gout_ref[l] = total[:, inner:]
        total = front_one[...].astype(F32) + front_two[...].astype(F32)
        gx_ref[l] = total[:, :inner]
        gdt_ref[l] = total[:, inner : inner + heads]
    gbc_ref[...] = tree_sum([ref[...] for ref in refs[4 * layers : 4 * layers + tensors]])


def gate_kernel(*refs, terms, ready):
    for source, target in zip(refs[:terms], refs[-terms:]):
        target[...] = source[...]


def away_kernel(*refs, half_size, offset, noted, ready):
    at_ref, part_ref, away_ref = refs[0], refs[1], refs[-1]
    block = (part_ref.shape[0] - offset) // (2 * half_size)
    width = part_ref.shape[1] - (LANES if noted else 0)
    lane = lax.broadcasted_iota(jnp.int32, (block, LANES), 1)
    for j in range(half_size):
        to = slice(j * block, (j + 1) * block)
        row = place(at_ref, j, 1 - at_ref[1], 2 * block, block) + offset
        go = pl.ds(pl.multiple_of(row, HALO), block)
        away_ref[to, :width] = part_ref[go, :width].astype(BF)
        if noted:
            away_ref[to, width:] = pair_lanes(part_ref[go, width : width + 1], lane)
    if offset:
        away_ref[half_size * block :, :] = part_ref[:offset, :].astype(BF)


def touch_kernel(*refs, ready):
    refs[-1][...] = jnp.zeros_like(refs[-1])


def tree_sum(values):
    values = [v.astype(F32) for v in values]
    while len(values) > 1:
        values = [a + b for a, b in zip(values[::2], values[1::2])]
    return values[0]


def add_kernel(*refs, terms, ready):
    refs[-1][...] = tree_sum([ref[...] for ref in refs[:terms]]).astype(refs[-1].dtype)


def pack_kernel(*refs, inner, layers, ready):
    out_ref = refs[-1]
    out_ref[...] = jnp.zeros_like(out_ref)
    for l in range(layers):
        ggain, sgrad, hgrad, gnorm = (
            refs[8 * l + 2 * i][...] + refs[8 * l + 2 * i + 1][...] for i in range(4)
        )
        out_ref[l, 0:5, :inner] = sgrad[0:5, :inner].astype(BF)
        out_ref[l, 5:6, :inner] = ggain[0:1, :].astype(BF)
        out_ref[l, 6:7, :inner] = sgrad[5:6, :inner].astype(BF)
        out_ref[l, 7:8, :LANES] = hgrad[0:1, :].astype(BF)
        out_ref[l, 7:8, LANES : 2 * LANES] = hgrad[1:2, :].astype(BF)
        out_ref[l, 8:13, : 2 * STATE] = sgrad[0:5, inner:].astype(BF)
        out_ref[l, 13:14, :] = gnorm[0:1, :].astype(BF)


class Queue:
    def __init__(self):
        self.last = None

    def run(
        self, kernel, operands, outs, scratch=(), scalars=0, far=(), far_out=(), staged=(),
        staged_out=(), after=(), limit=10,
    ):
        near = pl.BlockSpec(memory_space=pltpu.VMEM)
        distant = pl.BlockSpec(memory_space=pltpu.HBM)
        free = pl.BlockSpec(memory_space=pl.ANY)
        extra = list(after) + ([] if self.last is None else [self.last])
        outside = set(far) | set(staged)
        outside_out = set(far_out) | set(staged_out)
        count, staged, staged_out = len(operands), list(staged), list(staged_out)

        def wrapped(*refs):
            refs = list(refs)
            sems = refs.pop()
            base = count + len(extra)
            buffers = refs[len(refs) - len(staged) - len(staged_out) :]
            refs = refs[: len(refs) - len(buffers)]
            arriving = []
            for i, position in enumerate(staged):
                arriving.append(start_copy(refs[position], buffers[i], sems.at[i]))
                refs[position] = buffers[i]
            leaving = []
            for i, position in enumerate(staged_out, len(staged)):
                leaving.append((buffers[i], refs[base + position], sems.at[i]))
                refs[base + position] = buffers[i]

            def ready():
                for copy in arriving:
                    copy.wait()

            kernel(*refs, ready=ready)
            for copy in [start_copy(*parts) for parts in leaving]:
                copy.wait()

        specs = [pl.BlockSpec(memory_space=pltpu.SMEM)] * scalars
        specs += [distant if i in outside else near for i in range(scalars, count)]
        buffers = [(operands[i].shape, operands[i].dtype) for i in staged]
        buffers += [outs[i] for i in staged_out]
        operands = [
            pltpu.with_memory_space_constraint(v, pltpu.HBM) if i in outside else v
            for i, v in enumerate(operands)
        ]
        result = pl.pallas_call(
            wrapped,
            in_specs=specs + [free] * len(extra),
            out_specs=[distant if i in outside_out else near for i in range(len(outs))],
            out_shape=[
                pltpu.HBM(s, t) if i in outside_out else jax.ShapeDtypeStruct(s, t)
                for i, (s, t) in enumerate(outs)
            ],
            scratch_shapes=[
                pltpu.SemaphoreType.DMA(s) if t is None else pltpu.VMEM(s, t)
                for s, t in [*scratch, *buffers, ((max(len(buffers), 1),), None)]
            ],
            compiler_params=pltpu.CompilerParams(vmem_limit_bytes=limit * 1024 * 1024),
            cost_estimate=pl.CostEstimate(flops=1000, bytes_accessed=1000, transcendentals=0),
        )(*operands, *extra)
        self.last = result[-1]
        return result

    def gate(self, values, after):
        return self.run(
            functools.partial(gate_kernel, terms=len(values)), values,
            [(v.shape, v.dtype) for v in values], after=after,
        )

    def touch(self, values):
        self.run(touch_kernel, [], [((8, LANES), F32)], after=values)


def build(n_dp, n_tensor):
    axes = ("dp", "tensor")
    half_size = n_tensor // 2
    planes = [[d for d in range(n_dp) if d % 2 == c] for c in range(2)]
    plane_bits = [1 << b for b in range(1, n_dp.bit_length() - 1)]

    def pairs(route):
        found = []
        for d in range(n_dp):
            for t in range(n_tensor):
                goal = route(d, t)
                if goal is not None:
                    found.append((d * n_tensor + t, goal[0] * n_tensor + goal[1]))
        return found

    def send(value, route):
        return lax.ppermute(value, axes, pairs(route))

    def back(value, route):
        return lax.ppermute(value, axes, [(b, a) for a, b in pairs(route)])

    def to_core(d, t):
        return d ^ 1, t

    def to_plane(bits):
        return lambda d, t: (d ^ bits, t)

    def to_tensor(bits):
        return lambda d, t: (d, t ^ bits)

    def to_piece(j):
        return lambda d, t: (d, (t // half_size) * half_size + ((t % half_size) ^ j))

    def to_later(d, t):
        return (d, t + half_size) if t < half_size else None

    def to_halo(j):
        return lambda d, t: (d, half_size + j) if d % 2 == 1 and t == half_size - 1 else None

    def to_group(turn):
        def route(d, t):
            return (d & ~1) | (t % 2), t // 2 + half_size * ((d & 1) ^ turn)

        return route

    def matmul(left, right, dims=((1,), (0,))):
        return lax.dot_general(left, right, (dims, ((), ())), preferred_element_type=F32)

    def local(
        x_in, segments, norm_gain, w_z, w_x, w_bc, w_dt, conv_x, conv_x_bias, conv_bc, conv_bc_bias,
        dt_bias, a_log, d_skip, gate_gain, w_out, cotangent,
    ):
        inner = w_z.shape[2]
        heads = dt_bias.shape[1]
        piece, width = x_in.shape
        block = piece // 2
        count = half_size * piece
        rows = count + HALO
        chunks = count // CHUNK
        shard = w_z.shape[1]
        wide = inner + 2 * STATE
        place = lax.axis_index("tensor")
        dp_place = lax.axis_index("dp")
        core = dp_place % 2
        column = dp_place // 2
        half = place // half_size
        mine = place % half_size

        def cut(value, start, size):
            return lax.dynamic_slice(
                value, (start,) + (0,) * (value.ndim - 1), (size,) + value.shape[1:]
            )

        def put(value, part, start):
            return lax.dynamic_update_slice(value, part, (start,) + (0,) * (value.ndim - 1))

        def to_streams(value):
            keep, away = cut(value, core * block, block), cut(value, (1 - core) * block, block)
            came = send(away, to_core)
            return [jnp.where(core == 0, keep, came), jnp.where(core == 0, came, keep)]

        def from_streams(values):
            keep = jnp.where(core == 0, values[0], values[1])
            came = send(jnp.where(core == 0, values[1], values[0]), to_core)
            out = jnp.zeros((piece, width), F32)
            return put(put(out, keep, core * block), came, (1 - core) * block)

        def pad_lanes(value):
            return jnp.pad(value, ((0, 0), (0, LANES - value.shape[1])))

        queue = Queue()
        at = jnp.stack([mine, core, column, half]).astype(jnp.int32)
        chips = n_dp // 2

        def hold(value, after):
            return queue.run(hold_kernel, [value], [(value.shape, value.dtype)], after=after)[0]

        def regroup(value):
            return [send(value, to_group(0)), send(value, to_group(1))]

        bc_other = send(w_bc, to_core)
        def gather_plane(value):
            return lax.all_gather(value, "dp", axis=0, tiled=True, axis_index_groups=planes)

        def pick(parts, l, front, rest, after=()):
            outs = []
            if front:
                outs.append(((2 * shard, wide + LANES), BF))
            if rest:
                outs.append(((2 * shard, 2 * inner), BF))
            values = queue.run(
                functools.partial(
                    pick_kernel, inner=inner, shard=shard, layer=l, front=front, rest=rest
                ),
                [at, *parts] + ([w_bc, bc_other] if front else []),
                outs,
                scalars=1,
                after=after,
                staged_out=range(len(outs)),
            )
            values = [gather_plane(v) for v in values]
            if front:
                front_w[l] = [values[0]]
            if rest:
                rest_w[l] = values[-1]

        def front_part(l):
            return [w_x[l], pad_lanes(w_dt[l])]

        def rest_part(l):
            return [w_z[l], w_out[l].T]

        def row(value, size):
            return jnp.pad(value, ((0, 0), (0, size - value.shape[1])))[:, None]

        head_rows = jnp.concatenate([row(v, LANES) for v in (dt_bias, a_log, d_skip)], axis=2)
        head_rows = jnp.pad(head_rows, ((0, 0), (0, 0), (0, inner - 3 * LANES)))
        packed = jnp.concatenate(
            [conv_x, conv_x_bias[:, None], gate_gain[:, None], head_rows], axis=1
        )
        packed = send(packed, to_group(0))
        taps, bias, gain_own = packed[:, :4], packed[:, 4:5], packed[:, 5:6]
        dt_own, a_own, skip_own = (packed[:, 6, i * LANES : (i + 1) * LANES] for i in range(3))
        head_ok = jnp.arange(LANES) < heads
        rate_own = jnp.where(head_ok, jnp.exp(a_own), 0.0)
        skip_wide = jnp.repeat(skip_own[:, :heads], HEADDIM, axis=1)
        conv_w = jnp.concatenate(
            [
                jnp.concatenate([taps, conv_bc], axis=2),
                jnp.concatenate([bias, conv_bc_bias[:, None]], axis=2),
                jnp.zeros((LAYERS, 3, wide), F32),
            ],
            axis=1,
        )
        gate_p = jnp.concatenate(
            [gain_own, skip_wide[:, None], jnp.zeros((LAYERS, 6, inner), F32)], axis=1
        )
        head_p = jnp.concatenate(
            [dt_own[:, None], rate_own[:, None], jnp.zeros((LAYERS, 6, LANES), F32)], axis=1
        )
        member = np.arange(inner)[None, :] // HEADDIM == np.arange(LANES)[:, None]
        e2 = jnp.asarray(np.concatenate([member, member], axis=0), BF)
        hm = jnp.asarray(member.T, BF)

        seg = jnp.concatenate([jnp.full((HALO,), -1.0, F32), segments.astype(F32)])
        seg = cut(seg, half * count, rows)
        seg_other = send(seg, to_core)
        seg = jnp.stack([jnp.where(core == 0, seg, seg_other), jnp.where(core == 0, seg_other, seg)])
        tokens = seg[:, HALO:]
        lagged = [
            (tokens == seg[:, HALO - k : HALO - k + count]).astype(F32) for k in (1, 2, 3)
        ]
        by_chunk = tokens.reshape(2, chunks, CHUNK)
        last = by_chunk[:, :, -1]
        before = jnp.concatenate([seg[:, HALO - 1 : HALO], last[:, :-1]], axis=1)
        stays = (by_chunk == last[:, :, None]).astype(F32).reshape(2, count)
        enters = (by_chunk == before[:, :, None]).astype(F32).reshape(2, count)
        marks = jnp.stack(lagged + [stays, enters, tokens, tokens, tokens], axis=-1)
        marks = jnp.pad(marks, ((0, 0), (HALO, HALO), (0, 0)))
        seg_row = jnp.broadcast_to(tokens[:, None, :], (2, 8, count))
        links = (last == before).astype(F32)
        links = jnp.broadcast_to(links[:, :, None, None], (2, chunks, 8, LANES))
        links = links.reshape(2, chunks * 8, LANES)

        def exchange(value):
            return [value] + [send(value, to_piece(j)) for j in range(1, half_size)]

        def share(ours):
            return ours + [send(part, to_core) for part in ours]

        def pieces(values):
            return [send(values[j], to_piece(j)) for j in range(1, half_size)]

        mixer = functools.partial
        sizes = dict(inner=inner, half_size=half_size)
        noted = width + LANES
        gains = [jnp.broadcast_to(norm_gain[l][None], (8, width)) for l in range(LAYERS)]

        front_w, rest_w = [None] * LAYERS, [None] * LAYERS
        parts = regroup(jnp.concatenate(front_part(0), axis=1))
        start = to_streams(x_in)
        grads = to_streams(cotangent)
        residual = [[None, None] for _ in range(LAYERS + 1)]
        normed = [None, None]
        kept = [[{}, {}] for _ in range(LAYERS)]
        arrived = [None, None]

        def spread_tokens(s):
            arrived[s] = exchange(normed[s])

        def front(l, s, after=()):
            parts = [at, *share(arrived[s]), *front_w[l]]
            chips = len(front_w[l])
            (toks, raw, head, xb, aux, sloc, tail, edge, ends) = queue.run(
                mixer(front_kernel, chips=chips, **sizes),
                [*parts, marks[s], links[s], conv_w[l], head_p[l], e2],
                [((rows, width), BF), ((rows, wide + LANES), BF), ((HALO, wide), F32),
                 ((count, wide), BF), ((count, 2 * LANES), F32), ((chunks, STATE, inner), BF),
                 ((8, wide), F32), ((HALO, width), BF), ((STATE, inner), BF)],
                [((STATE, inner), F32), ((rows, wide + LANES), F32),
                 ((n_dp * shard, wide + LANES), BF), ((rows, width), BF),
                 ((rows, wide + LANES), BF), ((chips + 2,), None)],
                scalars=1,
                far=range(len(parts) - chips, len(parts)),
                far_out=(0, 1),
                staged=range(len(parts), len(parts) + 5),
                staged_out=(2, 3, 4, 5),
                limit=20,
            )
            tail, edge, ends = queue.gate([tail, edge, ends], after)
            kept[l][s].update(
                toks=toks, raw=raw, head=head, xb=xb, aux=aux, sloc=sloc, ends=ends,
                tail=send(tail, to_later), edge=send(edge, to_later), begins=send(ends, to_later),
            )

        def scan(l, s, after=()):
            v = kept[l][s]
            (xb, z, core_out, act, sst, part) = queue.run(
                mixer(scan_kernel, **sizes),
                [at, v["toks"], v["xb"], rest_w[l], v["aux"], v["sloc"], v["ends"], v["begins"],
                 v["tail"], v["head"], marks[s], seg_row[s], links[s], gate_p[l], conv_w[l], e2],
                [((count, wide), BF), ((count, inner), BF), ((count, inner), F32),
                 ((count, inner), BF), ((chunks + 1, STATE, inner), BF),
                 ((count, noted), F32)],
                [((count, wide), BF), ((count, inner), BF), ((count, inner), F32),
                 ((count, inner), BF), ((chunks + 1, STATE, inner), BF), ((rows, width), BF),
                 ((STATE, inner), F32), ((count, inner), F32), ((n_dp * shard, inner), BF),
                 ((n_dp * shard, inner), BF), ((8,), None)],
                scalars=1,
                after=[v["edge"]],
                far=(1, 3),
                far_out=range(5),
                staged=[2, 4, 5, 9, *range(10, 16)],
                limit=26,
            )
            v.update(xb=xb, z=z, core_out=core_out, act=act, sst=sst)
            send_away(v, part, 0, after)

        def send_away(v, part, offset, after):
            size = part.shape[1]
            away = queue.run(
                mixer(away_kernel, half_size=half_size, offset=offset, noted=offset == 0),
                [at, part], [((half_size * block + offset, size), BF)], scalars=1, after=after,
            )[0]
            v["sum"] = (part, send(away, to_core))

        def add_cores(l, s, has_note, after=()):
            part, came = kept[l][s]["sum"]
            size = part.shape[1]
            sums = queue.run(
                mixer(
                    sum_kernel, half_size=half_size, noted=has_note, offset=0 if has_note else HALO
                ),
                [at, part, came],
                [((block, size), F32)] + [((block, size), BF)] * (half_size - 1)
                + ([] if has_note else [((HALO, size), BF)]),
                scalars=1,
                after=after,
            )
            kept[l][s]["pieces"] = [sums[0]] + pieces(sums)
            if not has_note:
                kept[l][s]["halos"] = [back(sums[-1], to_halo(j)) for j in range(half_size)]

        def own(l, s):
            top = l == LAYERS - 1
            v = kept[l][s]
            mixed, gate, new, msg = queue.run(
                mixer(own_kernel, half_size=half_size, top=top),
                [*v["pieces"], residual[l][s], grads[s] if top else gains[l + 1]],
                [((block, width), F32), ((block, LANES), F32), ((block, width), F32),
                 ((block, noted if top else width), BF)],
                staged=(half_size, half_size + 1),
                staged_out=(0, 1, 2),
            )
            v.update(mixed=mixed, gate=gate)
            residual[l + 1][s] = new
            if top:
                arrived[s] = exchange(msg)
            else:
                normed[s] = msg
                spread_tokens(s)

        for s in range(2):
            residual[0][s], normed[s] = queue.run(
                first_kernel, [start[s], gains[0]], [((block, width), F32), ((block, width), BF)],
                staged_out=(0,),
            )
            spread_tokens(s)
        def sums_of(l, s):
            return kept[l][s]["pieces"][1:]

        pick(parts, 0, True, False)
        queue.touch([marks, seg_row, links, conv_w, gate_p, head_p])
        parts = regroup(hold(jnp.concatenate(rest_part(0), axis=1), []))
        pick(parts, 0, False, True, [*arrived[0], *arrived[1]])
        parts = [
            regroup(hold(jnp.concatenate(front_part(l) + rest_part(l), axis=1), []))
            for l in range(1, LAYERS)
        ]
        front(0, 0)
        front(0, 1, [kept[0][0]["begins"]])
        for l in range(1, LAYERS):
            pick(parts[l - 1], l, True, True)
        for l in range(LAYERS):
            scan(l, 0, arrived[1] if l > 0 else [kept[0][1]["begins"]])
            add_cores(l, 0, True)
            if l > 0:
                front(l, 1, sums_of(l, 0))
                own(l, 0)
                scan(l, 1, arrived[0])
            else:
                scan(l, 1, sums_of(l, 0))
                own(l, 0)
            add_cores(l, 1, True)
            if l + 1 < LAYERS:
                front(l + 1, 0, sums_of(l, 1))
                own(l, 1)

        def owners(messages):
            return [back(messages[0], to_group(0)), back(messages[1], to_group(1))]

        def split_rest(l):
            messages = queue.run(
                mixer(split_kernel, terms=1, shard=shard, inner=inner, front=False),
                [at, g_rest[l]],
                [((shard, 2 * inner), BF)] * 2,
                [(g_rest[l].shape, F32)],
                scalars=1,
                staged=(1,),
                limit=14,
            )
            done_rest[l] = owners(messages)

        def split_front(l, values, after=()):
            one, two, keep, away = queue.run(
                mixer(split_kernel, terms=len(values), shard=shard, inner=inner, front=True),
                [at, *values],
                [((shard, inner + LANES), BF)] * 2
                + [((shard, 2 * STATE), F32), ((shard, 2 * STATE), BF)],
                [(values[0].shape, F32)],
                scalars=1,
                after=after,
                limit=14,
            )
            done_front[l] = owners([one, two])
            bc_parts[l] = (keep, away)

        def offloaded_sum(value):
            return lax.psum_scatter(
                value, "dp", scatter_dimension=0, tiled=True, axis_index_groups=planes
            )

        def direct_start(values):
            return [values[0]] + [send(values[j], to_plane(2 * j)) for j in range(1, chips)]

        def add(parts, kind):
            return queue.run(
                mixer(add_kernel, terms=len(parts)), parts, [(parts[0].shape, kind)]
            )[0]

        all_tensor = [to_tensor(j) for j in range(1, n_tensor)]
        all_plane = [to_plane(2 * j) for j in range(1, n_dp // 2)]

        def gate_back(l, s, after=()):
            v = kept[l][s]
            (grows, gcore, gz, ggain, dsin) = queue.run(
                mixer(gate_back_kernel, **sizes),
                [at, *share(arrived[s]), rest_w[l], v["core_out"], v["z"], v["xb"], v["aux"], marks[s],
                 links[s], gate_p[l], e2],
                [((count, width), BF), ((count, inner), BF), ((rows, inner), BF), ((8, inner), F32),
                 ((STATE, inner), BF)],
                [((STATE, inner), F32), ((count, inner), F32), ((count, LANES), F32),
                 ((n_dp * shard, inner), BF), ((count, inner), F32), ((count, inner), BF),
                 ((count, wide), BF), ((count, width), BF), ((5,), None)],
                scalars=1,
                far=range(1 + 2 * half_size, 5 + 2 * half_size),
                far_out=(0,),
                staged_out=(1, 2),
                staged=range(5 + 2 * half_size, 10 + 2 * half_size),
                limit=20,
            )
            dsin, = queue.gate([dsin], after)
            v.update(grows=grows, gcore=gcore, gz=gz, ggain=ggain, dsout=back(dsin, to_later))

        def scan_back(l, s, after=()):
            v = kept[l][s]
            chips = len(front_w[l])
            (graw, sgrad, hgrad, part) = queue.run(
                mixer(scan_back_kernel, chips=chips, **sizes),
                [at, *front_w[l], rest_w[l], v["raw"], v["xb"], v["core_out"], v["sst"],
                 v["gcore"], v["gz"], v["aux"], v["dsout"], v["tail"], marks[s], seg_row[s], links[s],
                 gate_p[l], conv_w[l], head_p[l], e2, hm],
                [((rows, wide + LANES), BF), ((8, wide), F32), ((8, LANES), F32),
                 ((rows, width), F32)],
                [((STATE, inner), F32), ((count + 2 * HALO, wide), F32), ((CHUNK, inner), F32),
                 ((CHUNK, inner), F32), ((rows, wide + LANES), BF),
                 ((n_dp * shard, wide + LANES), BF), ((n_dp * shard, inner), BF),
                 ((count, wide), BF), ((count, inner), F32), ((chunks + 1, STATE, inner), BF),
                 ((chips + 5,), None)],
                scalars=1,
                far=range(1, chips + 6),
                staged=[*range(chips + 6, chips + 9), *range(chips + 10, chips + 19)],
                staged_out=(0,),
                limit=30,
            )
            send_away(v, part, HALO, after)
            v.update(graw=graw, sgrad=sgrad, hgrad=hgrad)

        def own_back(l, s, after=()):
            v = kept[l][s]
            bottom = l == 0
            before = [] if bottom else [kept[l - 1][s]["mixed"], kept[l - 1][s]["gate"]]
            result = queue.run(
                mixer(own_back_kernel, half_size=half_size, bottom=bottom),
                [*v["pieces"], *v["halos"], grads[s], residual[l][s], gains[l], *before],
                [((block, width), F32), ((8, width), F32)]
                + ([] if bottom else [((block, noted), BF)]),
                [((block, width), F32)],
                after=after,
                staged=range(2 * half_size, 2 * half_size + 3 + len(before)),
                staged_out=(0,),
            )
            grads[s], v["gnorm"] = result[:2]
            if not bottom:
                arrived[s] = exchange(result[2])

        def weights_back(l, names, pieces=0, after=()):
            one, two = kept[l]
            operands = []
            for left, right in names:
                operands += [one[left], one[right], two[left], two[right]]
            size = sum(one[right].shape[1] for _, right in names)
            halo = len(names) == 1
            if halo:
                operands += [one["edge"], two["edge"]]
            far = range(4 * len(names))
            count_out = chips if pieces else 1
            scratch = [(operands[i].shape, BF) for i in far] + [((width, size), BF)]
            result = queue.run(
                mixer(weight_kernel, terms=len(names), halo=halo, far=far, pieces=pieces),
                ([at] if pieces else []) + operands,
                [((width // count_out, size), BF)] * count_out,
                scratch + [((len(far) + len(names),), None)],
                scalars=1 if pieces else 0,
                far=[i + 1 for i in far] if pieces else far,
                far_out=() if pieces else (0,),
                staged=[len(operands) - 2 + bool(pieces), len(operands) - 1 + bool(pieces)] if halo else (),
                limit=22,
            )
            queue.touch(after)
            return result if pieces else result[0]

        rest_names = (("toks", "gz"), ("grows", "act"))
        front_names = (("toks", "graw"),)
        g_rest, g_front = [None] * LAYERS, [None] * LAYERS
        top = LAYERS - 1
        gate_back(top, 0, sums_of(top, 1))
        own(top, 1)
        gate_back(top, 1, [kept[top][0]["dsout"]])
        g_rest[top] = offloaded_sum(weights_back(top, rest_names, 0, [kept[top][1]["dsout"]]))
        done_rest, done_front, bc_parts = ([None] * LAYERS for _ in range(3))
        for l in reversed(range(LAYERS)):
            scan_back(l, 0)
            add_cores(l, 0, False)
            scan_back(l, 1, sums_of(l, 0) + kept[l][0]["halos"])
            if l == 0:
                own_back(l, 0)
                add_cores(l, 1, False)
                direct = direct_start(
                    weights_back(l, front_names, chips, sums_of(l, 1) + kept[l][1]["halos"])
                )
                for k in range(1, LAYERS):
                    split_front(k, [g_front[k]])
                split_rest(l)
                own_back(l, 1)
                earlier = [v for k in range(1, LAYERS) for v in done_front[k] + done_rest[k]]
                split_front(l, direct, done_rest[0] + earlier)
            else:
                own_back(l, 0)
                add_cores(l, 1, False)
                waiting = sums_of(l, 1) + kept[l][1]["halos"] + arrived[0]
                g_front[l] = offloaded_sum(weights_back(l, front_names, 0, waiting))
                own_back(l, 1)
                gate_back(l - 1, 0, arrived[1])
                gate_back(l - 1, 1, [kept[l - 1][0]["dsout"]])
                g_rest[l - 1] = offloaded_sum(
                    weights_back(l - 1, rest_names, 0, [kept[l - 1][1]["dsout"]])
                )
                split_rest(l)
        grad_in = from_streams(grads)
        output = from_streams(residual[LAYERS])

        names = ("ggain", "sgrad", "hgrad", "gnorm")
        packed = queue.run(
            mixer(pack_kernel, inner=inner, layers=LAYERS),
            [kept[l][s][k] for l in range(LAYERS) for k in names for s in range(2)],
            [((LAYERS, 2 * 8, width), BF)],
        )[0]
        packed = add([back(packed, to_group(0)), back(packed, to_group(1))], F32)
        common = packed[:, 8:].astype(BF)
        common = add([common] + [send(common, route) for route in all_tensor], F32)
        packed = jnp.concatenate([packed[:, :8], common], axis=1)
        low_packed = packed.astype(BF)
        packed = add([low_packed] + [send(low_packed, route) for route in all_plane], F32)

        g_bc = jnp.stack([keep for keep, _ in bc_parts]) + send(
            jnp.stack([away for _, away in bc_parts]), to_core
        ).astype(F32)
        g_bc = g_bc.astype(BF)
        parts = []
        for l in range(LAYERS):
            parts += [*done_rest[l], *done_front[l]]
        g_z, g_x, g_bc, g_dt, g_out = queue.run(
            mixer(final_kernel, layers=LAYERS, inner=inner, heads=heads, tensors=n_tensor),
            parts + [g_bc] + [send(g_bc, route) for route in all_tensor],
            [((LAYERS, shard, inner), F32), ((LAYERS, shard, inner), F32),
             ((LAYERS, shard, 2 * STATE), F32), ((LAYERS, shard, heads), F32),
             ((LAYERS, shard, inner), F32)],
            limit=16,
        )
        group, shared = packed[:, :8, :inner], packed[:, 8:]
        five = shared[:, :5, : 2 * STATE]
        head_grads = [group[:, 7, :heads], group[:, 7, LANES : LANES + heads]]
        head_grads.append(jnp.sum(group[:, 6].reshape(LAYERS, heads, HEADDIM), axis=2))
        return (
            output,
            grad_in,
            shared[:, 5],
            g_z,
            g_x,
            g_bc,
            g_dt,
            group[:, :4],
            group[:, 4],
            five[:, :4],
            five[:, 4],
            head_grads[0],
            head_grads[1],
            head_grads[2],
            group[:, 5],
            jnp.swapaxes(g_out, 1, 2),
        )

    return local


def solution(mesh):
    n_dp, n_tensor = mesh.shape["dp"], mesh.shape["tensor"]
    tokens = P(("dp", "tensor"), None)
    columns = P(None, "dp", "tensor")
    placed = (
        tokens,
        P("dp"),
        P(),
        columns,
        columns,
        P(None, "dp", None),
        columns,
        P(None, None, "tensor"),
        P(None, "tensor"),
        P(),
        P(),
        P(None, "tensor"),
        P(None, "tensor"),
        P(None, "tensor"),
        P(None, "tensor"),
        P(None, "tensor", "dp"),
        tokens,
    )
    return jax.shard_map(
        build(n_dp, n_tensor),
        mesh=mesh,
        in_specs=placed,
        out_specs=(
            tokens,
            tokens,
            P(),
            columns,
            columns,
            P(None, "dp", None),
            columns,
            P(None, None, "tensor"),
            P(None, "tensor"),
            P(),
            P(),
            P(None, "tensor"),
            P(None, "tensor"),
            P(None, "tensor"),
            P(None, "tensor"),
            P(None, "tensor", "dp"),
        ),
        check_vma=False,
    )
```

time: 799 us -> 763 us (0.955)
  Pallas kernels: 117 us -> 311 us
  matrix products: 132 us -> 0 us
  waiting for transfers between devices: 291 us -> 164 us
  starting transfers between devices: 130 us -> 196 us
  other arithmetic: 42.5 us -> 7.76 us
    pallas_call x8 -> x73, Pallas kernels: 117 us -> 311 us  [run(): pl.pallas_call(wrapped, in_specs=specs + [free] * len(extra), out_specs=[...]
    dot_general x24 -> x0, matrix products: 132 us -> none  [matmul(): lax.dot_general(left, right, (dims, ((), ())), preferred_element_type=F32)]
    ppermute x16 -> x22, waiting for transfers between devices: 106 us -> 29.5 us  [back(): return lax.ppermute(value, axes, [(b, a) for a, b in pairs(route)])]
    ppermute x53 -> x78, waiting for transfers between devices: 184 us -> 119 us  [send(): return lax.ppermute(value, axes, pairs(route))]
    ppermute x16 -> x22, starting transfers between devices: 26 us -> 78 us  [back(): return lax.ppermute(value, axes, [(b, a) for a, b in pairs(route)])]
    ppermute x53 -> x78, starting transfers between devices: 103 us -> 118 us  [send(): return lax.ppermute(value, axes, pairs(route))]
    all_gather x6 -> x4, waiting for transfers between devices: 0.79 us -> 14.1 us  [gather_plane(): lax.all_gather(value, 'dp', axis=0, tiled=True, axis_index_groups=planes)]
    concatenate x18 -> x5, other arithmetic: 11.5 us -> 2.11 us  [the longest x1 1.26 us: local(): jnp.concatenate(front_part(l) + rest_part(l), axis=1)]
  transfers between devices with their start and end apart: 79 -> 107, of which waited for: 40 -> 31; matrix products, arithmetic and copies ran while one was open for 25% -> 5% of each run, Pallas kernels for 10% -> 38%
where the time goes in v2:
time: 763 us; the launch traced here: 749 us
  Pallas kernels  311 us (41%)
  starting transfers between devices  196 us (26%)
  waiting for transfers between devices  164 us (21%)
  local copies, waits for them, and re-layouts  53.7 us (7%)
  between operations  16.9 us (2%)
  other arithmetic  7.76 us (1%)
    pallas_call x73, Pallas kernels, run(): pl.pallas_call(wrapped, in_specs=specs + [free] * len(extra), out_specs=[...  311 us
    ppermute x78, waiting for transfers between devices, send(): return lax.ppermute(value, axes, pairs(route))  119 us
    ppermute x78, starting transfers between devices, send(): return lax.ppermute(value, axes, pairs(route))  118 us
    ppermute x22, starting transfers between devices, back(): return lax.ppermute(value, axes, [(b, a) for a, b in pairs(route)])  78 us
    ppermute x22, waiting for transfers between devices, back(): return lax.ppermute(value, axes, [(b, a) for a, b in pairs(route)])  29.5 us
    unnamed x215, local copies, waits for them, and re-layouts  25.2 us
  transfers between devices with their start and end apart: 107, of which 31 were waited for; matrix products, arithmetic and copies ran while one was open for 5% of the time, Pallas kernels for 38%

profile of v2, /device:TPU:1, one launch (start us, length us, event | category | flops | bytes accessed | tf_op | source)
XLA Modules:
  0.0 749.2 jit_solution(6874317187972225611)
XLA Ops:
  27.8 11.0 %collective-permute-start.8 = (f32[2,7,768]{2,1,0:T(8,128)S(1)}, f32[2,7,768]{2,1,0:T(8,128)S(1)}, u32[]{:S(2)}, u32[]{:S(2)}) collective-permute-start(f32[2,7,768]{2,1,0:T(8,128)S(1)} %pad_maximum_fusion.3), channel_id=1, source_target_pairs={{0,0},{1,4},{2,1},{3,5},{4,2},{5,6},{6,3},{7,7},{8,8},{9,12},{10,9... | collective-permute-start | bytes 129032 | tf_op jit(solution)/shard_map/ppermute | solution.py:839
  59.9 20.1 %collective-permute-done.11.refs_6_.refs_2_ = bf16[128,1536]{1,0:T(8,128)(2,1)S(1)} collective-permute-done((bf16[128,1536]{1,0:T(8,128)(2,1)S(1)}, bf16[128,1536]{1,0:T(8,128)(2,1)S(1)}, u32[]{:S(2)}, u32[]{:S(2)}) %collective-permute-start.11) | collective-permute-done | bytes 393248 | tf_op jit(solution)/shard_map/ppermute | solution.py:839
  102.2 11.7 %shard_map.313 = (bf16[528,1536]{1,0:T(8,128)(2,1)}, bf16[528,1152]{1,0:T(8,128)(2,1)}, f32[16,1024]{1,0:T(8,128)}, bf16[512,1024]{1,0:T(8,128)(2,1)}, f32[512,2...) custom-call(s32[4]{0:T(128)S(1)} %pad_add_fusion.refs_0_, ...), custom_call_target="tpu_custom_call" | custom-call | flops 1000 | bytes 1000 | tf_op jit(solution)/shard_map/pallas_call | solution.py:795
  119.4 11.9 %shard_map.315 = (bf16[528,1536]{1,0:T(8,128)(2,1)}, bf16[528,1152]{1,0:T(8,128)(2,1)}, f32[16,1024]{1,0:T(8,128)}, bf16[512,1024]{1,0:T(8,128)(2,1)}, f32[512,2...) custom-call(s32[4]{0:T(128)S(1)} %pad_add_fusion.refs_0_, ...), custom_call_target="tpu_custom_call" | custom-call | flops 1000 | bytes 1000 | tf_op jit(solution)/shard_map/pallas_call | solution.py:795
  134.9 11.8 %collective-permute-start.14 = (bf16[16,1536]{1,0:T(8,128)(2,1)S(1)}, bf16[16,1536]{1,0:T(8,128)(2,1)S(1)}, u32[]{:S(2)}, u32[]{:S(2)}) collective-permute-start(bf16[16,1536]{1,0:T(8,128)(2,1)S(1)} %copy-done.71), channel_id=1, source_target_pairs={{0,2},{1,3},{4,6},{5,7},{8,10},{9,11},{12,14},{13,15},{16,18},{17,... | collective-permute-start | bytes 147464 | tf_op jit(solution)/shard_map/ppermute | solution.py:839
  150.8 11.0 %shard_map.318 = (bf16[512,1024]{1,0:T(8,128)(2,1)}, bf16[512,768]{1,0:T(8,128)(2,1)}, f32[512,768]{1,0:T(8,128)}, bf16[512,768]{1,0:T(8,128)(2,1)}, bf16[5,128,...) custom-call(s32[4]{0:T(128)S(1)} %pad_add_fusion.refs_0_, bf16[528,1536]{1,0:T(8,128)(2,1)} %get-tuple-element.195.refs_1_.refs_0_, ...), custom_call_target="tpu_custom_call" | custom-call | flops 1000 | bytes 1000 | tf_op jit(solution)/shard_map/pallas_call | solution.py:795
  182.2 10.7 %shard_map.321 = (bf16[512,1024]{1,0:T(8,128)(2,1)}, bf16[512,768]{1,0:T(8,128)(2,1)}, f32[512,768]{1,0:T(8,128)}, bf16[512,768]{1,0:T(8,128)(2,1)}, bf16[5,128,...) custom-call(s32[4]{0:T(128)S(1)} %pad_add_fusion.refs_0_, bf16[528,1536]{1,0:T(8,128)(2,1)} %get-tuple-element.215.refs_1_.refs_2_.refs_3_, ...), custom_call_target="tpu_custom_call" | custom-call | flops 1000 | bytes 1000 | tf_op jit(solution)/shard_map/pallas_call | solution.py:795
  211.6 11.2 %shard_map.325 = (bf16[528,1536]{1,0:T(8,128)(2,1)}, bf16[528,1152]{1,0:T(8,128)(2,1)}, f32[16,1024]{1,0:T(8,128)}, bf16[512,1024]{1,0:T(8,128)(2,1)}, f32[512,2...) custom-call(s32[4]{0:T(128)S(1)} %pad_add_fusion.refs_0_, ...), custom_call_target="tpu_custom_call" | custom-call | flops 1000 | bytes 1000 | tf_op jit(solution)/shard_map/pallas_call | solution.py:795
  240.0 14.1 %all-gather.11.cloned.1.call-done.refs_3_.refs_5_.refs_2_ = bf16[1536,1536]{1,0:T(8,128)(2,1)} async-done(((bf16[384,1536]{1,0:T(8,128)(2,1)}), bf16[1536,1536]{1,0:T(8,128)(2,1)}) %all-gather.11.cloned.1.call-update) | async-done | bytes 4718608 | tf_op jit(solution)/shard_map/all_gather | solution.py:925
  254.1 10.7 %shard_map.328 = (bf16[512,1024]{1,0:T(8,128)(2,1)}, bf16[512,768]{1,0:T(8,128)(2,1)}, f32[512,768]{1,0:T(8,128)}, bf16[512,768]{1,0:T(8,128)(2,1)}, bf16[5,128,...) custom-call(s32[4]{0:T(128)S(1)} %pad_add_fusion.refs_0_, bf16[528,1536]{1,0:T(8,128)(2,1)} %get-tuple-element.226.refs_1_.refs_0_, ...), custom_call_target="tpu_custom_call" | custom-call | flops 1000 | bytes 1000 | tf_op jit(solution)/shard_map/pallas_call | solution.py:795
  271.8 11.2 %shard_map.331 = (bf16[528,1536]{1,0:T(8,128)(2,1)}, bf16[528,1152]{1,0:T(8,128)(2,1)}, f32[16,1024]{1,0:T(8,128)}, bf16[512,1024]{1,0:T(8,128)(2,1)}, f32[512,2...) custom-call(s32[4]{0:T(128)S(1)} %pad_add_fusion.refs_0_, ...), custom_call_target="tpu_custom_call" | custom-call | flops 1000 | bytes 1000 | tf_op jit(solution)/shard_map/pallas_call | solution.py:795
  300.9 10.7 %shard_map.334 = (bf16[512,1024]{1,0:T(8,128)(2,1)}, bf16[512,768]{1,0:T(8,128)(2,1)}, f32[512,768]{1,0:T(8,128)}, bf16[512,768]{1,0:T(8,128)(2,1)}, bf16[5,128,...) custom-call(s32[4]{0:T(128)S(1)} %pad_add_fusion.refs_0_, bf16[528,1536]{1,0:T(8,128)(2,1)} %get-tuple-element.249.refs_1_.refs_2_, ...), custom_call_target="tpu_custom_call" | custom-call | flops 1000 | bytes 1000 | tf_op jit(solution)/shard_map/pallas_call | solution.py:795
  318.9 8.1 %shard_map.337 = (bf16[512,1536]{1,0:T(8,128)(2,1)}, bf16[512,768]{1,0:T(8,128)(2,1)}, bf16[528,768]{1,0:T(8,128)(2,1)}, f32[8,768]{1,0:T(8,128)S(1)}, bf16[128,768]{1,0:T(8,128)(2,1)S(1)}) custom-call(s32[4]{0:T(128)S(1)} %pad_add_fusion.refs_0_, bf16[128,1664]{1,0:T(8,128)(2,1)S(1)} %get-tuple-element.256.refs_17_.refs_2_.refs_1_, ...), custom_call_target="tpu_custom_call" | custom-call | flops 1000 | bytes 1000 | tf_op jit(solution)/shard_map/pallas_call | solution.py:795
  345.5 8.1 %shard_map.340 = (bf16[512,1536]{1,0:T(8,128)(2,1)}, bf16[512,768]{1,0:T(8,128)(2,1)}, bf16[528,768]{1,0:T(8,128)(2,1)}, f32[8,768]{1,0:T(8,128)S(1)}, bf16[128,768]{1,0:T(8,128)(2,1)S(1)}) custom-call(s32[4]{0:T(128)S(1)} %pad_add_fusion.refs_0_, bf16[128,1664]{1,0:T(8,128)(2,1)S(1)} %get-tuple-element.274.refs_1_.refs_14_, ...), custom_call_target="tpu_custom_call" | custom-call | flops 1000 | bytes 1000 | tf_op jit(solution)/shard_map/pallas_call | solution.py:795
  357.9 12.5 %shard_map.342.refs_1_ = bf16[1536,1536]{1,0:T(8,128)(2,1)} custom-call(bf16[528,1536]{1,0:T(8,128)(2,1)} %get-tuple-element.226.refs_1_.refs_0_, bf16[528,768]{1,0:T(8,128)(2,1)} %get-tuple-element.273.refs_1_.refs_8_, bf16[528,1536]{1,0:T(8,128)(2,1)} %get-tuple-element.249.refs_1_.refs_2_, bf16[528,768]{1,0:T(8,128)(2,1)} %get-tuple-element.279.refs_3_.refs_8_, ...), custom_call_target="tpu_custom_call" | custom-call | flops 1000 | bytes 1000 | tf_op jit(solution)/shard_map/pallas_call | solution.py:795
  371.9 9.6 %collective-permute-done.51.refs_0_.refs_10_ = bf16[128,768]{1,0:T(8,128)(2,1)S(1)} collective-permute-done((bf16[128,768]{1,0:T(8,128)(2,1)S(1)}, bf16[128,768]{1,0:T(8,128)(2,1)S(1)}, u32[]{:S(2)}, u32[]{:S(2)}) %collective-permute-start.51) | collective-permute-done | bytes 196640 | tf_op jit(solution)/shard_map/ppermute | solution.py:842
  383.9 20.2 %shard_map.344 = (bf16[528,1152]{1,0:T(8,128)(2,1)}, f32[8,1024]{1,0:T(8,128)S(1)}, f32[8,128]{1,0:T(8,128)S(1)}, f32[528,1536]{1,0:T(8,128)S(1)}) custom-call(s32[4]{0:T(128)S(1)} %pad_add_fusion.refs_0_, bf16[1536,1152]{1,0:T(8,128)(2,1)} %all-gather.9.cloned.1.call-done.refs_5_.refs_1_, ...), custom_call_target="tpu_custom_call" | custom-call | flops 1000 | bytes 1000 | tf_op jit(solution)/shard_map/pallas_call | solution.py:795
  409.7 20.1 %shard_map.347 = (bf16[528,1152]{1,0:T(8,128)(2,1)}, f32[8,1024]{1,0:T(8,128)S(1)}, f32[8,128]{1,0:T(8,128)S(1)}, f32[528,1536]{1,0:T(8,128)S(1)}) custom-call(s32[4]{0:T(128)S(1)} %pad_add_fusion.refs_0_, bf16[1536,1152]{1,0:T(8,128)(2,1)} %all-gather.9.cloned.1.call-done.refs_5_.refs_1_, ...), custom_call_target="tpu_custom_call" | custom-call | flops 1000 | bytes 1000 | tf_op jit(solution)/shard_map/pallas_call | solution.py:795
  437.2 13.6 %shard_map.351.refs_5_ = bf16[1536,1152]{1,0:T(8,128)(2,1)} custom-call(bf16[528,1536]{1,0:T(8,128)(2,1)} %get-tuple-element.226.refs_1_.refs_0_, bf16[528,1152]{1,0:T(8,128)(2,1)} %get-tuple-element.301.refs_1_, bf16[528,1536]{1,0:T(8,128)(2,1)} %get-tuple-element.249.refs_1_.refs_2_, bf16[528,1152]{1,0:T(8,128)(2,1)} %get-tuple-element.302.refs_3_, ...), custom_call_target="tpu_custom_call" | custom-call | flops 1000 | bytes 1000 | tf_op jit(solution)/shard_map/pallas_call | solution.py:795
  454.7 8.7 %collective-permute-done.56.refs_4_.refs_2_ = bf16[128,1664]{1,0:T(8,128)(2,1)S(1)} collective-permute-done((bf16[128,1664]{1,0:T(8,128)(2,1)}, bf16[128,1664]{1,0:T(8,128)(2,1)S(1)}, u32[]{:S(2)}, u32[]{:S(2)}) %collective-permute-start.56) | collective-permute-done | bytes 426016 | tf_op jit(solution)/shard_map/ppermute | solution.py:839
  463.4 8.4 %collective-permute-done.60.refs_0_.refs_1_ = bf16[128,1536]{1,0:T(8,128)(2,1)S(1)} collective-permute-done((bf16[128,1536]{1,0:T(8,128)(2,1)}, bf16[128,1536]{1,0:T(8,128)(2,1)S(1)}, u32[]{:S(2)}, u32[]{:S(2)}) %collective-permute-start.60) | collective-permute-done | bytes 393248 | tf_op jit(solution)/shard_map/ppermute | solution.py:839
  482.1 9.1 %collective-permute-done.63.refs_2_ = bf16[128,1664]{1,0:T(8,128)(2,1)S(1)} collective-permute-done((bf16[128,1664]{1,0:T(8,128)(2,1)S(1)}, bf16[128,1664]{1,0:T(8,128)(2,1)S(1)}, u32[]{:S(2)}, u32[]{:S(2)}) %collective-permute-start.63) | collective-permute-done | bytes 426016 | tf_op jit(solution)/shard_map/ppermute | solution.py:839
  491.2 8.1 %shard_map.354 = (bf16[512,1536]{1,0:T(8,128)(2,1)}, bf16[512,768]{1,0:T(8,128)(2,1)}, bf16[528,768]{1,0:T(8,128)(2,1)}, f32[8,768]{1,0:T(8,128)S(1)}, bf16[128,768]{1,0:T(8,128)(2,1)S(1)}) custom-call(s32[4]{0:T(128)S(1)} %pad_add_fusion.refs_0_, bf16[128,1664]{1,0:T(8,128)(2,1)S(1)} %copy-done.8, ...), custom_call_target="tpu_custom_call" | custom-call | flops 1000 | bytes 1000 | tf_op jit(solution)/shard_map/pallas_call | solution.py:795
  501.7 8.1 %shard_map.356 = (bf16[512,1536]{1,0:T(8,128)(2,1)}, bf16[512,768]{1,0:T(8,128)(2,1)}, bf16[528,768]{1,0:T(8,128)(2,1)}, f32[8,768]{1,0:T(8,128)S(1)}, bf16[128,768]{1,0:T(8,128)(2,1)S(1)}) custom-call(s32[4]{0:T(128)S(1)} %pad_add_fusion.refs_0_, bf16[128,1664]{1,0:T(8,128)(2,1)S(1)} %get-tuple-element.303.refs_14_.refs_1_, ...), custom_call_target="tpu_custom_call" | custom-call | flops 1000 | bytes 1000 | tf_op jit(solution)/shard_map/pallas_call | solution.py:795
  512.9 12.5 %shard_map.358.refs_1_ = bf16[1536,1536]{1,0:T(8,128)(2,1)} custom-call(bf16[528,1536]{1,0:T(8,128)(2,1)} %get-tuple-element.195.refs_1_.refs_0_, bf16[528,768]{1,0:T(8,128)(2,1)} %get-tuple-element.305.refs_1_.refs_8_, bf16[528,1536]{1,0:T(8,128)(2,1)} %get-tuple-element.215.refs_1_.refs_2_.refs_3_, bf16[528,768]{1,0:T(8,128)(2,1)} %get-tuple-element.311.refs_3_.refs_8_, ...), custom_call_target="tpu_custom_call" | custom-call | flops 1000 | bytes 1000 | tf_op jit(solution)/shard_map/pallas_call | solution.py:795
  526.8 11.2 %collective-permute-done.67.refs_0_.refs_10_ = bf16[128,768]{1,0:T(8,128)(2,1)S(1)} collective-permute-done((bf16[128,768]{1,0:T(8,128)(2,1)S(1)}, bf16[128,768]{1,0:T(8,128)(2,1)S(1)}, u32[]{:S(2)}, u32[]{:S(2)}) %collective-permute-start.67) | collective-permute-done | bytes 196640 | tf_op jit(solution)/shard_map/ppermute | solution.py:842
  543.4 20.2 %shard_map.361 = (bf16[528,1152]{1,0:T(8,128)(2,1)}, f32[8,1024]{1,0:T(8,128)S(1)}, f32[8,128]{1,0:T(8,128)S(1)}, f32[528,1536]{1,0:T(8,128)S(1)}) custom-call(s32[4]{0:T(128)S(1)} %pad_add_fusion.refs_0_, bf16[1536,1152]{1,0:T(8,128)(2,1)} %all-gather.5.cloned.1.call-done.refs_5_.refs_1_, ...), custom_call_target="tpu_custom_call" | custom-call | flops 1000 | bytes 1000 | tf_op jit(solution)/shard_map/pallas_call | solution.py:795
  569.3 20.2 %shard_map.364 = (bf16[528,1152]{1,0:T(8,128)(2,1)}, f32[8,1024]{1,0:T(8,128)S(1)}, f32[8,128]{1,0:T(8,128)S(1)}, f32[528,1536]{1,0:T(8,128)S(1)}) custom-call(s32[4]{0:T(128)S(1)} %pad_add_fusion.refs_0_, bf16[1536,1152]{1,0:T(8,128)(2,1)} %all-gather.5.cloned.1.call-done.refs_5_.refs_1_, ...), custom_call_target="tpu_custom_call" | custom-call | flops 1000 | bytes 1000 | tf_op jit(solution)/shard_map/pallas_call | solution.py:795
  606.5 12.5 %shard_map.368 = (bf16[384,1152]{1,0:T(8,128)(2,1)S(1)}, bf16[384,1152]{1,0:T(8,128)(2,1)S(1)}, bf16[384,1152]{1,0:T(8,128)(2,1)S(1)}, bf16[384,1152]{1,0:T(8,128)(2,1)S(1)}) custom-call(s32[4]{0:T(128)S(1)} %pad_add_fusion.refs_0_, bf16[528,1536]{1,0:T(8,128)(2,1)} %get-tuple-element.195.refs_1_.refs_0_, bf16[528,1152]{1,0:T(8,128)(2,1)} %get-tuple-element.332.refs_2_, ...), custom_call_target="tpu_custom_call" | custom-call | flops 1000 | bytes 1000 | tf_op jit(solution)/shard_map/pallas_call | solution.py:795
  627.4 19.8 %collective-permute-start.83 = (bf16[192,896]{1,0:T(8,128)(2,1)}, bf16[192,896]{1,0:T(8,128)(2,1)S(1)}, u32[]{:S(2)}, u32[]{:S(2)}) collective-permute-start(bf16[192,896]{1,0:T(8,128)(2,1)} %get-tuple-element.358), channel_id=1, source_target_pairs={{2,0},{6,1},{3,2},{7,3},{0,4},{4,5},{1,6},{5,7},{10,8},{14,9},{11,... | collective-permute-start | bytes 1032200 | tf_op jit(solution)/shard_map/ppermute | solution.py:842
  674.6 23.4 %collective-permute-start.86 = (bf16[2,16,1536]{2,1,0:T(8,128)(2,1)S(1)}, bf16[2,16,1536]{2,1,0:T(8,128)(2,1)S(1)}, u32[]{:S(2)}, u32[]{:S(2)}) collective-permute-start(bf16[2,16,1536]{2,1,0:T(8,128)(2,1)S(1)} %shard_map.374.refs_2_), channel_id=1, source_target_pairs={{0,0},{4,1},{1,2},{5,3},{2,4},{6,5},{3,6},{7,7},{8,8},{12,9},{9,10... | collective-permute-start | bytes 294920 | tf_op jit(solution)/shard_map/ppermute | solution.py:842
  725.8 12.0 %collective-permute-done.98.refs_10_ = bf16[2,192,256]{2,1,0:T(8,128)(2,1)} collective-permute-done((bf16[2,192,256]{2,1,0:T(8,128)(2,1)}, bf16[2,192,256]{2,1,0:T(8,128)(2,1)}, u32[]{:S(2)}, u32[]{:S(2)}) %collective-permute-start.98) | collective-permute-done | bytes 196640 | tf_op jit(solution)/shard_map/ppermute | solution.py:839
  (572 shorter events, 319.8 us)
Async XLA Ops:
  7.2 93.3 %all-gather.5.cloned.1.call-start = ((), (), s32[]{:S(2)}) async-start(), calls=%async_computation.3 | async-start | bytes 4423680 | tf_op jit(solution)/shard_map/all_gather | solution.py:925
  26.7 123.5 %all-gather.7.cloned.1.call-start = ((), (), s32[]{:S(2)}) async-start(), calls=%async_computation.4 | async-start | bytes 5898240 | tf_op jit(solution)/shard_map/all_gather | solution.py:925
  27.8 23.4 %collective-permute-start.8 = (f32[2,7,768]{2,1,0:T(8,128)S(1)}, f32[2,7,768]{2,1,0:T(8,128)S(1)}, u32[]{:S(2)}, u32[]{:S(2)}) collective-permute-start(f32[2,7,768]{2,1,0:T(8,128)S(1)} %pad_maximum_fusion.3), channel_id=1, source_target_pairs={{0,0},{1,4},{2,1},{3,5},{4,2},{5,6},{6,3},{7,7},{8,8},{9,12},{10,9... | collective-permute-start | bytes 129032 | tf_op jit(solution)/shard_map/ppermute | solution.py:839
  53.7 31.9 %collective-permute-start.10 = (bf16[192,1536]{1,0:T(8,128)(2,1)S(1)}, bf16[192,1536]{1,0:T(8,128)(2,1)S(1)}, u32[]{:S(2)}, u32[]{:S(2)}) collective-permute-start(bf16[192,1536]{1,0:T(8,128)(2,1)S(1)} %shard_map.310.refs_7_), channel_id=1, source_target_pairs={{0,2},{1,6},{2,3},{3,7},{4,0},{5,4},{6,1},{7,5},{8,10},{9,14},{10,... | collective-permute-start | bytes 1769480 | tf_op jit(solution)/shard_map/ppermute | solution.py:839
  53.7 31.9 %collective-permute-start.9 = (bf16[192,1536]{1,0:T(8,128)(2,1)S(1)}, bf16[192,1536]{1,0:T(8,128)(2,1)S(1)}, u32[]{:S(2)}, u32[]{:S(2)}) collective-permute-start(bf16[192,1536]{1,0:T(8,128)(2,1)S(1)} %shard_map.310.refs_7_), channel_id=1, source_target_pairs={{0,0},{1,4},{2,1},{3,5},{4,2},{5,6},{6,3},{7,7},{8,8},{9,12},{10,9... | collective-permute-start | bytes 1769480 | tf_op jit(solution)/shard_map/ppermute | solution.py:839
  58.4 21.6 %collective-permute-start.11 = (bf16[128,1536]{1,0:T(8,128)(2,1)S(1)}, bf16[128,1536]{1,0:T(8,128)(2,1)S(1)}, u32[]{:S(2)}, u32[]{:S(2)}) collective-permute-start(bf16[128,1536]{1,0:T(8,128)(2,1)S(1)} %get-tuple-element.194.refs_5_.refs_1_), channel_id=1, source_target_pairs={{0,1},{1,0},{2,3},{3,2},{4,5},{5,4},{6,7},{7,6},{8,9},{9,8},{10,11... | collective-permute-start | bytes 1179656 | tf_op jit(solution)/shard_map/ppermute | solution.py:839
  58.5 27.1 %collective-permute-start.1 = (bf16[128,1536]{1,0:T(8,128)(2,1)S(1)}, bf16[128,1536]{1,0:T(8,128)(2,1)S(1)}, u32[]{:S(2)}, u32[]{:S(2)}) collective-permute-start(bf16[128,1536]{1,0:T(8,128)(2,1)S(1)} %get-tuple-element.193.refs_2_.refs_3_.refs_1_), channel_id=1, source_target_pairs={{0,1},{1,0},{2,3},{3,2},{4,5},{5,4},{6,7},{7,6},{8,9},{9,8},{10,11... | collective-permute-start | bytes 1179656 | tf_op jit(solution)/shard_map/ppermute | solution.py:839
  88.1 123.5 %all-gather.9.cloned.1.call-start = ((), (), s32[]{:S(2)}) async-start(), calls=%async_computation.5 | async-start | bytes 4423680 | tf_op jit(solution)/shard_map/all_gather | solution.py:925
  90.4 41.0 %collective-permute-start.15 = (bf16[192,2432]{1,0:T(8,128)(2,1)S(1)}, bf16[192,2432]{1,0:T(8,128)(2,1)S(1)}, u32[]{:S(2)}, u32[]{:S(2)}) collective-permute-start(bf16[192,2432]{1,0:T(8,128)(2,1)S(1)} %shard_map.312.refs_11_), channel_id=1, source_target_pairs={{0,0},{1,4},{2,1},{3,5},{4,2},{5,6},{6,3},{7,7},{8,8},{9,12},{10,9... | collective-permute-start | bytes 2801672 | tf_op jit(solution)/shard_map/ppermute | solution.py:839
  93.2 38.2 %collective-permute-start.16 = (bf16[192,2432]{1,0:T(8,128)(2,1)S(1)}, bf16[192,2432]{1,0:T(8,128)(2,1)}, u32[]{:S(2)}, u32[]{:S(2)}) collective-permute-start(bf16[192,2432]{1,0:T(8,128)(2,1)S(1)} %shard_map.312.refs_11_), channel_id=1, source_target_pairs={{0,2},{1,6},{2,3},{3,7},{4,0},{5,4},{6,1},{7,5},{8,10},{9,14},{10,... | collective-permute-start | bytes 2801672 | tf_op jit(solution)/shard_map/ppermute | solution.py:839
  134.2 119.9 %all-gather.11.cloned.1.call-start = ((), (), s32[]{:S(2)}) async-start(), calls=%async_computation.6 | async-start | bytes 5898240 | tf_op jit(solution)/shard_map/all_gather | solution.py:925
  134.7 405.6 %reduce-scatter.4.cloned.1.call-start = ((), (), s32[]{:S(2)}) async-start(), calls=%async_computation.7 | async-start | bytes 5898240 | tf_op jit(solution)/shard_map/reduce_scatter | solution.py:1191
  165.9 27.1 %collective-permute-start.21 = (bf16[128,1664]{1,0:T(8,128)(2,1)S(1)}, bf16[128,1664]{1,0:T(8,128)(2,1)S(1)}, u32[]{:S(2)}, u32[]{:S(2)}) collective-permute-start(bf16[128,1664]{1,0:T(8,128)(2,1)S(1)} %get-tuple-element.213.refs_17_), channel_id=1, source_target_pairs={{0,1},{1,0},{2,3},{3,2},{4,5},{5,4},{6,7},{7,6},{8,9},{9,8},{10,11... | collective-permute-start | bytes 1277960 | tf_op jit(solution)/shard_map/ppermute | solution.py:839
  199.2 23.6 %collective-permute-start.28 = (bf16[128,1664]{1,0:T(8,128)(2,1)S(1)}, bf16[128,1664]{1,0:T(8,128)(2,1)S(1)}, u32[]{:S(2)}, u32[]{:S(2)}) collective-permute-start(bf16[128,1664]{1,0:T(8,128)(2,1)S(1)} %get-tuple-element.225.refs_11_), channel_id=1, source_target_pairs={{0,1},{1,0},{2,3},{3,2},{4,5},{5,4},{6,7},{7,6},{8,9},{9,8},{10,11... | collective-permute-start | bytes 1277960 | tf_op jit(solution)/shard_map/ppermute | solution.py:839
  225.5 39.3 %collective-permute-start.32 = (bf16[128,1536]{1,0:T(8,128)(2,1)S(1)}, bf16[128,1536]{1,0:T(8,128)(2,1)S(1)}, u32[]{:S(2)}, u32[]{:S(2)}) collective-permute-start(bf16[128,1536]{1,0:T(8,128)(2,1)S(1)} %get-tuple-element.239.refs_17_.refs_2_.refs_1_), channel_id=1, source_target_pairs={{0,1},{1,0},{2,3},{3,2},{4,5},{5,4},{6,7},{7,6},{8,9},{9,8},{10,11... | collective-permute-start | bytes 1179656 | tf_op jit(solution)/shard_map/ppermute | solution.py:839
  286.1 25.6 %collective-permute-start.41 = (bf16[128,1664]{1,0:T(8,128)(2,1)S(1)}, bf16[128,1664]{1,0:T(8,128)(2,1)S(1)}, u32[]{:S(2)}, u32[]{:S(2)}) collective-permute-start(bf16[128,1664]{1,0:T(8,128)(2,1)S(1)} %get-tuple-element.256.refs_17_.refs_2_.refs_1_), channel_id=1, source_target_pairs={{0,1},{1,0},{2,3},{3,2},{4,5},{5,4},{6,7},{7,6},{8,9},{9,8},{10,11... | collective-permute-start | bytes 1277960 | tf_op jit(solution)/shard_map/ppermute | solution.py:839
  370.4 252.3 %reduce-scatter.8.cloned.1.call-start = ((), (), s32[]{:S(2)}) async-start(), calls=%async_computation.9 | async-start | bytes 4423680 | tf_op jit(solution)/shard_map/reduce_scatter | solution.py:1191
  408.1 21.8 %collective-permute-start.53 = (bf16[128,1536]{1,0:T(8,128)(2,1)S(1)}, bf16[128,1536]{1,0:T(8,128)(2,1)S(1)}, u32[]{:S(2)}, u32[]{:S(2)}) collective-permute-start(bf16[128,1536]{1,0:T(8,128)(2,1)S(1)} %get-tuple-element.286), channel_id=1, source_target_pairs={{0,1},{1,0},{2,3},{3,2},{4,5},{5,4},{6,7},{7,6},{8,9},{9,8},{10,11... | collective-permute-start | bytes 1179656 | tf_op jit(solution)/shard_map/ppermute | solution.py:839
  408.1 21.7 %collective-permute-start.54 = (bf16[16,1536]{1,0:T(8,128)(2,1)S(1)}, bf16[16,1536]{1,0:T(8,128)(2,1)S(1)}, u32[]{:S(2)}, u32[]{:S(2)}) collective-permute-start(bf16[16,1536]{1,0:T(8,128)(2,1)S(1)} %get-tuple-element.287.refs_20_), channel_id=1, source_target_pairs={{6,5},{14,13},{22,21},{30,29}} | collective-permute-start | bytes 147464 | tf_op jit(solution)/shard_map/ppermute | solution.py:842
  408.8 21.1 %collective-permute-start.55 = (bf16[16,1536]{1,0:T(8,128)(2,1)S(1)}, bf16[16,1536]{1,0:T(8,128)(2,1)S(1)}, u32[]{:S(2)}, u32[]{:S(2)}) collective-permute-start(bf16[16,1536]{1,0:T(8,128)(2,1)S(1)} %get-tuple-element.287.refs_20_), channel_id=1, source_target_pairs={{7,5},{15,13},{23,21},{31,29}} | collective-permute-start | bytes 147464 | tf_op jit(solution)/shard_map/ppermute | solution.py:842
  450.8 199.0 %reduce-scatter.6.cloned.1.call-start = ((), (), s32[]{:S(2)}) async-start(), calls=%async_computation.8 | async-start | bytes 5898240 | tf_op jit(solution)/shard_map/reduce_scatter | solution.py:1191
  567.7 21.9 %collective-permute-start.69 = (bf16[128,1536]{1,0:T(8,128)(2,1)S(1)}, bf16[128,1536]{1,0:T(8,128)(2,1)S(1)}, u32[]{:S(2)}, u32[]{:S(2)}) collective-permute-start(bf16[128,1536]{1,0:T(8,128)(2,1)S(1)} %get-tuple-element.319), channel_id=1, source_target_pairs={{0,1},{1,0},{2,3},{3,2},{4,5},{5,4},{6,7},{7,6},{8,9},{9,8},{10,11... | collective-permute-start | bytes 1179656 | tf_op jit(solution)/shard_map/ppermute | solution.py:839
  567.8 21.8 %collective-permute-start.70 = (bf16[16,1536]{1,0:T(8,128)(2,1)S(1)}, bf16[16,1536]{1,0:T(8,128)(2,1)S(1)}, u32[]{:S(2)}, u32[]{:S(2)}) collective-permute-start(bf16[16,1536]{1,0:T(8,128)(2,1)S(1)} %get-tuple-element.320.refs_20_), channel_id=1, source_target_pairs={{6,5},{14,13},{22,21},{30,29}} | collective-permute-start | bytes 147464 | tf_op jit(solution)/shard_map/ppermute | solution.py:842
  568.4 21.1 %collective-permute-start.71 = (bf16[16,1536]{1,0:T(8,128)(2,1)S(1)}, bf16[16,1536]{1,0:T(8,128)(2,1)S(1)}, u32[]{:S(2)}, u32[]{:S(2)}) collective-permute-start(bf16[16,1536]{1,0:T(8,128)(2,1)S(1)} %get-tuple-element.320.refs_20_), channel_id=1, source_target_pairs={{7,5},{15,13},{23,21},{31,29}} | collective-permute-start | bytes 147464 | tf_op jit(solution)/shard_map/ppermute | solution.py:842
  592.7 54.5 %collective-permute-start.46 = (f32[128,1536]{1,0:T(8,128)}, f32[128,1536]{1,0:T(8,128)}, u32[]{:S(2)}, u32[]{:S(2)}) collective-permute-start(f32[128,1536]{1,0:T(8,128)} %get-tuple-element.524), channel_id=1, source_target_pairs={{0,4},{1,5},{2,6},{3,7},{4,0},{5,1},{6,2},{7,3},{8,12},{9,13},{10,... | collective-permute-start | bytes 2359304 | tf_op jit(solution)/shard_map/ppermute | solution.py:839
  593.0 55.3 %collective-permute-start.84 = (bf16[192,1536]{1,0:T(8,128)(2,1)}, bf16[192,1536]{1,0:T(8,128)(2,1)S(1)}, u32[]{:S(2)}, u32[]{:S(2)}) collective-permute-start(bf16[192,1536]{1,0:T(8,128)(2,1)} %get-tuple-element.359), channel_id=1, source_target_pairs={{0,0},{4,1},{1,2},{5,3},{2,4},{6,5},{3,6},{7,7},{8,8},{12,9},{9,10... | collective-permute-start | bytes 1769480 | tf_op jit(solution)/shard_map/ppermute | solution.py:842
  597.6 51.1 %collective-permute-start.85 = (bf16[192,1536]{1,0:T(8,128)(2,1)}, bf16[192,1536]{1,0:T(8,128)(2,1)S(1)}, u32[]{:S(2)}, u32[]{:S(2)}) collective-permute-start(bf16[192,1536]{1,0:T(8,128)(2,1)} %get-tuple-element.316.refs_20_), channel_id=1, source_target_pairs={{2,0},{6,1},{3,2},{7,3},{0,4},{4,5},{1,6},{5,7},{10,8},{14,9},{11,... | collective-permute-start | bytes 1769480 | tf_op jit(solution)/shard_map/ppermute | solution.py:842
  625.5 26.4 %collective-permute-start.82 = (bf16[192,896]{1,0:T(8,128)(2,1)}, bf16[192,896]{1,0:T(8,128)(2,1)S(1)}, u32[]{:S(2)}, u32[]{:S(2)}) collective-permute-start(bf16[192,896]{1,0:T(8,128)(2,1)} %get-tuple-element.357), channel_id=1, source_target_pairs={{0,0},{4,1},{1,2},{5,3},{2,4},{6,5},{3,6},{7,7},{8,8},{12,9},{9,10... | collective-permute-start | bytes 1032200 | tf_op jit(solution)/shard_map/ppermute | solution.py:842
  627.4 29.0 %collective-permute-start.83 = (bf16[192,896]{1,0:T(8,128)(2,1)}, bf16[192,896]{1,0:T(8,128)(2,1)S(1)}, u32[]{:S(2)}, u32[]{:S(2)}) collective-permute-start(bf16[192,896]{1,0:T(8,128)(2,1)} %get-tuple-element.358), channel_id=1, source_target_pairs={{2,0},{6,1},{3,2},{7,3},{0,4},{4,5},{1,6},{5,7},{10,8},{14,9},{11,... | collective-permute-start | bytes 1032200 | tf_op jit(solution)/shard_map/ppermute | solution.py:842
  648.3 22.4 %collective-permute-start.78 = (bf16[384,1152]{1,0:T(8,128)(2,1)}, bf16[384,1152]{1,0:T(8,128)(2,1)}, u32[]{:S(2)}, u32[]{:S(2)}) collective-permute-start(bf16[384,1152]{1,0:T(8,128)(2,1)} %copy-done.67), channel_id=1, source_target_pairs={{0,16},{1,17},{2,18},{3,19},{4,20},{5,21},{6,22},{7,23},{8,24},{9,... | collective-permute-start | bytes 2654216 | tf_op jit(solution)/shard_map/ppermute | solution.py:839
  648.7 22.0 %collective-permute-start.79 = (bf16[384,1152]{1,0:T(8,128)(2,1)}, bf16[384,1152]{1,0:T(8,128)(2,1)}, u32[]{:S(2)}, u32[]{:S(2)}) collective-permute-start(bf16[384,1152]{1,0:T(8,128)(2,1)} %copy-done.13), channel_id=1, source_target_pairs={{0,24},{1,25},{2,26},{3,27},{4,28},{5,29},{6,30},{7,31},{8,16},{9,... | collective-permute-start | bytes 2654216 | tf_op jit(solution)/shard_map/ppermute | solution.py:839
  674.6 25.0 %collective-permute-start.86 = (bf16[2,16,1536]{2,1,0:T(8,128)(2,1)S(1)}, bf16[2,16,1536]{2,1,0:T(8,128)(2,1)S(1)}, u32[]{:S(2)}, u32[]{:S(2)}) collective-permute-start(bf16[2,16,1536]{2,1,0:T(8,128)(2,1)S(1)} %shard_map.374.refs_2_), channel_id=1, source_target_pairs={{0,0},{4,1},{1,2},{5,3},{2,4},{6,5},{3,6},{7,7},{8,8},{12,9},{9,10... | collective-permute-start | bytes 294920 | tf_op jit(solution)/shard_map/ppermute | solution.py:842
  (178 other events, 1421.1 us)
Sparse Core Ops, SparseCore 0:
  26.8 54.2 all-gather.4
  88.2 57.3 all-gather.6
  147.4 47.2 all-gather.8
  196.9 57.0 all-gather.10
  370.5 54.3 reduce-scatter.3
  451.0 49.1 reduce-scatter.7
  525.6 55.7 reduce-scatter.5

commit v3 on v2

--- a/solution.py
+++ b/solution.py
@@ -582,7 +582,7 @@
         )
 
 
-def weight_kernel(*refs, terms, halo, far, pieces, ready):
+def weight_kernel(*refs, terms, tokens, halo, far, pieces, ready):
     refs = list(refs)
     sems = refs.pop()
     at_ref = refs.pop(0) if pieces else None
@@ -606,12 +606,13 @@
 
         def step_tile(r, carry):
             at = pl.ds(pl.multiple_of(r * tile, tile), tile)
-            total = dot(left_a[:, at], right_a[...], ((0,), (0,)))
-            total = total + dot(left_b[:, at], right_b[...], ((0,), (0,)))
+            skip_l, skip_r = left_a.shape[0] - tokens, right_a.shape[0] - tokens
+            total = dot(left_a[skip_l:, at], right_a[skip_r:, :], ((0,), (0,)))
+            total = total + dot(left_b[skip_l:, at], right_b[skip_r:, :], ((0,), (0,)))
             if halo:
-                edge_a, edge_b = refs[4 * terms : 4 * terms + 2]
-                total = total + dot(edge_a[:, at], right_a[:HALO, :], ((0,), (0,)))
-                total = total + dot(edge_b[:, at], right_b[:HALO, :], ((0,), (0,)))
+                edges = jnp.concatenate([edge[:, at] for edge in refs[4 * terms : 4 * terms + 2]])
+                heads = jnp.concatenate([right_a[:HALO, :], right_b[:HALO, :]])
+                total = total + dot(edges, heads, ((0,), (0,)))
             out_ref[at, low : low + size] = total.astype(BF)
             return carry
 
@@ -680,8 +681,12 @@
         away_ref[...] = buf_ref[rows, lanes].astype(BF)
 
 
-def final_kernel(*refs, layers, inner, heads, tensors, ready):
-    gz_ref, gx_ref, gbc_ref, gdt_ref, gout_ref = refs[-5:]
+def final_kernel(*refs, layers, inner, heads, tensors, chips, ready):
+    (gz_ref, gx_ref, gbc_ref, gdt_ref, gout_ref, taps_ref, bias_ref, taps_bc_ref, bias_bc_ref,
+     dt_ref, log_ref, skip_ref, gate_ref, norm_ref) = refs[-14:]
+    low = layers * (4 + tensors)
+    small = tree_sum([ref[...] for ref in refs[low : low + chips]])
+    hm_ref = refs[low + chips]
     for l in range(layers):
         rest_one, rest_two, front_one, front_two = refs[4 * l : 4 * l + 4]
         total = rest_one[...].astype(F32) + rest_two[...].astype(F32)
@@ -690,7 +695,24 @@
         total = front_one[...].astype(F32) + front_two[...].astype(F32)
         gx_ref[l] = total[:, :inner]
         gdt_ref[l] = total[:, inner : inner + heads]
-    gbc_ref[...] = tree_sum([ref[...] for ref in refs[4 * layers : 4 * layers + tensors]])
+        low = 4 * layers + l * tensors
+        gbc_ref[l] = tree_sum([ref[...] for ref in refs[low : low + tensors]])
+        row = slice(l, l + 1)
+        mine = small[l]
+        taps_ref[l] = mine[0:4, :inner]
+        bias_ref[row, :] = mine[4:5, :inner]
+        gate_ref[row, :] = mine[5:6, :inner]
+        skips = dot(mine[0:8, :inner], hm_ref[...].astype(F32), precision=EXACT)
+        skip_ref[row, :] = skips[6:7, :heads]
+        dt_ref[row, :] = mine[7:8, :heads]
+        log_ref[row, :] = mine[7:8, LANES : LANES + heads]
+        taps_bc_ref[l] = mine[8:12, : 2 * STATE]
+        bias_bc_ref[row, :] = mine[12:13, : 2 * STATE]
+        norm_ref[row, :] = mine[13:14, :]
+
+
+def nothing_kernel(*refs):
+    pass
 
 
 def gate_kernel(*refs, terms, ready):
@@ -816,6 +838,20 @@
             [(v.shape, v.dtype) for v in values], after=after,
         )
 
+    def pass_on(self, value, after):
+        free = pl.BlockSpec(memory_space=pl.ANY)
+        distant = pl.BlockSpec(memory_space=pltpu.HBM)
+        extra = list(after) + ([] if self.last is value else [self.last])
+        self.last = pl.pallas_call(
+            nothing_kernel,
+            in_specs=[distant] + [free] * len(extra),
+            out_specs=distant,
+            out_shape=pltpu.HBM(value.shape, value.dtype),
+            input_output_aliases={0: 0},
+            cost_estimate=pl.CostEstimate(flops=1000, bytes_accessed=1000, transcendentals=0),
+        )(pltpu.with_memory_space_constraint(value, pltpu.HBM), *extra)
+        return self.last
+
     def touch(self, values):
         self.run(touch_kernel, [], [((8, LANES), F32)], after=values)
 
@@ -924,7 +960,12 @@
         def gather_plane(value):
             return lax.all_gather(value, "dp", axis=0, tiled=True, axis_index_groups=planes)
 
-        def pick(parts, l, front, rest, after=()):
+        def direct_start(values):
+            return [values[0]] + [
+                send(values[j % len(values)], to_plane(2 * j)) for j in range(1, chips)
+            ]
+
+        def pick(parts, l, front, rest, after=(), direct=False):
             outs = []
             if front:
                 outs.append(((2 * shard, wide + LANES), BF))
@@ -940,6 +981,9 @@
                 after=after,
                 staged_out=range(len(outs)),
             )
+            if direct:
+                front_w[l] = direct_start(values)
+                return
             values = [gather_plane(v) for v in values]
             if front:
                 front_w[l] = [values[0]]
@@ -1055,6 +1099,9 @@
                 tail=send(tail, to_later), edge=send(edge, to_later), begins=send(ends, to_later),
             )
 
+        def states(l, s):
+            return [kept[l][s][k] for k in ("begins", "tail", "edge")]
+
         def scan(l, s, after=()):
             v = kept[l][s]
             (xb, z, core_out, act, sst, part) = queue.run(
@@ -1132,42 +1179,40 @@
             return kept[l][s]["pieces"][1:]
 
         pick(parts, 0, True, False)
-        queue.touch([marks, seg_row, links, conv_w, gate_p, head_p])
         parts = regroup(hold(jnp.concatenate(rest_part(0), axis=1), []))
         pick(parts, 0, False, True, [*arrived[0], *arrived[1]])
+        queue.touch([marks, seg_row, links, conv_w, gate_p, head_p])
         parts = [
             regroup(hold(jnp.concatenate(front_part(l) + rest_part(l), axis=1), []))
             for l in range(1, LAYERS)
         ]
         front(0, 0)
-        front(0, 1, [kept[0][0]["begins"]])
+        front(0, 1, states(0, 0))
         for l in range(1, LAYERS):
             pick(parts[l - 1], l, True, True)
         for l in range(LAYERS):
-            scan(l, 0, arrived[1] if l > 0 else [kept[0][1]["begins"]])
+            if l > 0:
+                front(l, 1, states(l, 0))
+            scan(l, 0, states(l, 1))
             add_cores(l, 0, True)
-            if l > 0:
-                front(l, 1, sums_of(l, 0))
-                own(l, 0)
-                scan(l, 1, arrived[0])
-            else:
-                scan(l, 1, sums_of(l, 0))
-                own(l, 0)
+            scan(l, 1, sums_of(l, 0))
+            own(l, 0)
             add_cores(l, 1, True)
             if l + 1 < LAYERS:
                 front(l + 1, 0, sums_of(l, 1))
-                own(l, 1)
+            own(l, 1)
 
         def owners(messages):
             return [back(messages[0], to_group(0)), back(messages[1], to_group(1))]
 
-        def split_rest(l):
+        def split_rest(l, after=()):
             messages = queue.run(
                 mixer(split_kernel, terms=1, shard=shard, inner=inner, front=False),
                 [at, g_rest[l]],
                 [((shard, 2 * inner), BF)] * 2,
                 [(g_rest[l].shape, F32)],
                 scalars=1,
+                after=after,
                 staged=(1,),
                 limit=14,
             )
@@ -1185,15 +1230,13 @@
                 limit=14,
             )
             done_front[l] = owners([one, two])
-            bc_parts[l] = (keep, away)
+            shared = (keep + send(away, to_core).astype(F32)).astype(BF)
+            g_bc[l] = [shared] + [send(shared, route) for route in all_tensor]
 
         def offloaded_sum(value):
             return lax.psum_scatter(
                 value, "dp", scatter_dimension=0, tiled=True, axis_index_groups=planes
             )
-
-        def direct_start(values):
-            return [values[0]] + [send(values[j], to_plane(2 * j)) for j in range(1, chips)]
 
         def add(parts, kind):
             return queue.run(
@@ -1203,7 +1246,7 @@
         all_tensor = [to_tensor(j) for j in range(1, n_tensor)]
         all_plane = [to_plane(2 * j) for j in range(1, n_dp // 2)]
 
-        def gate_back(l, s, after=()):
+        def gate_back(l, s, after=(), through=None):
             v = kept[l][s]
             (grows, gcore, gz, ggain, dsin) = queue.run(
                 mixer(gate_back_kernel, **sizes),
@@ -1221,7 +1264,10 @@
                 staged=range(5 + 2 * half_size, 10 + 2 * half_size),
                 limit=20,
             )
-            dsin, = queue.gate([dsin], after)
+            moved = [] if through is None else arrived[through][1:]
+            dsin, *moved = queue.gate([dsin, *moved], after)
+            if through is not None:
+                arrived[through] = arrived[through][:1] + moved
             v.update(grows=grows, gcore=gcore, gz=gz, ggain=ggain, dsout=back(dsin, to_later))
 
         def scan_back(l, s, after=()):
@@ -1279,7 +1325,9 @@
             count_out = chips if pieces else 1
             scratch = [(operands[i].shape, BF) for i in far] + [((width, size), BF)]
             result = queue.run(
-                mixer(weight_kernel, terms=len(names), halo=halo, far=far, pieces=pieces),
+                mixer(
+                    weight_kernel, terms=len(names), tokens=count, halo=halo, far=far, pieces=pieces
+                ),
                 ([at] if pieces else []) + operands,
                 [((width // count_out, size), BF)] * count_out,
                 scratch + [((len(far) + len(names),), None)],
@@ -1289,46 +1337,46 @@
                 staged=[len(operands) - 2 + bool(pieces), len(operands) - 1 + bool(pieces)] if halo else (),
                 limit=22,
             )
-            queue.touch(after)
-            return result if pieces else result[0]
+            if pieces:
+                return result
+            return queue.pass_on(result[0], after)
 
         rest_names = (("toks", "gz"), ("grows", "act"))
         front_names = (("toks", "graw"),)
         g_rest, g_front = [None] * LAYERS, [None] * LAYERS
         top = LAYERS - 1
-        gate_back(top, 0, sums_of(top, 1))
-        own(top, 1)
+        gate_back(top, 0, through=1)
         gate_back(top, 1, [kept[top][0]["dsout"]])
-        g_rest[top] = offloaded_sum(weights_back(top, rest_names, 0, [kept[top][1]["dsout"]]))
-        done_rest, done_front, bc_parts = ([None] * LAYERS for _ in range(3))
+        g_rest[top] = offloaded_sum(weights_back(top, rest_names))
+        done_rest, done_front, g_bc = ([None] * LAYERS for _ in range(3))
         for l in reversed(range(LAYERS)):
-            scan_back(l, 0)
+            ready = [kept[l][1]["dsout"]]
+            if l < top:
+                ready.append(done_rest[l + 1][1])
+            scan_back(l, 0, ready)
             add_cores(l, 0, False)
-            scan_back(l, 1, sums_of(l, 0) + kept[l][0]["halos"])
+            ready = sums_of(l, 0) + kept[l][0]["halos"]
+            if l < top:
+                split_front(l + 1, [g_front[l + 1]])
+                ready += done_front[l + 1]
+            scan_back(l, 1, ready)
+            own_back(l, 0)
+            add_cores(l, 1, False)
             if l == 0:
-                own_back(l, 0)
-                add_cores(l, 1, False)
-                direct = direct_start(
-                    weights_back(l, front_names, chips, sums_of(l, 1) + kept[l][1]["halos"])
-                )
-                for k in range(1, LAYERS):
-                    split_front(k, [g_front[k]])
+                direct = direct_start(weights_back(l, front_names, chips))
+                split_rest(l)
+                own_back(l, 1, [v for k in range(1, LAYERS) for v in g_bc[k]])
+                split_front(l, direct, done_rest[0])
+            else:
+                waiting = sums_of(l, 1) + kept[l][1]["halos"] + arrived[0]
+                g_front[l] = offloaded_sum(weights_back(l, front_names, 0, waiting))
                 split_rest(l)
                 own_back(l, 1)
-                earlier = [v for k in range(1, LAYERS) for v in done_front[k] + done_rest[k]]
-                split_front(l, direct, done_rest[0] + earlier)
-            else:
-                own_back(l, 0)
-                add_cores(l, 1, False)
-                waiting = sums_of(l, 1) + kept[l][1]["halos"] + arrived[0]
-                g_front[l] = offloaded_sum(weights_back(l, front_names, 0, waiting))
-                own_back(l, 1)
-                gate_back(l - 1, 0, arrived[1])
+                gate_back(l - 1, 0, through=1)
                 gate_back(l - 1, 1, [kept[l - 1][0]["dsout"]])
                 g_rest[l - 1] = offloaded_sum(
-                    weights_back(l - 1, rest_names, 0, [kept[l - 1][1]["dsout"]])
+                    weights_back(l - 1, rest_names, 0, [done_rest[l][0]])
                 )
-                split_rest(l)
         grad_in = from_streams(grads)
         output = from_streams(residual[LAYERS])
 
@@ -1343,44 +1391,29 @@
         common = add([common] + [send(common, route) for route in all_tensor], F32)
         packed = jnp.concatenate([packed[:, :8], common], axis=1)
         low_packed = packed.astype(BF)
-        packed = add([low_packed] + [send(low_packed, route) for route in all_plane], F32)
-
-        g_bc = jnp.stack([keep for keep, _ in bc_parts]) + send(
-            jnp.stack([away for _, away in bc_parts]), to_core
-        ).astype(F32)
-        g_bc = g_bc.astype(BF)
+        packed = [low_packed] + [send(low_packed, route) for route in all_plane]
+
         parts = []
         for l in range(LAYERS):
             parts += [*done_rest[l], *done_front[l]]
-        g_z, g_x, g_bc, g_dt, g_out = queue.run(
-            mixer(final_kernel, layers=LAYERS, inner=inner, heads=heads, tensors=n_tensor),
-            parts + [g_bc] + [send(g_bc, route) for route in all_tensor],
-            [((LAYERS, shard, inner), F32), ((LAYERS, shard, inner), F32),
-             ((LAYERS, shard, 2 * STATE), F32), ((LAYERS, shard, heads), F32),
-             ((LAYERS, shard, inner), F32)],
-            limit=16,
+        smalls = queue.run(
+            mixer(
+                final_kernel, layers=LAYERS, inner=inner, heads=heads, tensors=n_tensor, chips=chips
+            ),
+            parts + [v for parts_l in g_bc for v in parts_l] + packed + [hm],
+            [(shape, F32) for shape in (
+                (LAYERS, shard, inner), (LAYERS, shard, inner), (LAYERS, shard, 2 * STATE),
+                (LAYERS, shard, heads), (LAYERS, shard, inner), (LAYERS, 4, inner), (LAYERS, inner),
+                (LAYERS, 4, 2 * STATE), (LAYERS, 2 * STATE), (LAYERS, heads), (LAYERS, heads),
+                (LAYERS, heads), (LAYERS, inner), (LAYERS, width),
+            )],
+            limit=20,
         )
-        group, shared = packed[:, :8, :inner], packed[:, 8:]
-        five = shared[:, :5, : 2 * STATE]
-        head_grads = [group[:, 7, :heads], group[:, 7, LANES : LANES + heads]]
-        head_grads.append(jnp.sum(group[:, 6].reshape(LAYERS, heads, HEADDIM), axis=2))
+        (g_z, g_x, g_shared, g_dt, g_out, g_taps, g_bias, g_taps_bc, g_bias_bc, g_dt_bias, g_log,
+         g_skip, g_gate, g_norm) = smalls
         return (
-            output,
-            grad_in,
-            shared[:, 5],
-            g_z,
-            g_x,
-            g_bc,
-            g_dt,
-            group[:, :4],
-            group[:, 4],
-            five[:, :4],
-            five[:, 4],
-            head_grads[0],
-            head_grads[1],
-            head_grads[2],
-            group[:, 5],
-            jnp.swapaxes(g_out, 1, 2),
+            output, grad_in, g_norm, g_z, g_x, g_shared, g_dt, g_taps, g_bias, g_taps_bc, g_bias_bc,
+            g_dt_bias, g_log, g_skip, g_gate, jnp.swapaxes(g_out, 1, 2),
         )
 
     return local

time: 763 us -> 685 us (0.90)
  starting transfers between devices: 196 us -> 161 us
  waiting for transfers between devices: 164 us -> 136 us
    ppermute x22, starting transfers between devices: 78 us -> 45.2 us  [back(): return lax.ppermute(value, axes, [(b, a) for a, b in pairs(route)])]
    ppermute x22, waiting for transfers between devices: 29.5 us -> 8.69 us  [back(): return lax.ppermute(value, axes, [(b, a) for a, b in pairs(route)])]
    pallas_call x73 -> x68, Pallas kernels: 311 us -> 304 us  [run(): pl.pallas_call(wrapped, in_specs=specs + [free] * len(extra), out_specs=[...]
    unnamed x215 -> x205, local copies, waits for them, and re-layouts: 25.2 us -> 20.1 us
    ppermute x78 -> x82, starting transfers between devices: 118 us -> 116 us  [send(): return lax.ppermute(value, axes, pairs(route))]
    ppermute x78 -> x82, waiting for transfers between devices: 119 us -> 120 us  [send(): return lax.ppermute(value, axes, pairs(route))]
  transfers between devices with their start and end apart: 107 -> 111, of which waited for: 31 -> 29; matrix products, arithmetic and copies ran while one was open for 5% -> 5% of each run, Pallas kernels for 38% -> 43%
where the time goes in v3:
time: 685 us; the launch traced here: 673 us
  Pallas kernels  304 us (44%)
  starting transfers between devices  161 us (24%)
  waiting for transfers between devices  136 us (20%)
  local copies, waits for them, and re-layouts  47.9 us (7%)
  between operations  17 us (2%)
    pallas_call x68, Pallas kernels, run(): pl.pallas_call(wrapped, in_specs=specs + [free] * len(extra), out_specs=[...  304 us
    ppermute x82, waiting for transfers between devices, send(): return lax.ppermute(value, axes, pairs(route))  120 us
    ppermute x82, starting transfers between devices, send(): return lax.ppermute(value, axes, pairs(route))  116 us
    ppermute x22, starting transfers between devices, back(): return lax.ppermute(value, axes, [(b, a) for a, b in pairs(route)])  45.2 us
    unnamed x205, local copies, waits for them, and re-layouts  20.1 us
  transfers between devices with their start and end apart: 111, of which 29 were waited for; matrix products, arithmetic and copies ran while one was open for 5% of the time, Pallas kernels for 43%

profile of v3, /device:TPU:1, one launch (start us, length us, event | category | flops | bytes accessed | tf_op | source)
XLA Modules:
  0.0 672.9 jit_solution(5876266629032551240)
XLA Ops:
  28.7 9.3 %collective-permute-start.9 = (bf16[192,1536]{1,0:T(8,128)(2,1)S(1)}, bf16[192,1536]{1,0:T(8,128)(2,1)S(1)}, u32[]{:S(2)}, u32[]{:S(2)}) collective-permute-start(bf16[192,1536]{1,0:T(8,128)(2,1)S(1)} %shard_map.309.refs_7_), channel_id=1, source_target_pairs={{0,0},{1,4},{2,1},{3,5},{4,2},{5,6},{6,3},{7,7},{8,8},{9,12},{10,9... | collective-permute-start | bytes 1769480 | tf_op jit(solution)/shard_map/ppermute | solution.py:875
  41.1 18.6 %collective-permute-done.11.refs_6_.refs_2_ = bf16[128,1536]{1,0:T(8,128)(2,1)S(1)} collective-permute-done((bf16[128,1536]{1,0:T(8,128)(2,1)S(1)}, bf16[128,1536]{1,0:T(8,128)(2,1)S(1)}, u32[]{:S(2)}, u32[]{:S(2)}) %collective-permute-start.11) | collective-permute-done | bytes 393248 | tf_op jit(solution)/shard_map/ppermute | solution.py:875
  59.6 7.1 %collective-permute-done.1.refs_4_.refs_2_ = bf16[128,1536]{1,0:T(8,128)(2,1)S(1)} collective-permute-done((bf16[128,1536]{1,0:T(8,128)(2,1)S(1)}, bf16[128,1536]{1,0:T(8,128)(2,1)S(1)}, u32[]{:S(2)}, u32[]{:S(2)}) %collective-permute-start.1) | collective-permute-done | bytes 393248 | tf_op jit(solution)/shard_map/ppermute | solution.py:875
  104.7 11.7 %shard_map.313 = (bf16[528,1536]{1,0:T(8,128)(2,1)}, bf16[528,1152]{1,0:T(8,128)(2,1)}, f32[16,1024]{1,0:T(8,128)}, bf16[512,1024]{1,0:T(8,128)(2,1)}, f32[512,2...) custom-call(s32[4]{0:T(128)S(1)} %pad_add_fusion.refs_0_, ...), custom_call_target="tpu_custom_call" | custom-call | flops 1000 | bytes 1000 | tf_op jit(solution)/shard_map/pallas_call | solution.py:817
  124.1 11.9 %shard_map.315 = (bf16[528,1536]{1,0:T(8,128)(2,1)}, bf16[528,1152]{1,0:T(8,128)(2,1)}, f32[16,1024]{1,0:T(8,128)}, bf16[512,1024]{1,0:T(8,128)(2,1)}, f32[512,2...) custom-call(s32[4]{0:T(128)S(1)} %pad_add_fusion.refs_0_, ...), custom_call_target="tpu_custom_call" | custom-call | flops 1000 | bytes 1000 | tf_op jit(solution)/shard_map/pallas_call | solution.py:817
  139.8 12.5 %collective-permute-start.19 = (bf16[128,768]{1,0:T(8,128)(2,1)S(1)}, bf16[128,768]{1,0:T(8,128)(2,1)S(1)}, u32[]{:S(2)}, u32[]{:S(2)}) collective-permute-start(bf16[128,768]{1,0:T(8,128)(2,1)S(1)} %get-tuple-element.222.refs_5_.refs_6_), channel_id=1, source_target_pairs={{0,2},{1,3},{4,6},{5,7},{8,10},{9,11},{12,14},{13,15},{16,18},{17,... | collective-permute-start | bytes 589832 | tf_op jit(solution)/shard_map/ppermute | solution.py:875
  156.4 11.0 %shard_map.318 = (bf16[512,1024]{1,0:T(8,128)(2,1)}, bf16[512,768]{1,0:T(8,128)(2,1)}, f32[512,768]{1,0:T(8,128)}, bf16[512,768]{1,0:T(8,128)(2,1)}, bf16[5,128,...) custom-call(s32[4]{0:T(128)S(1)} %pad_add_fusion.refs_0_, bf16[528,1536]{1,0:T(8,128)(2,1)} %get-tuple-element.208.refs_1_.refs_0_, ...), custom_call_target="tpu_custom_call" | custom-call | flops 1000 | bytes 1000 | tf_op jit(solution)/shard_map/pallas_call | solution.py:817
  171.4 10.0 %collective-permute-start.23 = (bf16[128,1664]{1,0:T(8,128)(2,1)S(1)}, bf16[128,1664]{1,0:T(8,128)(2,1)S(1)}, u32[]{:S(2)}, u32[]{:S(2)}) collective-permute-start(bf16[128,1664]{1,0:T(8,128)(2,1)S(1)} %get-tuple-element.228.refs_17_), channel_id=1, source_target_pairs={{0,1},{1,0},{2,3},{3,2},{4,5},{5,4},{6,7},{7,6},{8,9},{9,8},{10,11... | collective-permute-start | bytes 1277960 | tf_op jit(solution)/shard_map/ppermute | solution.py:875
  182.1 11.1 %shard_map.321 = (bf16[512,1024]{1,0:T(8,128)(2,1)}, bf16[512,768]{1,0:T(8,128)(2,1)}, f32[512,768]{1,0:T(8,128)}, bf16[512,768]{1,0:T(8,128)(2,1)}, bf16[5,128,...) custom-call(s32[4]{0:T(128)S(1)} %pad_add_fusion.refs_0_, bf16[528,1536]{1,0:T(8,128)(2,1)} %get-tuple-element.230.refs_1_.refs_2_.refs_3_, ...), custom_call_target="tpu_custom_call" | custom-call | flops 1000 | bytes 1000 | tf_op jit(solution)/shard_map/pallas_call | solution.py:817
  200.8 7.6 %collective-permute-done.24.refs_2_ = bf16[128,1536]{1,0:T(8,128)(2,1)S(1)} collective-permute-done((bf16[128,1536]{1,0:T(8,128)(2,1)S(1)}, bf16[128,1536]{1,0:T(8,128)(2,1)S(1)}, u32[]{:S(2)}, u32[]{:S(2)}) %collective-permute-start.24) | collective-permute-done | bytes 393248 | tf_op jit(solution)/shard_map/ppermute | solution.py:875
  211.1 11.6 %shard_map.325 = (bf16[528,1536]{1,0:T(8,128)(2,1)}, bf16[528,1152]{1,0:T(8,128)(2,1)}, f32[16,1024]{1,0:T(8,128)}, bf16[512,1024]{1,0:T(8,128)(2,1)}, f32[512,2...) custom-call(s32[4]{0:T(128)S(1)} %pad_add_fusion.refs_0_, ...), custom_call_target="tpu_custom_call" | custom-call | flops 1000 | bytes 1000 | tf_op jit(solution)/shard_map/pallas_call | solution.py:817
  226.0 9.7 %collective-permute-done.32.refs_2_ = bf16[128,1536]{1,0:T(8,128)(2,1)S(1)} collective-permute-done((bf16[128,1536]{1,0:T(8,128)(2,1)S(1)}, bf16[128,1536]{1,0:T(8,128)(2,1)S(1)}, u32[]{:S(2)}, u32[]{:S(2)}) %collective-permute-start.32) | collective-permute-done | bytes 393248 | tf_op jit(solution)/shard_map/ppermute | solution.py:875
  241.3 11.3 %shard_map.328 = (bf16[528,1536]{1,0:T(8,128)(2,1)}, bf16[528,1152]{1,0:T(8,128)(2,1)}, f32[16,1024]{1,0:T(8,128)}, bf16[512,1024]{1,0:T(8,128)(2,1)}, f32[512,2...) custom-call(s32[4]{0:T(128)S(1)} %pad_add_fusion.refs_0_, ...), custom_call_target="tpu_custom_call" | custom-call | flops 1000 | bytes 1000 | tf_op jit(solution)/shard_map/pallas_call | solution.py:817
  263.3 10.7 %shard_map.330 = (bf16[512,1024]{1,0:T(8,128)(2,1)}, bf16[512,768]{1,0:T(8,128)(2,1)}, f32[512,768]{1,0:T(8,128)}, bf16[512,768]{1,0:T(8,128)(2,1)}, bf16[5,128,...) custom-call(s32[4]{0:T(128)S(1)} %pad_add_fusion.refs_0_, bf16[528,1536]{1,0:T(8,128)(2,1)} %get-tuple-element.239.refs_1_.refs_0_, ...), custom_call_target="tpu_custom_call" | custom-call | flops 1000 | bytes 1000 | tf_op jit(solution)/shard_map/pallas_call | solution.py:817
  279.7 10.6 %shard_map.333 = (bf16[512,1024]{1,0:T(8,128)(2,1)}, bf16[512,768]{1,0:T(8,128)(2,1)}, f32[512,768]{1,0:T(8,128)}, bf16[512,768]{1,0:T(8,128)(2,1)}, bf16[5,128,...) custom-call(s32[4]{0:T(128)S(1)} %pad_add_fusion.refs_0_, bf16[528,1536]{1,0:T(8,128)(2,1)} %get-tuple-element.263.refs_1_.refs_2_, ...), custom_call_target="tpu_custom_call" | custom-call | flops 1000 | bytes 1000 | tf_op jit(solution)/shard_map/pallas_call | solution.py:817
  299.2 8.5 %collective-permute-done.44.refs_2_ = bf16[128,1664]{1,0:T(8,128)(2,1)S(1)} collective-permute-done((bf16[128,1664]{1,0:T(8,128)(2,1)S(1)}, bf16[128,1664]{1,0:T(8,128)(2,1)S(1)}, u32[]{:S(2)}, u32[]{:S(2)}) %collective-permute-start.44) | collective-permute-done | bytes 426016 | tf_op jit(solution)/shard_map/ppermute | solution.py:875
  308.9 7.9 %collective-permute-done.42.refs_1_ = bf16[128,1664]{1,0:T(8,128)(2,1)S(1)} collective-permute-done((bf16[128,1664]{1,0:T(8,128)(2,1)S(1)}, bf16[128,1664]{1,0:T(8,128)(2,1)S(1)}, u32[]{:S(2)}, u32[]{:S(2)}) %collective-permute-start.42) | collective-permute-done | bytes 426016 | tf_op jit(solution)/shard_map/ppermute | solution.py:875
  321.9 8.1 %shard_map.338 = (bf16[512,1536]{1,0:T(8,128)(2,1)}, bf16[512,768]{1,0:T(8,128)(2,1)}, bf16[528,768]{1,0:T(8,128)(2,1)}, f32[8,768]{1,0:T(8,128)S(1)}, bf16[128,768]{1,0:T(8,128)(2,1)S(1)}) custom-call(s32[4]{0:T(128)S(1)} %pad_add_fusion.refs_0_, bf16[128,1664]{1,0:T(8,128)(2,1)S(1)} %get-tuple-element.270.refs_3_.refs_1_, ...), custom_call_target="tpu_custom_call" | custom-call | flops 1000 | bytes 1000 | tf_op jit(solution)/shard_map/pallas_call | solution.py:817
  333.7 8.1 %shard_map.340 = (bf16[512,1536]{1,0:T(8,128)(2,1)}, bf16[512,768]{1,0:T(8,128)(2,1)}, bf16[528,768]{1,0:T(8,128)(2,1)}, f32[8,768]{1,0:T(8,128)S(1)}, bf16[128,768]{1,0:T(8,128)(2,1)S(1)}) custom-call(s32[4]{0:T(128)S(1)} %pad_add_fusion.refs_0_, bf16[128,1664]{1,0:T(8,128)(2,1)S(1)} %get-tuple-element.284.refs_14_.refs_1_, ...), custom_call_target="tpu_custom_call" | custom-call | flops 1000 | bytes 1000 | tf_op jit(solution)/shard_map/pallas_call | solution.py:817
  345.8 11.3 %shard_map.342.refs_0_ = bf16[1536,1536]{1,0:T(8,128)(2,1)} custom-call(bf16[528,1536]{1,0:T(8,128)(2,1)} %get-tuple-element.239.refs_1_.refs_0_, bf16[528,768]{1,0:T(8,128)(2,1)} %get-tuple-element.286.refs_1_.refs_8_, bf16[528,1536]{1,0:T(8,128)(2,1)} %get-tuple-element.263.refs_1_.refs_2_, bf16[528,768]{1,0:T(8,128)(2,1)} %get-tuple-element.293.refs_3_.refs_8_, ...), custom_call_target="tpu_custom_call" | custom-call | flops 1000 | bytes 1000 | tf_op jit(solution)/shard_map/pallas_call | solution.py:817
  360.8 20.4 %shard_map.344 = (bf16[528,1152]{1,0:T(8,128)(2,1)}, f32[8,1024]{1,0:T(8,128)S(1)}, f32[8,128]{1,0:T(8,128)S(1)}, f32[528,1536]{1,0:T(8,128)S(1)}) custom-call(s32[4]{0:T(128)S(1)} %pad_add_fusion.refs_0_, bf16[1536,1152]{1,0:T(8,128)(2,1)} %all-gather.9.cloned.1.call-done.refs_5_.refs_1_, ...), custom_call_target="tpu_custom_call" | custom-call | flops 1000 | bytes 1000 | tf_op jit(solution)/shard_map/pallas_call | solution.py:817
  386.8 20.2 %shard_map.347 = (bf16[528,1152]{1,0:T(8,128)(2,1)}, f32[8,1024]{1,0:T(8,128)S(1)}, f32[8,128]{1,0:T(8,128)S(1)}, f32[528,1536]{1,0:T(8,128)S(1)}) custom-call(s32[4]{0:T(128)S(1)} %pad_add_fusion.refs_0_, bf16[1536,1152]{1,0:T(8,128)(2,1)} %all-gather.9.cloned.1.call-done.refs_5_.refs_1_, ...), custom_call_target="tpu_custom_call" | custom-call | flops 1000 | bytes 1000 | tf_op jit(solution)/shard_map/pallas_call | solution.py:817
  416.7 10.8 %shard_map.351.refs_0_ = bf16[1536,1152]{1,0:T(8,128)(2,1)} custom-call(bf16[528,1536]{1,0:T(8,128)(2,1)} %get-tuple-element.239.refs_1_.refs_0_, bf16[528,1152]{1,0:T(8,128)(2,1)} %get-tuple-element.316.refs_1_, bf16[528,1536]{1,0:T(8,128)(2,1)} %get-tuple-element.263.refs_1_.refs_2_, bf16[528,1152]{1,0:T(8,128)(2,1)} %get-tuple-element.317.refs_3_, ...), custom_call_target="tpu_custom_call" | custom-call | flops 1000 | bytes 1000 | tf_op jit(solution)/shard_map/pallas_call | solution.py:817
  447.3 8.8 %shard_map.355 = (bf16[512,1536]{1,0:T(8,128)(2,1)}, bf16[512,768]{1,0:T(8,128)(2,1)}, bf16[528,768]{1,0:T(8,128)(2,1)}, f32[8,768]{1,0:T(8,128)S(1)}, bf16[128,768]{1,0:T(8,128)(2,1)S(1)}) custom-call(s32[4]{0:T(128)S(1)} %pad_add_fusion.refs_0_, bf16[128,1664]{1,0:T(8,128)(2,1)S(1)} %copy-done.8, bf16[128,1664]{1,0:T(8,128)(2,1)S(1)} %copy-done.12, ...), custom_call_target="tpu_custom_call" | custom-call | flops 1000 | bytes 1000 | tf_op jit(solution)/shard_map/pallas_call | solution.py:817
  459.7 8.0 %shard_map.357 = (bf16[512,1536]{1,0:T(8,128)(2,1)}, bf16[512,768]{1,0:T(8,128)(2,1)}, bf16[528,768]{1,0:T(8,128)(2,1)}, f32[8,768]{1,0:T(8,128)S(1)}, bf16[128,768]{1,0:T(8,128)(2,1)S(1)}) custom-call(s32[4]{0:T(128)S(1)} %pad_add_fusion.refs_0_, bf16[128,1664]{1,0:T(8,128)(2,1)S(1)} %get-tuple-element.319.refs_14_.refs_1_, ...), custom_call_target="tpu_custom_call" | custom-call | flops 1000 | bytes 1000 | tf_op jit(solution)/shard_map/pallas_call | solution.py:817
  471.0 11.2 %shard_map.359.refs_0_ = bf16[1536,1536]{1,0:T(8,128)(2,1)} custom-call(bf16[528,1536]{1,0:T(8,128)(2,1)} %get-tuple-element.208.refs_1_.refs_0_, bf16[528,768]{1,0:T(8,128)(2,1)} %get-tuple-element.321.refs_1_.refs_8_, bf16[528,1536]{1,0:T(8,128)(2,1)} %get-tuple-element.230.refs_1_.refs_2_.refs_3_, bf16[528,768]{1,0:T(8,128)(2,1)} %get-tuple-element.328.refs_3_.refs_8_, ...), custom_call_target="tpu_custom_call" | custom-call | flops 1000 | bytes 1000 | tf_op jit(solution)/shard_map/pallas_call | solution.py:817
  487.7 20.1 %shard_map.361 = (bf16[528,1152]{1,0:T(8,128)(2,1)}, f32[8,1024]{1,0:T(8,128)S(1)}, f32[8,128]{1,0:T(8,128)S(1)}, f32[528,1536]{1,0:T(8,128)S(1)}) custom-call(s32[4]{0:T(128)S(1)} %pad_add_fusion.refs_0_, bf16[1536,1152]{1,0:T(8,128)(2,1)} %all-gather.5.cloned.1.call-done.refs_5_.refs_1_, ...), custom_call_target="tpu_custom_call" | custom-call | flops 1000 | bytes 1000 | tf_op jit(solution)/shard_map/pallas_call | solution.py:817
  524.1 20.9 %shard_map.365 = (bf16[528,1152]{1,0:T(8,128)(2,1)}, f32[8,1024]{1,0:T(8,128)S(1)}, f32[8,128]{1,0:T(8,128)S(1)}, f32[528,1536]{1,0:T(8,128)S(1)}) custom-call(s32[4]{0:T(128)S(1)} %pad_add_fusion.refs_0_, bf16[1536,1152]{1,0:T(8,128)(2,1)} %all-gather.5.cloned.1.call-done.refs_5_.refs_1_, ...), custom_call_target="tpu_custom_call" | custom-call | flops 1000 | bytes 1000 | tf_op jit(solution)/shard_map/pallas_call | solution.py:817
  557.8 11.1 %shard_map.369 = (bf16[384,1152]{1,0:T(8,128)(2,1)S(1)}, bf16[384,1152]{1,0:T(8,128)(2,1)}, bf16[384,1152]{1,0:T(8,128)(2,1)}, bf16[384,1152]{1,0:T(8,128)(2,1)}) custom-call(s32[4]{0:T(128)S(1)} %pad_add_fusion.refs_0_, bf16[528,1536]{1,0:T(8,128)(2,1)} %get-tuple-element.208.refs_1_.refs_0_, bf16[528,1152]{1,0:T(8,128)(2,1)} %get-tuple-element.354.refs_2_, ...), custom_call_target="tpu_custom_call" | custom-call | flops 1000 | bytes 1000 | tf_op jit(solution)/shard_map/pallas_call | solution.py:817
  599.2 10.6 %collective-permute-done.89.refs_4_ = bf16[384,1152]{1,0:T(8,128)(2,1)} collective-permute-done((bf16[384,1152]{1,0:T(8,128)(2,1)}, bf16[384,1152]{1,0:T(8,128)(2,1)}, u32[]{:S(2)}, u32[]{:S(2)}) %collective-permute-start.89) | collective-permute-done | bytes 884768 | tf_op jit(solution)/shard_map/ppermute | solution.py:875
  612.5 8.8 %collective-permute-start.96 = (bf16[2,16,1536]{2,1,0:T(8,128)(2,1)S(1)}, bf16[2,16,1536]{2,1,0:T(8,128)(2,1)S(1)}, u32[]{:S(2)}, u32[]{:S(2)}) collective-permute-start(bf16[2,16,1536]{2,1,0:T(8,128)(2,1)S(1)} %shard_map.373.refs_2_), channel_id=1, source_target_pairs={{0,0},{4,1},{1,2},{5,3},{2,4},{6,5},{3,6},{7,7},{8,8},{12,9},{9,10... | collective-permute-start | bytes 294920 | tf_op jit(solution)/shard_map/ppermute | solution.py:878
  636.5 18.5 %collective-permute-done.94.refs_10_ = bf16[192,256]{1,0:T(8,128)(2,1)S(1)} collective-permute-done((bf16[192,256]{1,0:T(8,128)(2,1)S(1)}, bf16[192,256]{1,0:T(8,128)(2,1)S(1)}, u32[]{:S(2)}, u32[]{:S(2)}) %collective-permute-start.94) | collective-permute-done | bytes 98336 | tf_op jit(solution)/shard_map/ppermute | solution.py:875
  (560 shorter events, 278.0 us)
Async XLA Ops:
  7.2 95.8 %all-gather.5.cloned.1.call-start = ((), (), s32[]{:S(2)}) async-start(), calls=%async_computation.3 | async-start | bytes 4423680 | tf_op jit(solution)/shard_map/all_gather | solution.py:961
  26.4 129.4 %all-gather.7.cloned.1.call-start = ((), (), s32[]{:S(2)}) async-start(), calls=%async_computation.4 | async-start | bytes 5898240 | tf_op jit(solution)/shard_map/all_gather | solution.py:961
  27.8 38.9 %collective-permute-start.10 = (bf16[192,1536]{1,0:T(8,128)(2,1)S(1)}, bf16[192,1536]{1,0:T(8,128)(2,1)S(1)}, u32[]{:S(2)}, u32[]{:S(2)}) collective-permute-start(bf16[192,1536]{1,0:T(8,128)(2,1)S(1)} %shard_map.309.refs_7_), channel_id=1, source_target_pairs={{0,2},{1,6},{2,3},{3,7},{4,0},{5,4},{6,1},{7,5},{8,10},{9,14},{10,... | collective-permute-start | bytes 1769480 | tf_op jit(solution)/shard_map/ppermute | solution.py:875
  28.7 38.0 %collective-permute-start.9 = (bf16[192,1536]{1,0:T(8,128)(2,1)S(1)}, bf16[192,1536]{1,0:T(8,128)(2,1)S(1)}, u32[]{:S(2)}, u32[]{:S(2)}) collective-permute-start(bf16[192,1536]{1,0:T(8,128)(2,1)S(1)} %shard_map.309.refs_7_), channel_id=1, source_target_pairs={{0,0},{1,4},{2,1},{3,5},{4,2},{5,6},{6,3},{7,7},{8,8},{9,12},{10,9... | collective-permute-start | bytes 1769480 | tf_op jit(solution)/shard_map/ppermute | solution.py:875
  41.0 25.7 %collective-permute-start.1 = (bf16[128,1536]{1,0:T(8,128)(2,1)S(1)}, bf16[128,1536]{1,0:T(8,128)(2,1)S(1)}, u32[]{:S(2)}, u32[]{:S(2)}) collective-permute-start(bf16[128,1536]{1,0:T(8,128)(2,1)S(1)} %get-tuple-element.206.refs_2_.refs_3_.refs_1_), channel_id=1, source_target_pairs={{0,1},{1,0},{2,3},{3,2},{4,5},{5,4},{6,7},{7,6},{8,9},{9,8},{10,11... | collective-permute-start | bytes 1179656 | tf_op jit(solution)/shard_map/ppermute | solution.py:875
  69.9 141.2 %all-gather.9.cloned.1.call-start = ((), (), s32[]{:S(2)}) async-start(), calls=%async_computation.5 | async-start | bytes 4423680 | tf_op jit(solution)/shard_map/all_gather | solution.py:961
  92.8 43.3 %collective-permute-start.15 = (bf16[192,2432]{1,0:T(8,128)(2,1)S(1)}, bf16[192,2432]{1,0:T(8,128)(2,1)}, u32[]{:S(2)}, u32[]{:S(2)}) collective-permute-start(bf16[192,2432]{1,0:T(8,128)(2,1)S(1)} %shard_map.312.refs_11_), channel_id=1, source_target_pairs={{0,0},{1,4},{2,1},{3,5},{4,2},{5,6},{6,3},{7,7},{8,8},{9,12},{10,9... | collective-permute-start | bytes 2801672 | tf_op jit(solution)/shard_map/ppermute | solution.py:875
  97.2 38.9 %collective-permute-start.16 = (bf16[192,2432]{1,0:T(8,128)(2,1)S(1)}, bf16[192,2432]{1,0:T(8,128)(2,1)}, u32[]{:S(2)}, u32[]{:S(2)}) collective-permute-start(bf16[192,2432]{1,0:T(8,128)(2,1)S(1)} %shard_map.312.refs_11_), channel_id=1, source_target_pairs={{0,2},{1,6},{2,3},{3,7},{4,0},{5,4},{6,1},{7,5},{8,10},{9,14},{10,... | collective-permute-start | bytes 2801672 | tf_op jit(solution)/shard_map/ppermute | solution.py:875
  139.1 124.2 %all-gather.11.cloned.1.call-start = ((), (), s32[]{:S(2)}) async-start(), calls=%async_computation.6 | async-start | bytes 5898240 | tf_op jit(solution)/shard_map/all_gather | solution.py:961
  139.6 294.3 %reduce-scatter.4.cloned.1.call-start = ((), (), s32[]{:S(2)}) async-start(), calls=%async_computation.7 | async-start | bytes 5898240 | tf_op jit(solution)/shard_map/reduce_scatter | solution.py:1237
  139.8 27.6 %collective-permute-start.19 = (bf16[128,768]{1,0:T(8,128)(2,1)S(1)}, bf16[128,768]{1,0:T(8,128)(2,1)S(1)}, u32[]{:S(2)}, u32[]{:S(2)}) collective-permute-start(bf16[128,768]{1,0:T(8,128)(2,1)S(1)} %get-tuple-element.222.refs_5_.refs_6_), channel_id=1, source_target_pairs={{0,2},{1,3},{4,6},{5,7},{8,10},{9,11},{12,14},{13,15},{16,18},{17,... | collective-permute-start | bytes 589832 | tf_op jit(solution)/shard_map/ppermute | solution.py:875
  198.8 23.9 %collective-permute-start.28 = (bf16[128,1664]{1,0:T(8,128)(2,1)S(1)}, bf16[128,1664]{1,0:T(8,128)(2,1)S(1)}, u32[]{:S(2)}, u32[]{:S(2)}) collective-permute-start(bf16[128,1664]{1,0:T(8,128)(2,1)S(1)} %get-tuple-element.238.refs_11_), channel_id=1, source_target_pairs={{0,1},{1,0},{2,3},{3,2},{4,5},{5,4},{6,7},{7,6},{8,9},{9,8},{10,11... | collective-permute-start | bytes 1277960 | tf_op jit(solution)/shard_map/ppermute | solution.py:875
  298.7 23.2 %collective-permute-start.45 = (bf16[128,1664]{1,0:T(8,128)(2,1)S(1)}, bf16[128,1664]{1,0:T(8,128)(2,1)S(1)}, u32[]{:S(2)}, u32[]{:S(2)}) collective-permute-start(bf16[128,1664]{1,0:T(8,128)(2,1)S(1)} %get-tuple-element.270.refs_3_.refs_1_), channel_id=1, source_target_pairs={{0,4},{1,5},{2,6},{3,7},{4,0},{5,1},{6,2},{7,3},{8,12},{9,13},{10,... | collective-permute-start | bytes 1277960 | tf_op jit(solution)/shard_map/ppermute | solution.py:875
  357.1 156.9 %reduce-scatter.6.cloned.1.call-start = ((), (), s32[]{:S(2)}) async-start(), calls=%async_computation.8 | async-start | bytes 4423680 | tf_op jit(solution)/shard_map/reduce_scatter | solution.py:1237
  357.2 24.1 %collective-permute-start.51 = (bf16[128,768]{1,0:T(8,128)(2,1)S(1)}, bf16[128,768]{1,0:T(8,128)(2,1)S(1)}, u32[]{:S(2)}, u32[]{:S(2)}) collective-permute-start(bf16[128,768]{1,0:T(8,128)(2,1)S(1)} %shard_map.341.refs_8_), channel_id=1, source_target_pairs={{2,0},{3,1},{6,4},{7,5},{10,8},{11,9},{14,12},{15,13},{18,16},{19,... | collective-permute-start | bytes 589832 | tf_op jit(solution)/shard_map/ppermute | solution.py:878
  432.7 148.8 %reduce-scatter.8.cloned.1.call-start = ((), (), s32[]{:S(2)}) async-start(), calls=%async_computation.9 | async-start | bytes 5898240 | tf_op jit(solution)/shard_map/reduce_scatter | solution.py:1237
  445.2 37.0 %collective-permute-start.67 = (bf16[192,1536]{1,0:T(8,128)(2,1)S(1)}, bf16[192,1536]{1,0:T(8,128)(2,1)S(1)}, u32[]{:S(2)}, u32[]{:S(2)}) collective-permute-start(bf16[192,1536]{1,0:T(8,128)(2,1)S(1)} %get-tuple-element.334), channel_id=1, source_target_pairs={{0,0},{4,1},{1,2},{5,3},{2,4},{6,5},{3,6},{7,7},{8,8},{12,9},{9,10... | collective-permute-start | bytes 1769480 | tf_op jit(solution)/shard_map/ppermute | solution.py:878
  484.1 23.8 %collective-permute-start.69 = (bf16[192,1536]{1,0:T(8,128)(2,1)S(1)}, bf16[192,1536]{1,0:T(8,128)(2,1)S(1)}, u32[]{:S(2)}, u32[]{:S(2)}) collective-permute-start(bf16[192,1536]{1,0:T(8,128)(2,1)S(1)} %copy-done.30), channel_id=1, source_target_pairs={{2,0},{6,1},{3,2},{7,3},{0,4},{4,5},{1,6},{5,7},{10,8},{14,9},{11,... | collective-permute-start | bytes 1769480 | tf_op jit(solution)/shard_map/ppermute | solution.py:878
  484.1 23.8 %collective-permute-start.68 = (bf16[128,768]{1,0:T(8,128)(2,1)S(1)}, bf16[128,768]{1,0:T(8,128)(2,1)S(1)}, u32[]{:S(2)}, u32[]{:S(2)}) collective-permute-start(bf16[128,768]{1,0:T(8,128)(2,1)S(1)} %shard_map.358.refs_8_), channel_id=1, source_target_pairs={{2,0},{3,1},{6,4},{7,5},{10,8},{11,9},{14,12},{15,13},{18,16},{19,... | collective-permute-start | bytes 589832 | tf_op jit(solution)/shard_map/ppermute | solution.py:878
  513.0 32.1 %collective-permute-start.71 = (bf16[128,1536]{1,0:T(8,128)(2,1)S(1)}, bf16[128,1536]{1,0:T(8,128)(2,1)S(1)}, u32[]{:S(2)}, u32[]{:S(2)}) collective-permute-start(bf16[128,1536]{1,0:T(8,128)(2,1)S(1)} %get-tuple-element.337), channel_id=1, source_target_pairs={{0,1},{1,0},{2,3},{3,2},{4,5},{5,4},{6,7},{7,6},{8,9},{9,8},{10,11... | collective-permute-start | bytes 1179656 | tf_op jit(solution)/shard_map/ppermute | solution.py:875
  515.9 29.1 %collective-permute-start.74 = (bf16[192,896]{1,0:T(8,128)(2,1)S(1)}, bf16[192,896]{1,0:T(8,128)(2,1)S(1)}, u32[]{:S(2)}, u32[]{:S(2)}) collective-permute-start(bf16[192,896]{1,0:T(8,128)(2,1)S(1)} %get-tuple-element.345), channel_id=1, source_target_pairs={{0,0},{4,1},{1,2},{5,3},{2,4},{6,5},{3,6},{7,7},{8,8},{12,9},{9,10... | collective-permute-start | bytes 1032200 | tf_op jit(solution)/shard_map/ppermute | solution.py:878
  518.9 26.2 %collective-permute-start.75 = (bf16[192,896]{1,0:T(8,128)(2,1)S(1)}, bf16[192,896]{1,0:T(8,128)(2,1)S(1)}, u32[]{:S(2)}, u32[]{:S(2)}) collective-permute-start(bf16[192,896]{1,0:T(8,128)(2,1)S(1)} %get-tuple-element.346), channel_id=1, source_target_pairs={{2,0},{6,1},{3,2},{7,3},{0,4},{4,5},{1,6},{5,7},{10,8},{14,9},{11,... | collective-permute-start | bytes 1032200 | tf_op jit(solution)/shard_map/ppermute | solution.py:878
  548.4 22.9 %collective-permute-start.81 = (bf16[192,256]{1,0:T(8,128)(2,1)S(1)}, bf16[192,256]{1,0:T(8,128)(2,1)S(1)}, u32[]{:S(2)}, u32[]{:S(2)}) collective-permute-start(bf16[192,256]{1,0:T(8,128)(2,1)S(1)} %add_convert_fusion.1.refs_7_.refs_12_), channel_id=1, source_target_pairs={{0,1},{1,0},{2,3},{3,2},{4,5},{5,4},{6,7},{7,6},{8,9},{9,8},{10,11... | collective-permute-start | bytes 294920 | tf_op jit(solution)/shard_map/ppermute | solution.py:875
  554.8 34.2 %collective-permute-start.77 = (bf16[128,1536]{1,0:T(8,128)(2,1)}, bf16[128,1536]{1,0:T(8,128)(2,1)S(1)}, u32[]{:S(2)}, u32[]{:S(2)}) collective-permute-start(bf16[128,1536]{1,0:T(8,128)(2,1)} %get-tuple-element.350), channel_id=1, source_target_pairs={{0,1},{1,0},{2,3},{3,2},{4,5},{5,4},{6,7},{7,6},{8,9},{9,8},{10,11... | collective-permute-start | bytes 1179656 | tf_op jit(solution)/shard_map/ppermute | solution.py:875
  569.0 30.1 %collective-permute-start.87 = (bf16[384,1152]{1,0:T(8,128)(2,1)}, bf16[384,1152]{1,0:T(8,128)(2,1)S(1)}, u32[]{:S(2)}, u32[]{:S(2)}) collective-permute-start(bf16[384,1152]{1,0:T(8,128)(2,1)} %get-tuple-element.361), channel_id=1, source_target_pairs={{0,8},{1,9},{2,10},{3,11},{4,12},{5,13},{6,14},{7,15},{8,0},{9,1},... | collective-permute-start | bytes 2654216 | tf_op jit(solution)/shard_map/ppermute | solution.py:875
  570.2 28.9 %collective-permute-start.88 = (bf16[384,1152]{1,0:T(8,128)(2,1)}, bf16[384,1152]{1,0:T(8,128)(2,1)}, u32[]{:S(2)}, u32[]{:S(2)}) collective-permute-start(bf16[384,1152]{1,0:T(8,128)(2,1)} %get-tuple-element.362), channel_id=1, source_target_pairs={{0,16},{1,17},{2,18},{3,19},{4,20},{5,21},{6,22},{7,23},{8,24},{9,... | collective-permute-start | bytes 2654216 | tf_op jit(solution)/shard_map/ppermute | solution.py:875
  571.9 37.9 %collective-permute-start.89 = (bf16[384,1152]{1,0:T(8,128)(2,1)}, bf16[384,1152]{1,0:T(8,128)(2,1)}, u32[]{:S(2)}, u32[]{:S(2)}) collective-permute-start(bf16[384,1152]{1,0:T(8,128)(2,1)} %get-tuple-element.356.refs_2_), channel_id=1, source_target_pairs={{0,24},{1,25},{2,26},{3,27},{4,28},{5,29},{6,30},{7,31},{8,16},{9,... | collective-permute-start | bytes 2654216 | tf_op jit(solution)/shard_map/ppermute | solution.py:875
  583.7 26.1 %collective-permute-start.85 = (bf16[192,1536]{1,0:T(8,128)(2,1)S(1)}, bf16[192,1536]{1,0:T(8,128)(2,1)S(1)}, u32[]{:S(2)}, u32[]{:S(2)}) collective-permute-start(bf16[192,1536]{1,0:T(8,128)(2,1)S(1)} %get-tuple-element.359), channel_id=1, source_target_pairs={{0,0},{4,1},{1,2},{5,3},{2,4},{6,5},{3,6},{7,7},{8,8},{12,9},{9,10... | collective-permute-start | bytes 1769480 | tf_op jit(solution)/shard_map/ppermute | solution.py:878
  599.1 28.5 %collective-permute-start.43 = (f32[128,1536]{1,0:T(8,128)S(1)}, f32[128,1536]{1,0:T(8,128)S(1)}, u32[]{:S(2)}, u32[]{:S(2)}) collective-permute-start(f32[128,1536]{1,0:T(8,128)S(1)} %get-tuple-element.550), channel_id=1, source_target_pairs={{0,4},{1,5},{2,6},{3,7},{4,0},{5,1},{6,2},{7,3},{8,12},{9,13},{10,... | collective-permute-start | bytes 2359304 | tf_op jit(solution)/shard_map/ppermute | solution.py:875
  621.7 35.5 %collective-permute-start.84 = (f32[128,1536]{1,0:T(8,128)S(1)}, f32[128,1536]{1,0:T(8,128)S(1)}, u32[]{:S(2)}, u32[]{:S(2)}) collective-permute-start(f32[128,1536]{1,0:T(8,128)S(1)} %get-tuple-element.548), channel_id=1, source_target_pairs={{0,4},{1,5},{2,6},{3,7},{4,0},{5,1},{6,2},{7,3},{8,12},{9,13},{10,... | collective-permute-start | bytes 2359304 | tf_op jit(solution)/shard_map/ppermute | solution.py:875
  628.8 33.7 %collective-permute-start.90 = (bf16[192,896]{1,0:T(8,128)(2,1)S(1)}, bf16[192,896]{1,0:T(8,128)(2,1)S(1)}, u32[]{:S(2)}, u32[]{:S(2)}) collective-permute-start(bf16[192,896]{1,0:T(8,128)(2,1)S(1)} %get-tuple-element.364), channel_id=1, source_target_pairs={{0,0},{4,1},{1,2},{5,3},{2,4},{6,5},{3,6},{7,7},{8,8},{12,9},{9,10... | collective-permute-start | bytes 1032200 | tf_op jit(solution)/shard_map/ppermute | solution.py:878
  632.5 30.1 %collective-permute-start.91 = (bf16[192,896]{1,0:T(8,128)(2,1)S(1)}, bf16[192,896]{1,0:T(8,128)(2,1)S(1)}, u32[]{:S(2)}, u32[]{:S(2)}) collective-permute-start(bf16[192,896]{1,0:T(8,128)(2,1)S(1)} %get-tuple-element.365), channel_id=1, source_target_pairs={{2,0},{6,1},{3,2},{7,3},{0,4},{4,5},{1,6},{5,7},{10,8},{14,9},{11,... | collective-permute-start | bytes 1032200 | tf_op jit(solution)/shard_map/ppermute | solution.py:878
  (179 other events, 1758.9 us)
Sparse Core Ops, SparseCore 0:
  26.5 54.2 all-gather.4
  83.2 57.0 all-gather.6
  142.2 61.6 all-gather.8
  206.2 57.0 all-gather.10
  357.2 54.4 reduce-scatter.3
  432.9 49.3 reduce-scatter.5
  485.3 57.0 reduce-scatter.7

commit v4 on v3

--- a/solution.py
+++ b/solution.py
@@ -14,7 +14,7 @@
 LAYERS = 2
 EPSILON = 1e-05
 HALO = 16
-CHUNK = 128
+CHUNK = 256
 LANES = 128
 
 BF = jnp.bfloat16
@@ -166,7 +166,6 @@
      extra_ref, z_ref, wz_ref, wo_ref, sems) = refs[-17:]
     copy_toks = start_copy(far_toks_ref, toks_ref, sems.at[2])
     copy_z = fetch_rest(rest_ref, 0, wz_ref, sems.at[0])
-    copy_out = fetch_rest(rest_ref, inner, wo_ref, sems.at[1])
     count = xb_ref.shape[0]
     wide = inner + 2 * STATE
     width = toks_ref.shape[1]
@@ -175,6 +174,7 @@
     first = lane < HEADDIM
     copy_toks.wait()
     copy_z.wait()
+    copy_out = fetch_rest(rest_ref, inner, wo_ref, sems.at[1])
     for low in range(0, inner, 2 * LANES):
         lanes = slice(low, min(low + 2 * LANES, inner))
         z_ref[:, lanes] = dot(toks_ref[HALO:, :], wz_ref[:, lanes])
@@ -360,11 +360,6 @@
     (far_grows_ref, gcore_ref, gz_ref, ggain_ref, dsin_ref, state_ref, gg_ref, coef_ref,
      wo_ref, core_ref, z_ref, xb_ref, grows_ref, sems) = refs[-14:]
     copy_out = fetch_rest(rest_ref, inner, wo_ref, sems.at[0])
-    copies = [
-        start_copy(far_core_ref, core_ref, sems.at[1]),
-        start_copy(far_z_ref, z_ref, sems.at[2]),
-        start_copy(far_xb_ref, xb_ref, sems.at[3]),
-    ]
     count = xb_ref.shape[0]
     chunks = count // CHUNK
     width = grows_ref.shape[1]
@@ -376,6 +371,11 @@
             grows_ref[at, :] = part[:, :width]
             coef_ref[at, :] = jnp.broadcast_to(read_pair(part[:, width:]), (block, LANES))
     leaving = start_copy(grows_ref, far_grows_ref, sems.at[4])
+    copies = [
+        start_copy(far_core_ref, core_ref, sems.at[1]),
+        start_copy(far_z_ref, z_ref, sems.at[2]),
+        start_copy(far_xb_ref, xb_ref, sems.at[3]),
+    ]
     copy_out.wait()
     for low in range(0, inner, 2 * LANES):
         lanes = slice(low, min(low + 2 * LANES, inner))
@@ -428,18 +428,16 @@
 def scan_back_kernel(*refs, inner, half_size, chips, ready):
     at_ref, refs = refs[0], refs[1:]
     pieces, refs = refs[:chips], refs[chips:]
-    (rest_ref, far_raw_ref, far_xb_ref, far_core_ref, far_sst_ref, gcore_ref, gz_ref, aux_ref,
+    (rest_ref, far_gz_ref, far_raw_ref, far_xb_ref, far_core_ref, far_sst_ref, gcore_ref, aux_ref,
      dso_ref, tail_ref, cm_ref, segr_ref, lnk_ref, gp_ref, cw_ref, hp_ref, e2_ref, hm_ref) = refs[:18]
     (graw_ref, sgrad_ref, hgrad_ref, part_ref, state_ref, dpre_ref, qv_ref, xd_ref,
-     raw_ref, wf_ref, wz_ref, xb_ref, core_ref, sst_ref, sems) = refs[-15:]
+     raw_ref, wf_ref, wz_ref, xb_ref, core_ref, sst_ref, gz_ref, sems) = refs[-16:]
     first_copies = [
         start_copy(far_xb_ref, xb_ref, sems.at[chips + 2]),
         start_copy(far_sst_ref, sst_ref, sems.at[chips + 3]),
         start_copy(far_core_ref, core_ref, sems.at[chips + 4]),
     ]
     copy_raw = start_copy(far_raw_ref, raw_ref, sems.at[chips])
-    copies = fetch_front(at_ref, pieces, wf_ref, sems)
-    copies.append(fetch_rest(rest_ref, 0, wz_ref, sems.at[chips + 1]))
     count = xb_ref.shape[0]
     chunks = count // CHUNK
     wide = inner + 2 * STATE
@@ -456,6 +454,9 @@
     for copy in first_copies:
         copy.wait()
     copy_raw.wait()
+    copies = fetch_front(at_ref, pieces, wf_ref, sems)
+    copies.append(fetch_rest(rest_ref, 0, wz_ref, sems.at[chips + 1]))
+    copies.append(start_copy(far_gz_ref, gz_ref, sems.at[chips + 5]))
     raw_ref[:HALO, :wide] = jnp.concatenate(
         [jnp.zeros((HALO - 8, wide), F32), tail_ref[...]], axis=0
     ).astype(BF)
@@ -588,12 +589,15 @@
     at_ref = refs.pop(0) if pieces else None
     out_ref = refs.pop()
     near = refs[-len(far) :]
-    outs = refs[len(refs) - len(far) - max(pieces, 1) : len(refs) - len(far)]
+    outs = refs[len(refs) - len(far) - max(2 * pieces, 1) : len(refs) - len(far)]
     leaving = []
     copies = {}
+    sources = {}
     for i, (place_of, target) in enumerate(zip(far, near)):
-        copies[place_of] = start_copy(refs[place_of], target, sems.at[i])
+        sources[place_of] = (refs[place_of], target, sems.at[i])
         refs[place_of] = target
+        if i < 4:
+            copies[place_of] = start_copy(*sources[place_of])
     ready()
     tile = 2 * LANES
     low = 0
@@ -601,8 +605,9 @@
         left_a, right_a, left_b, right_b = refs[4 * term : 4 * term + 4]
         size = right_a.shape[1]
         for place_of in range(4 * term, 4 * term + 4):
-            if place_of in copies:
-                copies[place_of].wait()
+            copies[place_of].wait()
+        for place_of in range(4 * term + 4, min(4 * term + 8, len(far))):
+            copies[place_of] = start_copy(*sources[place_of])
 
         def step_tile(r, carry):
             at = pl.ds(pl.multiple_of(r * tile, tile), tile)
@@ -626,10 +631,15 @@
     for copy in leaving:
         copy.wait()
     if pieces:
-        for j, piece_ref in enumerate(outs):
-            size = piece_ref.shape[0]
+        for j in range(pieces):
+            shared_ref, piece_ref = outs[j], outs[pieces + j]
+            size, wide = piece_ref.shape
             row = pl.multiple_of((at_ref[2] ^ j) * size, size)
-            piece_ref[...] = out_ref[pl.ds(row, size), :]
+            rows = pl.ds(row, size)
+            inner = wide - LANES
+            piece_ref[:, :inner] = out_ref[rows, :inner]
+            piece_ref[:, inner:] = out_ref[rows, inner + 2 * STATE :]
+            shared_ref[...] = out_ref[rows, inner : inner + 2 * STATE]
 
 
 def hold_kernel(*refs, ready):
@@ -656,25 +666,24 @@
             outs[-1][rows, :] = value[:, low:]
 
 
-def split_kernel(*refs, terms, shard, inner, front, ready):
+def split_kernel(*refs, terms, shard, inner, front, shared, ready):
     ready()
     at_ref, refs = refs[0], refs[1:]
     buf_ref = refs[-1]
     buf_ref[...] = tree_sum([ref[...] for ref in refs[:terms]])
     half, core = at_ref[3], at_ref[1]
+    outs = list(refs[-1 - 2 * (front + shared) : -1])
     if front:
-        one_ref, two_ref, keep_ref, away_ref = refs[-5:-1]
-    else:
-        one_ref, two_ref = refs[-3:-1]
-    for out_ref, side in ((one_ref, half), (two_ref, 1 - half)):
-        rows = pl.ds(pl.multiple_of(side * shard, HALO), shard)
-        if front:
-            out_ref[:, :inner] = buf_ref[rows, :inner].astype(BF)
-            out_ref[:, inner:] = buf_ref[rows, inner + 2 * STATE :].astype(BF)
-        else:
-            out_ref[...] = buf_ref[rows, :].astype(BF)
-    if front:
-        lanes = slice(inner, inner + 2 * STATE)
+        for out_ref, side in ((outs.pop(0), half), (outs.pop(0), 1 - half)):
+            rows = pl.ds(pl.multiple_of(side * shard, HALO), shard)
+            if front and shared:
+                out_ref[:, :inner] = buf_ref[rows, :inner].astype(BF)
+                out_ref[:, inner:] = buf_ref[rows, inner + 2 * STATE :].astype(BF)
+            else:
+                out_ref[...] = buf_ref[rows, :].astype(BF)
+    if shared:
+        keep_ref, away_ref = outs
+        lanes = slice(inner, inner + 2 * STATE) if front else slice(0, 2 * STATE)
         rows = pl.ds(pl.multiple_of(core * shard, HALO), shard)
         keep_ref[...] = buf_ref[rows, lanes]
         rows = pl.ds(pl.multiple_of((1 - core) * shard, HALO), shard)
@@ -1207,7 +1216,7 @@
 
         def split_rest(l, after=()):
             messages = queue.run(
-                mixer(split_kernel, terms=1, shard=shard, inner=inner, front=False),
+                mixer(split_kernel, terms=1, shard=shard, inner=inner, front=True, shared=False),
                 [at, g_rest[l]],
                 [((shard, 2 * inner), BF)] * 2,
                 [(g_rest[l].shape, F32)],
@@ -1218,20 +1227,25 @@
             )
             done_rest[l] = owners(messages)
 
-        def split_front(l, values, after=()):
-            one, two, keep, away = queue.run(
-                mixer(split_kernel, terms=len(values), shard=shard, inner=inner, front=True),
-                [at, *values],
-                [((shard, inner + LANES), BF)] * 2
-                + [((shard, 2 * STATE), F32), ((shard, 2 * STATE), BF)],
-                [(values[0].shape, F32)],
-                scalars=1,
-                after=after,
-                limit=14,
-            )
-            done_front[l] = owners([one, two])
+        def share_bc(l, keep, away):
             shared = (keep + send(away, to_core).astype(F32)).astype(BF)
             g_bc[l] = [shared] + [send(shared, route) for route in all_tensor]
+
+        def split_front(l, values, front, shared, after=()):
+            size = inner + LANES
+            outs = [((shard, size), BF)] * 2 if front else []
+            outs += [((shard, 2 * STATE), F32), ((shard, 2 * STATE), BF)] if shared else []
+            outs = queue.run(
+                mixer(
+                    split_kernel, terms=len(values), shard=shard, inner=inner, front=front,
+                    shared=shared,
+                ),
+                [at, *values], outs, [(values[0].shape, F32)], scalars=1, after=after, limit=14,
+            )
+            if front:
+                done_front[l] = owners(outs[:2])
+            if shared:
+                share_bc(l, *outs[-2:])
 
         def offloaded_sum(value):
             return lax.psum_scatter(
@@ -1275,8 +1289,8 @@
             chips = len(front_w[l])
             (graw, sgrad, hgrad, part) = queue.run(
                 mixer(scan_back_kernel, chips=chips, **sizes),
-                [at, *front_w[l], rest_w[l], v["raw"], v["xb"], v["core_out"], v["sst"],
-                 v["gcore"], v["gz"], v["aux"], v["dsout"], v["tail"], marks[s], seg_row[s], links[s],
+                [at, *front_w[l], rest_w[l], v["gz"], v["raw"], v["xb"], v["core_out"], v["sst"],
+                 v["gcore"], v["aux"], v["dsout"], v["tail"], marks[s], seg_row[s], links[s],
                  gate_p[l], conv_w[l], head_p[l], e2, hm],
                 [((rows, wide + LANES), BF), ((8, wide), F32), ((8, LANES), F32),
                  ((rows, width), F32)],
@@ -1284,10 +1298,10 @@
                  ((CHUNK, inner), F32), ((rows, wide + LANES), BF),
                  ((n_dp * shard, wide + LANES), BF), ((n_dp * shard, inner), BF),
                  ((count, wide), BF), ((count, inner), F32), ((chunks + 1, STATE, inner), BF),
-                 ((chips + 5,), None)],
+                 ((rows, inner), BF), ((chips + 6,), None)],
                 scalars=1,
-                far=range(1, chips + 6),
-                staged=[*range(chips + 6, chips + 9), *range(chips + 10, chips + 19)],
+                far=range(1, chips + 7),
+                staged=[chips + 7, chips + 8, *range(chips + 10, chips + 19)],
                 staged_out=(0,),
                 limit=30,
             )
@@ -1322,14 +1336,16 @@
             if halo:
                 operands += [one["edge"], two["edge"]]
             far = range(4 * len(names))
-            count_out = chips if pieces else 1
             scratch = [(operands[i].shape, BF) for i in far] + [((width, size), BF)]
             result = queue.run(
                 mixer(
                     weight_kernel, terms=len(names), tokens=count, halo=halo, far=far, pieces=pieces
                 ),
                 ([at] if pieces else []) + operands,
-                [((width // count_out, size), BF)] * count_out,
+                [((width // chips, 2 * STATE), BF)] * pieces
+                + [((width // chips, inner + LANES), BF)] * pieces
+                if pieces
+                else [((width, size), BF)],
                 scratch + [((len(far) + len(names),), None)],
                 scalars=1 if pieces else 0,
                 far=[i + 1 for i in far] if pieces else far,
@@ -1357,16 +1373,19 @@
             add_cores(l, 0, False)
             ready = sums_of(l, 0) + kept[l][0]["halos"]
             if l < top:
-                split_front(l + 1, [g_front[l + 1]])
+                split_front(l + 1, [g_front[l + 1]], True, True)
                 ready += done_front[l + 1]
             scan_back(l, 1, ready)
             own_back(l, 0)
             add_cores(l, 1, False)
             if l == 0:
-                direct = direct_start(weights_back(l, front_names, chips))
+                values = weights_back(l, front_names, chips)
+                direct_bc = direct_start(values[:chips])
+                direct = direct_start(values[chips:])
                 split_rest(l)
                 own_back(l, 1, [v for k in range(1, LAYERS) for v in g_bc[k]])
-                split_front(l, direct, done_rest[0])
+                split_front(l, direct_bc, False, True)
+                split_front(l, direct, True, False, done_rest[0])
             else:
                 waiting = sums_of(l, 1) + kept[l][1]["halos"] + arrived[0]
                 g_front[l] = offloaded_sum(weights_back(l, front_names, 0, waiting))

time: 685 us -> 680 us (level); the launches traced: 673 us -> 675 us
  waiting for transfers between devices: 136 us -> 124 us
  starting transfers between devices: 161 us -> 170 us
  Pallas kernels: 304 us -> 311 us
    ppermute x82 -> x85, waiting for transfers between devices: 120 us -> 104 us  [send(): return lax.ppermute(value, axes, pairs(route))]
    ppermute x22, waiting for transfers between devices: 8.69 us -> 19.2 us  [back(): return lax.ppermute(value, axes, [(b, a) for a, b in pairs(route)])]
    ppermute x82 -> x85, starting transfers between devices: 116 us -> 124 us  [send(): return lax.ppermute(value, axes, pairs(route))]
    pallas_call x68 -> x69, Pallas kernels: 304 us -> 311 us  [run(): pl.pallas_call(wrapped, in_specs=specs + [free] * len(extra), out_specs=[...]
    unnamed x205 -> x196, local copies, waits for them, and re-layouts: 20.1 us -> 19.3 us
  transfers between devices with their start and end apart: 111 -> 114, of which waited for: 29 -> 29; matrix products, arithmetic and copies ran while one was open for 5% -> 5% of each run, Pallas kernels for 43% -> 44%
where the time goes in v4:
time: 680 us; the launch traced here: 675 us
  Pallas kernels  311 us (46%)
  starting transfers between devices  170 us (25%)
  waiting for transfers between devices  124 us (18%)
  local copies, waits for them, and re-layouts  46.5 us (7%)
  between operations  17.1 us (3%)
    pallas_call x69, Pallas kernels, run(): pl.pallas_call(wrapped, in_specs=specs + [free] * len(extra), out_specs=[...  311 us
    ppermute x85, starting transfers between devices, send(): return lax.ppermute(value, axes, pairs(route))  124 us
    ppermute x85, waiting for transfers between devices, send(): return lax.ppermute(value, axes, pairs(route))  104 us
    ppermute x22, starting transfers between devices, back(): return lax.ppermute(value, axes, [(b, a) for a, b in pairs(route)])  45.5 us
    unnamed x196, local copies, waits for them, and re-layouts  19.3 us
    ppermute x22, waiting for transfers between devices, back(): return lax.ppermute(value, axes, [(b, a) for a, b in pairs(route)])  19.2 us
  transfers between devices with their start and end apart: 114, of which 29 were waited for; matrix products, arithmetic and copies ran while one was open for 5% of the time, Pallas kernels for 44%

profile of v4, /device:TPU:1, one launch (start us, length us, event | category | flops | bytes accessed | tf_op | source)
XLA Modules:
  0.0 675.0 jit_solution(12077706476829668488)
XLA Ops:
  28.7 9.3 %collective-permute-start.9 = (bf16[192,1536]{1,0:T(8,128)(2,1)S(1)}, bf16[192,1536]{1,0:T(8,128)(2,1)S(1)}, u32[]{:S(2)}, u32[]{:S(2)}) collective-permute-start(bf16[192,1536]{1,0:T(8,128)(2,1)S(1)} %shard_map.309.refs_7_), channel_id=1, source_target_pairs={{0,0},{1,4},{2,1},{3,5},{4,2},{5,6},{6,3},{7,7},{8,8},{9,12},{10,9... | collective-permute-start | bytes 1769480 | tf_op jit(solution)/shard_map/ppermute | solution.py:884
  41.1 18.6 %collective-permute-done.11.refs_6_.refs_2_ = bf16[128,1536]{1,0:T(8,128)(2,1)S(1)} collective-permute-done((bf16[128,1536]{1,0:T(8,128)(2,1)S(1)}, bf16[128,1536]{1,0:T(8,128)(2,1)S(1)}, u32[]{:S(2)}, u32[]{:S(2)}) %collective-permute-start.11) | collective-permute-done | bytes 393248 | tf_op jit(solution)/shard_map/ppermute | solution.py:884
  59.6 7.1 %collective-permute-done.1.refs_4_.refs_2_ = bf16[128,1536]{1,0:T(8,128)(2,1)S(1)} collective-permute-done((bf16[128,1536]{1,0:T(8,128)(2,1)S(1)}, bf16[128,1536]{1,0:T(8,128)(2,1)S(1)}, u32[]{:S(2)}, u32[]{:S(2)}) %collective-permute-start.1) | collective-permute-done | bytes 393248 | tf_op jit(solution)/shard_map/ppermute | solution.py:884
  104.6 11.3 %shard_map.313 = (bf16[528,1536]{1,0:T(8,128)(2,1)}, bf16[528,1152]{1,0:T(8,128)(2,1)}, f32[16,1024]{1,0:T(8,128)}, bf16[512,1024]{1,0:T(8,128)(2,1)}, f32[512,2...) custom-call(s32[4]{0:T(128)S(1)} %pad_add_fusion.refs_0_, ...), custom_call_target="tpu_custom_call" | custom-call | flops 1000 | bytes 1000 | tf_op jit(solution)/shard_map/pallas_call | solution.py:826
  124.0 11.5 %shard_map.315 = (bf16[528,1536]{1,0:T(8,128)(2,1)}, bf16[528,1152]{1,0:T(8,128)(2,1)}, f32[16,1024]{1,0:T(8,128)}, bf16[512,1024]{1,0:T(8,128)(2,1)}, f32[512,2...) custom-call(s32[4]{0:T(128)S(1)} %pad_add_fusion.refs_0_, ...), custom_call_target="tpu_custom_call" | custom-call | flops 1000 | bytes 1000 | tf_op jit(solution)/shard_map/pallas_call | solution.py:826
  139.3 13.1 %collective-permute-start.19 = (bf16[128,768]{1,0:T(8,128)(2,1)S(1)}, bf16[128,768]{1,0:T(8,128)(2,1)S(1)}, u32[]{:S(2)}, u32[]{:S(2)}) collective-permute-start(bf16[128,768]{1,0:T(8,128)(2,1)S(1)} %get-tuple-element.226.refs_5_.refs_6_), channel_id=1, source_target_pairs={{0,2},{1,3},{4,6},{5,7},{8,10},{9,11},{12,14},{13,15},{16,18},{17,... | collective-permute-start | bytes 589832 | tf_op jit(solution)/shard_map/ppermute | solution.py:884
  156.2 11.4 %shard_map.318 = (bf16[512,1024]{1,0:T(8,128)(2,1)}, bf16[512,768]{1,0:T(8,128)(2,1)}, f32[512,768]{1,0:T(8,128)}, bf16[512,768]{1,0:T(8,128)(2,1)}, bf16[3,128,...) custom-call(s32[4]{0:T(128)S(1)} %pad_add_fusion.refs_0_, bf16[528,1536]{1,0:T(8,128)(2,1)} %get-tuple-element.212.refs_1_.refs_0_, ...), custom_call_target="tpu_custom_call" | custom-call | flops 1000 | bytes 1000 | tf_op jit(solution)/shard_map/pallas_call | solution.py:826
  171.7 10.1 %collective-permute-start.23 = (bf16[128,1664]{1,0:T(8,128)(2,1)S(1)}, bf16[128,1664]{1,0:T(8,128)(2,1)S(1)}, u32[]{:S(2)}, u32[]{:S(2)}) collective-permute-start(bf16[128,1664]{1,0:T(8,128)(2,1)S(1)} %get-tuple-element.232.refs_17_), channel_id=1, source_target_pairs={{0,1},{1,0},{2,3},{3,2},{4,5},{5,4},{6,7},{7,6},{8,9},{9,8},{10,11... | collective-permute-start | bytes 1277960 | tf_op jit(solution)/shard_map/ppermute | solution.py:884
  182.4 11.0 %shard_map.321 = (bf16[512,1024]{1,0:T(8,128)(2,1)}, bf16[512,768]{1,0:T(8,128)(2,1)}, f32[512,768]{1,0:T(8,128)}, bf16[512,768]{1,0:T(8,128)(2,1)}, bf16[3,128,...) custom-call(s32[4]{0:T(128)S(1)} %pad_add_fusion.refs_0_, bf16[528,1536]{1,0:T(8,128)(2,1)} %get-tuple-element.234.refs_1_.refs_2_.refs_3_, ...), custom_call_target="tpu_custom_call" | custom-call | flops 1000 | bytes 1000 | tf_op jit(solution)/shard_map/pallas_call | solution.py:826
  201.0 7.7 %collective-permute-done.24.refs_2_ = bf16[128,1536]{1,0:T(8,128)(2,1)S(1)} collective-permute-done((bf16[128,1536]{1,0:T(8,128)(2,1)S(1)}, bf16[128,1536]{1,0:T(8,128)(2,1)S(1)}, u32[]{:S(2)}, u32[]{:S(2)}) %collective-permute-start.24) | collective-permute-done | bytes 393248 | tf_op jit(solution)/shard_map/ppermute | solution.py:884
  211.3 23.3 %shard_map.325 = (bf16[528,1536]{1,0:T(8,128)(2,1)}, bf16[528,1152]{1,0:T(8,128)(2,1)}, f32[16,1024]{1,0:T(8,128)}, bf16[512,1024]{1,0:T(8,128)(2,1)}, f32[512,2...) custom-call(s32[4]{0:T(128)S(1)} %pad_add_fusion.refs_0_, ...), custom_call_target="tpu_custom_call" | custom-call | flops 1000 | bytes 1000 | tf_op jit(solution)/shard_map/pallas_call | solution.py:826
  238.2 9.6 %collective-permute-done.32.refs_2_ = bf16[128,1536]{1,0:T(8,128)(2,1)S(1)} collective-permute-done((bf16[128,1536]{1,0:T(8,128)(2,1)S(1)}, bf16[128,1536]{1,0:T(8,128)(2,1)S(1)}, u32[]{:S(2)}, u32[]{:S(2)}) %collective-permute-start.32) | collective-permute-done | bytes 393248 | tf_op jit(solution)/shard_map/ppermute | solution.py:884
  252.9 10.9 %shard_map.328 = (bf16[528,1536]{1,0:T(8,128)(2,1)}, bf16[528,1152]{1,0:T(8,128)(2,1)}, f32[16,1024]{1,0:T(8,128)}, bf16[512,1024]{1,0:T(8,128)(2,1)}, f32[512,2...) custom-call(s32[4]{0:T(128)S(1)} %pad_add_fusion.refs_0_, ...), custom_call_target="tpu_custom_call" | custom-call | flops 1000 | bytes 1000 | tf_op jit(solution)/shard_map/pallas_call | solution.py:826
  267.8 10.7 %shard_map.330 = (bf16[512,1024]{1,0:T(8,128)(2,1)}, bf16[512,768]{1,0:T(8,128)(2,1)}, f32[512,768]{1,0:T(8,128)}, bf16[512,768]{1,0:T(8,128)(2,1)}, bf16[3,128,...) custom-call(s32[4]{0:T(128)S(1)} %pad_add_fusion.refs_0_, bf16[528,1536]{1,0:T(8,128)(2,1)} %get-tuple-element.243.refs_1_.refs_0_, ...), custom_call_target="tpu_custom_call" | custom-call | flops 1000 | bytes 1000 | tf_op jit(solution)/shard_map/pallas_call | solution.py:826
  285.7 10.7 %shard_map.333 = (bf16[512,1024]{1,0:T(8,128)(2,1)}, bf16[512,768]{1,0:T(8,128)(2,1)}, f32[512,768]{1,0:T(8,128)}, bf16[512,768]{1,0:T(8,128)(2,1)}, bf16[3,128,...) custom-call(s32[4]{0:T(128)S(1)} %pad_add_fusion.refs_0_, bf16[528,1536]{1,0:T(8,128)(2,1)} %get-tuple-element.267.refs_1_.refs_2_, ...), custom_call_target="tpu_custom_call" | custom-call | flops 1000 | bytes 1000 | tf_op jit(solution)/shard_map/pallas_call | solution.py:826
  305.2 8.5 %collective-permute-done.44.refs_2_ = bf16[128,1664]{1,0:T(8,128)(2,1)S(1)} collective-permute-done((bf16[128,1664]{1,0:T(8,128)(2,1)S(1)}, bf16[128,1664]{1,0:T(8,128)(2,1)S(1)}, u32[]{:S(2)}, u32[]{:S(2)}) %collective-permute-start.44) | collective-permute-done | bytes 426016 | tf_op jit(solution)/shard_map/ppermute | solution.py:884
  314.9 7.9 %collective-permute-done.42.refs_1_ = bf16[128,1664]{1,0:T(8,128)(2,1)S(1)} collective-permute-done((bf16[128,1664]{1,0:T(8,128)(2,1)S(1)}, bf16[128,1664]{1,0:T(8,128)(2,1)S(1)}, u32[]{:S(2)}, u32[]{:S(2)}) %collective-permute-start.42) | collective-permute-done | bytes 426016 | tf_op jit(solution)/shard_map/ppermute | solution.py:884
  327.8 7.5 %shard_map.338 = (bf16[512,1536]{1,0:T(8,128)(2,1)}, bf16[512,768]{1,0:T(8,128)(2,1)}, bf16[528,768]{1,0:T(8,128)(2,1)}, f32[8,768]{1,0:T(8,128)S(1)}, bf16[128,768]{1,0:T(8,128)(2,1)S(1)}) custom-call(s32[4]{0:T(128)S(1)} %pad_add_fusion.refs_0_, bf16[128,1664]{1,0:T(8,128)(2,1)S(1)} %get-tuple-element.274.refs_3_.refs_1_, ...), custom_call_target="tpu_custom_call" | custom-call | flops 1000 | bytes 1000 | tf_op jit(solution)/shard_map/pallas_call | solution.py:826
  339.9 7.5 %shard_map.340 = (bf16[512,1536]{1,0:T(8,128)(2,1)}, bf16[512,768]{1,0:T(8,128)(2,1)}, bf16[528,768]{1,0:T(8,128)(2,1)}, f32[8,768]{1,0:T(8,128)S(1)}, bf16[128,768]{1,0:T(8,128)(2,1)S(1)}) custom-call(s32[4]{0:T(128)S(1)} %pad_add_fusion.refs_0_, bf16[128,1664]{1,0:T(8,128)(2,1)S(1)} %get-tuple-element.282.refs_14_.refs_1_, ...), custom_call_target="tpu_custom_call" | custom-call | flops 1000 | bytes 1000 | tf_op jit(solution)/shard_map/pallas_call | solution.py:826
  351.8 11.3 %shard_map.342.refs_0_ = bf16[1536,1536]{1,0:T(8,128)(2,1)} custom-call(bf16[528,1536]{1,0:T(8,128)(2,1)} %get-tuple-element.243.refs_1_.refs_0_, bf16[528,768]{1,0:T(8,128)(2,1)} %get-tuple-element.283.refs_1_.refs_3_, bf16[528,1536]{1,0:T(8,128)(2,1)} %get-tuple-element.267.refs_1_.refs_2_, bf16[528,768]{1,0:T(8,128)(2,1)} %get-tuple-element.293.refs_3_, ...), custom_call_target="tpu_custom_call" | custom-call | flops 1000 | bytes 1000 | tf_op jit(solution)/shard_map/pallas_call | solution.py:826
  366.8 20.2 %shard_map.344 = (bf16[528,1152]{1,0:T(8,128)(2,1)}, f32[8,1024]{1,0:T(8,128)S(1)}, f32[8,128]{1,0:T(8,128)S(1)}, f32[528,1536]{1,0:T(8,128)S(1)}) custom-call(s32[4]{0:T(128)S(1)} %pad_add_fusion.refs_0_, bf16[1536,1152]{1,0:T(8,128)(2,1)} %all-gather.9.cloned.1.call-done.refs_5_.refs_1_, ...), custom_call_target="tpu_custom_call" | custom-call | flops 1000 | bytes 1000 | tf_op jit(solution)/shard_map/pallas_call | solution.py:826
  392.6 19.5 %shard_map.347 = (bf16[528,1152]{1,0:T(8,128)(2,1)}, f32[8,1024]{1,0:T(8,128)S(1)}, f32[8,128]{1,0:T(8,128)S(1)}, f32[528,1536]{1,0:T(8,128)S(1)}) custom-call(s32[4]{0:T(128)S(1)} %pad_add_fusion.refs_0_, bf16[1536,1152]{1,0:T(8,128)(2,1)} %all-gather.9.cloned.1.call-done.refs_5_.refs_1_, ...), custom_call_target="tpu_custom_call" | custom-call | flops 1000 | bytes 1000 | tf_op jit(solution)/shard_map/pallas_call | solution.py:826
  421.9 10.7 %shard_map.351.refs_0_ = bf16[1536,1152]{1,0:T(8,128)(2,1)} custom-call(bf16[528,1536]{1,0:T(8,128)(2,1)} %get-tuple-element.243.refs_1_.refs_0_, bf16[528,1152]{1,0:T(8,128)(2,1)} %get-tuple-element.318.refs_1_, bf16[528,1536]{1,0:T(8,128)(2,1)} %get-tuple-element.267.refs_1_.refs_2_, bf16[528,1152]{1,0:T(8,128)(2,1)} %get-tuple-element.319.refs_3_, ...), custom_call_target="tpu_custom_call" | custom-call | flops 1000 | bytes 1000 | tf_op jit(solution)/shard_map/pallas_call | solution.py:826
  452.7 8.3 %shard_map.355 = (bf16[512,1536]{1,0:T(8,128)(2,1)}, bf16[512,768]{1,0:T(8,128)(2,1)}, bf16[528,768]{1,0:T(8,128)(2,1)}, f32[8,768]{1,0:T(8,128)S(1)}, bf16[128,768]{1,0:T(8,128)(2,1)S(1)}) custom-call(s32[4]{0:T(128)S(1)} %pad_add_fusion.refs_0_, bf16[128,1664]{1,0:T(8,128)(2,1)S(1)} %copy-done.8, bf16[128,1664]{1,0:T(8,128)(2,1)S(1)} %copy-done.12, ...), custom_call_target="tpu_custom_call" | custom-call | flops 1000 | bytes 1000 | tf_op jit(solution)/shard_map/pallas_call | solution.py:826
  464.8 7.6 %shard_map.357 = (bf16[512,1536]{1,0:T(8,128)(2,1)}, bf16[512,768]{1,0:T(8,128)(2,1)}, bf16[528,768]{1,0:T(8,128)(2,1)}, f32[8,768]{1,0:T(8,128)S(1)}, bf16[128,768]{1,0:T(8,128)(2,1)S(1)}) custom-call(s32[4]{0:T(128)S(1)} %pad_add_fusion.refs_0_, bf16[128,1664]{1,0:T(8,128)(2,1)S(1)} %get-tuple-element.321.refs_14_.refs_1_, ...), custom_call_target="tpu_custom_call" | custom-call | flops 1000 | bytes 1000 | tf_op jit(solution)/shard_map/pallas_call | solution.py:826
  476.2 11.2 %shard_map.359.refs_0_ = bf16[1536,1536]{1,0:T(8,128)(2,1)} custom-call(bf16[528,1536]{1,0:T(8,128)(2,1)} %get-tuple-element.212.refs_1_.refs_0_, bf16[528,768]{1,0:T(8,128)(2,1)} %get-tuple-element.322.refs_1_.refs_3_, bf16[528,1536]{1,0:T(8,128)(2,1)} %get-tuple-element.234.refs_1_.refs_2_.refs_3_, bf16[528,768]{1,0:T(8,128)(2,1)} %get-tuple-element.332.refs_3_, ...), custom_call_target="tpu_custom_call" | custom-call | flops 1000 | bytes 1000 | tf_op jit(solution)/shard_map/pallas_call | solution.py:826
  492.9 19.4 %shard_map.361 = (bf16[528,1152]{1,0:T(8,128)(2,1)}, f32[8,1024]{1,0:T(8,128)S(1)}, f32[8,128]{1,0:T(8,128)S(1)}, f32[528,1536]{1,0:T(8,128)S(1)}) custom-call(s32[4]{0:T(128)S(1)} %pad_add_fusion.refs_0_, bf16[1536,1152]{1,0:T(8,128)(2,1)} %all-gather.5.cloned.1.call-done.refs_5_.refs_1_, ...), custom_call_target="tpu_custom_call" | custom-call | flops 1000 | bytes 1000 | tf_op jit(solution)/shard_map/pallas_call | solution.py:826
  528.2 19.4 %shard_map.365 = (bf16[528,1152]{1,0:T(8,128)(2,1)}, f32[8,1024]{1,0:T(8,128)S(1)}, f32[8,128]{1,0:T(8,128)S(1)}, f32[528,1536]{1,0:T(8,128)S(1)}) custom-call(s32[4]{0:T(128)S(1)} %pad_add_fusion.refs_0_, bf16[1536,1152]{1,0:T(8,128)(2,1)} %all-gather.5.cloned.1.call-done.refs_5_.refs_1_, ...), custom_call_target="tpu_custom_call" | custom-call | flops 1000 | bytes 1000 | tf_op jit(solution)/shard_map/pallas_call | solution.py:826
  554.8 10.9 %shard_map.369 = (bf16[384,256]{1,0:T(8,128)(2,1)S(1)}, bf16[384,256]{1,0:T(8,128)(2,1)S(1)}, bf16[384,256]{1,0:T(8,128)(2,1)}, bf16[384,256]{1,0:T(8,128)(2,1)}...) custom-call(s32[4]{0:T(128)S(1)} %pad_add_fusion.refs_0_, ...), custom_call_target="tpu_custom_call" | custom-call | flops 1000 | bytes 1000 | tf_op jit(solution)/shard_map/pallas_call | solution.py:826
  587.0 8.5 %collective-permute-start.85 = (bf16[192,1536]{1,0:T(8,128)(2,1)S(1)}, bf16[192,1536]{1,0:T(8,128)(2,1)S(1)}, u32[]{:S(2)}, u32[]{:S(2)}) collective-permute-start(bf16[192,1536]{1,0:T(8,128)(2,1)S(1)} %get-tuple-element.363), channel_id=1, source_target_pairs={{0,0},{4,1},{1,2},{5,3},{2,4},{6,5},{3,6},{7,7},{8,8},{12,9},{9,10... | collective-permute-start | bytes 1769480 | tf_op jit(solution)/shard_map/ppermute | solution.py:887
  605.5 10.9 %collective-permute-done.88.refs_3_ = bf16[384,896]{1,0:T(8,128)(2,1)} collective-permute-done((bf16[384,896]{1,0:T(8,128)(2,1)}, bf16[384,896]{1,0:T(8,128)(2,1)}, u32[]{:S(2)}, u32[]{:S(2)}) %collective-permute-start.88) | collective-permute-done | bytes 688160 | tf_op jit(solution)/shard_map/ppermute | solution.py:884
  654.6 9.9 %collective-permute-done.93.refs_2_ = bf16[192,896]{1,0:T(8,128)(2,1)S(1)} collective-permute-done((bf16[192,896]{1,0:T(8,128)(2,1)S(1)}, bf16[192,896]{1,0:T(8,128)(2,1)S(1)}, u32[]{:S(2)}, u32[]{:S(2)}) %collective-permute-start.93) | collective-permute-done | bytes 344096 | tf_op jit(solution)/shard_map/ppermute | solution.py:887
  (557 shorter events, 282.6 us)
Async XLA Ops:
  7.2 95.8 %all-gather.5.cloned.1.call-start = ((), (), s32[]{:S(2)}) async-start(), calls=%async_computation.3 | async-start | bytes 4423680 | tf_op jit(solution)/shard_map/all_gather | solution.py:970
  26.4 129.2 %all-gather.7.cloned.1.call-start = ((), (), s32[]{:S(2)}) async-start(), calls=%async_computation.4 | async-start | bytes 5898240 | tf_op jit(solution)/shard_map/all_gather | solution.py:970
  27.8 38.9 %collective-permute-start.10 = (bf16[192,1536]{1,0:T(8,128)(2,1)S(1)}, bf16[192,1536]{1,0:T(8,128)(2,1)S(1)}, u32[]{:S(2)}, u32[]{:S(2)}) collective-permute-start(bf16[192,1536]{1,0:T(8,128)(2,1)S(1)} %shard_map.309.refs_7_), channel_id=1, source_target_pairs={{0,2},{1,6},{2,3},{3,7},{4,0},{5,4},{6,1},{7,5},{8,10},{9,14},{10,... | collective-permute-start | bytes 1769480 | tf_op jit(solution)/shard_map/ppermute | solution.py:884
  28.7 38.0 %collective-permute-start.9 = (bf16[192,1536]{1,0:T(8,128)(2,1)S(1)}, bf16[192,1536]{1,0:T(8,128)(2,1)S(1)}, u32[]{:S(2)}, u32[]{:S(2)}) collective-permute-start(bf16[192,1536]{1,0:T(8,128)(2,1)S(1)} %shard_map.309.refs_7_), channel_id=1, source_target_pairs={{0,0},{1,4},{2,1},{3,5},{4,2},{5,6},{6,3},{7,7},{8,8},{9,12},{10,9... | collective-permute-start | bytes 1769480 | tf_op jit(solution)/shard_map/ppermute | solution.py:884
  41.0 25.7 %collective-permute-start.1 = (bf16[128,1536]{1,0:T(8,128)(2,1)S(1)}, bf16[128,1536]{1,0:T(8,128)(2,1)S(1)}, u32[]{:S(2)}, u32[]{:S(2)}) collective-permute-start(bf16[128,1536]{1,0:T(8,128)(2,1)S(1)} %get-tuple-element.210.refs_2_.refs_3_.refs_1_), channel_id=1, source_target_pairs={{0,1},{1,0},{2,3},{3,2},{4,5},{5,4},{6,7},{7,6},{8,9},{9,8},{10,11... | collective-permute-start | bytes 1179656 | tf_op jit(solution)/shard_map/ppermute | solution.py:884
  69.9 141.4 %all-gather.9.cloned.1.call-start = ((), (), s32[]{:S(2)}) async-start(), calls=%async_computation.5 | async-start | bytes 4423680 | tf_op jit(solution)/shard_map/all_gather | solution.py:970
  92.8 42.8 %collective-permute-start.15 = (bf16[192,2432]{1,0:T(8,128)(2,1)S(1)}, bf16[192,2432]{1,0:T(8,128)(2,1)}, u32[]{:S(2)}, u32[]{:S(2)}) collective-permute-start(bf16[192,2432]{1,0:T(8,128)(2,1)S(1)} %shard_map.312.refs_11_), channel_id=1, source_target_pairs={{0,0},{1,4},{2,1},{3,5},{4,2},{5,6},{6,3},{7,7},{8,8},{9,12},{10,9... | collective-permute-start | bytes 2801672 | tf_op jit(solution)/shard_map/ppermute | solution.py:884
  97.2 38.4 %collective-permute-start.16 = (bf16[192,2432]{1,0:T(8,128)(2,1)S(1)}, bf16[192,2432]{1,0:T(8,128)(2,1)}, u32[]{:S(2)}, u32[]{:S(2)}) collective-permute-start(bf16[192,2432]{1,0:T(8,128)(2,1)S(1)} %shard_map.312.refs_11_), channel_id=1, source_target_pairs={{0,2},{1,6},{2,3},{3,7},{4,0},{5,4},{6,1},{7,5},{8,10},{9,14},{10,... | collective-permute-start | bytes 2801672 | tf_op jit(solution)/shard_map/ppermute | solution.py:884
  99.9 21.8 %collective-permute-start.18 = (bf16[128,1536]{1,0:T(8,128)(2,1)S(1)}, bf16[128,1536]{1,0:T(8,128)(2,1)}, u32[]{:S(2)}, u32[]{:S(2)}) collective-permute-start(bf16[128,1536]{1,0:T(8,128)(2,1)S(1)} %copy-done.18), channel_id=1, source_target_pairs={{0,4},{1,5},{2,6},{3,7},{4,0},{5,1},{6,2},{7,3},{8,12},{9,13},{10,... | collective-permute-start | bytes 1179656 | tf_op jit(solution)/shard_map/ppermute | solution.py:884
  138.6 129.2 %all-gather.11.cloned.1.call-start = ((), (), s32[]{:S(2)}) async-start(), calls=%async_computation.6 | async-start | bytes 5898240 | tf_op jit(solution)/shard_map/all_gather | solution.py:970
  139.2 300.0 %reduce-scatter.4.cloned.1.call-start = ((), (), s32[]{:S(2)}) async-start(), calls=%async_computation.7 | async-start | bytes 5898240 | tf_op jit(solution)/shard_map/reduce_scatter | solution.py:1251
  139.3 28.4 %collective-permute-start.19 = (bf16[128,768]{1,0:T(8,128)(2,1)S(1)}, bf16[128,768]{1,0:T(8,128)(2,1)S(1)}, u32[]{:S(2)}, u32[]{:S(2)}) collective-permute-start(bf16[128,768]{1,0:T(8,128)(2,1)S(1)} %get-tuple-element.226.refs_5_.refs_6_), channel_id=1, source_target_pairs={{0,2},{1,3},{4,6},{5,7},{8,10},{9,11},{12,14},{13,15},{16,18},{17,... | collective-permute-start | bytes 589832 | tf_op jit(solution)/shard_map/ppermute | solution.py:884
  199.1 35.5 %collective-permute-start.28 = (bf16[128,1664]{1,0:T(8,128)(2,1)S(1)}, bf16[128,1664]{1,0:T(8,128)(2,1)S(1)}, u32[]{:S(2)}, u32[]{:S(2)}) collective-permute-start(bf16[128,1664]{1,0:T(8,128)(2,1)S(1)} %get-tuple-element.242.refs_11_), channel_id=1, source_target_pairs={{0,1},{1,0},{2,3},{3,2},{4,5},{5,4},{6,7},{7,6},{8,9},{9,8},{10,11... | collective-permute-start | bytes 1277960 | tf_op jit(solution)/shard_map/ppermute | solution.py:884
  304.6 23.2 %collective-permute-start.45 = (bf16[128,1664]{1,0:T(8,128)(2,1)S(1)}, bf16[128,1664]{1,0:T(8,128)(2,1)S(1)}, u32[]{:S(2)}, u32[]{:S(2)}) collective-permute-start(bf16[128,1664]{1,0:T(8,128)(2,1)S(1)} %get-tuple-element.274.refs_3_.refs_1_), channel_id=1, source_target_pairs={{0,4},{1,5},{2,6},{3,7},{4,0},{5,1},{6,2},{7,3},{8,12},{9,13},{10,... | collective-permute-start | bytes 1277960 | tf_op jit(solution)/shard_map/ppermute | solution.py:884
  363.1 154.0 %reduce-scatter.6.cloned.1.call-start = ((), (), s32[]{:S(2)}) async-start(), calls=%async_computation.8 | async-start | bytes 4423680 | tf_op jit(solution)/shard_map/reduce_scatter | solution.py:1251
  363.1 23.8 %collective-permute-start.51 = (bf16[128,768]{1,0:T(8,128)(2,1)S(1)}, bf16[128,768]{1,0:T(8,128)(2,1)S(1)}, u32[]{:S(2)}, u32[]{:S(2)}) collective-permute-start(bf16[128,768]{1,0:T(8,128)(2,1)S(1)} %shard_map.341.refs_8_), channel_id=1, source_target_pairs={{2,0},{3,1},{6,4},{7,5},{10,8},{11,9},{14,12},{15,13},{18,16},{19,... | collective-permute-start | bytes 589832 | tf_op jit(solution)/shard_map/ppermute | solution.py:887
  438.0 145.3 %reduce-scatter.8.cloned.1.call-start = ((), (), s32[]{:S(2)}) async-start(), calls=%async_computation.9 | async-start | bytes 5898240 | tf_op jit(solution)/shard_map/reduce_scatter | solution.py:1251
  450.3 37.1 %collective-permute-start.67 = (bf16[192,1536]{1,0:T(8,128)(2,1)S(1)}, bf16[192,1536]{1,0:T(8,128)(2,1)S(1)}, u32[]{:S(2)}, u32[]{:S(2)}) collective-permute-start(bf16[192,1536]{1,0:T(8,128)(2,1)S(1)} %get-tuple-element.338), channel_id=1, source_target_pairs={{0,0},{4,1},{1,2},{5,3},{2,4},{6,5},{3,6},{7,7},{8,8},{12,9},{9,10... | collective-permute-start | bytes 1769480 | tf_op jit(solution)/shard_map/ppermute | solution.py:887
  489.3 23.0 %collective-permute-start.69 = (bf16[192,1536]{1,0:T(8,128)(2,1)S(1)}, bf16[192,1536]{1,0:T(8,128)(2,1)S(1)}, u32[]{:S(2)}, u32[]{:S(2)}) collective-permute-start(bf16[192,1536]{1,0:T(8,128)(2,1)S(1)} %copy-done.30), channel_id=1, source_target_pairs={{2,0},{6,1},{3,2},{7,3},{0,4},{4,5},{1,6},{5,7},{10,8},{14,9},{11,... | collective-permute-start | bytes 1769480 | tf_op jit(solution)/shard_map/ppermute | solution.py:887
  489.3 23.1 %collective-permute-start.68 = (bf16[128,768]{1,0:T(8,128)(2,1)S(1)}, bf16[128,768]{1,0:T(8,128)(2,1)S(1)}, u32[]{:S(2)}, u32[]{:S(2)}) collective-permute-start(bf16[128,768]{1,0:T(8,128)(2,1)S(1)} %shard_map.358.refs_8_), channel_id=1, source_target_pairs={{2,0},{3,1},{6,4},{7,5},{10,8},{11,9},{14,12},{15,13},{18,16},{19,... | collective-permute-start | bytes 589832 | tf_op jit(solution)/shard_map/ppermute | solution.py:887
  517.0 30.8 %collective-permute-start.71 = (bf16[128,1536]{1,0:T(8,128)(2,1)S(1)}, bf16[128,1536]{1,0:T(8,128)(2,1)S(1)}, u32[]{:S(2)}, u32[]{:S(2)}) collective-permute-start(bf16[128,1536]{1,0:T(8,128)(2,1)S(1)} %get-tuple-element.341), channel_id=1, source_target_pairs={{0,1},{1,0},{2,3},{3,2},{4,5},{5,4},{6,7},{7,6},{8,9},{9,8},{10,11... | collective-permute-start | bytes 1179656 | tf_op jit(solution)/shard_map/ppermute | solution.py:884
  519.0 28.7 %collective-permute-start.74 = (bf16[192,896]{1,0:T(8,128)(2,1)S(1)}, bf16[192,896]{1,0:T(8,128)(2,1)S(1)}, u32[]{:S(2)}, u32[]{:S(2)}) collective-permute-start(bf16[192,896]{1,0:T(8,128)(2,1)S(1)} %get-tuple-element.349), channel_id=1, source_target_pairs={{0,0},{4,1},{1,2},{5,3},{2,4},{6,5},{3,6},{7,7},{8,8},{12,9},{9,10... | collective-permute-start | bytes 1032200 | tf_op jit(solution)/shard_map/ppermute | solution.py:887
  522.9 24.8 %collective-permute-start.75 = (bf16[192,896]{1,0:T(8,128)(2,1)S(1)}, bf16[192,896]{1,0:T(8,128)(2,1)S(1)}, u32[]{:S(2)}, u32[]{:S(2)}) collective-permute-start(bf16[192,896]{1,0:T(8,128)(2,1)S(1)} %get-tuple-element.350), channel_id=1, source_target_pairs={{2,0},{6,1},{3,2},{7,3},{0,4},{4,5},{1,6},{5,7},{10,8},{14,9},{11,... | collective-permute-start | bytes 1032200 | tf_op jit(solution)/shard_map/ppermute | solution.py:887
  553.1 42.3 %collective-permute-start.77 = (bf16[128,1536]{1,0:T(8,128)(2,1)}, bf16[128,1536]{1,0:T(8,128)(2,1)}, u32[]{:S(2)}, u32[]{:S(2)}) collective-permute-start(bf16[128,1536]{1,0:T(8,128)(2,1)} %get-tuple-element.354), channel_id=1, source_target_pairs={{0,1},{1,0},{2,3},{3,2},{4,5},{5,4},{6,7},{7,6},{8,9},{9,8},{10,11... | collective-permute-start | bytes 1179656 | tf_op jit(solution)/shard_map/ppermute | solution.py:884
  581.4 24.0 %collective-permute-start.87 = (bf16[384,896]{1,0:T(8,128)(2,1)}, bf16[384,896]{1,0:T(8,128)(2,1)}, u32[]{:S(2)}, u32[]{:S(2)}) collective-permute-start(bf16[384,896]{1,0:T(8,128)(2,1)} %get-tuple-element.365), channel_id=1, source_target_pairs={{0,8},{1,9},{2,10},{3,11},{4,12},{5,13},{6,14},{7,15},{8,0},{9,1},... | collective-permute-start | bytes 2064392 | tf_op jit(solution)/shard_map/ppermute | solution.py:884
  582.2 34.2 %collective-permute-start.88 = (bf16[384,896]{1,0:T(8,128)(2,1)}, bf16[384,896]{1,0:T(8,128)(2,1)}, u32[]{:S(2)}, u32[]{:S(2)}) collective-permute-start(bf16[384,896]{1,0:T(8,128)(2,1)} %get-tuple-element.366), channel_id=1, source_target_pairs={{0,16},{1,17},{2,18},{3,19},{4,20},{5,21},{6,22},{7,23},{8,24},{9,... | collective-permute-start | bytes 2064392 | tf_op jit(solution)/shard_map/ppermute | solution.py:884
  585.4 34.4 %collective-permute-start.89 = (bf16[384,896]{1,0:T(8,128)(2,1)S(1)}, bf16[384,896]{1,0:T(8,128)(2,1)S(1)}, u32[]{:S(2)}, u32[]{:S(2)}) collective-permute-start(bf16[384,896]{1,0:T(8,128)(2,1)S(1)} %get-tuple-element.360.refs_2_), channel_id=1, source_target_pairs={{0,24},{1,25},{2,26},{3,27},{4,28},{5,29},{6,30},{7,31},{8,16},{9,... | collective-permute-start | bytes 2064392 | tf_op jit(solution)/shard_map/ppermute | solution.py:884
  587.0 33.0 %collective-permute-start.85 = (bf16[192,1536]{1,0:T(8,128)(2,1)S(1)}, bf16[192,1536]{1,0:T(8,128)(2,1)S(1)}, u32[]{:S(2)}, u32[]{:S(2)}) collective-permute-start(bf16[192,1536]{1,0:T(8,128)(2,1)S(1)} %get-tuple-element.363), channel_id=1, source_target_pairs={{0,0},{4,1},{1,2},{5,3},{2,4},{6,5},{3,6},{7,7},{8,8},{12,9},{9,10... | collective-permute-start | bytes 1769480 | tf_op jit(solution)/shard_map/ppermute | solution.py:887
  595.5 24.4 %collective-permute-start.86 = (bf16[192,1536]{1,0:T(8,128)(2,1)S(1)}, bf16[192,1536]{1,0:T(8,128)(2,1)S(1)}, u32[]{:S(2)}, u32[]{:S(2)}) collective-permute-start(bf16[192,1536]{1,0:T(8,128)(2,1)S(1)} %get-tuple-element.361.refs_11_), channel_id=1, source_target_pairs={{2,0},{6,1},{3,2},{7,3},{0,4},{4,5},{1,6},{5,7},{10,8},{14,9},{11,... | collective-permute-start | bytes 1769480 | tf_op jit(solution)/shard_map/ppermute | solution.py:887
  605.4 28.6 %collective-permute-start.43 = (f32[128,1536]{1,0:T(8,128)S(1)}, f32[128,1536]{1,0:T(8,128)S(1)}, u32[]{:S(2)}, u32[]{:S(2)}) collective-permute-start(f32[128,1536]{1,0:T(8,128)S(1)} %get-tuple-element.558), channel_id=1, source_target_pairs={{0,4},{1,5},{2,6},{3,7},{4,0},{5,1},{6,2},{7,3},{8,12},{9,13},{10,... | collective-permute-start | bytes 2359304 | tf_op jit(solution)/shard_map/ppermute | solution.py:884
  619.8 29.7 %collective-permute-start.84 = (f32[128,1536]{1,0:T(8,128)S(1)}, f32[128,1536]{1,0:T(8,128)S(1)}, u32[]{:S(2)}, u32[]{:S(2)}) collective-permute-start(f32[128,1536]{1,0:T(8,128)S(1)} %get-tuple-element.556), channel_id=1, source_target_pairs={{0,4},{1,5},{2,6},{3,7},{4,0},{5,1},{6,2},{7,3},{8,12},{9,13},{10,... | collective-permute-start | bytes 2359304 | tf_op jit(solution)/shard_map/ppermute | solution.py:884
  640.1 24.5 %collective-permute-start.94 = (bf16[192,896]{1,0:T(8,128)(2,1)S(1)}, bf16[192,896]{1,0:T(8,128)(2,1)S(1)}, u32[]{:S(2)}, u32[]{:S(2)}) collective-permute-start(bf16[192,896]{1,0:T(8,128)(2,1)S(1)} %get-tuple-element.374.refs_16_), channel_id=1, source_target_pairs={{2,0},{6,1},{3,2},{7,3},{0,4},{4,5},{1,6},{5,7},{10,8},{14,9},{11,... | collective-permute-start | bytes 1032200 | tf_op jit(solution)/shard_map/ppermute | solution.py:887
  (176 other events, 1752.1 us)
Sparse Core Ops, SparseCore 0:
  26.5 54.2 all-gather.4
  83.2 57.0 all-gather.6
  142.2 61.7 all-gather.8
  206.3 57.0 all-gather.10
  363.2 55.4 reduce-scatter.3
  438.1 49.5 reduce-scatter.5
  490.7 57.0 reduce-scatter.7

commit v5 on v4

--- a/solution.py
+++ b/solution.py
@@ -39,7 +39,8 @@
 
 def head_sum(values, hm_ref):
     high, low = split(values)
-    return dot(high, hm_ref[...]) + dot(low, hm_ref[...])
+    rest = (values - high.astype(F32) - low.astype(F32)).astype(BF)
+    return dot(high, hm_ref[...]) + (dot(low, hm_ref[...]) + dot(rest, hm_ref[...]))
 
 
 def softplus(values):

time: 680 us -> 680 us (level)
  Pallas kernels: 311 us -> 303 us
    pallas_call x69, Pallas kernels: 311 us -> 303 us  [run(): pl.pallas_call(wrapped, in_specs=specs + [free] * len(extra), out_specs=[...]
    all_gather x4, waiting for transfers between devices: 0.03 us -> 7.22 us  [gather_plane(): lax.all_gather(value, 'dp', axis=0, tiled=True, axis_index_groups=planes)]
  transfers between devices with their start and end apart: 114 -> 114, of which waited for: 29 -> 31; matrix products, arithmetic and copies ran while one was open for 5% -> 5% of each run, Pallas kernels for 44% -> 43%
where the time goes in v5:
time: 680 us; the launch traced here: 672 us
  Pallas kernels  303 us (45%)
  starting transfers between devices  169 us (25%)
  waiting for transfers between devices  130 us (19%)
  local copies, waits for them, and re-layouts  45.4 us (7%)
  between operations  17.1 us (3%)
    pallas_call x69, Pallas kernels, run(): pl.pallas_call(wrapped, in_specs=specs + [free] * len(extra), out_specs=[...  303 us
    ppermute x85, starting transfers between devices, send(): return lax.ppermute(value, axes, pairs(route))  121 us
    ppermute x85, waiting for transfers between devices, send(): return lax.ppermute(value, axes, pairs(route))  103 us
    ppermute x22, starting transfers between devices, back(): return lax.ppermute(value, axes, [(b, a) for a, b in pairs(route)])  47.3 us
    ppermute x22, waiting for transfers between devices, back(): return lax.ppermute(value, axes, [(b, a) for a, b in pairs(route)])  19.3 us
    unnamed x196, local copies, waits for them, and re-layouts  18.2 us
  transfers between devices with their start and end apart: 114, of which 31 were waited for; matrix products, arithmetic and copies ran while one was open for 5% of the time, Pallas kernels for 43%

profile of v5, /device:TPU:1, one launch (start us, length us, event | category | flops | bytes accessed | tf_op | source)
XLA Modules:
  0.0 671.6 jit_solution(14159697162914972969)
XLA Ops:
  28.7 9.3 %collective-permute-start.9 = (bf16[192,1536]{1,0:T(8,128)(2,1)S(1)}, bf16[192,1536]{1,0:T(8,128)(2,1)S(1)}, u32[]{:S(2)}, u32[]{:S(2)}) collective-permute-start(bf16[192,1536]{1,0:T(8,128)(2,1)S(1)} %shard_map.309.refs_7_), channel_id=1, source_target_pairs={{0,0},{1,4},{2,1},{3,5},{4,2},{5,6},{6,3},{7,7},{8,8},{9,12},{10,9... | collective-permute-start | bytes 1769480 | tf_op jit(solution)/shard_map/ppermute | solution.py:885
  41.1 18.6 %collective-permute-done.11.refs_6_.refs_2_ = bf16[128,1536]{1,0:T(8,128)(2,1)S(1)} collective-permute-done((bf16[128,1536]{1,0:T(8,128)(2,1)S(1)}, bf16[128,1536]{1,0:T(8,128)(2,1)S(1)}, u32[]{:S(2)}, u32[]{:S(2)}) %collective-permute-start.11) | collective-permute-done | bytes 393248 | tf_op jit(solution)/shard_map/ppermute | solution.py:885
  104.6 11.3 %shard_map.313 = (bf16[528,1536]{1,0:T(8,128)(2,1)}, bf16[528,1152]{1,0:T(8,128)(2,1)}, f32[16,1024]{1,0:T(8,128)}, bf16[512,1024]{1,0:T(8,128)(2,1)}, f32[512,2...) custom-call(s32[4]{0:T(128)S(1)} %pad_add_fusion.refs_0_, ...), custom_call_target="tpu_custom_call" | custom-call | flops 1000 | bytes 1000 | tf_op jit(solution)/shard_map/pallas_call | solution.py:827
  123.9 11.5 %shard_map.315 = (bf16[528,1536]{1,0:T(8,128)(2,1)}, bf16[528,1152]{1,0:T(8,128)(2,1)}, f32[16,1024]{1,0:T(8,128)}, bf16[512,1024]{1,0:T(8,128)(2,1)}, f32[512,2...) custom-call(s32[4]{0:T(128)S(1)} %pad_add_fusion.refs_0_, ...), custom_call_target="tpu_custom_call" | custom-call | flops 1000 | bytes 1000 | tf_op jit(solution)/shard_map/pallas_call | solution.py:827
  139.2 13.1 %collective-permute-start.19 = (bf16[128,768]{1,0:T(8,128)(2,1)S(1)}, bf16[128,768]{1,0:T(8,128)(2,1)S(1)}, u32[]{:S(2)}, u32[]{:S(2)}) collective-permute-start(bf16[128,768]{1,0:T(8,128)(2,1)S(1)} %get-tuple-element.226.refs_5_.refs_6_), channel_id=1, source_target_pairs={{0,2},{1,3},{4,6},{5,7},{8,10},{9,11},{12,14},{13,15},{16,18},{17,... | collective-permute-start | bytes 589832 | tf_op jit(solution)/shard_map/ppermute | solution.py:885
  156.2 11.3 %shard_map.318 = (bf16[512,1024]{1,0:T(8,128)(2,1)}, bf16[512,768]{1,0:T(8,128)(2,1)}, f32[512,768]{1,0:T(8,128)}, bf16[512,768]{1,0:T(8,128)(2,1)}, bf16[3,128,...) custom-call(s32[4]{0:T(128)S(1)} %pad_add_fusion.refs_0_, bf16[528,1536]{1,0:T(8,128)(2,1)} %get-tuple-element.212.refs_1_.refs_0_, ...), custom_call_target="tpu_custom_call" | custom-call | flops 1000 | bytes 1000 | tf_op jit(solution)/shard_map/pallas_call | solution.py:827
  171.6 10.1 %collective-permute-start.23 = (bf16[128,1664]{1,0:T(8,128)(2,1)S(1)}, bf16[128,1664]{1,0:T(8,128)(2,1)S(1)}, u32[]{:S(2)}, u32[]{:S(2)}) collective-permute-start(bf16[128,1664]{1,0:T(8,128)(2,1)S(1)} %get-tuple-element.232.refs_17_), channel_id=1, source_target_pairs={{0,1},{1,0},{2,3},{3,2},{4,5},{5,4},{6,7},{7,6},{8,9},{9,8},{10,11... | collective-permute-start | bytes 1277960 | tf_op jit(solution)/shard_map/ppermute | solution.py:885
  182.3 11.0 %shard_map.321 = (bf16[512,1024]{1,0:T(8,128)(2,1)}, bf16[512,768]{1,0:T(8,128)(2,1)}, f32[512,768]{1,0:T(8,128)}, bf16[512,768]{1,0:T(8,128)(2,1)}, bf16[3,128,...) custom-call(s32[4]{0:T(128)S(1)} %pad_add_fusion.refs_0_, bf16[528,1536]{1,0:T(8,128)(2,1)} %get-tuple-element.234.refs_1_.refs_2_.refs_3_, ...), custom_call_target="tpu_custom_call" | custom-call | flops 1000 | bytes 1000 | tf_op jit(solution)/shard_map/pallas_call | solution.py:827
  201.0 7.6 %collective-permute-done.24.refs_2_ = bf16[128,1536]{1,0:T(8,128)(2,1)S(1)} collective-permute-done((bf16[128,1536]{1,0:T(8,128)(2,1)S(1)}, bf16[128,1536]{1,0:T(8,128)(2,1)S(1)}, u32[]{:S(2)}, u32[]{:S(2)}) %collective-permute-start.24) | collective-permute-done | bytes 393248 | tf_op jit(solution)/shard_map/ppermute | solution.py:885
  211.3 11.7 %shard_map.325 = (bf16[528,1536]{1,0:T(8,128)(2,1)}, bf16[528,1152]{1,0:T(8,128)(2,1)}, f32[16,1024]{1,0:T(8,128)}, bf16[512,1024]{1,0:T(8,128)(2,1)}, f32[512,2...) custom-call(s32[4]{0:T(128)S(1)} %pad_add_fusion.refs_0_, ...), custom_call_target="tpu_custom_call" | custom-call | flops 1000 | bytes 1000 | tf_op jit(solution)/shard_map/pallas_call | solution.py:827
  226.5 9.5 %collective-permute-done.32.refs_2_ = bf16[128,1536]{1,0:T(8,128)(2,1)S(1)} collective-permute-done((bf16[128,1536]{1,0:T(8,128)(2,1)S(1)}, bf16[128,1536]{1,0:T(8,128)(2,1)S(1)}, u32[]{:S(2)}, u32[]{:S(2)}) %collective-permute-start.32) | collective-permute-done | bytes 393248 | tf_op jit(solution)/shard_map/ppermute | solution.py:885
  241.2 10.9 %shard_map.328 = (bf16[528,1536]{1,0:T(8,128)(2,1)}, bf16[528,1152]{1,0:T(8,128)(2,1)}, f32[16,1024]{1,0:T(8,128)}, bf16[512,1024]{1,0:T(8,128)(2,1)}, f32[512,2...) custom-call(s32[4]{0:T(128)S(1)} %pad_add_fusion.refs_0_, ...), custom_call_target="tpu_custom_call" | custom-call | flops 1000 | bytes 1000 | tf_op jit(solution)/shard_map/pallas_call | solution.py:827
  256.1 7.2 %all-gather.11.cloned.1.call-done.refs_3_.refs_5_.refs_2_ = bf16[1536,1536]{1,0:T(8,128)(2,1)} async-done(((bf16[384,1536]{1,0:T(8,128)(2,1)}), bf16[1536,1536]{1,0:T(8,128)(2,1)}) %all-gather.11.cloned.1.call-update) | async-done | bytes 4718608 | tf_op jit(solution)/shard_map/all_gather | solution.py:971
  263.3 10.7 %shard_map.330 = (bf16[512,1024]{1,0:T(8,128)(2,1)}, bf16[512,768]{1,0:T(8,128)(2,1)}, f32[512,768]{1,0:T(8,128)}, bf16[512,768]{1,0:T(8,128)(2,1)}, bf16[3,128,...) custom-call(s32[4]{0:T(128)S(1)} %pad_add_fusion.refs_0_, bf16[528,1536]{1,0:T(8,128)(2,1)} %get-tuple-element.243.refs_1_.refs_0_, ...), custom_call_target="tpu_custom_call" | custom-call | flops 1000 | bytes 1000 | tf_op jit(solution)/shard_map/pallas_call | solution.py:827
  279.8 10.7 %shard_map.333 = (bf16[512,1024]{1,0:T(8,128)(2,1)}, bf16[512,768]{1,0:T(8,128)(2,1)}, f32[512,768]{1,0:T(8,128)}, bf16[512,768]{1,0:T(8,128)(2,1)}, bf16[3,128,...) custom-call(s32[4]{0:T(128)S(1)} %pad_add_fusion.refs_0_, bf16[528,1536]{1,0:T(8,128)(2,1)} %get-tuple-element.267.refs_1_.refs_2_, ...), custom_call_target="tpu_custom_call" | custom-call | flops 1000 | bytes 1000 | tf_op jit(solution)/shard_map/pallas_call | solution.py:827
  299.2 8.5 %collective-permute-done.44.refs_2_ = bf16[128,1664]{1,0:T(8,128)(2,1)S(1)} collective-permute-done((bf16[128,1664]{1,0:T(8,128)(2,1)S(1)}, bf16[128,1664]{1,0:T(8,128)(2,1)S(1)}, u32[]{:S(2)}, u32[]{:S(2)}) %collective-permute-start.44) | collective-permute-done | bytes 426016 | tf_op jit(solution)/shard_map/ppermute | solution.py:885
  308.9 7.9 %collective-permute-done.42.refs_1_ = bf16[128,1664]{1,0:T(8,128)(2,1)S(1)} collective-permute-done((bf16[128,1664]{1,0:T(8,128)(2,1)S(1)}, bf16[128,1664]{1,0:T(8,128)(2,1)S(1)}, u32[]{:S(2)}, u32[]{:S(2)}) %collective-permute-start.42) | collective-permute-done | bytes 426016 | tf_op jit(solution)/shard_map/ppermute | solution.py:885
  321.9 7.5 %shard_map.338 = (bf16[512,1536]{1,0:T(8,128)(2,1)}, bf16[512,768]{1,0:T(8,128)(2,1)}, bf16[528,768]{1,0:T(8,128)(2,1)}, f32[8,768]{1,0:T(8,128)S(1)}, bf16[128,768]{1,0:T(8,128)(2,1)S(1)}) custom-call(s32[4]{0:T(128)S(1)} %pad_add_fusion.refs_0_, bf16[128,1664]{1,0:T(8,128)(2,1)S(1)} %get-tuple-element.274.refs_3_.refs_1_, ...), custom_call_target="tpu_custom_call" | custom-call | flops 1000 | bytes 1000 | tf_op jit(solution)/shard_map/pallas_call | solution.py:827
  333.7 7.5 %shard_map.340 = (bf16[512,1536]{1,0:T(8,128)(2,1)}, bf16[512,768]{1,0:T(8,128)(2,1)}, bf16[528,768]{1,0:T(8,128)(2,1)}, f32[8,768]{1,0:T(8,128)S(1)}, bf16[128,768]{1,0:T(8,128)(2,1)S(1)}) custom-call(s32[4]{0:T(128)S(1)} %pad_add_fusion.refs_0_, bf16[128,1664]{1,0:T(8,128)(2,1)S(1)} %get-tuple-element.282.refs_14_.refs_1_, ...), custom_call_target="tpu_custom_call" | custom-call | flops 1000 | bytes 1000 | tf_op jit(solution)/shard_map/pallas_call | solution.py:827
  345.8 11.3 %shard_map.342.refs_0_ = bf16[1536,1536]{1,0:T(8,128)(2,1)} custom-call(bf16[528,1536]{1,0:T(8,128)(2,1)} %get-tuple-element.243.refs_1_.refs_0_, bf16[528,768]{1,0:T(8,128)(2,1)} %get-tuple-element.283.refs_1_.refs_3_, bf16[528,1536]{1,0:T(8,128)(2,1)} %get-tuple-element.267.refs_1_.refs_2_, bf16[528,768]{1,0:T(8,128)(2,1)} %get-tuple-element.293.refs_3_, ...), custom_call_target="tpu_custom_call" | custom-call | flops 1000 | bytes 1000 | tf_op jit(solution)/shard_map/pallas_call | solution.py:827
  360.8 20.4 %shard_map.344 = (bf16[528,1152]{1,0:T(8,128)(2,1)}, f32[8,1024]{1,0:T(8,128)S(1)}, f32[8,128]{1,0:T(8,128)S(1)}, f32[528,1536]{1,0:T(8,128)S(1)}) custom-call(s32[4]{0:T(128)S(1)} %pad_add_fusion.refs_0_, bf16[1536,1152]{1,0:T(8,128)(2,1)} %all-gather.9.cloned.1.call-done.refs_5_.refs_1_, ...), custom_call_target="tpu_custom_call" | custom-call | flops 1000 | bytes 1000 | tf_op jit(solution)/shard_map/pallas_call | solution.py:827
  386.8 20.2 %shard_map.347 = (bf16[528,1152]{1,0:T(8,128)(2,1)}, f32[8,1024]{1,0:T(8,128)S(1)}, f32[8,128]{1,0:T(8,128)S(1)}, f32[528,1536]{1,0:T(8,128)S(1)}) custom-call(s32[4]{0:T(128)S(1)} %pad_add_fusion.refs_0_, bf16[1536,1152]{1,0:T(8,128)(2,1)} %all-gather.9.cloned.1.call-done.refs_5_.refs_1_, ...), custom_call_target="tpu_custom_call" | custom-call | flops 1000 | bytes 1000 | tf_op jit(solution)/shard_map/pallas_call | solution.py:827
  416.7 10.7 %shard_map.351.refs_0_ = bf16[1536,1152]{1,0:T(8,128)(2,1)} custom-call(bf16[528,1536]{1,0:T(8,128)(2,1)} %get-tuple-element.243.refs_1_.refs_0_, bf16[528,1152]{1,0:T(8,128)(2,1)} %get-tuple-element.318.refs_1_, bf16[528,1536]{1,0:T(8,128)(2,1)} %get-tuple-element.267.refs_1_.refs_2_, bf16[528,1152]{1,0:T(8,128)(2,1)} %get-tuple-element.319.refs_3_, ...), custom_call_target="tpu_custom_call" | custom-call | flops 1000 | bytes 1000 | tf_op jit(solution)/shard_map/pallas_call | solution.py:827
  447.3 8.3 %shard_map.355 = (bf16[512,1536]{1,0:T(8,128)(2,1)}, bf16[512,768]{1,0:T(8,128)(2,1)}, bf16[528,768]{1,0:T(8,128)(2,1)}, f32[8,768]{1,0:T(8,128)S(1)}, bf16[128,768]{1,0:T(8,128)(2,1)S(1)}) custom-call(s32[4]{0:T(128)S(1)} %pad_add_fusion.refs_0_, bf16[128,1664]{1,0:T(8,128)(2,1)S(1)} %copy-done.8, bf16[128,1664]{1,0:T(8,128)(2,1)S(1)} %copy-done.12, ...), custom_call_target="tpu_custom_call" | custom-call | flops 1000 | bytes 1000 | tf_op jit(solution)/shard_map/pallas_call | solution.py:827
  460.6 7.6 %shard_map.357 = (bf16[512,1536]{1,0:T(8,128)(2,1)}, bf16[512,768]{1,0:T(8,128)(2,1)}, bf16[528,768]{1,0:T(8,128)(2,1)}, f32[8,768]{1,0:T(8,128)S(1)}, bf16[128,768]{1,0:T(8,128)(2,1)S(1)}) custom-call(s32[4]{0:T(128)S(1)} %pad_add_fusion.refs_0_, bf16[128,1664]{1,0:T(8,128)(2,1)S(1)} %get-tuple-element.321.refs_14_.refs_1_, ...), custom_call_target="tpu_custom_call" | custom-call | flops 1000 | bytes 1000 | tf_op jit(solution)/shard_map/pallas_call | solution.py:827
  472.2 11.2 %shard_map.359.refs_0_ = bf16[1536,1536]{1,0:T(8,128)(2,1)} custom-call(bf16[528,1536]{1,0:T(8,128)(2,1)} %get-tuple-element.212.refs_1_.refs_0_, bf16[528,768]{1,0:T(8,128)(2,1)} %get-tuple-element.322.refs_1_.refs_3_, bf16[528,1536]{1,0:T(8,128)(2,1)} %get-tuple-element.234.refs_1_.refs_2_.refs_3_, bf16[528,768]{1,0:T(8,128)(2,1)} %get-tuple-element.332.refs_3_, ...), custom_call_target="tpu_custom_call" | custom-call | flops 1000 | bytes 1000 | tf_op jit(solution)/shard_map/pallas_call | solution.py:827
  489.2 20.5 %shard_map.361 = (bf16[528,1152]{1,0:T(8,128)(2,1)}, f32[8,1024]{1,0:T(8,128)S(1)}, f32[8,128]{1,0:T(8,128)S(1)}, f32[528,1536]{1,0:T(8,128)S(1)}) custom-call(s32[4]{0:T(128)S(1)} %pad_add_fusion.refs_0_, bf16[1536,1152]{1,0:T(8,128)(2,1)} %all-gather.5.cloned.1.call-done.refs_5_.refs_1_, ...), custom_call_target="tpu_custom_call" | custom-call | flops 1000 | bytes 1000 | tf_op jit(solution)/shard_map/pallas_call | solution.py:827
  525.2 20.8 %shard_map.365 = (bf16[528,1152]{1,0:T(8,128)(2,1)}, f32[8,1024]{1,0:T(8,128)S(1)}, f32[8,128]{1,0:T(8,128)S(1)}, f32[528,1536]{1,0:T(8,128)S(1)}) custom-call(s32[4]{0:T(128)S(1)} %pad_add_fusion.refs_0_, bf16[1536,1152]{1,0:T(8,128)(2,1)} %all-gather.5.cloned.1.call-done.refs_5_.refs_1_, ...), custom_call_target="tpu_custom_call" | custom-call | flops 1000 | bytes 1000 | tf_op jit(solution)/shard_map/pallas_call | solution.py:827
  553.1 10.9 %shard_map.369 = (bf16[384,256]{1,0:T(8,128)(2,1)S(1)}, bf16[384,256]{1,0:T(8,128)(2,1)S(1)}, bf16[384,256]{1,0:T(8,128)(2,1)}, bf16[384,256]{1,0:T(8,128)(2,1)}...) custom-call(s32[4]{0:T(128)S(1)} %pad_add_fusion.refs_0_, ...), custom_call_target="tpu_custom_call" | custom-call | flops 1000 | bytes 1000 | tf_op jit(solution)/shard_map/pallas_call | solution.py:827
  582.0 10.4 %collective-permute-start.85 = (bf16[192,1536]{1,0:T(8,128)(2,1)S(1)}, bf16[192,1536]{1,0:T(8,128)(2,1)S(1)}, u32[]{:S(2)}, u32[]{:S(2)}) collective-permute-start(bf16[192,1536]{1,0:T(8,128)(2,1)S(1)} %get-tuple-element.363), channel_id=1, source_target_pairs={{0,0},{4,1},{1,2},{5,3},{2,4},{6,5},{3,6},{7,7},{8,8},{12,9},{9,10... | collective-permute-start | bytes 1769480 | tf_op jit(solution)/shard_map/ppermute | solution.py:888
  602.3 10.4 %collective-permute-done.88.refs_3_ = bf16[384,896]{1,0:T(8,128)(2,1)} collective-permute-done((bf16[384,896]{1,0:T(8,128)(2,1)}, bf16[384,896]{1,0:T(8,128)(2,1)}, u32[]{:S(2)}, u32[]{:S(2)}) %collective-permute-start.88) | collective-permute-done | bytes 688160 | tf_op jit(solution)/shard_map/ppermute | solution.py:885
  651.7 9.4 %collective-permute-done.93.refs_2_ = bf16[192,896]{1,0:T(8,128)(2,1)S(1)} collective-permute-done((bf16[192,896]{1,0:T(8,128)(2,1)S(1)}, bf16[192,896]{1,0:T(8,128)(2,1)S(1)}, u32[]{:S(2)}, u32[]{:S(2)}) %collective-permute-start.93) | collective-permute-done | bytes 344096 | tf_op jit(solution)/shard_map/ppermute | solution.py:888
  (557 shorter events, 286.4 us)
Async XLA Ops:
  7.2 95.8 %all-gather.5.cloned.1.call-start = ((), (), s32[]{:S(2)}) async-start(), calls=%async_computation.3 | async-start | bytes 4423680 | tf_op jit(solution)/shard_map/all_gather | solution.py:971
  26.4 129.2 %all-gather.7.cloned.1.call-start = ((), (), s32[]{:S(2)}) async-start(), calls=%async_computation.4 | async-start | bytes 5898240 | tf_op jit(solution)/shard_map/all_gather | solution.py:971
  27.8 38.9 %collective-permute-start.10 = (bf16[192,1536]{1,0:T(8,128)(2,1)S(1)}, bf16[192,1536]{1,0:T(8,128)(2,1)S(1)}, u32[]{:S(2)}, u32[]{:S(2)}) collective-permute-start(bf16[192,1536]{1,0:T(8,128)(2,1)S(1)} %shard_map.309.refs_7_), channel_id=1, source_target_pairs={{0,2},{1,6},{2,3},{3,7},{4,0},{5,4},{6,1},{7,5},{8,10},{9,14},{10,... | collective-permute-start | bytes 1769480 | tf_op jit(solution)/shard_map/ppermute | solution.py:885
  28.7 38.0 %collective-permute-start.9 = (bf16[192,1536]{1,0:T(8,128)(2,1)S(1)}, bf16[192,1536]{1,0:T(8,128)(2,1)S(1)}, u32[]{:S(2)}, u32[]{:S(2)}) collective-permute-start(bf16[192,1536]{1,0:T(8,128)(2,1)S(1)} %shard_map.309.refs_7_), channel_id=1, source_target_pairs={{0,0},{1,4},{2,1},{3,5},{4,2},{5,6},{6,3},{7,7},{8,8},{9,12},{10,9... | collective-permute-start | bytes 1769480 | tf_op jit(solution)/shard_map/ppermute | solution.py:885
  41.0 25.7 %collective-permute-start.1 = (bf16[128,1536]{1,0:T(8,128)(2,1)S(1)}, bf16[128,1536]{1,0:T(8,128)(2,1)S(1)}, u32[]{:S(2)}, u32[]{:S(2)}) collective-permute-start(bf16[128,1536]{1,0:T(8,128)(2,1)S(1)} %get-tuple-element.210.refs_2_.refs_3_.refs_1_), channel_id=1, source_target_pairs={{0,1},{1,0},{2,3},{3,2},{4,5},{5,4},{6,7},{7,6},{8,9},{9,8},{10,11... | collective-permute-start | bytes 1179656 | tf_op jit(solution)/shard_map/ppermute | solution.py:885
  69.9 141.4 %all-gather.9.cloned.1.call-start = ((), (), s32[]{:S(2)}) async-start(), calls=%async_computation.5 | async-start | bytes 4423680 | tf_op jit(solution)/shard_map/all_gather | solution.py:971
  92.8 42.7 %collective-permute-start.15 = (bf16[192,2432]{1,0:T(8,128)(2,1)S(1)}, bf16[192,2432]{1,0:T(8,128)(2,1)}, u32[]{:S(2)}, u32[]{:S(2)}) collective-permute-start(bf16[192,2432]{1,0:T(8,128)(2,1)S(1)} %shard_map.312.refs_11_), channel_id=1, source_target_pairs={{0,0},{1,4},{2,1},{3,5},{4,2},{5,6},{6,3},{7,7},{8,8},{9,12},{10,9... | collective-permute-start | bytes 2801672 | tf_op jit(solution)/shard_map/ppermute | solution.py:885
  97.2 38.3 %collective-permute-start.16 = (bf16[192,2432]{1,0:T(8,128)(2,1)S(1)}, bf16[192,2432]{1,0:T(8,128)(2,1)}, u32[]{:S(2)}, u32[]{:S(2)}) collective-permute-start(bf16[192,2432]{1,0:T(8,128)(2,1)S(1)} %shard_map.312.refs_11_), channel_id=1, source_target_pairs={{0,2},{1,6},{2,3},{3,7},{4,0},{5,4},{6,1},{7,5},{8,10},{9,14},{10,... | collective-permute-start | bytes 2801672 | tf_op jit(solution)/shard_map/ppermute | solution.py:885
  138.5 124.8 %all-gather.11.cloned.1.call-start = ((), (), s32[]{:S(2)}) async-start(), calls=%async_computation.6 | async-start | bytes 5898240 | tf_op jit(solution)/shard_map/all_gather | solution.py:971
  139.1 295.2 %reduce-scatter.4.cloned.1.call-start = ((), (), s32[]{:S(2)}) async-start(), calls=%async_computation.7 | async-start | bytes 5898240 | tf_op jit(solution)/shard_map/reduce_scatter | solution.py:1252
  139.2 28.3 %collective-permute-start.19 = (bf16[128,768]{1,0:T(8,128)(2,1)S(1)}, bf16[128,768]{1,0:T(8,128)(2,1)S(1)}, u32[]{:S(2)}, u32[]{:S(2)}) collective-permute-start(bf16[128,768]{1,0:T(8,128)(2,1)S(1)} %get-tuple-element.226.refs_5_.refs_6_), channel_id=1, source_target_pairs={{0,2},{1,3},{4,6},{5,7},{8,10},{9,11},{12,14},{13,15},{16,18},{17,... | collective-permute-start | bytes 589832 | tf_op jit(solution)/shard_map/ppermute | solution.py:885
  199.0 24.0 %collective-permute-start.28 = (bf16[128,1664]{1,0:T(8,128)(2,1)S(1)}, bf16[128,1664]{1,0:T(8,128)(2,1)S(1)}, u32[]{:S(2)}, u32[]{:S(2)}) collective-permute-start(bf16[128,1664]{1,0:T(8,128)(2,1)S(1)} %get-tuple-element.242.refs_11_), channel_id=1, source_target_pairs={{0,1},{1,0},{2,3},{3,2},{4,5},{5,4},{6,7},{7,6},{8,9},{9,8},{10,11... | collective-permute-start | bytes 1277960 | tf_op jit(solution)/shard_map/ppermute | solution.py:885
  298.6 23.2 %collective-permute-start.45 = (bf16[128,1664]{1,0:T(8,128)(2,1)S(1)}, bf16[128,1664]{1,0:T(8,128)(2,1)S(1)}, u32[]{:S(2)}, u32[]{:S(2)}) collective-permute-start(bf16[128,1664]{1,0:T(8,128)(2,1)S(1)} %get-tuple-element.274.refs_3_.refs_1_), channel_id=1, source_target_pairs={{0,4},{1,5},{2,6},{3,7},{4,0},{5,1},{6,2},{7,3},{8,12},{9,13},{10,... | collective-permute-start | bytes 1277960 | tf_op jit(solution)/shard_map/ppermute | solution.py:885
  357.1 157.4 %reduce-scatter.6.cloned.1.call-start = ((), (), s32[]{:S(2)}) async-start(), calls=%async_computation.8 | async-start | bytes 4423680 | tf_op jit(solution)/shard_map/reduce_scatter | solution.py:1252
  357.2 24.1 %collective-permute-start.51 = (bf16[128,768]{1,0:T(8,128)(2,1)S(1)}, bf16[128,768]{1,0:T(8,128)(2,1)S(1)}, u32[]{:S(2)}, u32[]{:S(2)}) collective-permute-start(bf16[128,768]{1,0:T(8,128)(2,1)S(1)} %shard_map.341.refs_8_), channel_id=1, source_target_pairs={{2,0},{3,1},{6,4},{7,5},{10,8},{11,9},{14,12},{15,13},{18,16},{19,... | collective-permute-start | bytes 589832 | tf_op jit(solution)/shard_map/ppermute | solution.py:888
  432.7 145.9 %reduce-scatter.8.cloned.1.call-start = ((), (), s32[]{:S(2)}) async-start(), calls=%async_computation.9 | async-start | bytes 5898240 | tf_op jit(solution)/shard_map/reduce_scatter | solution.py:1252
  445.3 38.2 %collective-permute-start.67 = (bf16[192,1536]{1,0:T(8,128)(2,1)S(1)}, bf16[192,1536]{1,0:T(8,128)(2,1)S(1)}, u32[]{:S(2)}, u32[]{:S(2)}) collective-permute-start(bf16[192,1536]{1,0:T(8,128)(2,1)S(1)} %get-tuple-element.338), channel_id=1, source_target_pairs={{0,0},{4,1},{1,2},{5,3},{2,4},{6,5},{3,6},{7,7},{8,8},{12,9},{9,10... | collective-permute-start | bytes 1769480 | tf_op jit(solution)/shard_map/ppermute | solution.py:888
  485.4 24.3 %collective-permute-start.69 = (bf16[192,1536]{1,0:T(8,128)(2,1)S(1)}, bf16[192,1536]{1,0:T(8,128)(2,1)S(1)}, u32[]{:S(2)}, u32[]{:S(2)}) collective-permute-start(bf16[192,1536]{1,0:T(8,128)(2,1)S(1)} %copy-done.30), channel_id=1, source_target_pairs={{2,0},{6,1},{3,2},{7,3},{0,4},{4,5},{1,6},{5,7},{10,8},{14,9},{11,... | collective-permute-start | bytes 1769480 | tf_op jit(solution)/shard_map/ppermute | solution.py:888
  485.4 24.3 %collective-permute-start.68 = (bf16[128,768]{1,0:T(8,128)(2,1)S(1)}, bf16[128,768]{1,0:T(8,128)(2,1)S(1)}, u32[]{:S(2)}, u32[]{:S(2)}) collective-permute-start(bf16[128,768]{1,0:T(8,128)(2,1)S(1)} %shard_map.358.refs_8_), channel_id=1, source_target_pairs={{2,0},{3,1},{6,4},{7,5},{10,8},{11,9},{14,12},{15,13},{18,16},{19,... | collective-permute-start | bytes 589832 | tf_op jit(solution)/shard_map/ppermute | solution.py:888
  514.4 31.7 %collective-permute-start.71 = (bf16[128,1536]{1,0:T(8,128)(2,1)S(1)}, bf16[128,1536]{1,0:T(8,128)(2,1)S(1)}, u32[]{:S(2)}, u32[]{:S(2)}) collective-permute-start(bf16[128,1536]{1,0:T(8,128)(2,1)S(1)} %get-tuple-element.341), channel_id=1, source_target_pairs={{0,1},{1,0},{2,3},{3,2},{4,5},{5,4},{6,7},{7,6},{8,9},{9,8},{10,11... | collective-permute-start | bytes 1179656 | tf_op jit(solution)/shard_map/ppermute | solution.py:885
  516.4 29.6 %collective-permute-start.74 = (bf16[192,896]{1,0:T(8,128)(2,1)S(1)}, bf16[192,896]{1,0:T(8,128)(2,1)S(1)}, u32[]{:S(2)}, u32[]{:S(2)}) collective-permute-start(bf16[192,896]{1,0:T(8,128)(2,1)S(1)} %get-tuple-element.349), channel_id=1, source_target_pairs={{0,0},{4,1},{1,2},{5,3},{2,4},{6,5},{3,6},{7,7},{8,8},{12,9},{9,10... | collective-permute-start | bytes 1032200 | tf_op jit(solution)/shard_map/ppermute | solution.py:888
  520.3 25.7 %collective-permute-start.75 = (bf16[192,896]{1,0:T(8,128)(2,1)S(1)}, bf16[192,896]{1,0:T(8,128)(2,1)S(1)}, u32[]{:S(2)}, u32[]{:S(2)}) collective-permute-start(bf16[192,896]{1,0:T(8,128)(2,1)S(1)} %get-tuple-element.350), channel_id=1, source_target_pairs={{2,0},{6,1},{3,2},{7,3},{0,4},{4,5},{1,6},{5,7},{10,8},{14,9},{11,... | collective-permute-start | bytes 1032200 | tf_op jit(solution)/shard_map/ppermute | solution.py:888
  523.6 22.4 %collective-permute-start.72 = (bf16[16,1536]{1,0:T(8,128)(2,1)S(1)}, bf16[16,1536]{1,0:T(8,128)(2,1)S(1)}, u32[]{:S(2)}, u32[]{:S(2)}) collective-permute-start(bf16[16,1536]{1,0:T(8,128)(2,1)S(1)} %get-tuple-element.342.refs_2_), channel_id=1, source_target_pairs={{6,5},{14,13},{22,21},{30,29}} | collective-permute-start | bytes 147464 | tf_op jit(solution)/shard_map/ppermute | solution.py:888
  551.5 40.9 %collective-permute-start.77 = (bf16[128,1536]{1,0:T(8,128)(2,1)}, bf16[128,1536]{1,0:T(8,128)(2,1)}, u32[]{:S(2)}, u32[]{:S(2)}) collective-permute-start(bf16[128,1536]{1,0:T(8,128)(2,1)} %get-tuple-element.354), channel_id=1, source_target_pairs={{0,1},{1,0},{2,3},{3,2},{4,5},{5,4},{6,7},{7,6},{8,9},{9,8},{10,11... | collective-permute-start | bytes 1179656 | tf_op jit(solution)/shard_map/ppermute | solution.py:885
  576.4 25.7 %collective-permute-start.87 = (bf16[384,896]{1,0:T(8,128)(2,1)}, bf16[384,896]{1,0:T(8,128)(2,1)}, u32[]{:S(2)}, u32[]{:S(2)}) collective-permute-start(bf16[384,896]{1,0:T(8,128)(2,1)} %get-tuple-element.365), channel_id=1, source_target_pairs={{0,8},{1,9},{2,10},{3,11},{4,12},{5,13},{6,14},{7,15},{8,0},{9,1},... | collective-permute-start | bytes 2064392 | tf_op jit(solution)/shard_map/ppermute | solution.py:885
  578.2 34.5 %collective-permute-start.88 = (bf16[384,896]{1,0:T(8,128)(2,1)}, bf16[384,896]{1,0:T(8,128)(2,1)}, u32[]{:S(2)}, u32[]{:S(2)}) collective-permute-start(bf16[384,896]{1,0:T(8,128)(2,1)} %get-tuple-element.366), channel_id=1, source_target_pairs={{0,16},{1,17},{2,18},{3,19},{4,20},{5,21},{6,22},{7,23},{8,24},{9,... | collective-permute-start | bytes 2064392 | tf_op jit(solution)/shard_map/ppermute | solution.py:885
  580.8 35.0 %collective-permute-start.89 = (bf16[384,896]{1,0:T(8,128)(2,1)S(1)}, bf16[384,896]{1,0:T(8,128)(2,1)S(1)}, u32[]{:S(2)}, u32[]{:S(2)}) collective-permute-start(bf16[384,896]{1,0:T(8,128)(2,1)S(1)} %get-tuple-element.360.refs_2_), channel_id=1, source_target_pairs={{0,24},{1,25},{2,26},{3,27},{4,28},{5,29},{6,30},{7,31},{8,16},{9,... | collective-permute-start | bytes 2064392 | tf_op jit(solution)/shard_map/ppermute | solution.py:885
  582.0 33.8 %collective-permute-start.85 = (bf16[192,1536]{1,0:T(8,128)(2,1)S(1)}, bf16[192,1536]{1,0:T(8,128)(2,1)S(1)}, u32[]{:S(2)}, u32[]{:S(2)}) collective-permute-start(bf16[192,1536]{1,0:T(8,128)(2,1)S(1)} %get-tuple-element.363), channel_id=1, source_target_pairs={{0,0},{4,1},{1,2},{5,3},{2,4},{6,5},{3,6},{7,7},{8,8},{12,9},{9,10... | collective-permute-start | bytes 1769480 | tf_op jit(solution)/shard_map/ppermute | solution.py:888
  592.4 23.4 %collective-permute-start.86 = (bf16[192,1536]{1,0:T(8,128)(2,1)S(1)}, bf16[192,1536]{1,0:T(8,128)(2,1)S(1)}, u32[]{:S(2)}, u32[]{:S(2)}) collective-permute-start(bf16[192,1536]{1,0:T(8,128)(2,1)S(1)} %get-tuple-element.361.refs_11_), channel_id=1, source_target_pairs={{2,0},{6,1},{3,2},{7,3},{0,4},{4,5},{1,6},{5,7},{10,8},{14,9},{11,... | collective-permute-start | bytes 1769480 | tf_op jit(solution)/shard_map/ppermute | solution.py:888
  602.2 28.5 %collective-permute-start.43 = (f32[128,1536]{1,0:T(8,128)S(1)}, f32[128,1536]{1,0:T(8,128)S(1)}, u32[]{:S(2)}, u32[]{:S(2)}) collective-permute-start(f32[128,1536]{1,0:T(8,128)S(1)} %get-tuple-element.558), channel_id=1, source_target_pairs={{0,4},{1,5},{2,6},{3,7},{4,0},{5,1},{6,2},{7,3},{8,12},{9,13},{10,... | collective-permute-start | bytes 2359304 | tf_op jit(solution)/shard_map/ppermute | solution.py:885
  615.7 30.3 %collective-permute-start.84 = (f32[128,1536]{1,0:T(8,128)S(1)}, f32[128,1536]{1,0:T(8,128)S(1)}, u32[]{:S(2)}, u32[]{:S(2)}) collective-permute-start(f32[128,1536]{1,0:T(8,128)S(1)} %get-tuple-element.556), channel_id=1, source_target_pairs={{0,4},{1,5},{2,6},{3,7},{4,0},{5,1},{6,2},{7,3},{8,12},{9,13},{10,... | collective-permute-start | bytes 2359304 | tf_op jit(solution)/shard_map/ppermute | solution.py:885
  636.7 24.5 %collective-permute-start.94 = (bf16[192,896]{1,0:T(8,128)(2,1)S(1)}, bf16[192,896]{1,0:T(8,128)(2,1)S(1)}, u32[]{:S(2)}, u32[]{:S(2)}) collective-permute-start(bf16[192,896]{1,0:T(8,128)(2,1)S(1)} %get-tuple-element.374.refs_16_), channel_id=1, source_target_pairs={{2,0},{6,1},{3,2},{7,3},{0,4},{4,5},{1,6},{5,7},{10,8},{14,9},{11,... | collective-permute-start | bytes 1032200 | tf_op jit(solution)/shard_map/ppermute | solution.py:888
  (176 other events, 1780.1 us)
Sparse Core Ops, SparseCore 0:
  26.5 54.2 all-gather.4
  83.2 57.0 all-gather.6
  142.2 61.6 all-gather.8
  206.2 57.0 all-gather.10
  357.2 54.4 reduce-scatter.3
  432.9 49.3 reduce-scatter.5
  485.2 57.0 reduce-scatter.7

commit v6 on v4

--- a/solution.py
+++ b/solution.py
@@ -14,7 +14,7 @@
 LAYERS = 2
 EPSILON = 1e-05
 HALO = 16
-CHUNK = 256
+CHUNK = 128
 LANES = 128
 
 BF = jnp.bfloat16
@@ -1190,11 +1190,11 @@
         pick(parts, 0, True, False)
         parts = regroup(hold(jnp.concatenate(rest_part(0), axis=1), []))
         pick(parts, 0, False, True, [*arrived[0], *arrived[1]])
-        queue.touch([marks, seg_row, links, conv_w, gate_p, head_p])
         parts = [
             regroup(hold(jnp.concatenate(front_part(l) + rest_part(l), axis=1), []))
             for l in range(1, LAYERS)
         ]
+        queue.touch([marks, seg_row, links, conv_w, gate_p, head_p])
         front(0, 0)
         front(0, 1, states(0, 0))
         for l in range(1, LAYERS):

time: 680 us -> 684 us (level)
  starting transfers between devices: 170 us -> 179 us
  waiting for transfers between devices: 124 us -> 116 us
    ppermute x85, starting transfers between devices: 124 us -> 133 us  [send(): return lax.ppermute(value, axes, pairs(route))]
    unnamed x196 -> x227, local copies, waits for them, and re-layouts: 19.3 us -> 21 us
  transfers between devices with their start and end apart: 114 -> 114, of which waited for: 29 -> 31; matrix products, arithmetic and copies ran while one was open for 5% -> 5% of each run, Pallas kernels for 44% -> 43%
where the time goes in v6:
time: 684 us; the launch traced here: 675 us
  Pallas kernels  307 us (45%)
  starting transfers between devices  179 us (26%)
  waiting for transfers between devices  116 us (17%)
  local copies, waits for them, and re-layouts  50.8 us (7%)
  between operations  17.2 us (3%)
    pallas_call x69, Pallas kernels, run(): pl.pallas_call(wrapped, in_specs=specs + [free] * len(extra), out_specs=[...  307 us
    ppermute x85, starting transfers between devices, send(): return lax.ppermute(value, axes, pairs(route))  133 us
    ppermute x85, waiting for transfers between devices, send(): return lax.ppermute(value, axes, pairs(route))  98 us
    ppermute x22, starting transfers between devices, back(): return lax.ppermute(value, axes, [(b, a) for a, b in pairs(route)])  45 us
    unnamed x227, local copies, waits for them, and re-layouts  21 us
    ppermute x22, waiting for transfers between devices, back(): return lax.ppermute(value, axes, [(b, a) for a, b in pairs(route)])  17.5 us
  transfers between devices with their start and end apart: 114, of which 31 were waited for; matrix products, arithmetic and copies ran while one was open for 5% of the time, Pallas kernels for 43%

profile of v6, /device:TPU:1, one launch (start us, length us, event | category | flops | bytes accessed | tf_op | source)
XLA Modules:
  0.0 675.5 jit_solution(15397033072041995649)
XLA Ops:
  29.1 9.3 %collective-permute-start.9 = (bf16[192,1536]{1,0:T(8,128)(2,1)S(1)}, bf16[192,1536]{1,0:T(8,128)(2,1)S(1)}, u32[]{:S(2)}, u32[]{:S(2)}) collective-permute-start(bf16[192,1536]{1,0:T(8,128)(2,1)S(1)} %shard_map.309.refs_7_), channel_id=1, source_target_pairs={{0,0},{1,4},{2,1},{3,5},{4,2},{5,6},{6,3},{7,7},{8,8},{9,12},{10,9... | collective-permute-start | bytes 1769480 | tf_op jit(solution)/shard_map/ppermute | solution.py:884
  41.5 18.7 %collective-permute-done.11.refs_6_.refs_2_ = bf16[128,1536]{1,0:T(8,128)(2,1)} collective-permute-done((bf16[128,1536]{1,0:T(8,128)(2,1)}, bf16[128,1536]{1,0:T(8,128)(2,1)}, u32[]{:S(2)}, u32[]{:S(2)}) %collective-permute-start.11) | collective-permute-done | bytes 393248 | tf_op jit(solution)/shard_map/ppermute | solution.py:884
  104.4 11.2 %shard_map.313 = (bf16[528,1536]{1,0:T(8,128)(2,1)}, bf16[528,1152]{1,0:T(8,128)(2,1)}, f32[16,1024]{1,0:T(8,128)}, bf16[512,1024]{1,0:T(8,128)(2,1)}, f32[512,2...) custom-call(s32[4]{0:T(128)S(1)} %pad_add_fusion.refs_0_, ...), custom_call_target="tpu_custom_call" | custom-call | flops 1000 | bytes 1000 | tf_op jit(solution)/shard_map/pallas_call | solution.py:826
  122.5 12.1 %shard_map.315 = (bf16[528,1536]{1,0:T(8,128)(2,1)}, bf16[528,1152]{1,0:T(8,128)(2,1)}, f32[16,1024]{1,0:T(8,128)}, bf16[512,1024]{1,0:T(8,128)(2,1)}, f32[512,2...) custom-call(s32[4]{0:T(128)S(1)} %pad_add_fusion.refs_0_, ...), custom_call_target="tpu_custom_call" | custom-call | flops 1000 | bytes 1000 | tf_op jit(solution)/shard_map/pallas_call | solution.py:826
  139.2 13.0 %collective-permute-start.19 = (bf16[128,768]{1,0:T(8,128)(2,1)S(1)}, bf16[128,768]{1,0:T(8,128)(2,1)S(1)}, u32[]{:S(2)}, u32[]{:S(2)}) collective-permute-start(bf16[128,768]{1,0:T(8,128)(2,1)S(1)} %copy-done.30), channel_id=1, source_target_pairs={{0,2},{1,3},{4,6},{5,7},{8,10},{9,11},{12,14},{13,15},{16,18},{17,... | collective-permute-start | bytes 589832 | tf_op jit(solution)/shard_map/ppermute | solution.py:884
  156.4 10.9 %shard_map.318 = (bf16[512,1024]{1,0:T(8,128)(2,1)}, bf16[512,768]{1,0:T(8,128)(2,1)}, f32[512,768]{1,0:T(8,128)}, bf16[512,768]{1,0:T(8,128)(2,1)}, bf16[5,128,...) custom-call(s32[4]{0:T(128)S(1)} %pad_add_fusion.refs_0_, bf16[528,1536]{1,0:T(8,128)(2,1)} %get-tuple-element.212.refs_1_.refs_0_, ...), custom_call_target="tpu_custom_call" | custom-call | flops 1000 | bytes 1000 | tf_op jit(solution)/shard_map/pallas_call | solution.py:826
  171.4 10.7 %collective-permute-start.23 = (bf16[128,1664]{1,0:T(8,128)(2,1)S(1)}, bf16[128,1664]{1,0:T(8,128)(2,1)S(1)}, u32[]{:S(2)}, u32[]{:S(2)}) collective-permute-start(bf16[128,1664]{1,0:T(8,128)(2,1)S(1)} %get-tuple-element.232.refs_17_), channel_id=1, source_target_pairs={{0,1},{1,0},{2,3},{3,2},{4,5},{5,4},{6,7},{7,6},{8,9},{9,8},{10,11... | collective-permute-start | bytes 1277960 | tf_op jit(solution)/shard_map/ppermute | solution.py:884
  182.8 11.1 %shard_map.321 = (bf16[512,1024]{1,0:T(8,128)(2,1)}, bf16[512,768]{1,0:T(8,128)(2,1)}, f32[512,768]{1,0:T(8,128)}, bf16[512,768]{1,0:T(8,128)(2,1)}, bf16[5,128,...) custom-call(s32[4]{0:T(128)S(1)} %pad_add_fusion.refs_0_, bf16[528,1536]{1,0:T(8,128)(2,1)} %get-tuple-element.234.refs_1_.refs_2_.refs_3_, ...), custom_call_target="tpu_custom_call" | custom-call | flops 1000 | bytes 1000 | tf_op jit(solution)/shard_map/pallas_call | solution.py:826
  201.5 7.6 %collective-permute-done.24.refs_2_ = bf16[128,1536]{1,0:T(8,128)(2,1)S(1)} collective-permute-done((bf16[128,1536]{1,0:T(8,128)(2,1)S(1)}, bf16[128,1536]{1,0:T(8,128)(2,1)S(1)}, u32[]{:S(2)}, u32[]{:S(2)}) %collective-permute-start.24) | collective-permute-done | bytes 393248 | tf_op jit(solution)/shard_map/ppermute | solution.py:884
  211.8 11.7 %shard_map.325 = (bf16[528,1536]{1,0:T(8,128)(2,1)}, bf16[528,1152]{1,0:T(8,128)(2,1)}, f32[16,1024]{1,0:T(8,128)}, bf16[512,1024]{1,0:T(8,128)(2,1)}, f32[512,2...) custom-call(s32[4]{0:T(128)S(1)} %pad_add_fusion.refs_0_, ...), custom_call_target="tpu_custom_call" | custom-call | flops 1000 | bytes 1000 | tf_op jit(solution)/shard_map/pallas_call | solution.py:826
  227.2 9.4 %collective-permute-done.32.refs_2_ = bf16[128,1536]{1,0:T(8,128)(2,1)S(1)} collective-permute-done((bf16[128,1536]{1,0:T(8,128)(2,1)S(1)}, bf16[128,1536]{1,0:T(8,128)(2,1)S(1)}, u32[]{:S(2)}, u32[]{:S(2)}) %collective-permute-start.32) | collective-permute-done | bytes 393248 | tf_op jit(solution)/shard_map/ppermute | solution.py:884
  240.4 10.9 %collective-permute-start.30 = (f32[8,1024]{1,0:T(8,128)S(1)}, f32[8,1024]{1,0:T(8,128)S(1)}, u32[]{:S(2)}, u32[]{:S(2)}) collective-permute-start(f32[8,1024]{1,0:T(8,128)S(1)} %get-tuple-element.251), channel_id=1, source_target_pairs={{0,2},{1,3},{4,6},{5,7},{8,10},{9,11},{12,14},{13,15},{16,18},{17,... | collective-permute-start | bytes 98312 | tf_op jit(solution)/shard_map/ppermute | solution.py:884
  251.4 11.4 %shard_map.328 = (bf16[528,1536]{1,0:T(8,128)(2,1)}, bf16[528,1152]{1,0:T(8,128)(2,1)}, f32[16,1024]{1,0:T(8,128)}, bf16[512,1024]{1,0:T(8,128)(2,1)}, f32[512,2...) custom-call(s32[4]{0:T(128)S(1)} %pad_add_fusion.refs_0_, ...), custom_call_target="tpu_custom_call" | custom-call | flops 1000 | bytes 1000 | tf_op jit(solution)/shard_map/pallas_call | solution.py:826
  266.8 10.9 %shard_map.330 = (bf16[512,1024]{1,0:T(8,128)(2,1)}, bf16[512,768]{1,0:T(8,128)(2,1)}, f32[512,768]{1,0:T(8,128)}, bf16[512,768]{1,0:T(8,128)(2,1)}, bf16[5,128,...) custom-call(s32[4]{0:T(128)S(1)} %pad_add_fusion.refs_0_, bf16[528,1536]{1,0:T(8,128)(2,1)} %get-tuple-element.243.refs_1_.refs_0_, ...), custom_call_target="tpu_custom_call" | custom-call | flops 1000 | bytes 1000 | tf_op jit(solution)/shard_map/pallas_call | solution.py:826
  282.1 10.8 %shard_map.333 = (bf16[512,1024]{1,0:T(8,128)(2,1)}, bf16[512,768]{1,0:T(8,128)(2,1)}, f32[512,768]{1,0:T(8,128)}, bf16[512,768]{1,0:T(8,128)(2,1)}, bf16[5,128,...) custom-call(s32[4]{0:T(128)S(1)} %pad_add_fusion.refs_0_, bf16[528,1536]{1,0:T(8,128)(2,1)} %get-tuple-element.267.refs_1_.refs_2_, ...), custom_call_target="tpu_custom_call" | custom-call | flops 1000 | bytes 1000 | tf_op jit(solution)/shard_map/pallas_call | solution.py:826
  302.3 8.4 %collective-permute-done.44.refs_2_ = bf16[128,1664]{1,0:T(8,128)(2,1)S(1)} collective-permute-done((bf16[128,1664]{1,0:T(8,128)(2,1)S(1)}, bf16[128,1664]{1,0:T(8,128)(2,1)S(1)}, u32[]{:S(2)}, u32[]{:S(2)}) %collective-permute-start.44) | collective-permute-done | bytes 426016 | tf_op jit(solution)/shard_map/ppermute | solution.py:884
  312.0 7.9 %collective-permute-done.42.refs_1_ = bf16[128,1664]{1,0:T(8,128)(2,1)S(1)} collective-permute-done((bf16[128,1664]{1,0:T(8,128)(2,1)S(1)}, bf16[128,1664]{1,0:T(8,128)(2,1)S(1)}, u32[]{:S(2)}, u32[]{:S(2)}) %collective-permute-start.42) | collective-permute-done | bytes 426016 | tf_op jit(solution)/shard_map/ppermute | solution.py:884
  324.6 8.1 %shard_map.338 = (bf16[512,1536]{1,0:T(8,128)(2,1)}, bf16[512,768]{1,0:T(8,128)(2,1)}, bf16[528,768]{1,0:T(8,128)(2,1)}, f32[8,768]{1,0:T(8,128)S(1)}, bf16[128,768]{1,0:T(8,128)(2,1)S(1)}) custom-call(s32[4]{0:T(128)S(1)} %pad_add_fusion.refs_0_, bf16[128,1664]{1,0:T(8,128)(2,1)S(1)} %get-tuple-element.274.refs_3_.refs_1_, ...), custom_call_target="tpu_custom_call" | custom-call | flops 1000 | bytes 1000 | tf_op jit(solution)/shard_map/pallas_call | solution.py:826
  336.8 8.1 %shard_map.340 = (bf16[512,1536]{1,0:T(8,128)(2,1)}, bf16[512,768]{1,0:T(8,128)(2,1)}, bf16[528,768]{1,0:T(8,128)(2,1)}, f32[8,768]{1,0:T(8,128)S(1)}, bf16[128,768]{1,0:T(8,128)(2,1)S(1)}) custom-call(s32[4]{0:T(128)S(1)} %pad_add_fusion.refs_0_, bf16[128,1664]{1,0:T(8,128)(2,1)S(1)} %get-tuple-element.282.refs_14_.refs_1_, ...), custom_call_target="tpu_custom_call" | custom-call | flops 1000 | bytes 1000 | tf_op jit(solution)/shard_map/pallas_call | solution.py:826
  348.9 11.3 %shard_map.342.refs_0_ = bf16[1536,1536]{1,0:T(8,128)(2,1)} custom-call(bf16[528,1536]{1,0:T(8,128)(2,1)} %get-tuple-element.243.refs_1_.refs_0_, bf16[528,768]{1,0:T(8,128)(2,1)} %get-tuple-element.283.refs_1_.refs_3_, bf16[528,1536]{1,0:T(8,128)(2,1)} %get-tuple-element.267.refs_1_.refs_2_, bf16[528,768]{1,0:T(8,128)(2,1)} %get-tuple-element.293.refs_3_, ...), custom_call_target="tpu_custom_call" | custom-call | flops 1000 | bytes 1000 | tf_op jit(solution)/shard_map/pallas_call | solution.py:826
  363.9 21.0 %shard_map.344 = (bf16[528,1152]{1,0:T(8,128)(2,1)}, f32[8,1024]{1,0:T(8,128)S(1)}, f32[8,128]{1,0:T(8,128)S(1)}, f32[528,1536]{1,0:T(8,128)S(1)}) custom-call(s32[4]{0:T(128)S(1)} %pad_add_fusion.refs_0_, bf16[1536,1152]{1,0:T(8,128)(2,1)} %all-gather.9.cloned.1.call-done.refs_5_.refs_1_, ...), custom_call_target="tpu_custom_call" | custom-call | flops 1000 | bytes 1000 | tf_op jit(solution)/shard_map/pallas_call | solution.py:826
  390.7 20.2 %shard_map.347 = (bf16[528,1152]{1,0:T(8,128)(2,1)}, f32[8,1024]{1,0:T(8,128)S(1)}, f32[8,128]{1,0:T(8,128)S(1)}, f32[528,1536]{1,0:T(8,128)S(1)}) custom-call(s32[4]{0:T(128)S(1)} %pad_add_fusion.refs_0_, bf16[1536,1152]{1,0:T(8,128)(2,1)} %all-gather.9.cloned.1.call-done.refs_5_.refs_1_, ...), custom_call_target="tpu_custom_call" | custom-call | flops 1000 | bytes 1000 | tf_op jit(solution)/shard_map/pallas_call | solution.py:826
  420.8 10.7 %shard_map.351.refs_0_ = bf16[1536,1152]{1,0:T(8,128)(2,1)} custom-call(bf16[528,1536]{1,0:T(8,128)(2,1)} %get-tuple-element.243.refs_1_.refs_0_, bf16[528,1152]{1,0:T(8,128)(2,1)} %get-tuple-element.318.refs_1_, bf16[528,1536]{1,0:T(8,128)(2,1)} %get-tuple-element.267.refs_1_.refs_2_, bf16[528,1152]{1,0:T(8,128)(2,1)} %get-tuple-element.319.refs_3_, ...), custom_call_target="tpu_custom_call" | custom-call | flops 1000 | bytes 1000 | tf_op jit(solution)/shard_map/pallas_call | solution.py:826
  451.2 9.1 %shard_map.355 = (bf16[512,1536]{1,0:T(8,128)(2,1)}, bf16[512,768]{1,0:T(8,128)(2,1)}, bf16[528,768]{1,0:T(8,128)(2,1)}, f32[8,768]{1,0:T(8,128)S(1)}, bf16[128,768]{1,0:T(8,128)(2,1)S(1)}) custom-call(s32[4]{0:T(128)S(1)} %pad_add_fusion.refs_0_, bf16[128,1664]{1,0:T(8,128)(2,1)S(1)} %copy-done.8, bf16[128,1664]{1,0:T(8,128)(2,1)S(1)} %copy-done.13, ...), custom_call_target="tpu_custom_call" | custom-call | flops 1000 | bytes 1000 | tf_op jit(solution)/shard_map/pallas_call | solution.py:826
  463.7 8.2 %shard_map.357 = (bf16[512,1536]{1,0:T(8,128)(2,1)}, bf16[512,768]{1,0:T(8,128)(2,1)}, bf16[528,768]{1,0:T(8,128)(2,1)}, f32[8,768]{1,0:T(8,128)S(1)}, bf16[128,768]{1,0:T(8,128)(2,1)S(1)}) custom-call(s32[4]{0:T(128)S(1)} %pad_add_fusion.refs_0_, bf16[128,1664]{1,0:T(8,128)(2,1)S(1)} %get-tuple-element.321.refs_14_.refs_1_, ...), custom_call_target="tpu_custom_call" | custom-call | flops 1000 | bytes 1000 | tf_op jit(solution)/shard_map/pallas_call | solution.py:826
  475.0 11.2 %shard_map.359.refs_0_ = bf16[1536,1536]{1,0:T(8,128)(2,1)} custom-call(bf16[528,1536]{1,0:T(8,128)(2,1)} %get-tuple-element.212.refs_1_.refs_0_, bf16[528,768]{1,0:T(8,128)(2,1)} %get-tuple-element.322.refs_1_.refs_3_, bf16[528,1536]{1,0:T(8,128)(2,1)} %get-tuple-element.234.refs_1_.refs_2_.refs_3_, bf16[528,768]{1,0:T(8,128)(2,1)} %get-tuple-element.332.refs_3_, ...), custom_call_target="tpu_custom_call" | custom-call | flops 1000 | bytes 1000 | tf_op jit(solution)/shard_map/pallas_call | solution.py:826
  491.7 20.2 %shard_map.361 = (bf16[528,1152]{1,0:T(8,128)(2,1)}, f32[8,1024]{1,0:T(8,128)S(1)}, f32[8,128]{1,0:T(8,128)S(1)}, f32[528,1536]{1,0:T(8,128)S(1)}) custom-call(s32[4]{0:T(128)S(1)} %pad_add_fusion.refs_0_, bf16[1536,1152]{1,0:T(8,128)(2,1)} %all-gather.5.cloned.1.call-done.refs_5_.refs_1_, ...), custom_call_target="tpu_custom_call" | custom-call | flops 1000 | bytes 1000 | tf_op jit(solution)/shard_map/pallas_call | solution.py:826
  528.0 20.8 %shard_map.365 = (bf16[528,1152]{1,0:T(8,128)(2,1)}, f32[8,1024]{1,0:T(8,128)S(1)}, f32[8,128]{1,0:T(8,128)S(1)}, f32[528,1536]{1,0:T(8,128)S(1)}) custom-call(s32[4]{0:T(128)S(1)} %pad_add_fusion.refs_0_, bf16[1536,1152]{1,0:T(8,128)(2,1)} %all-gather.5.cloned.1.call-done.refs_5_.refs_1_, ...), custom_call_target="tpu_custom_call" | custom-call | flops 1000 | bytes 1000 | tf_op jit(solution)/shard_map/pallas_call | solution.py:826
  556.0 10.9 %shard_map.369 = (bf16[384,256]{1,0:T(8,128)(2,1)S(1)}, bf16[384,256]{1,0:T(8,128)(2,1)S(1)}, bf16[384,256]{1,0:T(8,128)(2,1)}, bf16[384,256]{1,0:T(8,128)(2,1)}...) custom-call(s32[4]{0:T(128)S(1)} %pad_add_fusion.refs_0_, ...), custom_call_target="tpu_custom_call" | custom-call | flops 1000 | bytes 1000 | tf_op jit(solution)/shard_map/pallas_call | solution.py:826
  587.5 8.6 %collective-permute-start.85 = (bf16[192,1536]{1,0:T(8,128)(2,1)S(1)}, bf16[192,1536]{1,0:T(8,128)(2,1)S(1)}, u32[]{:S(2)}, u32[]{:S(2)}) collective-permute-start(bf16[192,1536]{1,0:T(8,128)(2,1)S(1)} %get-tuple-element.363), channel_id=1, source_target_pairs={{0,0},{4,1},{1,2},{5,3},{2,4},{6,5},{3,6},{7,7},{8,8},{12,9},{9,10... | collective-permute-start | bytes 1769480 | tf_op jit(solution)/shard_map/ppermute | solution.py:887
  607.9 9.3 %collective-permute-done.88.refs_3_ = bf16[384,896]{1,0:T(8,128)(2,1)} collective-permute-done((bf16[384,896]{1,0:T(8,128)(2,1)}, bf16[384,896]{1,0:T(8,128)(2,1)}, u32[]{:S(2)}, u32[]{:S(2)}) %collective-permute-start.88) | collective-permute-done | bytes 688160 | tf_op jit(solution)/shard_map/ppermute | solution.py:884
  655.4 9.6 %collective-permute-done.93.refs_2_ = bf16[192,896]{1,0:T(8,128)(2,1)S(1)} collective-permute-done((bf16[192,896]{1,0:T(8,128)(2,1)S(1)}, bf16[192,896]{1,0:T(8,128)(2,1)S(1)}, u32[]{:S(2)}, u32[]{:S(2)}) %collective-permute-start.93) | collective-permute-done | bytes 344096 | tf_op jit(solution)/shard_map/ppermute | solution.py:887
  (589 shorter events, 284.6 us)
Async XLA Ops:
  7.2 94.6 %all-gather.5.cloned.1.call-start = ((), (), s32[]{:S(2)}) async-start(), calls=%async_computation.3 | async-start | bytes 4423680 | tf_op jit(solution)/shard_map/all_gather | solution.py:970
  27.0 128.8 %all-gather.7.cloned.1.call-start = ((), (), s32[]{:S(2)}) async-start(), calls=%async_computation.4 | async-start | bytes 5898240 | tf_op jit(solution)/shard_map/all_gather | solution.py:970
  28.3 38.9 %collective-permute-start.10 = (bf16[192,1536]{1,0:T(8,128)(2,1)S(1)}, bf16[192,1536]{1,0:T(8,128)(2,1)S(1)}, u32[]{:S(2)}, u32[]{:S(2)}) collective-permute-start(bf16[192,1536]{1,0:T(8,128)(2,1)S(1)} %shard_map.309.refs_7_), channel_id=1, source_target_pairs={{0,2},{1,6},{2,3},{3,7},{4,0},{5,4},{6,1},{7,5},{8,10},{9,14},{10,... | collective-permute-start | bytes 1769480 | tf_op jit(solution)/shard_map/ppermute | solution.py:884
  29.1 38.0 %collective-permute-start.9 = (bf16[192,1536]{1,0:T(8,128)(2,1)S(1)}, bf16[192,1536]{1,0:T(8,128)(2,1)S(1)}, u32[]{:S(2)}, u32[]{:S(2)}) collective-permute-start(bf16[192,1536]{1,0:T(8,128)(2,1)S(1)} %shard_map.309.refs_7_), channel_id=1, source_target_pairs={{0,0},{1,4},{2,1},{3,5},{4,2},{5,6},{6,3},{7,7},{8,8},{9,12},{10,9... | collective-permute-start | bytes 1769480 | tf_op jit(solution)/shard_map/ppermute | solution.py:884
  41.4 25.7 %collective-permute-start.1 = (bf16[128,1536]{1,0:T(8,128)(2,1)S(1)}, bf16[128,1536]{1,0:T(8,128)(2,1)S(1)}, u32[]{:S(2)}, u32[]{:S(2)}) collective-permute-start(bf16[128,1536]{1,0:T(8,128)(2,1)S(1)} %get-tuple-element.210.refs_2_.refs_3_.refs_1_), channel_id=1, source_target_pairs={{0,1},{1,0},{2,3},{3,2},{4,5},{5,4},{6,7},{7,6},{8,9},{9,8},{10,11... | collective-permute-start | bytes 1179656 | tf_op jit(solution)/shard_map/ppermute | solution.py:884
  69.6 142.3 %all-gather.9.cloned.1.call-start = ((), (), s32[]{:S(2)}) async-start(), calls=%async_computation.5 | async-start | bytes 4423680 | tf_op jit(solution)/shard_map/all_gather | solution.py:970
  92.5 42.9 %collective-permute-start.15 = (bf16[192,2432]{1,0:T(8,128)(2,1)S(1)}, bf16[192,2432]{1,0:T(8,128)(2,1)S(1)}, u32[]{:S(2)}, u32[]{:S(2)}) collective-permute-start(bf16[192,2432]{1,0:T(8,128)(2,1)S(1)} %shard_map.311.refs_6_), channel_id=1, source_target_pairs={{0,0},{1,4},{2,1},{3,5},{4,2},{5,6},{6,3},{7,7},{8,8},{9,12},{10,9... | collective-permute-start | bytes 2801672 | tf_op jit(solution)/shard_map/ppermute | solution.py:884
  97.1 38.3 %collective-permute-start.16 = (bf16[192,2432]{1,0:T(8,128)(2,1)S(1)}, bf16[192,2432]{1,0:T(8,128)(2,1)}, u32[]{:S(2)}, u32[]{:S(2)}) collective-permute-start(bf16[192,2432]{1,0:T(8,128)(2,1)S(1)} %shard_map.311.refs_6_), channel_id=1, source_target_pairs={{0,2},{1,6},{2,3},{3,7},{4,0},{5,4},{6,1},{7,5},{8,10},{9,14},{10,... | collective-permute-start | bytes 2801672 | tf_op jit(solution)/shard_map/ppermute | solution.py:884
  138.3 128.5 %all-gather.11.cloned.1.call-start = ((), (), s32[]{:S(2)}) async-start(), calls=%async_computation.6 | async-start | bytes 5898240 | tf_op jit(solution)/shard_map/all_gather | solution.py:970
  138.8 299.1 %reduce-scatter.4.cloned.1.call-start = ((), (), s32[]{:S(2)}) async-start(), calls=%async_computation.7 | async-start | bytes 5898240 | tf_op jit(solution)/shard_map/reduce_scatter | solution.py:1251
  139.2 28.1 %collective-permute-start.19 = (bf16[128,768]{1,0:T(8,128)(2,1)S(1)}, bf16[128,768]{1,0:T(8,128)(2,1)S(1)}, u32[]{:S(2)}, u32[]{:S(2)}) collective-permute-start(bf16[128,768]{1,0:T(8,128)(2,1)S(1)} %copy-done.30), channel_id=1, source_target_pairs={{0,2},{1,3},{4,6},{5,7},{8,10},{9,11},{12,14},{13,15},{16,18},{17,... | collective-permute-start | bytes 589832 | tf_op jit(solution)/shard_map/ppermute | solution.py:884
  199.7 23.9 %collective-permute-start.28 = (bf16[128,1664]{1,0:T(8,128)(2,1)S(1)}, bf16[128,1664]{1,0:T(8,128)(2,1)S(1)}, u32[]{:S(2)}, u32[]{:S(2)}) collective-permute-start(bf16[128,1664]{1,0:T(8,128)(2,1)S(1)} %get-tuple-element.242.refs_11_), channel_id=1, source_target_pairs={{0,1},{1,0},{2,3},{3,2},{4,5},{5,4},{6,7},{7,6},{8,9},{9,8},{10,11... | collective-permute-start | bytes 1277960 | tf_op jit(solution)/shard_map/ppermute | solution.py:884
  226.5 24.8 %collective-permute-start.33 = (bf16[128,1536]{1,0:T(8,128)(2,1)S(1)}, bf16[128,1536]{1,0:T(8,128)(2,1)S(1)}, u32[]{:S(2)}, u32[]{:S(2)}) collective-permute-start(bf16[128,1536]{1,0:T(8,128)(2,1)S(1)} %get-tuple-element.256.refs_1_.refs_11_), channel_id=1, source_target_pairs={{0,4},{1,5},{2,6},{3,7},{4,0},{5,1},{6,2},{7,3},{8,12},{9,13},{10,... | collective-permute-start | bytes 1179656 | tf_op jit(solution)/shard_map/ppermute | solution.py:884
  237.8 25.0 %collective-permute-start.29 = (bf16[128,768]{1,0:T(8,128)(2,1)S(1)}, bf16[128,768]{1,0:T(8,128)(2,1)S(1)}, u32[]{:S(2)}, u32[]{:S(2)}) collective-permute-start(bf16[128,768]{1,0:T(8,128)(2,1)S(1)} %get-tuple-element.250.refs_4_.refs_6_), channel_id=1, source_target_pairs={{0,2},{1,3},{4,6},{5,7},{8,10},{9,11},{12,14},{13,15},{16,18},{17,... | collective-permute-start | bytes 589832 | tf_op jit(solution)/shard_map/ppermute | solution.py:884
  360.2 157.7 %reduce-scatter.6.cloned.1.call-start = ((), (), s32[]{:S(2)}) async-start(), calls=%async_computation.8 | async-start | bytes 4423680 | tf_op jit(solution)/shard_map/reduce_scatter | solution.py:1251
  360.2 24.6 %collective-permute-start.51 = (bf16[128,768]{1,0:T(8,128)(2,1)S(1)}, bf16[128,768]{1,0:T(8,128)(2,1)S(1)}, u32[]{:S(2)}, u32[]{:S(2)}) collective-permute-start(bf16[128,768]{1,0:T(8,128)(2,1)S(1)} %shard_map.341.refs_8_), channel_id=1, source_target_pairs={{2,0},{3,1},{6,4},{7,5},{10,8},{11,9},{14,12},{15,13},{18,16},{19,... | collective-permute-start | bytes 589832 | tf_op jit(solution)/shard_map/ppermute | solution.py:887
  436.8 146.2 %reduce-scatter.8.cloned.1.call-start = ((), (), s32[]{:S(2)}) async-start(), calls=%async_computation.9 | async-start | bytes 5898240 | tf_op jit(solution)/shard_map/reduce_scatter | solution.py:1251
  449.2 36.9 %collective-permute-start.67 = (bf16[192,1536]{1,0:T(8,128)(2,1)S(1)}, bf16[192,1536]{1,0:T(8,128)(2,1)S(1)}, u32[]{:S(2)}, u32[]{:S(2)}) collective-permute-start(bf16[192,1536]{1,0:T(8,128)(2,1)S(1)} %get-tuple-element.338), channel_id=1, source_target_pairs={{0,0},{4,1},{1,2},{5,3},{2,4},{6,5},{3,6},{7,7},{8,8},{12,9},{9,10... | collective-permute-start | bytes 1769480 | tf_op jit(solution)/shard_map/ppermute | solution.py:887
  488.1 23.8 %collective-permute-start.69 = (bf16[192,1536]{1,0:T(8,128)(2,1)S(1)}, bf16[192,1536]{1,0:T(8,128)(2,1)S(1)}, u32[]{:S(2)}, u32[]{:S(2)}) collective-permute-start(bf16[192,1536]{1,0:T(8,128)(2,1)S(1)} %copy-done.34), channel_id=1, source_target_pairs={{2,0},{6,1},{3,2},{7,3},{0,4},{4,5},{1,6},{5,7},{10,8},{14,9},{11,... | collective-permute-start | bytes 1769480 | tf_op jit(solution)/shard_map/ppermute | solution.py:887
  488.1 23.8 %collective-permute-start.68 = (bf16[128,768]{1,0:T(8,128)(2,1)S(1)}, bf16[128,768]{1,0:T(8,128)(2,1)S(1)}, u32[]{:S(2)}, u32[]{:S(2)}) collective-permute-start(bf16[128,768]{1,0:T(8,128)(2,1)S(1)} %shard_map.358.refs_8_), channel_id=1, source_target_pairs={{2,0},{3,1},{6,4},{7,5},{10,8},{11,9},{14,12},{15,13},{18,16},{19,... | collective-permute-start | bytes 589832 | tf_op jit(solution)/shard_map/ppermute | solution.py:887
  516.6 32.3 %collective-permute-start.71 = (bf16[128,1536]{1,0:T(8,128)(2,1)S(1)}, bf16[128,1536]{1,0:T(8,128)(2,1)S(1)}, u32[]{:S(2)}, u32[]{:S(2)}) collective-permute-start(bf16[128,1536]{1,0:T(8,128)(2,1)S(1)} %get-tuple-element.341), channel_id=1, source_target_pairs={{0,1},{1,0},{2,3},{3,2},{4,5},{5,4},{6,7},{7,6},{8,9},{9,8},{10,11... | collective-permute-start | bytes 1179656 | tf_op jit(solution)/shard_map/ppermute | solution.py:884
  519.8 29.0 %collective-permute-start.74 = (bf16[192,896]{1,0:T(8,128)(2,1)S(1)}, bf16[192,896]{1,0:T(8,128)(2,1)S(1)}, u32[]{:S(2)}, u32[]{:S(2)}) collective-permute-start(bf16[192,896]{1,0:T(8,128)(2,1)S(1)} %get-tuple-element.349), channel_id=1, source_target_pairs={{0,0},{4,1},{1,2},{5,3},{2,4},{6,5},{3,6},{7,7},{8,8},{12,9},{9,10... | collective-permute-start | bytes 1032200 | tf_op jit(solution)/shard_map/ppermute | solution.py:887
  522.5 26.3 %collective-permute-start.75 = (bf16[192,896]{1,0:T(8,128)(2,1)S(1)}, bf16[192,896]{1,0:T(8,128)(2,1)S(1)}, u32[]{:S(2)}, u32[]{:S(2)}) collective-permute-start(bf16[192,896]{1,0:T(8,128)(2,1)S(1)} %get-tuple-element.350), channel_id=1, source_target_pairs={{2,0},{6,1},{3,2},{7,3},{0,4},{4,5},{1,6},{5,7},{10,8},{14,9},{11,... | collective-permute-start | bytes 1032200 | tf_op jit(solution)/shard_map/ppermute | solution.py:887
  554.3 41.8 %collective-permute-start.77 = (bf16[128,1536]{1,0:T(8,128)(2,1)}, bf16[128,1536]{1,0:T(8,128)(2,1)}, u32[]{:S(2)}, u32[]{:S(2)}) collective-permute-start(bf16[128,1536]{1,0:T(8,128)(2,1)} %get-tuple-element.354), channel_id=1, source_target_pairs={{0,1},{1,0},{2,3},{3,2},{4,5},{5,4},{6,7},{7,6},{8,9},{9,8},{10,11... | collective-permute-start | bytes 1179656 | tf_op jit(solution)/shard_map/ppermute | solution.py:884
  581.9 25.9 %collective-permute-start.87 = (bf16[384,896]{1,0:T(8,128)(2,1)}, bf16[384,896]{1,0:T(8,128)(2,1)}, u32[]{:S(2)}, u32[]{:S(2)}) collective-permute-start(bf16[384,896]{1,0:T(8,128)(2,1)} %get-tuple-element.365), channel_id=1, source_target_pairs={{0,8},{1,9},{2,10},{3,11},{4,12},{5,13},{6,14},{7,15},{8,0},{9,1},... | collective-permute-start | bytes 2064392 | tf_op jit(solution)/shard_map/ppermute | solution.py:884
  582.7 34.5 %collective-permute-start.88 = (bf16[384,896]{1,0:T(8,128)(2,1)}, bf16[384,896]{1,0:T(8,128)(2,1)}, u32[]{:S(2)}, u32[]{:S(2)}) collective-permute-start(bf16[384,896]{1,0:T(8,128)(2,1)} %get-tuple-element.366), channel_id=1, source_target_pairs={{0,16},{1,17},{2,18},{3,19},{4,20},{5,21},{6,22},{7,23},{8,24},{9,... | collective-permute-start | bytes 2064392 | tf_op jit(solution)/shard_map/ppermute | solution.py:884
  585.0 34.7 %collective-permute-start.89 = (bf16[384,896]{1,0:T(8,128)(2,1)S(1)}, bf16[384,896]{1,0:T(8,128)(2,1)S(1)}, u32[]{:S(2)}, u32[]{:S(2)}) collective-permute-start(bf16[384,896]{1,0:T(8,128)(2,1)S(1)} %get-tuple-element.360.refs_2_), channel_id=1, source_target_pairs={{0,24},{1,25},{2,26},{3,27},{4,28},{5,29},{6,30},{7,31},{8,16},{9,... | collective-permute-start | bytes 2064392 | tf_op jit(solution)/shard_map/ppermute | solution.py:884
  587.5 32.4 %collective-permute-start.85 = (bf16[192,1536]{1,0:T(8,128)(2,1)S(1)}, bf16[192,1536]{1,0:T(8,128)(2,1)S(1)}, u32[]{:S(2)}, u32[]{:S(2)}) collective-permute-start(bf16[192,1536]{1,0:T(8,128)(2,1)S(1)} %get-tuple-element.363), channel_id=1, source_target_pairs={{0,0},{4,1},{1,2},{5,3},{2,4},{6,5},{3,6},{7,7},{8,8},{12,9},{9,10... | collective-permute-start | bytes 1769480 | tf_op jit(solution)/shard_map/ppermute | solution.py:887
  596.1 23.8 %collective-permute-start.86 = (bf16[192,1536]{1,0:T(8,128)(2,1)S(1)}, bf16[192,1536]{1,0:T(8,128)(2,1)S(1)}, u32[]{:S(2)}, u32[]{:S(2)}) collective-permute-start(bf16[192,1536]{1,0:T(8,128)(2,1)S(1)} %get-tuple-element.361.refs_11_), channel_id=1, source_target_pairs={{2,0},{6,1},{3,2},{7,3},{0,4},{4,5},{1,6},{5,7},{10,8},{14,9},{11,... | collective-permute-start | bytes 1769480 | tf_op jit(solution)/shard_map/ppermute | solution.py:887
  607.8 26.8 %collective-permute-start.43 = (f32[128,1536]{1,0:T(8,128)S(1)}, f32[128,1536]{1,0:T(8,128)S(1)}, u32[]{:S(2)}, u32[]{:S(2)}) collective-permute-start(f32[128,1536]{1,0:T(8,128)S(1)} %get-tuple-element.558), channel_id=1, source_target_pairs={{0,4},{1,5},{2,6},{3,7},{4,0},{5,1},{6,2},{7,3},{8,12},{9,13},{10,... | collective-permute-start | bytes 2359304 | tf_op jit(solution)/shard_map/ppermute | solution.py:884
  619.8 30.4 %collective-permute-start.84 = (f32[128,1536]{1,0:T(8,128)S(1)}, f32[128,1536]{1,0:T(8,128)S(1)}, u32[]{:S(2)}, u32[]{:S(2)}) collective-permute-start(f32[128,1536]{1,0:T(8,128)S(1)} %get-tuple-element.556), channel_id=1, source_target_pairs={{0,4},{1,5},{2,6},{3,7},{4,0},{5,1},{6,2},{7,3},{8,12},{9,13},{10,... | collective-permute-start | bytes 2359304 | tf_op jit(solution)/shard_map/ppermute | solution.py:884
  640.6 24.5 %collective-permute-start.94 = (bf16[192,896]{1,0:T(8,128)(2,1)S(1)}, bf16[192,896]{1,0:T(8,128)(2,1)S(1)}, u32[]{:S(2)}, u32[]{:S(2)}) collective-permute-start(bf16[192,896]{1,0:T(8,128)(2,1)S(1)} %get-tuple-element.374.refs_16_), channel_id=1, source_target_pairs={{2,0},{6,1},{3,2},{7,3},{0,4},{4,5},{1,6},{5,7},{10,8},{14,9},{11,... | collective-permute-start | bytes 1032200 | tf_op jit(solution)/shard_map/ppermute | solution.py:887
  (193 other events, 1918.9 us)
Sparse Core Ops, SparseCore 0:
  27.1 54.2 all-gather.4
  83.8 57.0 all-gather.6
  142.8 61.4 all-gather.8
  206.6 57.0 all-gather.10
  360.3 55.4 reduce-scatter.3
  436.9 49.7 reduce-scatter.5
  489.7 57.0 reduce-scatter.7
